TPU v7x, 512 devices: a whole 4x4x16 slice. The times are simulated.
512 devices in a mesh: seq: 128 (over y, z, x_lo), head: 4 (over x_hi, core).
Axes of the slice: x: 4 (x_hi: 2, x_lo: 2; x = x_hi * 2 + x_lo), y: 4, z: 16, core: 2. Of those that a mesh axis runs over, the one named last changes fastest.
Arguments:
- queries: bfloat16 [32768, 8192], P('seq', 'head'), may hold values from -40 to 40
- key_rows: bfloat16 [32768, 8192], P('seq', 'head'), may hold values from -20 to 20
- value_rows: bfloat16 [32768, 8192], P('seq', 'head'), may hold values from -8 to 8
Outputs:
- attended: bfloat16 [32768, 8192], P('seq', 'head')
All inputs are finite; a program needn't handle non-finite values.
Results may differ from a plain program's by a relative error of at most 0.0043.
Values may be sent and summed in bfloat16 or wider, within the bound.
No kernel may reach another device: no remote copies, remote signals or barrier semaphores. Data moves between devices by JAX's collectives and lax.ppermute only.
A program may use at most 128 MiB of HBM per device.

v0:
```python
from functools import reduce
import math

import jax
import jax.numpy as jnp
from jax import lax
from jax.sharding import Mesh
from jax.sharding import PartitionSpec as P

HEAD_DIM = 128
BLOCK = 128
POOL = 64
MID_REACH = 3
FAR_REACH = 9
SEQ = ("seq_0", "seq_1", "seq_2")


def for_sending(shard):
    return jax.tree.map(lambda a: a.astype(jnp.bfloat16) if a.dtype == jnp.float32 else a, shard)


def passed_along(block, axis, distance):
    devices = range(lax.axis_size(axis))
    route = [(i - distance, i) for i in devices if i - distance in devices]
    return lax.ppermute(block, axis, route)


def padded(cells, sides, width):
    for axis, dim in sides:
        count = lax.axis_size(axis)
        ends = count - 1
        head = lax.slice_in_dim(cells, 0, width, axis=dim)
        tail = lax.slice_in_dim(cells, cells.shape[dim] - width, cells.shape[dim], axis=dim)
        cells = jnp.concatenate(
            [
                lax.ppermute(tail, axis, [(i, (i + 1) % count) for i in range(ends)]),
                cells,
                lax.ppermute(head, axis, [((i + 1) % count, i) for i in range(ends)]),
            ],
            axis=dim,
        )
    return cells


def laid_out(pieces, dim):
    lengths = list(pieces.shape[1:])
    lengths[dim] *= pieces.shape[0]
    return jnp.moveaxis(pieces, 0, dim).reshape(lengths)


def stacked_from(shard, axes, turns):
    pieces = shard
    for k in turns:
        pieces = lax.all_gather(pieces, axes[k])
    done = turns[::-1]
    back = [done.index(k) for k in range(len(axes))]
    pieces = pieces.transpose(*back, *range(len(axes), pieces.ndim))
    return pieces.reshape(-1, *shard.shape)


def gathered_by_axis(shard, axes, turns, dim):
    return laid_out(stacked_from(shard, axes, turns), dim)


def pool_pairs(source):
    paired = source.astype(jnp.float32).reshape(
        source.shape[0], source.shape[1] // 2, 2, source.shape[2]
    )
    return (0.5 * (paired[:, :, 0] + paired[:, :, 1])).astype(jnp.bfloat16)


def pool_groups(source, group_rows):
    grouped = source.astype(jnp.float32).reshape(
        source.shape[0], source.shape[1] // group_rows, group_rows, source.shape[2]
    )
    return jnp.mean(grouped, axis=2).astype(jnp.bfloat16)


def keep_rows(piece, toward, kept_rows):
    if toward < 0:
        return piece[:, piece.shape[1] - kept_rows :]
    return piece[:, :kept_rows]


def reach_middle(source, toward, highest, kept_rows):
    collected = {}
    current = source
    for distance in range(1, highest + 1):
        sending = keep_rows(current, toward, kept_rows) if distance == highest else current
        current = jax.tree.map(
            lambda part, own: part.astype(own.dtype),
            passed_along(for_sending(sending), SEQ, -toward),
            sending,
        )
        collected[distance] = current
    return collected


def reach_far(anchor, anchor_at, toward, lowest, highest, kept_rows):
    collected = {}
    current = anchor
    for distance in range(anchor_at + 1, highest + 1):
        sending = keep_rows(current, toward, kept_rows) if distance == highest else current
        current = jax.tree.map(
            lambda part, own: part.astype(own.dtype),
            passed_along(for_sending(sending), SEQ, -toward),
            sending,
        )
        if distance >= lowest:
            collected[distance] = current
    return collected


def per_device(queries, key_rows, value_rows):
    rows_dev = queries.shape[0]
    blocks_dev = rows_dev // BLOCK
    total_rows = rows_dev * lax.axis_size(SEQ)
    total_blocks = total_rows // BLOCK
    me_index = lax.axis_index(SEQ)
    mid_top = (MID_REACH + blocks_dev - 1) // blocks_dev
    far_top = (FAR_REACH + blocks_dev - 1) // blocks_dev
    near_far = (MID_REACH + 1) // blocks_dev
    far_low = max(1, near_far)
    half_block = BLOCK // 2
    quarter_block = BLOCK // 4
    mid_blocks = MID_REACH - (mid_top - 1) * blocks_dev
    far_blocks = FAR_REACH - (far_top - 1) * blocks_dev
    mid_blocks = blocks_dev
    if far_top <= mid_top:
        far_blocks = blocks_dev
    stacked = jnp.stack((key_rows, value_rows))
    pair_two = pool_pairs(stacked)
    pair_four = pool_pairs(pair_two)
    pair_coarse = pool_groups(pair_four, POOL // 4)
    fine_window = padded(stacked, ((SEQ, 1),), BLOCK)
    lower_mid = reach_middle(pair_two, -1, mid_top, mid_blocks * half_block)
    upper_mid = reach_middle(pair_two, 1, mid_top, mid_blocks * half_block)
    lower_far = {
        distance: pool_pairs(lower_mid[distance])
        for distance in range(far_low, min(mid_top, far_top) + 1)
    }
    upper_far = {
        distance: pool_pairs(upper_mid[distance])
        for distance in range(far_low, min(mid_top, far_top) + 1)
    }
    lower_anchor = pool_pairs(lower_mid[mid_top])
    upper_anchor = pool_pairs(upper_mid[mid_top])
    lower_far.update(
        reach_far(lower_anchor, mid_top, -1, far_low, far_top, far_blocks * quarter_block)
    )
    upper_far.update(
        reach_far(upper_anchor, mid_top, 1, far_low, far_top, far_blocks * quarter_block)
    )
    coarse_all = gathered_by_axis(pair_coarse, SEQ, (2, 0, 1), 1)
    mid_parts = (
        [lower_mid[distance] for distance in range(mid_top, 0, -1)]
        + [pair_two]
        + [upper_mid[distance] for distance in range(1, mid_top + 1)]
    )
    mid_window = jnp.concatenate(mid_parts, axis=1)
    own_part = [pair_four] if near_far == 0 else []
    lower_window = jnp.concatenate(
        [lower_far[distance] for distance in range(far_top, far_low - 1, -1)] + own_part, axis=1
    )
    upper_window = jnp.concatenate(
        own_part + [upper_far[distance] for distance in range(far_low, far_top + 1)], axis=1
    )
    mid_side = (mid_top - 1) * blocks_dev + mid_blocks
    far_side = (far_top - 1) * blocks_dev + far_blocks
    coarse_block = POOL * jnp.arange(total_rows // POOL, dtype=jnp.int32) // BLOCK
    score_scale = 1.0 / math.sqrt(HEAD_DIM)
    mid_span = (MID_REACH - 1) * half_block
    far_span = (FAR_REACH - MID_REACH) * quarter_block

    def one_head(head_index, output):
        column = head_index * HEAD_DIM
        query_cols = lax.dynamic_slice_in_dim(queries, column, HEAD_DIM, 1).reshape(
            blocks_dev, BLOCK, HEAD_DIM
        )

        def head_cols(window_rows):
            sliced = lax.dynamic_slice_in_dim(window_rows, column, HEAD_DIM, 2)
            return (sliced[0], sliced[1])

        fine_pair = head_cols(fine_window)
        mid_pair = head_cols(mid_window)
        lower_pair = head_cols(lower_window)
        upper_pair = head_cols(upper_window)
        coarse_pair = head_cols(coarse_all)

        def block_attend(block_index, query_block):
            here = me_index * blocks_dev + block_index
            level_specs = [
                (fine_pair, block_index * BLOCK, 3 * BLOCK, here - 1, BLOCK, 0.0),
                (
                    mid_pair,
                    (mid_side + block_index - MID_REACH) * half_block,
                    mid_span,
                    here - MID_REACH,
                    half_block,
                    math.log(2.0),
                ),
                (
                    mid_pair,
                    (mid_side + block_index + 2) * half_block,
                    mid_span,
                    here + 2,
                    half_block,
                    math.log(2.0),
                ),
                (
                    lower_pair,
                    (far_side + block_index - FAR_REACH) * quarter_block,
                    far_span,
                    here - FAR_REACH,
                    quarter_block,
                    math.log(4.0),
                ),
                (
                    upper_pair,
                    (block_index + MID_REACH + 1 - near_far * blocks_dev) * quarter_block,
                    far_span,
                    here + MID_REACH + 1,
                    quarter_block,
                    math.log(4.0),
                ),
            ]
            level_items = []
            for pair_rows, anchor_row, span, first_block, unit_rows, log_size in level_specs:
                key_part = lax.dynamic_slice_in_dim(pair_rows[0], anchor_row, span, 0)
                value_part = lax.dynamic_slice_in_dim(pair_rows[1], anchor_row, span, 0)
                atom_block = first_block + jnp.arange(span, dtype=jnp.int32) // unit_rows
                allowed = (atom_block >= 0) & (atom_block < total_blocks)
                level_items.append((key_part, value_part, allowed, log_size))
            coarse_allowed = jnp.abs(coarse_block - here) > FAR_REACH
            level_items.append((coarse_pair[0], coarse_pair[1], coarse_allowed, math.log(POOL)))
            score_list = []
            for key_part, value_part, allowed, log_size in level_items:
                scores = (
                    jnp.einsum(
                        "qe,ke->qk", query_block, key_part, preferred_element_type=jnp.float32
                    )
                    * score_scale
                    + log_size
                )
                score_list.append(jnp.where(allowed[None, :], scores, -jnp.inf))
            row_top = reduce(jnp.maximum, [jnp.max(scores, axis=1) for scores in score_list])
            denominator = jnp.zeros((BLOCK,), jnp.float32)
            weighted = jnp.zeros((BLOCK, HEAD_DIM), jnp.float32)
            for scores, level_item in zip(score_list, level_items):
                exp_terms = jnp.exp(scores - row_top[:, None])
                denominator = denominator + jnp.sum(exp_terms, axis=1)
                weighted = weighted + jnp.dot(
                    exp_terms.astype(jnp.bfloat16),
                    level_item[1],
                    preferred_element_type=jnp.float32,
                )
            return (weighted / denominator[:, None]).astype(jnp.bfloat16)

        results = jax.vmap(block_attend)(jnp.arange(blocks_dev, dtype=jnp.int32), query_cols)
        return lax.dynamic_update_slice_in_dim(
            output, results.reshape(rows_dev, HEAD_DIM), column, 1
        )

    return lax.fori_loop(0, queries.shape[1] // HEAD_DIM, one_head, jnp.zeros_like(queries))


def solution(mesh):
    torus = Mesh(
        mesh.devices.reshape(4, 16, 2, mesh.shape["head"]), ("seq_0", "seq_1", "seq_2", "head")
    )
    in_specs = (P(SEQ, "head"), P(SEQ, "head"), P(SEQ, "head"))
    out_specs = P(SEQ, "head")
    return jax.shard_map(
        per_device, mesh=torus, in_specs=in_specs, out_specs=out_specs, check_vma=False
    )
```

profile of v0, /device:TPU:24, one launch (start us, length us, event | category | flops | bytes accessed | tf_op | source)
XLA Modules:
  0.0 481.4 jit_solution(9388738242841884608)
XLA Ops:
  6.5 1.8 stack.18
  10.1 1.9 copy-done
  15.1 4.6 all-gather
  19.7 15.4 %all-gather.1 = bf16[8,2,4,2048]{3,2,1,0:T(4,128)(2,1)} all-gather(bf16[2,2,4,2048]{3,2,1,0:T(4,128)(2,1)S(1)} %bitcast.258), channel_id=3, replica_groups=mesh['seq_0'=4,'seq_1'=16,'seq_2'=2,'head'=4] {'seq_0'}, dimensions={0}, use_global_device_ids=true | all-gather | bytes 327680 | tf_op jit(solution)/shard_map/all_gather | solution.py:54
  35.1 2.7 fusion.86
  37.8 8.9 %collective-permute-start.4 = (bf16[2,128,2048]{2,1,0:T(8,128)(2,1)S(1)}, bf16[2,128,2048]{2,1,0:T(8,128)(2,1)}, u32[]{:S(2)}, u32[]{:S(2)}) collective-permute-start(bf16[2,128,2048]{2,1,0:T(8,128)(2,1)S(1)} %fusion.86), channel_id=1, source_target_pairs={{4,0},{8,4},{12,8},{16,12},{20,16},{24,20},{28,24},{32,28},{36,32}... | collective-permute-start | bytes 3145736 | tf_op jit(solution)/shard_map/ppermute | solution.py:25
  46.8 1.9 collective-permute-start.2
  48.7 33.3 %collective-permute-done.4 = bf16[2,128,2048]{2,1,0:T(8,128)(2,1)} collective-permute-done((bf16[2,128,2048]{2,1,0:T(8,128)(2,1)S(1)}, bf16[2,128,2048]{2,1,0:T(8,128)(2,1)}, u32[]{:S(2)}, u32[]{:S(2)}) %collective-permute-start.4) | collective-permute-done | bytes 1048608 | tf_op jit(solution)/shard_map/ppermute | solution.py:25
  82.0 9.0 %collective-permute-start.5 = (bf16[2,128,2048]{2,1,0:T(8,128)(2,1)}, bf16[2,128,2048]{2,1,0:T(8,128)(2,1)S(1)}, u32[]{:S(2)}, u32[]{:S(2)}) collective-permute-start(bf16[2,128,2048]{2,1,0:T(8,128)(2,1)} %collective-permute-done.4), channel_id=1, source_target_pairs={{4,0},{8,4},{12,8},{16,12},{20,16},{24,20},{28,24},{32,28},{36,32}... | collective-permute-start | bytes 3145736 | tf_op jit(solution)/shard_map/ppermute | solution.py:25
  91.3 1.9 collective-permute-start.3
  94.7 1.9 collective-permute-start
  96.6 6.9 %collective-permute-start.1 = (bf16[2,128,2048]{2,1,0:T(8,128)(2,1)}, bf16[2,128,2048]{2,1,0:T(8,128)(2,1)}, u32[]{:S(2)}, u32[]{:S(2)}) collective-permute-start(bf16[2,128,2048]{2,1,0:T(8,128)(2,1)} %get-tuple-element.686), channel_id=1, source_target_pairs={{4,0},{8,4},{12,8},{16,12},{20,16},{24,20},{28,24},{32,28},{36,32}... | collective-permute-start | bytes 3145736 | tf_op jit(solution)/shard_map/ppermute | solution.py:38
  103.5 29.1 %collective-permute-done.5 = bf16[2,128,2048]{2,1,0:T(8,128)(2,1)S(1)} collective-permute-done((bf16[2,128,2048]{2,1,0:T(8,128)(2,1)}, bf16[2,128,2048]{2,1,0:T(8,128)(2,1)S(1)}, u32[]{:S(2)}, u32[]{:S(2)}) %collective-permute-start.5) | collective-permute-done | bytes 1048608 | tf_op jit(solution)/shard_map/ppermute | solution.py:25
  134.8 31.7 %collective-permute-start.9 = (bf16[2,64,2048]{2,0,1:T(2,128)(2,1)S(1)}, bf16[2,64,2048]{2,0,1:T(2,128)(2,1)S(1)}, u32[]{:S(2)}, u32[]{:S(2)}) collective-permute-start(bf16[2,64,2048]{2,0,1:T(2,128)(2,1)S(1)} %fusion.62), channel_id=1, source_target_pairs={{4,0},{8,4},{12,8},{16,12},{20,16},{24,20},{28,24},{32,28},{36,32}... | collective-permute-start | bytes 1572872 | tf_op jit(solution)/shard_map/ppermute | solution.py:25
  167.0 2.3 copy.46
  170.3 4.4 collective-permute-start.6
  174.7 14.8 %collective-permute-done = bf16[2,128,2048]{2,1,0:T(8,128)(2,1)} collective-permute-done((bf16[2,128,2048]{2,1,0:T(8,128)(2,1)}, bf16[2,128,2048]{2,1,0:T(8,128)(2,1)}, u32[]{:S(2)}, u32[]{:S(2)}) %collective-permute-start) | collective-permute-done | bytes 1048608 | tf_op jit(solution)/shard_map/ppermute | solution.py:36
  189.5 3.6 pad_maximum_fusion
  195.7 9.8 %collective-permute-start.10 = (bf16[2,64,2048]{2,0,1:T(2,128)(2,1)S(1)}, bf16[2,64,2048]{2,0,1:T(2,128)(2,1)S(1)}, u32[]{:S(2)}, u32[]{:S(2)}) collective-permute-start(bf16[2,64,2048]{2,0,1:T(2,128)(2,1)S(1)} %collective-permute-done.9), channel_id=1, source_target_pairs={{4,0},{8,4},{12,8},{16,12},{20,16},{24,20},{28,24},{32,28},{36,32}... | collective-permute-start | bytes 1572872 | tf_op jit(solution)/shard_map/ppermute | solution.py:25
  205.5 2.1 collective-permute-start.7
  208.1 5.6 %collective-permute-done.10 = bf16[2,64,2048]{2,0,1:T(2,128)(2,1)S(1)} collective-permute-done((bf16[2,64,2048]{2,0,1:T(2,128)(2,1)S(1)}, bf16[2,64,2048]{2,0,1:T(2,128)(2,1)S(1)}, u32[]{:S(2)}, u32[]{:S(2)}) %collective-permute-start.10) | collective-permute-done | bytes 524320 | tf_op jit(solution)/shard_map/ppermute | solution.py:25
  213.9 13.4 %collective-permute-start.11 = (bf16[2,32,2048]{2,0,1:T(2,128)(2,1)S(1)}, bf16[2,32,2048]{2,0,1:T(2,128)(2,1)S(1)}, u32[]{:S(2)}, u32[]{:S(2)}) collective-permute-start(bf16[2,32,2048]{2,0,1:T(2,128)(2,1)S(1)} %slice.321), channel_id=1, source_target_pairs={{4,0},{8,4},{12,8},{16,12},{20,16},{24,20},{28,24},{32,28},{36,32}... | collective-permute-start | bytes 786440 | tf_op jit(solution)/shard_map/ppermute | solution.py:25
  228.9 1.9 collective-permute-start.8
  231.2 3.7 pad_maximum_fusion.2
  234.9 9.6 %collective-permute-done.8 = bf16[2,32,2048]{2,0,1:T(2,128)(2,1)S(1)} collective-permute-done((bf16[2,32,2048]{2,0,1:T(2,128)(2,1)S(1)}, bf16[2,32,2048]{2,0,1:T(2,128)(2,1)S(1)}, u32[]{:S(2)}, u32[]{:S(2)}) %collective-permute-start.8) | collective-permute-done | bytes 262176 | tf_op jit(solution)/shard_map/ppermute | solution.py:25
  244.4 3.6 pad_maximum_fusion.1
  248.1 4.3 copy.50
  252.3 10.5 %copy.51 = bf16[2,128,4,2048]{3,0,2,1:T(2,128)(2,1)} copy(bf16[2,128,4,2048]{3,2,0,1:T(4,128)(2,1)S(1)} %bitcast.229) | data formatting | bytes 8388608 | tf_op jit(solution)/shard_map/transpose | solution.py:48
  264.0 210.6 %while.59 = (s32[]{:T(128)}, bf16[256,2048]{1,0:T(8,128)(2,1)}, s32[]{:T(128)}, bf16[256,2048]{1,0:T(8,128)(2,1)}, bf16[2,512,2048]{2,1,0:T(8,128)(2,1)}, /*inde...) while((s32[]{:T(128)}, bf16[256,2048]{1,0:T(8,128)(2,1)}, ...), condition=%wide.region_14.15_spmd.clone, body=%wide.region_1.14_spmd.clone.sunk | while | flops 204628032 | bytes 12840321 | solution.py:265
  310.6 1.7 constant_dynamic-slice_fusion.32
  415.9 1.7 constant_dynamic-slice_fusion.32
  442.3 1.7 constant_dynamic-slice_fusion.32
  (1717 shorter events, 240.2 us)
Async XLA Ops:
  6.5 2.2 copy-start.3
  6.5 241.6 %all-gather.5.cloned.1.call-start = ((), (), s32[]{:S(2)}) async-start(), calls=%async_computation | async-start | bytes 4456448 | tf_op jit(solution)/shard_map/all_gather | solution.py:54
  10.1 2.0 copy-start
  35.1 58.1 %copy-start.2 = (bf16[256,2048]{1,0:T(8,128)(2,1)S(1)}, bf16[256,2048]{1,0:T(8,128)(2,1)}, u32[]{:S(2)}) copy-start(bf16[256,2048]{1,0:T(8,128)(2,1)} %param.6) | copy-start | bytes 3145732
  37.8 44.2 %collective-permute-start.4 = (bf16[2,128,2048]{2,1,0:T(8,128)(2,1)S(1)}, bf16[2,128,2048]{2,1,0:T(8,128)(2,1)}, u32[]{:S(2)}, u32[]{:S(2)}) collective-permute-start(bf16[2,128,2048]{2,1,0:T(8,128)(2,1)S(1)} %fusion.86), channel_id=1, source_target_pairs={{4,0},{8,4},{12,8},{16,12},{20,16},{24,20},{28,24},{32,28},{36,32}... | collective-permute-start | bytes 3145736 | tf_op jit(solution)/shard_map/ppermute | solution.py:25
  46.8 44.5 %collective-permute-start.2 = (bf16[2,128,2048]{2,1,0:T(8,128)(2,1)S(1)}, bf16[2,128,2048]{2,1,0:T(8,128)(2,1)}, u32[]{:S(2)}, u32[]{:S(2)}) collective-permute-start(bf16[2,128,2048]{2,1,0:T(8,128)(2,1)S(1)} %fusion.86), channel_id=1, source_target_pairs={{0,4},{4,8},{8,12},{12,16},{16,20},{20,24},{24,28},{28,32},{32,36}... | collective-permute-start | bytes 3145736 | tf_op jit(solution)/shard_map/ppermute | solution.py:25
  82.0 50.6 %collective-permute-start.5 = (bf16[2,128,2048]{2,1,0:T(8,128)(2,1)}, bf16[2,128,2048]{2,1,0:T(8,128)(2,1)S(1)}, u32[]{:S(2)}, u32[]{:S(2)}) collective-permute-start(bf16[2,128,2048]{2,1,0:T(8,128)(2,1)} %collective-permute-done.4), channel_id=1, source_target_pairs={{4,0},{8,4},{12,8},{16,12},{20,16},{24,20},{28,24},{32,28},{36,32}... | collective-permute-start | bytes 3145736 | tf_op jit(solution)/shard_map/ppermute | solution.py:25
  91.3 75.7 %collective-permute-start.3 = (bf16[2,128,2048]{2,1,0:T(8,128)(2,1)}, bf16[2,128,2048]{2,1,0:T(8,128)(2,1)}, u32[]{:S(2)}, u32[]{:S(2)}) collective-permute-start(bf16[2,128,2048]{2,1,0:T(8,128)(2,1)} %collective-permute-done.2), channel_id=1, source_target_pairs={{0,4},{4,8},{8,12},{12,16},{16,20},{20,24},{24,28},{28,32},{32,36}... | collective-permute-start | bytes 3145736 | tf_op jit(solution)/shard_map/ppermute | solution.py:25
  94.7 94.8 %collective-permute-start = (bf16[2,128,2048]{2,1,0:T(8,128)(2,1)}, bf16[2,128,2048]{2,1,0:T(8,128)(2,1)}, u32[]{:S(2)}, u32[]{:S(2)}) collective-permute-start(bf16[2,128,2048]{2,1,0:T(8,128)(2,1)} %get-tuple-element.685), channel_id=1, source_target_pairs={{0,4},{4,8},{8,12},{12,16},{16,20},{20,24},{24,28},{28,32},{32,36}... | collective-permute-start | bytes 3145736 | tf_op jit(solution)/shard_map/ppermute | solution.py:36
  96.6 92.9 %collective-permute-start.1 = (bf16[2,128,2048]{2,1,0:T(8,128)(2,1)}, bf16[2,128,2048]{2,1,0:T(8,128)(2,1)}, u32[]{:S(2)}, u32[]{:S(2)}) collective-permute-start(bf16[2,128,2048]{2,1,0:T(8,128)(2,1)} %get-tuple-element.686), channel_id=1, source_target_pairs={{4,0},{8,4},{12,8},{16,12},{20,16},{24,20},{28,24},{32,28},{36,32}... | collective-permute-start | bytes 3145736 | tf_op jit(solution)/shard_map/ppermute | solution.py:38
  134.8 61.0 %collective-permute-start.9 = (bf16[2,64,2048]{2,0,1:T(2,128)(2,1)S(1)}, bf16[2,64,2048]{2,0,1:T(2,128)(2,1)S(1)}, u32[]{:S(2)}, u32[]{:S(2)}) collective-permute-start(bf16[2,64,2048]{2,0,1:T(2,128)(2,1)S(1)} %fusion.62), channel_id=1, source_target_pairs={{4,0},{8,4},{12,8},{16,12},{20,16},{24,20},{28,24},{32,28},{36,32}... | collective-permute-start | bytes 1572872 | tf_op jit(solution)/shard_map/ppermute | solution.py:25
  170.3 35.2 %collective-permute-start.6 = (bf16[2,64,2048]{2,0,1:T(2,128)(2,1)S(1)}, bf16[2,64,2048]{2,0,1:T(2,128)(2,1)S(1)}, u32[]{:S(2)}, u32[]{:S(2)}) collective-permute-start(bf16[2,64,2048]{2,0,1:T(2,128)(2,1)S(1)} %fusion.61), channel_id=1, source_target_pairs={{0,4},{4,8},{8,12},{12,16},{16,20},{20,24},{24,28},{28,32},{32,36}... | collective-permute-start | bytes 1572872 | tf_op jit(solution)/shard_map/ppermute | solution.py:25
  189.5 18.2 %copy-start.1 = (f32[2,128,2,2048]{3,1,2,0:T(8,128)S(1)}, f32[2,128,2,2048]{3,1,2,0:T(8,128)}, u32[]{:S(2)}) copy-start(f32[2,128,2,2048]{3,1,2,0:T(8,128)} %copy-done) | copy-start | bytes 12582916
  195.7 17.9 %collective-permute-start.10 = (bf16[2,64,2048]{2,0,1:T(2,128)(2,1)S(1)}, bf16[2,64,2048]{2,0,1:T(2,128)(2,1)S(1)}, u32[]{:S(2)}, u32[]{:S(2)}) collective-permute-start(bf16[2,64,2048]{2,0,1:T(2,128)(2,1)S(1)} %collective-permute-done.9), channel_id=1, source_target_pairs={{4,0},{8,4},{12,8},{16,12},{20,16},{24,20},{28,24},{32,28},{36,32}... | collective-permute-start | bytes 1572872 | tf_op jit(solution)/shard_map/ppermute | solution.py:25
  205.5 23.1 %collective-permute-start.7 = (bf16[2,64,2048]{2,0,1:T(2,128)(2,1)S(1)}, bf16[2,64,2048]{2,0,1:T(2,128)(2,1)S(1)}, u32[]{:S(2)}, u32[]{:S(2)}) collective-permute-start(bf16[2,64,2048]{2,0,1:T(2,128)(2,1)S(1)} %collective-permute-done.6), channel_id=1, source_target_pairs={{0,4},{4,8},{8,12},{12,16},{16,20},{20,24},{24,28},{28,32},{32,36}... | collective-permute-start | bytes 1572872 | tf_op jit(solution)/shard_map/ppermute | solution.py:25
  213.9 17.3 %collective-permute-start.11 = (bf16[2,32,2048]{2,0,1:T(2,128)(2,1)S(1)}, bf16[2,32,2048]{2,0,1:T(2,128)(2,1)S(1)}, u32[]{:S(2)}, u32[]{:S(2)}) collective-permute-start(bf16[2,32,2048]{2,0,1:T(2,128)(2,1)S(1)} %slice.321), channel_id=1, source_target_pairs={{4,0},{8,4},{12,8},{16,12},{20,16},{24,20},{28,24},{32,28},{36,32}... | collective-permute-start | bytes 786440 | tf_op jit(solution)/shard_map/ppermute | solution.py:25
  228.7 6.2 %copy-start.4 = (bf16[2,640,2048]{2,1,0:T(8,128)(2,1)}, bf16[2,640,2048]{2,1,0:T(8,128)(2,1)S(1)}, u32[]{:S(2)}) copy-start(bf16[2,640,2048]{2,1,0:T(8,128)(2,1)S(1)} %constant_dynamic-update-slice_fusion.1) | copy-start | bytes 15728644
  228.9 15.6 %collective-permute-start.8 = (bf16[2,32,2048]{2,0,1:T(2,128)(2,1)S(1)}, bf16[2,32,2048]{2,0,1:T(2,128)(2,1)S(1)}, u32[]{:S(2)}, u32[]{:S(2)}) collective-permute-start(bf16[2,32,2048]{2,0,1:T(2,128)(2,1)S(1)} %slice.318), channel_id=1, source_target_pairs={{0,4},{4,8},{8,12},{12,16},{16,20},{20,24},{24,28},{28,32},{32,36}... | collective-permute-start | bytes 786440 | tf_op jit(solution)/shard_map/ppermute | solution.py:25
Sparse Core Ops, SparseCore 0:
  35.2 97.4 all-gather.4
where the time goes:
time: 489 us; the launch traced here: 481 us
  local copies, waits for them, and re-layouts  167 us (34%)
  starting transfers between devices  94 us (19%)
  waiting for transfers between devices  93.5 us (19%)
  matrix products  45.9 us (9%)
  other arithmetic  34.7 us (7%)
  blocking collectives  19.9 us (4%)
  between operations  13.7 us (3%)
  loops' own time  12.9 us (3%)
    ppermute x10, starting transfers between devices, passed_along(): return lax.ppermute(block, axis, route)  85.1 us
    ppermute x10, waiting for transfers between devices, passed_along(): return lax.ppermute(block, axis, route)  78.7 us
    slice x32, local copies, waits for them, and re-layouts, head_cols(): return (sliced[0], sliced[1])  52.6 us
    squeeze x32, local copies, waits for them, and re-layouts, head_cols(): return (sliced[0], sliced[1])  32.4 us
    gather x640, local copies, waits for them, and re-layouts  23.6 us
    dot_general x96, matrix products, block_attend(): jnp.dot(exp_terms.astype(jnp.bfloat16), level_item[1], preferred_element_...  23.2 us
    dot_general x96, matrix products, block_attend(): jnp.einsum('qe,ke->qk', query_block, key_part, preferred_element_type=jnp...  22.7 us
    all_gather x2, blocking collectives, stacked_from(): pieces = lax.all_gather(pieces, axes[k])  19.9 us
  transfers between devices with their start and end apart: 13, of which 8 were waited for; matrix products, arithmetic and copies ran while one was open for 5% of the time, Pallas kernels for 0%

commit v1 on v0

v1 whole, which is shorter than its diff:
```python
import functools
import math

import jax
import jax.numpy as jnp
from jax import lax
from jax.experimental import pallas as pl
from jax.experimental.pallas import tpu as pltpu
from jax.sharding import Mesh
from jax.sharding import PartitionSpec as P

D = 128
BLOCK = 128
FAR_REACH = 9
SEQ = ("y", "z", "xl")
YZ = ("y", "z")
Z = "z"
BF = jnp.bfloat16
F32 = jnp.float32
SCALE = math.log2(math.e) / math.sqrt(D)


def halved(x, scratch):
    rows, cols = x.shape
    parts = []
    for c in range(cols // D):
        scratch[c, 0:rows] = x[:, c * D : (c + 1) * D]
        even = scratch[c, pl.ds(0, rows // 2, stride=2)]
        odd = scratch[c, pl.ds(1, rows // 2, stride=2)]
        parts.append((0.5 * (even + odd)).astype(BF))
    return parts[0] if len(parts) == 1 else jnp.concatenate(parts, axis=1)


def coarse_kernel(own_ref, send_ref, out_ref, scratch):
    pieces = []
    for ref in (own_ref, send_ref):
        four = halved(halved(ref[0].astype(F32), scratch).astype(F32), scratch)
        rows, cols = four.shape
        pieces.append(jnp.sum(four.astype(F32).reshape(rows // 16, 16, cols), axis=1) * (1.0 / 16))
    pieces.append(jnp.zeros((16 - 2 * (rows // 16), cols), F32))
    out_ref[0] = jnp.concatenate(pieces, axis=0).astype(BF)


def coarse_rows(own, send):
    _, rows, cols = own.shape
    width = 512
    return pl.pallas_call(
        coarse_kernel,
        grid=(2, cols // width),
        in_specs=[pl.BlockSpec((1, rows, width), lambda i, c: (i, 0, c))] * 2,
        out_specs=pl.BlockSpec((1, 16, width), lambda i, c: (i, 0, c)),
        out_shape=jax.ShapeDtypeStruct((2, 16, cols), BF),
        scratch_shapes=[pltpu.VMEM((width // D, rows, D), F32)],
        cost_estimate=pl.CostEstimate(flops=rows * cols * 8, bytes_accessed=8 * rows * cols, transcendentals=0),
    )(own, send)


def pool_kernel(own_ref, got_ref, up_ref, down_ref, mid_ref, far_ref, scratch):
    low = lax.axis_index("xl") == 0
    first = jnp.where(low, own_ref[0], got_ref[0])
    second = jnp.where(low, got_ref[0], own_ref[0])
    mid_first = halved(first.astype(F32), scratch)
    mid_second = halved(second.astype(F32), scratch)
    far_first = halved(mid_first.astype(F32), scratch)
    far_second = halved(mid_second.astype(F32), scratch)
    mid_ref[0, 0:128] = mid_first
    mid_ref[0, 128:256] = mid_second
    far_ref[0, 0:64] = far_first
    far_ref[0, 64:128] = far_second
    up_ref[0, 0:128] = second[128:256]
    up_ref[0, 128:192] = mid_first[64:128]
    up_ref[0, 192:256] = mid_second[0:64]
    up_ref[0, 256:288] = far_first[0:32]
    down_ref[0, 0:128] = first[0:128]
    down_ref[0, 128:192] = mid_first[64:128]
    down_ref[0, 192:256] = mid_second[0:64]
    down_ref[0, 256:288] = far_second[32:64]


def pooled(own, got):
    _, rows, cols = own.shape
    width = 512
    sizes = (288, 288, 256, 128)
    return pl.pallas_call(
        pool_kernel,
        grid=(2, cols // width),
        in_specs=[pl.BlockSpec((1, rows, width), lambda i, c: (i, 0, c))] * 2,
        out_specs=[pl.BlockSpec((1, n, width), lambda i, c: (i, 0, c)) for n in sizes],
        out_shape=[jax.ShapeDtypeStruct((2, n, cols), BF) for n in sizes],
        scratch_shapes=[pltpu.VMEM((width // D, rows, D), F32)],
        cost_estimate=pl.CostEstimate(flops=rows * cols * 8, bytes_accessed=16 * rows * cols, transcendentals=0),
    )(own, got)


def forward_kernel(below_ref, above_ref, up_ref, down_ref, near_ref, scratch):
    below, above = below_ref[0], above_ref[0]
    below_near = halved(below[0:128].astype(F32), scratch)
    above_near = halved(above[0:128].astype(F32), scratch)
    near_ref[0, 0:64] = below_near
    near_ref[0, 64:128] = above_near
    up_ref[0, 0:32] = below[256:288]
    up_ref[0, 32:128] = halved(jnp.concatenate([below[128:256], below_near], axis=0).astype(F32), scratch)
    down_ref[0, 0:96] = halved(jnp.concatenate([above_near, above[128:256]], axis=0).astype(F32), scratch)
    down_ref[0, 96:128] = above[256:288]


def forwarded(below, above):
    _, rows, cols = below.shape
    width = 512
    return pl.pallas_call(
        forward_kernel,
        grid=(2, cols // width),
        in_specs=[pl.BlockSpec((1, rows, width), lambda i, c: (i, 0, c))] * 2,
        out_specs=[pl.BlockSpec((1, 128, width), lambda i, c: (i, 0, c))] * 3,
        out_shape=[jax.ShapeDtypeStruct((2, 128, cols), BF)] * 3,
        scratch_shapes=[pltpu.VMEM((width // D, 192, D), F32)],
        cost_estimate=pl.CostEstimate(flops=2048 * cols, bytes_accessed=3000 * cols, transcendentals=0),
    )(below, above)


def attend_kernel(
    q_own, q_got, kv_own, kv_got, mid, far, below1, above1, up, down, near, below2, above2, below3, above3,
    coarse0, coarse1, coarse2, coarse3,
    own_out, send_out,
    kf, vf, km, vm, kr, vr, kc, vc, kfar, vfar, mask,
):
    low = lax.axis_index("xl") == 0
    y = lax.axis_index("y")
    ny, nz = lax.axis_size("y"), lax.axis_size(Z)
    zz = y * nz + lax.axis_index(Z)
    last = ny * nz - 1
    coarse_n = 4 * coarse0.shape[1]

    @pl.when(pl.program_id(0) == 0)
    def _():
        def flags(blocks, first, unit, ref):
            block = first + lax.broadcasted_iota(jnp.int32, (blocks * unit, D), 0) // unit + 4 * zz
            good = (block >= 0) & (block < 4 * (last + 1))
            ref[:, D : 2 * D] = jnp.where(good, 1.0, 0.0).astype(BF)

        flags(6, -1, 128, vf)
        flags(10, -3, 64, vm)
        flags(22, -9, 32, vr)
        vc[:, D : 2 * D] = jnp.ones((coarse_n, D), BF)
        for b in range(4):
            at = lax.broadcasted_iota(jnp.int32, (16, coarse_n), 1)
            turn = at // (8 * nz)
            other = (y + jnp.where(turn == 0, 0, jnp.where(turn == 1, ny - 1, jnp.where(turn == 2, 1, 2)))) % ny
            block = (other * nz + (at // 8) % nz) * 4 + (at % 8) // 2
            gap = jnp.abs(block - (4 * zz + b))
            mask[b * 16 : (b + 1) * 16, :] = jnp.where(gap > FAR_REACH, 1.0, 0.0).astype(BF)

    has = [zz >= n for n in range(4)]
    has_up = [zz <= last - n for n in range(4)]

    def pick(when_low, when_high, i, start, stop):
        return jnp.where(low, when_low[i, start:stop], when_high[i, start:stop])

    for i, (fine_w, mid_w, far_w) in enumerate(((kf, km, kr), (vf, vm, vr))):
        is_key = i == 0

        def put(ref, start, rows, present, fallback):
            n = rows.shape[0]
            ref[start : start + n, 0:D] = jnp.where(present, rows, fallback) if is_key else rows

        first, second = pick(kv_own, kv_got, i, 0, 256), pick(kv_got, kv_own, i, 0, 256)
        fine_w[128:384, 0:D] = first
        fine_w[384:640, 0:D] = second
        put(fine_w, 0, below1[i, 0:128], has[1], first[0:128])
        put(fine_w, 640, above1[i, 0:128], has_up[1], second[128:256])
        mid_w[192:448, 0:D] = mid[i]
        m0, m3 = mid[i, 0:64], mid[i, 192:256]
        put(mid_w, 0, below1[i, 128:192], has[1], m0)
        put(mid_w, 64, below1[i, 192:256], has[1], m0)
        put(mid_w, 128, near[i, 0:64], has[1], m0)
        put(mid_w, 448, near[i, 64:128], has_up[1], m3)
        put(mid_w, 512, above1[i, 128:192], has_up[1], m3)
        put(mid_w, 576, above1[i, 192:256], has_up[1], m3)
        far_w[288:416, 0:D] = far[i]
        f0, f3 = far[i, 0:32], far[i, 96:128]
        f0_4 = jnp.concatenate([f0] * 4, axis=0)
        f3_4 = jnp.concatenate([f3] * 4, axis=0)
        put(far_w, 0, below3[i], has[3], f0)
        put(far_w, 32, below2[i], has[2], f0_4)
        put(far_w, 160, up[i], has[1], f0_4)
        put(far_w, 416, down[i], has_up[1], f3_4)
        put(far_w, 544, above2[i], has_up[2], f3_4)
        put(far_w, 672, above3[i], has_up[3], f3)
    step = coarse_n // 4
    for t, part in enumerate((coarse0, coarse1, coarse2, coarse3)):
        kc[t * step : (t + 1) * step] = part[0]
        vc[t * step : (t + 1) * step, 0:D] = part[1]

    qo, qg = q_own[...], q_got[...]
    q_first = jnp.where(low, qo, qg)
    q_second = jnp.where(low, qg, qo)

    def scores(a, b):
        return lax.dot_general(a, b, (((1,), (1,)), ((), ())), preferred_element_type=F32)

    results = []
    for b in range(4):
        q = (q_first if b < 2 else q_second)[(b % 2) * 128 : (b % 2 + 1) * 128]
        kfar[0:192] = kr[b * 32 : b * 32 + 192]
        kfar[192:384] = kr[(b + 13) * 32 : (b + 13) * 32 + 192]
        vfar[0:192] = vr[b * 32 : b * 32 + 192]
        vfar[192:384] = vr[(b + 13) * 32 : (b + 13) * 32 + 192]
        mlo, mup = b * 64, (b + 5) * 64
        parts = [
            (kf[b * 128 : b * 128 + 384], vf[b * 128 : b * 128 + 384], 0.0, None),
            (km[mlo : mlo + 128], vm[mlo : mlo + 128], 1.0, None),
            (km[mup : mup + 128], vm[mup : mup + 128], 1.0, None),
            (kfar[...], vfar[...], 2.0, None),
            (kc[...], vc[...], 6.0, mask[b * 16 : b * 16 + 1, :]),
        ]
        all_scores = [scores(q, key) for key, _, _, _ in parts]
        tops = [
            jnp.max(s, axis=1, keepdims=True) * SCALE + size
            for s, (_, _, size, _) in zip(all_scores, parts)
        ]
        top = functools.reduce(jnp.maximum, tops)
        total = jnp.zeros((BLOCK, 2 * D), F32)
        for s, (_, value, size, keep) in zip(all_scores, parts):
            weights = jnp.exp2(s * SCALE - (top - size)).astype(BF)
            if keep is not None:
                weights = weights * keep
            total = total + jnp.dot(weights, value, preferred_element_type=F32)
        results.append((total[:, 0:D] / total[:, D : 2 * D]).astype(BF))
    out_first = jnp.concatenate(results[0:2], axis=0)
    out_second = jnp.concatenate(results[2:4], axis=0)
    own_out[...] = jnp.where(low, out_first, out_second)
    send_out[...] = jnp.where(low, out_second, out_first)


def attend(arrays):
    rows, cols = arrays[0].shape

    def spec(a):
        lead = a.shape[:-1]
        return pl.BlockSpec(lead + (D,), lambda h, n=len(lead): (0,) * n + (h,))

    coarse_n = 4 * arrays[-1].shape[1]
    out = jax.ShapeDtypeStruct((rows, cols), BF)
    return pl.pallas_call(
        attend_kernel,
        grid=(cols // D,),
        in_specs=[spec(a) for a in arrays],
        out_specs=[spec(out), spec(out)],
        out_shape=[out, out],
        scratch_shapes=[
            pltpu.VMEM((768, D), BF), pltpu.VMEM((768, 2 * D), BF),
            pltpu.VMEM((640, D), BF), pltpu.VMEM((640, 2 * D), BF),
            pltpu.VMEM((704, D), BF), pltpu.VMEM((704, 2 * D), BF),
            pltpu.VMEM((coarse_n, D), BF), pltpu.VMEM((coarse_n, 2 * D), BF),
            pltpu.VMEM((384, D), BF), pltpu.VMEM((384, 2 * D), BF),
            pltpu.VMEM((64, coarse_n), BF),
        ],
        compiler_params=pltpu.CompilerParams(vmem_limit_bytes=58 * 2**20),
        cost_estimate=pl.CostEstimate(
            flops=cols // D * 512 * 1536 * 2 * 384, bytes_accessed=16 * 2**20, transcendentals=cols // D * 512 * 1536
        ),
    )(*arrays)


def moved(a, axis, step):
    n = lax.axis_size(axis)
    return lax.ppermute(a, axis, [(i, (i + step) % n) for i in range(n)])


def shifted(a, step):
    n = lax.axis_size(YZ)
    return lax.ppermute(a, YZ, [(i, i + step) for i in range(n) if 0 <= i + step < n])


def per_device(queries, key_rows, value_rows):
    xl = lax.axis_index("xl")
    low = xl == 0
    half = queries.shape[1] // 2

    def mine(a):
        return lax.dynamic_slice_in_dim(a, xl * half, half, a.ndim - 1)

    def theirs(a):
        return lax.dynamic_slice_in_dim(a, (1 - xl) * half, half, a.ndim - 1)

    def swapped(a):
        return moved(a, "xl", 1)

    kv_send = jnp.stack([theirs(key_rows), theirs(value_rows)])
    kv_got = swapped(kv_send)
    kv_own = jnp.stack([mine(key_rows), mine(value_rows)])
    gathered = lax.all_gather(coarse_rows(kv_own, kv_send)[:, 0:8], Z)
    nz = gathered.shape[0]
    to_send = gathered[:, :, 4:8].reshape(nz * 8, half)
    q_send = theirs(queries)
    got = swapped(jnp.concatenate([q_send, to_send], axis=0))
    q_got = got[0 : q_send.shape[0]]
    coarse_got = got[q_send.shape[0] :].reshape(nz, 2, 4, half)
    coarse_own = gathered[:, :, 0:4]
    units = jnp.concatenate(
        [jnp.where(low, coarse_own, coarse_got), jnp.where(low, coarse_got, coarse_own)], axis=2
    )
    units = jnp.moveaxis(units, 1, 0).reshape(2, -1, half)
    coarse = (units, moved(units, "y", 1), moved(units, "y", -1), moved(units, "y", 2))
    q_own = mine(queries)
    kv_got, _ = lax.optimization_barrier((kv_got, gathered))
    up1, down1, mid, far = pooled(kv_own, kv_got)
    below1, above1 = shifted(up1, 1), shifted(down1, -1)
    below3, above3 = shifted(far[:, 96:128], 3), shifted(far[:, 0:32], -3)
    up, down, near = forwarded(below1, above1)
    below2, above2 = shifted(up, 1), shifted(down, -1)
    own_out, send_out = attend((
        q_own, q_got, kv_own, kv_got, mid, far, below1, above1, up, down, near, below2, above2, below3, above3,
        *coarse,
    ))
    got_out = swapped(send_out)
    return jnp.where(
        low,
        jnp.concatenate([own_out, got_out], axis=1),
        jnp.concatenate([got_out, own_out], axis=1),
    )


def solution(mesh):
    torus = Mesh(
        mesh.devices.reshape(4, 16, 2, mesh.shape["head"]), ("y", "z", "xl", "head")
    )
    spec = P(SEQ, "head")
    return jax.shard_map(
        per_device, mesh=torus, in_specs=(spec, spec, spec), out_specs=spec, check_vma=False
    )
```

time: 489 us -> 163 us (0.33)
  the two profiles are of different devices: /device:TPU:24 before, /device:TPU:18 now
where the time goes in v1:
time: 163 us; the launch traced here: 162 us
  starting transfers between devices  39.7 us (24%)
  blocking collectives  38.5 us (24%)
  waiting for transfers between devices  35.4 us (22%)
  Pallas kernels  31.6 us (19%)
  local copies, waits for them, and re-layouts  11.5 us (7%)
  other arithmetic  5.14 us (3%)
    all_gather x1, blocking collectives, per_device(): gathered = lax.all_gather(coarse_rows(kv_own, kv_send)[:, 0:8], Z)  38.5 us
    ppermute x6, starting transfers between devices, shifted(): lax.ppermute(a, YZ, [(i, i + step) for i in range(n) if 0 <= i + step < n])  23.7 us
    ppermute x6, waiting for transfers between devices, moved(): return lax.ppermute(a, axis, [(i, (i + step) % n) for i in range(n)])  23.6 us
    pallas_call x1, Pallas kernels, attend(): pl.pallas_call(attend_kernel, grid=(cols // D,), in_specs=[spec(a) for a...  19.1 us
    ppermute x6, starting transfers between devices, moved(): return lax.ppermute(a, axis, [(i, (i + step) % n) for i in range(n)])  16 us
    ppermute x6, waiting for transfers between devices, shifted(): lax.ppermute(a, YZ, [(i, i + step) for i in range(n) if 0 <= i + step < n])  11.8 us
    pallas_call x1, Pallas kernels, pooled(): pl.pallas_call(pool_kernel, grid=(2, cols // width), in_specs=[pl.BlockSp...  4.66 us
    pallas_call x1, Pallas kernels, forwarded(): pl.pallas_call(forward_kernel, grid=(2, cols // width), in_specs=[pl.Bloc...  4.07 us
  transfers between devices with their start and end apart: 12, of which 3 were waited for; matrix products, arithmetic and copies ran while one was open for 6% of the time, Pallas kernels for 8%

profile of v1, /device:TPU:18, one launch (start us, length us, event | category | flops | bytes accessed | tf_op | source)
XLA Modules:
  0.0 162.1 jit_solution(373999191608069176)
XLA Ops:
  0.0 1.7 %dynamic-slice_bitcast_fusion = (bf16[1,256,1024]{2,1,0:T(8,128)(2,1)S(1)}, bf16[1,256,1024]{2,1,0:T(8,128)(2,1)S(1)}, bf16[1,256,1024]{2,1,0:T(8,128)(2,1)S(1)}, bf16[1,256,1024]{2,1,0:T(8,128)(2,1)S(1)}) fusion(bf16[256,2048]{1,0:T(8,128)(2,1)} %param.5, s32[]{:T(128)S(6)} %select_n.32, s32[]{:T(128)S(6)} %select_n.31, bf16[256,2048]{1,0:T(8,128)(2,1)} %param.4), kind=kLoop, calls=%fused_computation.5 | loop fusion | bytes 4194312 | tf_op jit(solution)/shard_map/stack | solution.py:289
  1.9 2.4 %collective-permute-start.1 = (bf16[2,256,1024]{2,1,0:T(8,128)(2,1)S(1)}, bf16[2,256,1024]{2,1,0:T(8,128)(2,1)S(1)}, u32[]{:S(2)}, u32[]{:S(2)}) collective-permute-start(bf16[2,256,1024]{2,1,0:T(8,128)(2,1)S(1)} %pad_maximum_fusion.1.send_ref), channel_id=1, source_target_pairs={{0,4},{4,0},{1,5},{5,1},{2,6},{6,2},{3,7},{7,3},{8,12},{12,8},{9,1... | collective-permute-start | bytes 3145736 | tf_op jit(solution)/shard_map/ppermute | solution.py:267
  4.3 1.1 pad_maximum_fusion.own_ref.kv_own
  5.4 3.8 %shard_map.37 = bf16[2,16,1024]{2,1,0:T(8,128)(2,1)} custom-call(bf16[2,256,1024]{2,1,0:T(8,128)(2,1)} %pad_maximum_fusion.own_ref.kv_own, bf16[2,256,1024]{2,1,0:T(8,128)(2,1)} %copy-done), custom_call_target="tpu_custom_call" | custom-call | flops 2097152 | bytes 2097152 | tf_op jit(solution)/shard_map/pallas_call | solution.py:47
  9.1 0.8 slice.28
  10.0 38.5 %all-gather = bf16[32,8,1024]{2,1,0:T(8,128)(2,1)S(1)} all-gather(bf16[2,8,1024]{2,1,0:T(8,128)(2,1)S(1)} %slice.28), channel_id=2, replica_groups=mesh['y'=4,'z'=16,'xl'=2,'head'=4] {'z'}, dimensions={0}, use_global_device_ids=true | all-gather | bytes 557056 | tf_op jit(solution)/shard_map/all_gather | solution.py:292
  48.5 1.1 fusion
  49.6 1.0 reshape.9
  50.6 0.9 constant_dynamic-slice_fusion
  51.5 0.9 pad_maximum_fusion.2
  52.4 3.4 %collective-permute-start = (bf16[384,1024]{1,0:T(8,128)(2,1)}, bf16[384,1024]{1,0:T(8,128)(2,1)}, u32[]{:S(2)}, u32[]{:S(2)}) collective-permute-start(bf16[384,1024]{1,0:T(8,128)(2,1)} %pad_maximum_fusion.2), channel_id=1, source_target_pairs={{0,4},{4,0},{1,5},{5,1},{2,6},{6,2},{3,7},{7,3},{8,12},{12,8},{9,1... | collective-permute-start | bytes 2359304 | tf_op jit(solution)/shard_map/ppermute | solution.py:267
  55.8 1.0 copy-done.3
  56.8 4.7 %shard_map.38 = (bf16[2,288,1024]{2,1,0:T(8,128)(2,1)}, bf16[2,288,1024]{2,1,0:T(8,128)(2,1)}, bf16[2,256,1024]{2,1,0:T(8,128)(2,1)}, bf16[2,128,1024]{2,1,0:T(8,128)(2,1)}) custom-call(bf16[2,256,1024]{2,1,0:T(8,128)(2,1)} %pad_maximum_fusion.own_ref.kv_own, bf16[2,256,1024]{2,1,0:T(8,128)(2,1)} %copy-done.3), custom_call_target="tpu_custom_call" | custom-call | flops 2097152 | bytes 4194304 | tf_op jit(solution)/shard_map/pallas_call | solution.py:84
  61.5 2.0 %collective-permute-start.2 = (bf16[2,288,1024]{2,1,0:T(8,128)(2,1)}, bf16[2,288,1024]{2,1,0:T(8,128)(2,1)S(1)}, u32[]{:S(2)}, u32[]{:S(2)}) collective-permute-start(bf16[2,288,1024]{2,1,0:T(8,128)(2,1)} %get-tuple-element.18), channel_id=1, source_target_pairs={{0,8},{8,16},{16,24},{24,32},{32,40},{40,48},{48,56},{56,64},{64,7... | collective-permute-start | bytes 3538952 | tf_op jit(solution)/shard_map/ppermute | solution.py:272
  63.5 6.0 %collective-permute-start.3 = (bf16[2,288,1024]{2,1,0:T(8,128)(2,1)}, bf16[2,288,1024]{2,1,0:T(8,128)(2,1)S(1)}, u32[]{:S(2)}, u32[]{:S(2)}) collective-permute-start(bf16[2,288,1024]{2,1,0:T(8,128)(2,1)} %get-tuple-element.19), channel_id=1, source_target_pairs={{8,0},{16,8},{24,16},{32,24},{40,32},{48,40},{56,48},{64,56},{72,6... | collective-permute-start | bytes 3538952 | tf_op jit(solution)/shard_map/ppermute | solution.py:272
  69.6 1.0 slice.32
  70.7 1.0 fusion.1
  71.6 1.9 %collective-permute-start.7 = (bf16[2,32,1024]{2,1,0:T(8,128)(2,1)S(1)}, bf16[2,32,1024]{2,1,0:T(8,128)(2,1)S(1)}, u32[]{:S(2)}, u32[]{:S(2)}) collective-permute-start(bf16[2,32,1024]{2,1,0:T(8,128)(2,1)S(1)} %get-tuple-element.35), channel_id=1, source_target_pairs={{24,0},{32,8},{40,16},{48,24},{56,32},{64,40},{72,48},{80,56},{88,... | collective-permute-start | bytes 393224 | tf_op jit(solution)/shard_map/ppermute | solution.py:272
  73.6 5.7 %collective-permute-start.6 = (bf16[2,32,1024]{2,1,0:T(8,128)(2,1)S(1)}, bf16[2,32,1024]{2,1,0:T(8,128)(2,1)S(1)}, u32[]{:S(2)}, u32[]{:S(2)}) collective-permute-start(bf16[2,32,1024]{2,1,0:T(8,128)(2,1)S(1)} %get-tuple-element.36), channel_id=1, source_target_pairs={{0,24},{8,32},{16,40},{24,48},{32,56},{40,64},{48,72},{56,80},{64,... | collective-permute-start | bytes 393224 | tf_op jit(solution)/shard_map/ppermute | solution.py:272
  79.8 1.9 %collective-permute-start.10 = (bf16[2,128,1024]{2,1,0:T(8,128)(2,1)S(1)}, bf16[2,128,1024]{2,1,0:T(8,128)(2,1)}, u32[]{:S(2)}, u32[]{:S(2)}) collective-permute-start(bf16[2,128,1024]{2,1,0:T(8,128)(2,1)S(1)} %maximum_bitcast_fusion.coarse0), channel_id=1, source_target_pairs={{0,256},{128,384},{256,0},{384,128},{1,257},{129,385},{257,1},{385... | collective-permute-start | bytes 1572872 | tf_op jit(solution)/shard_map/ppermute | solution.py:267
  81.7 11.8 %collective-permute-done.2.below_ref.below1 = bf16[2,288,1024]{2,1,0:T(8,128)(2,1)S(1)} collective-permute-done((bf16[2,288,1024]{2,1,0:T(8,128)(2,1)}, bf16[2,288,1024]{2,1,0:T(8,128)(2,1)S(1)}, u32[]{:S(2)}, u32[]{:S(2)}) %collective-permute-start.2) | collective-permute-done | bytes 1179680 | tf_op jit(solution)/shard_map/ppermute | solution.py:272
  93.6 2.2 %collective-permute-start.9 = (bf16[2,128,1024]{2,1,0:T(8,128)(2,1)S(1)}, bf16[2,128,1024]{2,1,0:T(8,128)(2,1)}, u32[]{:S(2)}, u32[]{:S(2)}) collective-permute-start(bf16[2,128,1024]{2,1,0:T(8,128)(2,1)S(1)} %maximum_bitcast_fusion.coarse0), channel_id=1, source_target_pairs={{0,384},{128,0},{256,128},{384,256},{1,385},{129,1},{257,129},{385... | collective-permute-start | bytes 1572872 | tf_op jit(solution)/shard_map/ppermute | solution.py:267
  95.8 3.6 %collective-permute-start.8 = (bf16[2,128,1024]{2,1,0:T(8,128)(2,1)S(1)}, bf16[2,128,1024]{2,1,0:T(8,128)(2,1)}, u32[]{:S(2)}, u32[]{:S(2)}) collective-permute-start(bf16[2,128,1024]{2,1,0:T(8,128)(2,1)S(1)} %maximum_bitcast_fusion.coarse0), channel_id=1, source_target_pairs={{0,128},{128,256},{256,384},{384,0},{1,129},{129,257},{257,385},{3... | collective-permute-start | bytes 1572872 | tf_op jit(solution)/shard_map/ppermute | solution.py:267
  99.4 4.1 %shard_map.39 = (bf16[2,128,1024]{2,1,0:T(8,128)(2,1)}, bf16[2,128,1024]{2,1,0:T(8,128)(2,1)}, bf16[2,128,1024]{2,1,0:T(8,128)(2,1)}) custom-call(bf16[2,288,1024]{2,1,0:T(8,128)(2,1)} %copy-done.1, bf16[2,288,1024]{2,1,0:T(8,128)(2,1)} %copy-done.2), custom_call_target="tpu_custom_call" | custom-call | flops 2097152 | bytes 3072000 | tf_op jit(solution)/shard_map/pallas_call | solution.py:110
  103.5 1.9 %collective-permute-start.4 = (bf16[2,128,1024]{2,1,0:T(8,128)(2,1)}, bf16[2,128,1024]{2,1,0:T(8,128)(2,1)S(1)}, u32[]{:S(2)}, u32[]{:S(2)}) collective-permute-start(bf16[2,128,1024]{2,1,0:T(8,128)(2,1)} %get-tuple-element.20.up), channel_id=1, source_target_pairs={{0,8},{8,16},{16,24},{24,32},{32,40},{40,48},{48,56},{56,64},{64,7... | collective-permute-start | bytes 1572872 | tf_op jit(solution)/shard_map/ppermute | solution.py:272
  105.5 6.0 %collective-permute-start.5 = (bf16[2,128,1024]{2,1,0:T(8,128)(2,1)}, bf16[2,128,1024]{2,1,0:T(8,128)(2,1)S(1)}, u32[]{:S(2)}, u32[]{:S(2)}) collective-permute-start(bf16[2,128,1024]{2,1,0:T(8,128)(2,1)} %get-tuple-element.21.down), channel_id=1, source_target_pairs={{8,0},{16,8},{24,16},{32,24},{40,32},{48,40},{56,48},{64,56},{72,6... | collective-permute-start | bytes 1572872 | tf_op jit(solution)/shard_map/ppermute | solution.py:272
  111.5 1.9 %slice.30.q_got = bf16[256,1024]{1,0:T(8,128)(2,1)} slice(bf16[384,1024]{1,0:T(8,128)(2,1)} %collective-permute-done), slice={[0:256], [0:1024]} | slice | bytes 1048576 | tf_op jit(solution)/shard_map/slice | solution.py:297
  113.4 10.2 %collective-permute-done.8.coarse1 = bf16[2,128,1024]{2,1,0:T(8,128)(2,1)} collective-permute-done((bf16[2,128,1024]{2,1,0:T(8,128)(2,1)S(1)}, bf16[2,128,1024]{2,1,0:T(8,128)(2,1)}, u32[]{:S(2)}, u32[]{:S(2)}) %collective-permute-start.8) | collective-permute-done | bytes 524320 | tf_op jit(solution)/shard_map/ppermute | solution.py:267
  124.6 19.1 %shard_map.40 = (bf16[256,1024]{1,0:T(8,128)(2,1)}, bf16[256,1024]{1,0:T(8,128)(2,1)}) custom-call(bf16[256,1024]{1,0:T(8,128)(2,1)} %get-tuple-element.26.q_own, bf16[256,1024]{1,0:T(8,128)(2,1)} %slice.30.q_got, bf16[2,256,1024]{2,1,0:T(8,128)(2,1)} %pad_maximum_fusion.own_ref.kv_own, bf16[2,256,1024]{2,1,0:T(8,128)(2,1)} %copy-done.3, ...), custom_call_target="tpu_custom_call" | custom-call | flops 4831838208 | bytes 16777216 | tf_op jit(solution)/shard_map/pallas_call | solution.py:244
  143.7 2.4 %collective-permute-start.11 = (bf16[256,1024]{1,0:T(8,128)(2,1)}, bf16[256,1024]{1,0:T(8,128)(2,1)S(1)}, u32[]{:S(2)}, u32[]{:S(2)}) collective-permute-start(bf16[256,1024]{1,0:T(8,128)(2,1)} %get-tuple-element.24), channel_id=1, source_target_pairs={{0,4},{4,0},{1,5},{5,1},{2,6},{6,2},{3,7},{7,3},{8,12},{12,8},{9,1... | collective-permute-start | bytes 1572872 | tf_op jit(solution)/shard_map/ppermute | solution.py:267
  146.1 13.4 %collective-permute-done.11 = bf16[256,1024]{1,0:T(8,128)(2,1)S(1)} collective-permute-done((bf16[256,1024]{1,0:T(8,128)(2,1)}, bf16[256,1024]{1,0:T(8,128)(2,1)S(1)}, u32[]{:S(2)}, u32[]{:S(2)}) %collective-permute-start.11) | collective-permute-done | bytes 524320 | tf_op jit(solution)/shard_map/ppermute | solution.py:267
  159.5 2.6 %maximum_select_fusion = bf16[256,2048]{1,0:T(8,128)(2,1)} fusion(bf16[256,1024]{1,0:T(8,128)(2,1)S(1)} %collective-permute-done.11, bf16[256,1024]{1,0:T(8,128)(2,1)} %get-tuple-element.23, pred[]{:T(512)S(6)} %eq.3), kind=kLoop, calls=%fused_computation.2 | loop fusion | flops 4718592 | bytes 2097153 | tf_op jit(solution)/shard_map/jit(_where)/select_n | solution.py:317
  (34 shorter events, 1.7 us)
Async XLA Ops:
  1.8 3.5 %copy-start = (bf16[2,256,1024]{2,1,0:T(8,128)(2,1)}, bf16[2,256,1024]{2,1,0:T(8,128)(2,1)S(1)}, u32[]{:S(2)}) copy-start(bf16[2,256,1024]{2,1,0:T(8,128)(2,1)S(1)} %pad_maximum_fusion.1.send_ref) | copy-start | bytes 3145732
  1.9 54.0 %collective-permute-start.1 = (bf16[2,256,1024]{2,1,0:T(8,128)(2,1)S(1)}, bf16[2,256,1024]{2,1,0:T(8,128)(2,1)S(1)}, u32[]{:S(2)}, u32[]{:S(2)}) collective-permute-start(bf16[2,256,1024]{2,1,0:T(8,128)(2,1)S(1)} %pad_maximum_fusion.1.send_ref), channel_id=1, source_target_pairs={{0,4},{4,0},{1,5},{5,1},{2,6},{6,2},{3,7},{7,3},{8,12},{12,8},{9,1... | collective-permute-start | bytes 3145736 | tf_op jit(solution)/shard_map/ppermute | solution.py:267
  9.1 41.4 %copy-start.4 = (bf16[256,2048]{1,0:T(8,128)(2,1)S(1)}, bf16[256,2048]{1,0:T(8,128)(2,1)}, u32[]{:S(2)}) copy-start(bf16[256,2048]{1,0:T(8,128)(2,1)} %param.3) | copy-start | bytes 3145732
  52.4 17.1 %collective-permute-start = (bf16[384,1024]{1,0:T(8,128)(2,1)}, bf16[384,1024]{1,0:T(8,128)(2,1)}, u32[]{:S(2)}, u32[]{:S(2)}) collective-permute-start(bf16[384,1024]{1,0:T(8,128)(2,1)} %pad_maximum_fusion.2), channel_id=1, source_target_pairs={{0,4},{4,0},{1,5},{5,1},{2,6},{6,2},{3,7},{7,3},{8,12},{12,8},{9,1... | collective-permute-start | bytes 2359304 | tf_op jit(solution)/shard_map/ppermute | solution.py:267
  55.8 1.0 copy-start.3
  61.5 17.8 %copy-start.5 = (bf16[16,2,4,1024]{3,2,1,0:T(4,128)(2,1)S(1)}, bf16[16,2,4,1024]{3,2,1,0:T(4,128)(2,1)}, u32[]{:S(2)}) copy-start(bf16[16,2,4,1024]{3,2,1,0:T(4,128)(2,1)} %get-tuple-element.33) | copy-start | bytes 786436
  61.5 32.1 %collective-permute-start.2 = (bf16[2,288,1024]{2,1,0:T(8,128)(2,1)}, bf16[2,288,1024]{2,1,0:T(8,128)(2,1)S(1)}, u32[]{:S(2)}, u32[]{:S(2)}) collective-permute-start(bf16[2,288,1024]{2,1,0:T(8,128)(2,1)} %get-tuple-element.18), channel_id=1, source_target_pairs={{0,8},{8,16},{16,24},{24,32},{32,40},{40,48},{48,56},{56,64},{64,7... | collective-permute-start | bytes 3538952 | tf_op jit(solution)/shard_map/ppermute | solution.py:272
  63.5 32.2 %collective-permute-start.3 = (bf16[2,288,1024]{2,1,0:T(8,128)(2,1)}, bf16[2,288,1024]{2,1,0:T(8,128)(2,1)S(1)}, u32[]{:S(2)}, u32[]{:S(2)}) collective-permute-start(bf16[2,288,1024]{2,1,0:T(8,128)(2,1)} %get-tuple-element.19), channel_id=1, source_target_pairs={{8,0},{16,8},{24,16},{32,24},{40,32},{48,40},{56,48},{64,56},{72,6... | collective-permute-start | bytes 3538952 | tf_op jit(solution)/shard_map/ppermute | solution.py:272
  71.6 31.9 %collective-permute-start.7 = (bf16[2,32,1024]{2,1,0:T(8,128)(2,1)S(1)}, bf16[2,32,1024]{2,1,0:T(8,128)(2,1)S(1)}, u32[]{:S(2)}, u32[]{:S(2)}) collective-permute-start(bf16[2,32,1024]{2,1,0:T(8,128)(2,1)S(1)} %get-tuple-element.35), channel_id=1, source_target_pairs={{24,0},{32,8},{40,16},{48,24},{56,32},{64,40},{72,48},{80,56},{88,... | collective-permute-start | bytes 393224 | tf_op jit(solution)/shard_map/ppermute | solution.py:272
  73.6 31.9 %collective-permute-start.6 = (bf16[2,32,1024]{2,1,0:T(8,128)(2,1)S(1)}, bf16[2,32,1024]{2,1,0:T(8,128)(2,1)S(1)}, u32[]{:S(2)}, u32[]{:S(2)}) collective-permute-start(bf16[2,32,1024]{2,1,0:T(8,128)(2,1)S(1)} %get-tuple-element.36), channel_id=1, source_target_pairs={{0,24},{8,32},{16,40},{24,48},{32,56},{40,64},{48,72},{56,80},{64,... | collective-permute-start | bytes 393224 | tf_op jit(solution)/shard_map/ppermute | solution.py:272
  79.8 43.8 %copy-start.6 = (bf16[2,128,1024]{2,1,0:T(8,128)(2,1)}, bf16[2,128,1024]{2,1,0:T(8,128)(2,1)S(1)}, u32[]{:S(2)}) copy-start(bf16[2,128,1024]{2,1,0:T(8,128)(2,1)S(1)} %maximum_bitcast_fusion.coarse0) | copy-start | bytes 1572868
  79.8 33.6 %collective-permute-start.10 = (bf16[2,128,1024]{2,1,0:T(8,128)(2,1)S(1)}, bf16[2,128,1024]{2,1,0:T(8,128)(2,1)}, u32[]{:S(2)}, u32[]{:S(2)}) collective-permute-start(bf16[2,128,1024]{2,1,0:T(8,128)(2,1)S(1)} %maximum_bitcast_fusion.coarse0), channel_id=1, source_target_pairs={{0,256},{128,384},{256,0},{384,128},{1,257},{129,385},{257,1},{385... | collective-permute-start | bytes 1572872 | tf_op jit(solution)/shard_map/ppermute | solution.py:267
  93.5 5.9 %copy-start.1 = (bf16[2,288,1024]{2,1,0:T(8,128)(2,1)}, bf16[2,288,1024]{2,1,0:T(8,128)(2,1)S(1)}, u32[]{:S(2)}) copy-start(bf16[2,288,1024]{2,1,0:T(8,128)(2,1)S(1)} %collective-permute-done.2.below_ref.below1) | copy-start | bytes 3538948
  93.6 19.9 %collective-permute-start.9 = (bf16[2,128,1024]{2,1,0:T(8,128)(2,1)S(1)}, bf16[2,128,1024]{2,1,0:T(8,128)(2,1)}, u32[]{:S(2)}, u32[]{:S(2)}) collective-permute-start(bf16[2,128,1024]{2,1,0:T(8,128)(2,1)S(1)} %maximum_bitcast_fusion.coarse0), channel_id=1, source_target_pairs={{0,384},{128,0},{256,128},{384,256},{1,385},{129,1},{257,129},{385... | collective-permute-start | bytes 1572872 | tf_op jit(solution)/shard_map/ppermute | solution.py:267
  95.8 3.7 %copy-start.2 = (bf16[2,288,1024]{2,1,0:T(8,128)(2,1)}, bf16[2,288,1024]{2,1,0:T(8,128)(2,1)S(1)}, u32[]{:S(2)}) copy-start(bf16[2,288,1024]{2,1,0:T(8,128)(2,1)S(1)} %collective-permute-done.3.above_ref.above1) | copy-start | bytes 3538948
  95.8 27.8 %collective-permute-start.8 = (bf16[2,128,1024]{2,1,0:T(8,128)(2,1)S(1)}, bf16[2,128,1024]{2,1,0:T(8,128)(2,1)}, u32[]{:S(2)}, u32[]{:S(2)}) collective-permute-start(bf16[2,128,1024]{2,1,0:T(8,128)(2,1)S(1)} %maximum_bitcast_fusion.coarse0), channel_id=1, source_target_pairs={{0,128},{128,256},{256,384},{384,0},{1,129},{129,257},{257,385},{3... | collective-permute-start | bytes 1572872 | tf_op jit(solution)/shard_map/ppermute | solution.py:267
  103.5 20.1 %copy-start.9 = (bf16[2,32,1024]{2,1,0:T(8,128)(2,1)}, bf16[2,32,1024]{2,1,0:T(8,128)(2,1)S(1)}, u32[]{:S(2)}) copy-start(bf16[2,32,1024]{2,1,0:T(8,128)(2,1)S(1)} %collective-permute-done.7.above3) | copy-start | bytes 393220
  103.5 20.1 %collective-permute-start.4 = (bf16[2,128,1024]{2,1,0:T(8,128)(2,1)}, bf16[2,128,1024]{2,1,0:T(8,128)(2,1)S(1)}, u32[]{:S(2)}, u32[]{:S(2)}) collective-permute-start(bf16[2,128,1024]{2,1,0:T(8,128)(2,1)} %get-tuple-element.20.up), channel_id=1, source_target_pairs={{0,8},{8,16},{16,24},{24,32},{32,40},{40,48},{48,56},{56,64},{64,7... | collective-permute-start | bytes 1572872 | tf_op jit(solution)/shard_map/ppermute | solution.py:272
  105.5 18.2 %copy-start.10 = (bf16[2,32,1024]{2,1,0:T(8,128)(2,1)}, bf16[2,32,1024]{2,1,0:T(8,128)(2,1)S(1)}, u32[]{:S(2)}) copy-start(bf16[2,32,1024]{2,1,0:T(8,128)(2,1)S(1)} %collective-permute-done.6.below3) | copy-start | bytes 393220
  105.5 18.2 %collective-permute-start.5 = (bf16[2,128,1024]{2,1,0:T(8,128)(2,1)}, bf16[2,128,1024]{2,1,0:T(8,128)(2,1)S(1)}, u32[]{:S(2)}, u32[]{:S(2)}) collective-permute-start(bf16[2,128,1024]{2,1,0:T(8,128)(2,1)} %get-tuple-element.21.down), channel_id=1, source_target_pairs={{8,0},{16,8},{24,16},{32,24},{40,32},{48,40},{56,48},{64,56},{72,6... | collective-permute-start | bytes 1572872 | tf_op jit(solution)/shard_map/ppermute | solution.py:272
  123.6 0.8 copy-start.7
  123.6 1.0 copy-start.8
  143.7 15.8 %collective-permute-start.11 = (bf16[256,1024]{1,0:T(8,128)(2,1)}, bf16[256,1024]{1,0:T(8,128)(2,1)S(1)}, u32[]{:S(2)}, u32[]{:S(2)}) collective-permute-start(bf16[256,1024]{1,0:T(8,128)(2,1)} %get-tuple-element.24), channel_id=1, source_target_pairs={{0,4},{4,0},{1,5},{5,1},{2,6},{6,2},{3,7},{7,3},{8,12},{12,8},{9,1... | collective-permute-start | bytes 1572872 | tf_op jit(solution)/shard_map/ppermute | solution.py:267

commit v2 on v1

v2 whole, which is shorter than its diff:
```python
import functools
import math

import jax
import jax.numpy as jnp
from jax import lax
from jax.experimental import pallas as pl
from jax.experimental.pallas import tpu as pltpu
from jax.sharding import Mesh
from jax.sharding import PartitionSpec as P

D = 128
BLOCK = 128
FAR_REACH = 9
SEQ = ("y", "z", "xl")
YZ = ("y", "z")
Z = "z"
BF = jnp.bfloat16
F32 = jnp.float32
SCALE = math.log2(math.e) / math.sqrt(D)
VMEM = pltpu.CompilerParams(vmem_limit_bytes=58 * 2**20)


def taking(microseconds):
    return pl.CostEstimate(flops=0, bytes_accessed=int(microseconds * 3.6e6), transcendentals=0)


def halved(x, scratch):
    rows, cols = x.shape
    parts = []
    for c in range(cols // D):
        scratch[c, 0:rows] = x[:, c * D : (c + 1) * D]
        even = scratch[c, pl.ds(0, rows // 2, stride=2)]
        odd = scratch[c, pl.ds(1, rows // 2, stride=2)]
        parts.append((0.5 * (even + odd)).astype(BF))
    return parts[0] if len(parts) == 1 else jnp.concatenate(parts, axis=1)


def column(width, other=False):
    n = 8 * D // width

    def index(i, xl):
        return (0, (1 - xl[0] if other else xl[0]) * n + i)

    return index


def native_kernel(xl, k_own, k_send, v_own, v_send, unit_ref, far_ref, scratch):
    pieces = []
    for i, refs in enumerate(((k_own, k_send), (v_own, v_send))):
        for j, ref in enumerate(refs):
            four = halved(halved(ref[...].astype(F32), scratch).astype(F32), scratch)
            far_ref[j, i] = four
            rows, cols = four.shape
            pieces.append(jnp.sum(four.astype(F32).reshape(rows // 16, 16, cols), axis=1) * (1.0 / 16))
    unit_ref[...] = jnp.concatenate(pieces, axis=0).astype(BF)


def native_rows(xl, k, v):
    rows, cols = k.shape[0], k.shape[1] // 2
    width = 512
    own, send = (pl.BlockSpec((rows, width), column(width, other)) for other in (False, True))
    return pl.pallas_call(
        native_kernel,
        grid_spec=pltpu.PrefetchScalarGridSpec(
            num_scalar_prefetch=1,
            grid=(cols // width,),
            in_specs=[own, send, own, send],
            out_specs=[
                pl.BlockSpec((16, width), lambda c, xl: (0, c)),
                pl.BlockSpec((2, 2, rows // 4, width), lambda c, xl: (0, 0, 0, c)),
            ],
            scratch_shapes=[pltpu.VMEM((width // D, rows, D), F32)],
        ),
        out_shape=[jax.ShapeDtypeStruct((16, cols), BF), jax.ShapeDtypeStruct((2, 2, rows // 4, cols), BF)],
        compiler_params=VMEM,
        cost_estimate=taking(4),
    )(xl, k, k, v, v)


def pool_kernel(xl, k_ref, v_ref, got_ref, up_ref, down_ref, mid_ref, far_ref, scratch):
    low = xl[0] == 0
    for i, ref in enumerate((k_ref, v_ref)):
        own, got = ref[...], got_ref[i]
        first = jnp.where(low, own, got)
        second = jnp.where(low, got, own)
        mid_first = halved(first.astype(F32), scratch)
        mid_second = halved(second.astype(F32), scratch)
        far_first = halved(mid_first.astype(F32), scratch)
        far_second = halved(mid_second.astype(F32), scratch)
        mid_ref[i, 0:128] = mid_first
        mid_ref[i, 128:256] = mid_second
        far_ref[i, 0:64] = far_first
        far_ref[i, 64:128] = far_second
        up_ref[i, 0:128] = second[128:256]
        up_ref[i, 128:192] = mid_first[64:128]
        up_ref[i, 192:256] = mid_second[0:64]
        up_ref[i, 256:288] = far_first[0:32]
        down_ref[i, 0:128] = first[0:128]
        down_ref[i, 128:192] = mid_first[64:128]
        down_ref[i, 192:256] = mid_second[0:64]
        down_ref[i, 256:288] = far_second[32:64]


def pooled(xl, k, v, got):
    _, rows, cols = got.shape
    width = 256
    sizes = (288, 288, 256, 128)
    own = pl.BlockSpec((rows, width), column(width))
    return pl.pallas_call(
        pool_kernel,
        grid_spec=pltpu.PrefetchScalarGridSpec(
            num_scalar_prefetch=1,
            grid=(cols // width,),
            in_specs=[own, own, pl.BlockSpec((2, rows, width), lambda c, xl: (0, 0, c))],
            out_specs=[pl.BlockSpec((2, n, width), lambda c, xl: (0, 0, c)) for n in sizes],
            scratch_shapes=[pltpu.VMEM((width // D, rows, D), F32)],
        ),
        out_shape=[jax.ShapeDtypeStruct((2, n, cols), BF) for n in sizes],
        compiler_params=VMEM, cost_estimate=taking(5),
    )(xl, k, v, got)


def flags(blocks, first, unit, ref):
    ny, nz = lax.axis_size("y"), lax.axis_size("z")
    at = 4 * (lax.axis_index("y") * nz + lax.axis_index("z"))
    block = first + lax.broadcasted_iota(jnp.int32, (blocks * unit, D), 0) // unit + at
    ref[:, D : 2 * D] = jnp.where((block >= 0) & (block < 4 * ny * nz), 1.0, 0.0).astype(BF)


def present():
    ny, nz = lax.axis_size("y"), lax.axis_size("z")
    zz = lax.axis_index("y") * nz + lax.axis_index("z")
    return [zz >= n for n in range(4)], [zz <= ny * nz - 1 - n for n in range(4)]


def put(ref, start, rows, here, fallback):
    ref[start : start + rows.shape[0], 0:D] = rows if fallback is None else jnp.where(here, rows, fallback)


def scores(q, key):
    return lax.dot_general(q, key, (((1,), (1,)), ((), ())), preferred_element_type=F32)


def weighted(parts, top):
    total = jnp.zeros((BLOCK, 2 * D), F32)
    for s, value, size, keep in parts:
        weights = jnp.exp2(s * SCALE - (top - size)).astype(BF)
        if keep is not None:
            weights = weights * keep
        total = total + jnp.dot(weights, value, preferred_element_type=F32)
    return total


def top_of(parts):
    return functools.reduce(
        jnp.maximum, [jnp.max(s, axis=1, keepdims=True) * SCALE + size for s, _, size, _ in parts]
    )


def near_kernel(
    xl, q_own, q_got, k_own, v_own, kv_got, mid, far, below1, above1,
    below_own, below_got, above_own, above_got, edge_own, edge_got,
    out, stat, kf, vf, km, vm, kr, vr, kfar, vfar, scratch,
):
    low = xl[0] == 0

    @pl.when(pl.program_id(0) == 0)
    def _():
        flags(6, -1, 128, vf)
        flags(10, -3, 64, vm)
        flags(22, -9, 32, vr)

    has, has_up = present()
    for i, (own_ref, fine_w, mid_w, far_w) in enumerate(((k_own, kf, km, kr), (v_own, vf, vm, vr))):
        is_key = i == 0

        def spare(rows):
            return rows if is_key else None

        own, got = own_ref[...], kv_got[i]
        first, second = jnp.where(low, own, got), jnp.where(low, got, own)
        fine_w[128:384, 0:D] = first
        fine_w[384:640, 0:D] = second
        put(fine_w, 0, below1[i, 0:128], has[1], spare(first[0:128]))
        put(fine_w, 640, above1[i, 0:128], has_up[1], spare(second[128:256]))
        mid_w[192:448, 0:D] = mid[i]
        m0, m3 = spare(mid[i, 0:64]), spare(mid[i, 192:256])
        mid_below = halved(below1[i, 0:128].astype(F32), scratch)
        mid_above = halved(above1[i, 0:128].astype(F32), scratch)
        put(mid_w, 0, below1[i, 128:192], has[1], m0)
        put(mid_w, 64, below1[i, 192:256], has[1], m0)
        put(mid_w, 128, mid_below, has[1], m0)
        put(mid_w, 448, mid_above, has_up[1], m3)
        put(mid_w, 512, above1[i, 128:192], has_up[1], m3)
        put(mid_w, 576, above1[i, 192:256], has_up[1], m3)
        far_w[288:416, 0:D] = far[i]
        f0, f3 = far[i, 0:32], far[i, 96:128]
        f0_2, f3_2 = spare(jnp.concatenate([f0] * 2, axis=0)), spare(jnp.concatenate([f3] * 2, axis=0))
        f0_3, f3_3 = spare(jnp.concatenate([f0] * 3, axis=0)), spare(jnp.concatenate([f3] * 3, axis=0))
        put(far_w, 0, jnp.where(low, edge_got[i], edge_own[i]), has[3], spare(f0))
        put(far_w, 32, jnp.where(low, below_own[i], below_got[i]), has[2], f0_2)
        put(far_w, 96, jnp.where(low, below_got[i], below_own[i]), has[2], f0_2)
        put(far_w, 160, below1[i, 256:288], has[1], spare(f0))
        rows = jnp.concatenate([below1[i, 128:256], mid_below], axis=0)
        put(far_w, 192, halved(rows.astype(F32), scratch), has[1], f0_3)
        rows = jnp.concatenate([mid_above, above1[i, 128:256]], axis=0)
        put(far_w, 416, halved(rows.astype(F32), scratch), has_up[1], f3_3)
        put(far_w, 512, above1[i, 256:288], has_up[1], spare(f3))
        put(far_w, 544, jnp.where(low, above_own[i], above_got[i]), has_up[2], f3_2)
        put(far_w, 608, jnp.where(low, above_got[i], above_own[i]), has_up[2], f3_2)
        put(far_w, 672, jnp.where(low, edge_own[i], edge_got[i]), has_up[3], spare(f3))
    qo, qg = q_own[...], q_got[...]
    queries = (jnp.where(low, qo, qg), jnp.where(low, qg, qo))
    left = lax.broadcasted_iota(jnp.int32, (BLOCK, D), 1) < D // 2
    for b in range(4):
        q = queries[b // 2][(b % 2) * 128 : (b % 2 + 1) * 128]
        kfar[0:192] = kr[b * 32 : b * 32 + 192]
        kfar[192:384] = kr[(b + 13) * 32 : (b + 13) * 32 + 192]
        vfar[0:192] = vr[b * 32 : b * 32 + 192]
        vfar[192:384] = vr[(b + 13) * 32 : (b + 13) * 32 + 192]
        lo, up = b * 64, (b + 5) * 64
        parts = [
            (scores(q, kf[b * 128 : b * 128 + 384]), vf[b * 128 : b * 128 + 384], 0.0, None),
            (scores(q, km[lo : lo + 128]), vm[lo : lo + 128], 1.0, None),
            (scores(q, km[up : up + 128]), vm[up : up + 128], 1.0, None),
            (scores(q, kfar[...]), vfar[...], 2.0, None),
        ]
        top = top_of(parts)
        total = weighted(parts, top)
        out[b * 128 : (b + 1) * 128] = total[:, 0:D]
        stat[b * 128 : (b + 1) * 128] = jnp.where(left, top, total[:, D : 2 * D])


def far_kernel(xl, q_own, q_got, coarse, near_out, near_stat, own_out, send_out, kc, vc, mask):
    low = xl[0] == 0
    y = lax.axis_index("y")
    ny, nz = lax.axis_size("y"), lax.axis_size("z")
    coarse_n = coarse.shape[0] * coarse.shape[2]

    @pl.when(pl.program_id(0) == 0)
    def _():
        vc[:, D : 2 * D] = jnp.ones((coarse_n, D), BF)
        at = lax.broadcasted_iota(jnp.int32, (16, coarse_n), 1)
        turn = (at // 8) % ny
        other = (y + jnp.where(turn == 0, 0, jnp.where(turn == 1, ny - 1, jnp.where(turn == 2, 1, 2)))) % ny
        block = (other * nz + at // (8 * ny)) * 4 + (at % 8) // 2
        for b in range(4):
            gap = jnp.abs(block - (4 * (y * nz + lax.axis_index("z")) + b))
            mask[b * 16 : (b + 1) * 16, :] = jnp.where(gap > FAR_REACH, 1.0, 0.0).astype(BF)

    kc[...] = coarse[:, 0].reshape(coarse_n, D)
    vc[:, 0:D] = coarse[:, 1].reshape(coarse_n, D)
    qo, qg = q_own[...], q_got[...]
    queries = (jnp.where(low, qo, qg), jnp.where(low, qg, qo))
    results = []
    for b in range(4):
        q = queries[b // 2][(b % 2) * 128 : (b % 2 + 1) * 128]
        parts = [(scores(q, kc[...]), vc[...], 6.0, mask[b * 16 : b * 16 + 1, :])]
        here = slice(b * 128, (b + 1) * 128)
        near_top, near_sum = near_stat[here, 0:1], near_stat[here, D - 1 : D]
        top = jnp.maximum(top_of(parts), near_top)
        total = weighted(parts, top)
        scale = jnp.exp2(near_top - top)
        upper = total[:, 0:D] + near_out[here] * scale
        results.append((upper / (total[:, D : 2 * D] + near_sum * scale)).astype(BF))
    out_first = jnp.concatenate(results[0:2], axis=0)
    out_second = jnp.concatenate(results[2:4], axis=0)
    own_out[...] = jnp.where(low, out_first, out_second)
    send_out[...] = jnp.where(low, out_second, out_first)


def by_head(a):
    lead = a.shape[:-1]
    return pl.BlockSpec(lead + (D,), lambda h, xl, n=len(lead): (0,) * n + (h,))


def attend_call(kernel, xl, own, arrays, outs, out_specs, scratch, cost):
    rows, cols = own[0].shape[0], own[0].shape[1] // 2
    spec_own = pl.BlockSpec((rows, D), column(D))
    order = [(own[0], spec_own), (arrays[0], by_head(arrays[0]))]
    order += [(a, spec_own) for a in own[1:]] + [(a, by_head(a)) for a in arrays[1:]]
    return pl.pallas_call(
        kernel,
        grid_spec=pltpu.PrefetchScalarGridSpec(
            num_scalar_prefetch=1,
            grid=(cols // D,),
            in_specs=[spec for _, spec in order],
            out_specs=out_specs,
            scratch_shapes=scratch,
        ),
        out_shape=outs,
        compiler_params=VMEM,
        cost_estimate=taking(cost),
    )(xl, *(a for a, _ in order))


def attend_near(xl, q, q_got, k, v, arrays):
    rows, cols = q.shape[0], q.shape[1] // 2
    outs = [jax.ShapeDtypeStruct((2 * rows, cols), F32)] * 2
    scratch = [
        pltpu.VMEM((768, D), BF), pltpu.VMEM((768, 2 * D), BF),
        pltpu.VMEM((640, D), BF), pltpu.VMEM((640, 2 * D), BF),
        pltpu.VMEM((704, D), BF), pltpu.VMEM((704, 2 * D), BF),
        pltpu.VMEM((384, D), BF), pltpu.VMEM((384, 2 * D), BF),
        pltpu.VMEM((1, 192, D), F32),
    ]
    return attend_call(
        near_kernel, xl, (q, k, v), (q_got, *arrays), outs, [by_head(a) for a in outs], scratch, 15
    )


def attend_far(xl, q, q_got, arrays):
    rows, cols = q.shape[0], q.shape[1] // 2
    outs = [jax.ShapeDtypeStruct((rows, 2 * cols), BF), jax.ShapeDtypeStruct((rows, cols), BF)]
    coarse_n = arrays[0].shape[0] * arrays[0].shape[2]
    scratch = [
        pltpu.VMEM((coarse_n, D), BF), pltpu.VMEM((coarse_n, 2 * D), BF),
        pltpu.VMEM((64, coarse_n), BF),
    ]
    return attend_call(
        far_kernel, xl, (q,), (q_got, *arrays), outs,
        [pl.BlockSpec((rows, D), column(D)), by_head(outs[1])], scratch, 9,
    )


def moved(a, axis, step):
    n = lax.axis_size(axis)
    return lax.ppermute(a, axis, [(i, (i + step) % n) for i in range(n)])


def shifted(a, step):
    n = lax.axis_size(YZ)
    return lax.ppermute(a, YZ, [(i, i + step) for i in range(n) if 0 <= i + step < n])


def outward(a):
    n = lax.axis_size(YZ)
    route = [(2 * i, 2 * i - 2) for i in range(1, n)] + [(2 * i + 1, 2 * i + 3) for i in range(n - 1)]
    return lax.ppermute(a, SEQ, route)


def per_device(queries, key_rows, value_rows):
    xl = lax.axis_index("xl")
    low = xl == 0
    at = xl.reshape(1)
    half = queries.shape[1] // 2

    def theirs(a):
        return lax.dynamic_slice_in_dim(a, (1 - xl) * half, half, a.ndim - 1)

    def swapped(a):
        return moved(a, "xl", 1)

    kv_send, keys, values = lax.optimization_barrier(
        (jnp.stack([theirs(key_rows), theirs(value_rows)]), key_rows, value_rows)
    )
    kv_got = swapped(kv_send)
    unit, fours = native_rows(at, keys, values)
    turned = (moved(unit, "y", 1), moved(unit, "y", -1), moved(unit, "y", 2))
    below2, above2 = shifted(fours, 2), shifted(fours, -2)
    units = jnp.concatenate([unit, *turned], axis=0)
    units_got = swapped(units)
    kept = units.reshape(4, 2, 8, half)[:, :, 0:4]
    came = units_got.reshape(4, 2, 8, half)[:, :, 4:8]
    units = jnp.concatenate([jnp.where(low, kept, came), jnp.where(low, came, kept)], axis=2)
    units = jnp.moveaxis(units, 1, 0).reshape(2, 32, half)
    units, _, _, _ = lax.optimization_barrier((units, kv_got, below2, above2))
    coarse = lax.all_gather(units, "z")
    edge = outward(jnp.where(low, above2[:, :, 0:32], below2[:, :, 32:64]))
    sent = (theirs(queries), below2[1], above2[1], edge[1])
    up1, down1, mid, far = pooled(at, key_rows, value_rows, kv_got)
    message = jnp.concatenate([a.reshape(-1, half) for a in sent], axis=0)
    message, up1, down1 = lax.optimization_barrier((message, up1, down1))
    got = swapped(message)
    q_got, below_got, above_got, edge_got = (
        got[i:j].reshape(a.shape) for a, i, j in zip(sent, (0, 256, 384, 512), (256, 384, 512, 576))
    )
    below1, above1 = shifted(up1, 1), shifted(down1, -1)
    near_out, near_stat = attend_near(
        at, queries, q_got, key_rows, value_rows,
        (kv_got, mid, far, below1, above1, below2[0], below_got, above2[0], above_got, edge[0], edge_got),
    )
    out, send_out = attend_far(at, queries, q_got, (coarse, near_out, near_stat))
    return lax.dynamic_update_slice_in_dim(out, swapped(send_out), (1 - xl) * half, 1)


def solution(mesh):
    torus = Mesh(
        mesh.devices.reshape(4, 16, 2, mesh.shape["head"]), ("y", "z", "xl", "head")
    )
    spec = P(SEQ, "head")
    return jax.shard_map(
        per_device, mesh=torus, in_specs=(spec, spec, spec), out_specs=spec, check_vma=False
    )
```

time: 163 us -> 174 us (1.067)
  the two profiles are of different devices: /device:TPU:18 before, /device:TPU:24 now
where the time goes in v2:
time: 174 us
  waiting for transfers between devices  65.9 us (38%)
  starting transfers between devices  47.9 us (28%)
  Pallas kernels  35.8 us (21%)
  between operations  13.6 us (8%)
  local copies, waits for them, and re-layouts  8.55 us (5%)
  other arithmetic  1.98 us (1%)
    ppermute x7, waiting for transfers between devices, moved(): return lax.ppermute(a, axis, [(i, (i + step) % n) for i in range(n)])  38 us
    pallas_call x2, Pallas kernels, attend_call(): pl.pallas_call(kernel, grid_spec=pltpu.PrefetchScalarGridSpec(num_scalar_...  28.1 us
    ppermute x4, waiting for transfers between devices, shifted(): lax.ppermute(a, YZ, [(i, i + step) for i in range(n) if 0 <= i + step < n])  23.7 us
    ppermute x7, starting transfers between devices, moved(): return lax.ppermute(a, axis, [(i, (i + step) % n) for i in range(n)])  21.3 us
    ppermute x4, starting transfers between devices, shifted(): lax.ppermute(a, YZ, [(i, i + step) for i in range(n) if 0 <= i + step < n])  21.1 us
    ppermute x1, starting transfers between devices, outward(): return lax.ppermute(a, SEQ, route)  5.55 us
    pallas_call x1, Pallas kernels, pooled(): pl.pallas_call(pool_kernel, grid_spec=pltpu.PrefetchScalarGridSpec(num_sc...  4.71 us
    ppermute x1, waiting for transfers between devices, outward(): return lax.ppermute(a, SEQ, route)  4.13 us
  transfers between devices with their start and end apart: 13, of which 8 were waited for; matrix products, arithmetic and copies ran while one was open for 4% of the time, Pallas kernels for 14%

profile of v2, /device:TPU:24, one launch (start us, length us, event | category | flops | bytes accessed | tf_op | source)
XLA Modules:
  0.0 173.7 jit_solution(3797580330528138891)
XLA Ops:
  6.5 1.3 dynamic-slice_bitcast_fusion
  7.8 1.1 pad_maximum_fusion.1
  8.9 3.4 %collective-permute-start.3 = (bf16[2,256,1024]{2,1,0:T(8,128)(2,1)}, bf16[2,256,1024]{2,1,0:T(8,128)(2,1)S(1)}, u32[]{:S(2)}, u32[]{:S(2)}) collective-permute-start(bf16[2,256,1024]{2,1,0:T(8,128)(2,1)} %pad_maximum_fusion.1), channel_id=1, source_target_pairs={{0,4},{4,0},{1,5},{5,1},{2,6},{6,2},{3,7},{7,3},{8,12},{12,8},{9,1... | collective-permute-start | bytes 3145736 | tf_op jit(solution)/shard_map/ppermute | solution.py:329
  12.3 3.1 %shard_map.37 = (bf16[16,1024]{1,0:T(8,128)(2,1)}, bf16[2,2,64,1024]{3,2,1,0:T(8,128)(2,1)}) custom-call(s32[1]{0:T(128)} %bitcast.xl, bf16[256,2048]{1,0:T(8,128)(2,1)} %k_own.2, bf16[256,2048]{1,0:T(8,128)(2,1)} %k_own.2, bf16[256,2048]{1,0:T(8,128)(2,1)} %v_own.2, bf16[256,2048]{1,0:T(8,128)(2,1)} %v_own.2), custom_call_target="tpu_custom_call" | custom-call | bytes 14400000 | tf_op jit(solution)/shard_map/pallas_call | solution.py:63
  15.3 5.2 %collective-permute-start = (bf16[2,2,64,1024]{3,2,1,0:T(8,128)(2,1)}, bf16[2,2,64,1024]{3,2,1,0:T(8,128)(2,1)S(1)}, u32[]{:S(2)}, u32[]{:S(2)}) collective-permute-start(bf16[2,2,64,1024]{3,2,1,0:T(8,128)(2,1)} %get-tuple-element.24), channel_id=1, source_target_pairs={{0,16},{8,24},{16,32},{24,40},{32,48},{40,56},{48,64},{56,72},{64,... | collective-permute-start | bytes 1572872 | tf_op jit(solution)/shard_map/ppermute | solution.py:334
  20.5 8.8 %collective-permute-start.1 = (bf16[2,2,64,1024]{3,2,1,0:T(8,128)(2,1)}, bf16[2,2,64,1024]{3,2,1,0:T(8,128)(2,1)S(1)}, u32[]{:S(2)}, u32[]{:S(2)}) collective-permute-start(bf16[2,2,64,1024]{3,2,1,0:T(8,128)(2,1)} %get-tuple-element.24), channel_id=1, source_target_pairs={{16,0},{24,8},{32,16},{40,24},{48,32},{56,40},{64,48},{72,56},{80,... | collective-permute-start | bytes 1572872 | tf_op jit(solution)/shard_map/ppermute | solution.py:334
  29.3 1.9 %collective-permute-start.5 = (bf16[16,1024]{1,0:T(8,128)(2,1)}, bf16[16,1024]{1,0:T(8,128)(2,1)S(1)}, u32[]{:S(2)}, u32[]{:S(2)}) collective-permute-start(bf16[16,1024]{1,0:T(8,128)(2,1)} %get-tuple-element.29), channel_id=1, source_target_pairs={{0,128},{128,256},{256,384},{384,0},{1,129},{129,257},{257,385},{3... | collective-permute-start | bytes 98312 | tf_op jit(solution)/shard_map/ppermute | solution.py:329
  31.2 3.9 %collective-permute-start.6 = (bf16[16,1024]{1,0:T(8,128)(2,1)}, bf16[16,1024]{1,0:T(8,128)(2,1)S(1)}, u32[]{:S(2)}, u32[]{:S(2)}) collective-permute-start(bf16[16,1024]{1,0:T(8,128)(2,1)} %get-tuple-element.29), channel_id=1, source_target_pairs={{0,384},{128,0},{256,128},{384,256},{1,385},{129,1},{257,129},{385... | collective-permute-start | bytes 98312 | tf_op jit(solution)/shard_map/ppermute | solution.py:329
  35.1 0.8 constant_dynamic-update-slice_fusion.3
  35.9 2.8 %collective-permute-start.7 = (bf16[16,1024]{1,0:T(8,128)(2,1)}, bf16[16,1024]{1,0:T(8,128)(2,1)S(1)}, u32[]{:S(2)}, u32[]{:S(2)}) collective-permute-start(bf16[16,1024]{1,0:T(8,128)(2,1)} %get-tuple-element.29), channel_id=1, source_target_pairs={{0,256},{128,384},{256,0},{384,128},{1,257},{129,385},{257,1},{385... | collective-permute-start | bytes 98312 | tf_op jit(solution)/shard_map/ppermute | solution.py:329
  38.8 4.6 %collective-permute-done.7 = bf16[16,1024]{1,0:T(8,128)(2,1)S(1)} collective-permute-done((bf16[16,1024]{1,0:T(8,128)(2,1)}, bf16[16,1024]{1,0:T(8,128)(2,1)S(1)}, u32[]{:S(2)}, u32[]{:S(2)}) %collective-permute-start.7) | collective-permute-done | bytes 32800 | tf_op jit(solution)/shard_map/ppermute | solution.py:329
  43.4 2.4 %collective-permute-start.8 = (bf16[64,1024]{1,0:T(8,128)(2,1)S(1)}, bf16[64,1024]{1,0:T(8,128)(2,1)S(1)}, u32[]{:S(2)}, u32[]{:S(2)}) collective-permute-start(bf16[64,1024]{1,0:T(8,128)(2,1)S(1)} %constant_dynamic-update-slice_fusion), channel_id=1, source_target_pairs={{0,4},{4,0},{1,5},{5,1},{2,6},{6,2},{3,7},{7,3},{8,12},{12,8},{9,1... | collective-permute-start | bytes 393224 | tf_op jit(solution)/shard_map/ppermute | solution.py:329
  45.9 4.4 %collective-permute-done.8 = bf16[64,1024]{1,0:T(8,128)(2,1)S(1)} collective-permute-done((bf16[64,1024]{1,0:T(8,128)(2,1)S(1)}, bf16[64,1024]{1,0:T(8,128)(2,1)S(1)}, u32[]{:S(2)}, u32[]{:S(2)}) %collective-permute-start.8) | collective-permute-done | bytes 131104 | tf_op jit(solution)/shard_map/ppermute | solution.py:329
  51.9 5.5 %collective-permute-start.2 = (bf16[2,2,32,1024]{3,2,1,0:T(8,128)(2,1)S(1)}, bf16[2,2,32,1024]{3,2,1,0:T(8,128)(2,1)S(1)}, u32[]{:S(2)}, u32[]{:S(2)}) collective-permute-start(bf16[2,2,32,1024]{3,2,1,0:T(8,128)(2,1)S(1)} %slice_select_fusion), channel_id=1, source_target_pairs={{8,0},{16,8},{24,16},{32,24},{40,32},{48,40},{56,48},{64,56},{72,6... | collective-permute-start | bytes 786440 | tf_op jit(solution)/shard_map/ppermute | solution.py:340
  57.4 0.7 slice_bitcast_fusion.1
  58.2 0.7 slice_bitcast_fusion
  58.9 4.1 %collective-permute-done.2 = bf16[2,2,32,1024]{3,2,1,0:T(8,128)(2,1)S(1)} collective-permute-done((bf16[2,2,32,1024]{3,2,1,0:T(8,128)(2,1)S(1)}, bf16[2,2,32,1024]{3,2,1,0:T(8,128)(2,1)S(1)}, u32[]{:S(2)}, u32[]{:S(2)}) %collective-permute-start.2) | collective-permute-done | bytes 262176 | tf_op jit(solution)/shard_map/ppermute | solution.py:340
  63.8 4.7 %shard_map.38 = (bf16[2,288,1024]{2,1,0:T(8,128)(2,1)}, bf16[2,288,1024]{2,1,0:T(8,128)(2,1)}, bf16[2,256,1024]{2,1,0:T(8,128)(2,1)}, bf16[2,128,1024]{2,1,0:T(8,128)(2,1)}) custom-call(s32[1]{0:T(128)} %bitcast.xl, bf16[256,2048]{1,0:T(8,128)(2,1)} %k_own.2, bf16[256,2048]{1,0:T(8,128)(2,1)} %v_own.2, bf16[2,256,1024]{2,1,0:T(8,128)(2,1)} %copy-done.1), custom_call_target="tpu_custom_call" | custom-call | bytes 18000000 | tf_op jit(solution)/shard_map/pallas_call | solution.py:110
  68.5 3.1 %collective-permute-start.4 = (bf16[576,1024]{1,0:T(8,128)(2,1)S(1)}, bf16[576,1024]{1,0:T(8,128)(2,1)S(1)}, u32[]{:S(2)}, u32[]{:S(2)}) collective-permute-start(bf16[576,1024]{1,0:T(8,128)(2,1)S(1)} %pad_maximum_fusion), channel_id=1, source_target_pairs={{0,4},{4,0},{1,5},{5,1},{2,6},{6,2},{3,7},{7,3},{8,12},{12,8},{9,1... | collective-permute-start | bytes 3538952 | tf_op jit(solution)/shard_map/ppermute | solution.py:329
  71.7 5.2 %collective-permute-start.10 = (bf16[2,288,1024]{2,1,0:T(8,128)(2,1)}, bf16[2,288,1024]{2,1,0:T(8,128)(2,1)S(1)}, u32[]{:S(2)}, u32[]{:S(2)}) collective-permute-start(bf16[2,288,1024]{2,1,0:T(8,128)(2,1)} %get-tuple-element.34), channel_id=1, source_target_pairs={{8,0},{16,8},{24,16},{32,24},{40,32},{48,40},{56,48},{64,56},{72,6... | collective-permute-start | bytes 3538952 | tf_op jit(solution)/shard_map/ppermute | solution.py:334
  76.9 1.9 %collective-permute-start.9 = (bf16[2,288,1024]{2,1,0:T(8,128)(2,1)}, bf16[2,288,1024]{2,1,0:T(8,128)(2,1)S(1)}, u32[]{:S(2)}, u32[]{:S(2)}) collective-permute-start(bf16[2,288,1024]{2,1,0:T(8,128)(2,1)} %get-tuple-element.33), channel_id=1, source_target_pairs={{0,8},{8,16},{16,24},{24,32},{32,40},{40,48},{48,56},{56,64},{64,7... | collective-permute-start | bytes 3538952 | tf_op jit(solution)/shard_map/ppermute | solution.py:334
  78.8 18.5 %collective-permute-done.4 = bf16[576,1024]{1,0:T(8,128)(2,1)S(1)} collective-permute-done((bf16[576,1024]{1,0:T(8,128)(2,1)S(1)}, bf16[576,1024]{1,0:T(8,128)(2,1)S(1)}, u32[]{:S(2)}, u32[]{:S(2)}) %collective-permute-start.4) | collective-permute-done | bytes 1179680 | tf_op jit(solution)/shard_map/ppermute | solution.py:329
  97.3 0.8 slice.61.q_got
  98.8 0.8 fusion
  99.6 17.9 %collective-permute-done.10.above1 = bf16[2,288,1024]{2,1,0:T(8,128)(2,1)S(1)} collective-permute-done((bf16[2,288,1024]{2,1,0:T(8,128)(2,1)}, bf16[2,288,1024]{2,1,0:T(8,128)(2,1)S(1)}, u32[]{:S(2)}, u32[]{:S(2)}) %collective-permute-start.10) | collective-permute-done | bytes 1179680 | tf_op jit(solution)/shard_map/ppermute | solution.py:334
  117.6 5.1 %collective-permute-done.9.below1 = bf16[2,288,1024]{2,1,0:T(8,128)(2,1)S(1)} collective-permute-done((bf16[2,288,1024]{2,1,0:T(8,128)(2,1)}, bf16[2,288,1024]{2,1,0:T(8,128)(2,1)S(1)}, u32[]{:S(2)}, u32[]{:S(2)}) %collective-permute-start.9) | collective-permute-done | bytes 1179680 | tf_op jit(solution)/shard_map/ppermute | solution.py:334
  122.7 1.1 copy-done.3
  123.8 16.3 %shard_map.39 = (f32[512,1024]{1,0:T(8,128)}, f32[512,1024]{1,0:T(8,128)}) custom-call(s32[1]{0:T(128)} %bitcast.xl, bf16[256,2048]{1,0:T(8,128)(2,1)} %q_own.3, bf16[256,1024]{1,0:T(8,128)(2,1)} %slice.61.q_got, bf16[256,2048]{1,0:T(8,128)(2,1)} %k_own.2, bf16[256,2048]{1,0:T(8,128)(2,1)} %v_own.2, bf16[2,256,1024]{2,1,0:T(8,128)(2,1)} %copy-done.1, ...), custom_call_target="tpu_custom_call" | custom-call | bytes 54000000 | tf_op jit(solution)/shard_map/pallas_call | solution.py:283
  140.2 11.7 %shard_map.40 = (bf16[256,2048]{1,0:T(8,128)(2,1)}, bf16[256,1024]{1,0:T(8,128)(2,1)}) custom-call(s32[1]{0:T(128)} %bitcast.xl, bf16[256,2048]{1,0:T(8,128)(2,1)} %q_own.3, bf16[256,1024]{1,0:T(8,128)(2,1)} %slice.61.q_got, bf16[16,2,32,1024]{3,2,1,0:T(8,128)(2,1)} %bitcast.25, f32[512,1024]{1,0:T(8,128)} %get-tuple-element.35.near_out, ...), custom_call_target="tpu_custom_call" | custom-call | bytes 32400000 | tf_op jit(solution)/shard_map/pallas_call | solution.py:283
  151.9 3.6 %collective-permute-start.11 = (bf16[256,1024]{1,0:T(8,128)(2,1)}, bf16[256,1024]{1,0:T(8,128)(2,1)S(1)}, u32[]{:S(2)}, u32[]{:S(2)}) collective-permute-start(bf16[256,1024]{1,0:T(8,128)(2,1)} %get-tuple-element.38), channel_id=1, source_target_pairs={{0,4},{4,0},{1,5},{5,1},{2,6},{6,2},{3,7},{7,3},{8,12},{12,8},{9,1... | collective-permute-start | bytes 1572872 | tf_op jit(solution)/shard_map/ppermute | solution.py:329
  155.6 10.5 %collective-permute-done.11 = bf16[256,1024]{1,0:T(8,128)(2,1)S(1)} collective-permute-done((bf16[256,1024]{1,0:T(8,128)(2,1)}, bf16[256,1024]{1,0:T(8,128)(2,1)S(1)}, u32[]{:S(2)}, u32[]{:S(2)}) %collective-permute-start.11) | collective-permute-done | bytes 524320 | tf_op jit(solution)/shard_map/ppermute | solution.py:329
  166.1 0.8 constant_dynamic-update-slice_fusion.4
  (25 shorter events, 3.0 us)
Async XLA Ops:
  6.5 133.7 %all-gather.3.cloned.1.call-start = ((), (), s32[]{:S(2)}) async-start(), calls=%async_computation | async-start | bytes 2228224 | tf_op jit(solution)/shard_map/all_gather | solution.py:369
  8.9 42.9 %collective-permute-start.3 = (bf16[2,256,1024]{2,1,0:T(8,128)(2,1)}, bf16[2,256,1024]{2,1,0:T(8,128)(2,1)S(1)}, u32[]{:S(2)}, u32[]{:S(2)}) collective-permute-start(bf16[2,256,1024]{2,1,0:T(8,128)(2,1)} %pad_maximum_fusion.1), channel_id=1, source_target_pairs={{0,4},{4,0},{1,5},{5,1},{2,6},{6,2},{3,7},{7,3},{8,12},{12,8},{9,1... | collective-permute-start | bytes 3145736 | tf_op jit(solution)/shard_map/ppermute | solution.py:329
  12.3 39.5 %copy-start = (bf16[256,2048]{1,0:T(8,128)(2,1)S(1)}, bf16[256,2048]{1,0:T(8,128)(2,1)}, u32[]{:S(2)}) copy-start(bf16[256,2048]{1,0:T(8,128)(2,1)} %q_own.3) | copy-start | bytes 3145732
  15.3 35.8 %collective-permute-start = (bf16[2,2,64,1024]{3,2,1,0:T(8,128)(2,1)}, bf16[2,2,64,1024]{3,2,1,0:T(8,128)(2,1)S(1)}, u32[]{:S(2)}, u32[]{:S(2)}) collective-permute-start(bf16[2,2,64,1024]{3,2,1,0:T(8,128)(2,1)} %get-tuple-element.24), channel_id=1, source_target_pairs={{0,16},{8,24},{16,32},{24,40},{32,48},{40,56},{48,64},{56,72},{64,... | collective-permute-start | bytes 1572872 | tf_op jit(solution)/shard_map/ppermute | solution.py:334
  20.5 31.2 %collective-permute-start.1 = (bf16[2,2,64,1024]{3,2,1,0:T(8,128)(2,1)}, bf16[2,2,64,1024]{3,2,1,0:T(8,128)(2,1)S(1)}, u32[]{:S(2)}, u32[]{:S(2)}) collective-permute-start(bf16[2,2,64,1024]{3,2,1,0:T(8,128)(2,1)} %get-tuple-element.24), channel_id=1, source_target_pairs={{16,0},{24,8},{32,16},{40,24},{48,32},{56,40},{64,48},{72,56},{80,... | collective-permute-start | bytes 1572872 | tf_op jit(solution)/shard_map/ppermute | solution.py:334
  29.3 6.6 %collective-permute-start.5 = (bf16[16,1024]{1,0:T(8,128)(2,1)}, bf16[16,1024]{1,0:T(8,128)(2,1)S(1)}, u32[]{:S(2)}, u32[]{:S(2)}) collective-permute-start(bf16[16,1024]{1,0:T(8,128)(2,1)} %get-tuple-element.29), channel_id=1, source_target_pairs={{0,128},{128,256},{256,384},{384,0},{1,129},{129,257},{257,385},{3... | collective-permute-start | bytes 98312 | tf_op jit(solution)/shard_map/ppermute | solution.py:329
  31.2 7.6 %collective-permute-start.6 = (bf16[16,1024]{1,0:T(8,128)(2,1)}, bf16[16,1024]{1,0:T(8,128)(2,1)S(1)}, u32[]{:S(2)}, u32[]{:S(2)}) collective-permute-start(bf16[16,1024]{1,0:T(8,128)(2,1)} %get-tuple-element.29), channel_id=1, source_target_pairs={{0,384},{128,0},{256,128},{384,256},{1,385},{129,1},{257,129},{385... | collective-permute-start | bytes 98312 | tf_op jit(solution)/shard_map/ppermute | solution.py:329
  35.9 7.5 %collective-permute-start.7 = (bf16[16,1024]{1,0:T(8,128)(2,1)}, bf16[16,1024]{1,0:T(8,128)(2,1)S(1)}, u32[]{:S(2)}, u32[]{:S(2)}) collective-permute-start(bf16[16,1024]{1,0:T(8,128)(2,1)} %get-tuple-element.29), channel_id=1, source_target_pairs={{0,256},{128,384},{256,0},{384,128},{1,257},{129,385},{257,1},{385... | collective-permute-start | bytes 98312 | tf_op jit(solution)/shard_map/ppermute | solution.py:329
  43.4 6.8 %collective-permute-start.8 = (bf16[64,1024]{1,0:T(8,128)(2,1)S(1)}, bf16[64,1024]{1,0:T(8,128)(2,1)S(1)}, u32[]{:S(2)}, u32[]{:S(2)}) collective-permute-start(bf16[64,1024]{1,0:T(8,128)(2,1)S(1)} %constant_dynamic-update-slice_fusion), channel_id=1, source_target_pairs={{0,4},{4,0},{1,5},{5,1},{2,6},{6,2},{3,7},{7,3},{8,12},{12,8},{9,1... | collective-permute-start | bytes 393224 | tf_op jit(solution)/shard_map/ppermute | solution.py:329
  51.8 6.4 %copy-start.1 = (bf16[2,256,1024]{2,1,0:T(8,128)(2,1)}, bf16[2,256,1024]{2,1,0:T(8,128)(2,1)S(1)}, u32[]{:S(2)}) copy-start(bf16[2,256,1024]{2,1,0:T(8,128)(2,1)S(1)} %collective-permute-done.3.got_ref.kv_got) | copy-start | bytes 3145732
  51.9 11.2 %collective-permute-start.2 = (bf16[2,2,32,1024]{3,2,1,0:T(8,128)(2,1)S(1)}, bf16[2,2,32,1024]{3,2,1,0:T(8,128)(2,1)S(1)}, u32[]{:S(2)}, u32[]{:S(2)}) collective-permute-start(bf16[2,2,32,1024]{3,2,1,0:T(8,128)(2,1)S(1)} %slice_select_fusion), channel_id=1, source_target_pairs={{8,0},{16,8},{24,16},{32,24},{40,32},{48,40},{56,48},{64,56},{72,6... | collective-permute-start | bytes 786440 | tf_op jit(solution)/shard_map/ppermute | solution.py:340
  68.5 28.8 %collective-permute-start.4 = (bf16[576,1024]{1,0:T(8,128)(2,1)S(1)}, bf16[576,1024]{1,0:T(8,128)(2,1)S(1)}, u32[]{:S(2)}, u32[]{:S(2)}) collective-permute-start(bf16[576,1024]{1,0:T(8,128)(2,1)S(1)} %pad_maximum_fusion), channel_id=1, source_target_pairs={{0,4},{4,0},{1,5},{5,1},{2,6},{6,2},{3,7},{7,3},{8,12},{12,8},{9,1... | collective-permute-start | bytes 3538952 | tf_op jit(solution)/shard_map/ppermute | solution.py:329
  71.7 45.9 %collective-permute-start.10 = (bf16[2,288,1024]{2,1,0:T(8,128)(2,1)}, bf16[2,288,1024]{2,1,0:T(8,128)(2,1)S(1)}, u32[]{:S(2)}, u32[]{:S(2)}) collective-permute-start(bf16[2,288,1024]{2,1,0:T(8,128)(2,1)} %get-tuple-element.34), channel_id=1, source_target_pairs={{8,0},{16,8},{24,16},{32,24},{40,32},{48,40},{56,48},{64,56},{72,6... | collective-permute-start | bytes 3538952 | tf_op jit(solution)/shard_map/ppermute | solution.py:334
  76.9 45.8 %collective-permute-start.9 = (bf16[2,288,1024]{2,1,0:T(8,128)(2,1)}, bf16[2,288,1024]{2,1,0:T(8,128)(2,1)S(1)}, u32[]{:S(2)}, u32[]{:S(2)}) collective-permute-start(bf16[2,288,1024]{2,1,0:T(8,128)(2,1)} %get-tuple-element.33), channel_id=1, source_target_pairs={{0,8},{8,16},{16,24},{24,32},{32,40},{40,48},{48,56},{56,64},{64,7... | collective-permute-start | bytes 3538952 | tf_op jit(solution)/shard_map/ppermute | solution.py:334
  117.6 5.1 %copy-start.2 = (bf16[2,288,1024]{2,1,0:T(8,128)(2,1)}, bf16[2,288,1024]{2,1,0:T(8,128)(2,1)S(1)}, u32[]{:S(2)}) copy-start(bf16[2,288,1024]{2,1,0:T(8,128)(2,1)S(1)} %collective-permute-done.10.above1) | copy-start | bytes 3538948
  122.7 1.1 copy-start.3
  151.9 14.1 %collective-permute-start.11 = (bf16[256,1024]{1,0:T(8,128)(2,1)}, bf16[256,1024]{1,0:T(8,128)(2,1)S(1)}, u32[]{:S(2)}, u32[]{:S(2)}) collective-permute-start(bf16[256,1024]{1,0:T(8,128)(2,1)} %get-tuple-element.38), channel_id=1, source_target_pairs={{0,4},{4,0},{1,5},{5,1},{2,6},{6,2},{3,7},{7,3},{8,12},{12,8},{9,1... | collective-permute-start | bytes 1572872 | tf_op jit(solution)/shard_map/ppermute | solution.py:329
Sparse Core Ops, SparseCore 0:
  51.9 76.1 all-gather.2

commit v3 on v2

--- a/solution.py
+++ b/solution.py
@@ -12,6 +12,7 @@
 D = 128
 BLOCK = 128
 FAR_REACH = 9
+LOWEST = 7
 SEQ = ("y", "z", "xl")
 YZ = ("y", "z")
 Z = "z"
@@ -50,7 +51,7 @@
     for i, refs in enumerate(((k_own, k_send), (v_own, v_send))):
         for j, ref in enumerate(refs):
             four = halved(halved(ref[...].astype(F32), scratch).astype(F32), scratch)
-            far_ref[j, i] = four
+            far_ref[j, i] = jnp.where(xl[0] == 0, four[0:32], four[32:64])
             rows, cols = four.shape
             pieces.append(jnp.sum(four.astype(F32).reshape(rows // 16, 16, cols), axis=1) * (1.0 / 16))
     unit_ref[...] = jnp.concatenate(pieces, axis=0).astype(BF)
@@ -68,14 +69,37 @@
             in_specs=[own, send, own, send],
             out_specs=[
                 pl.BlockSpec((16, width), lambda c, xl: (0, c)),
-                pl.BlockSpec((2, 2, rows // 4, width), lambda c, xl: (0, 0, 0, c)),
+                pl.BlockSpec((2, 2, rows // 8, width), lambda c, xl: (0, 0, 0, c)),
             ],
             scratch_shapes=[pltpu.VMEM((width // D, rows, D), F32)],
         ),
-        out_shape=[jax.ShapeDtypeStruct((16, cols), BF), jax.ShapeDtypeStruct((2, 2, rows // 4, cols), BF)],
+        out_shape=[jax.ShapeDtypeStruct((16, cols), BF), jax.ShapeDtypeStruct((2, 2, rows // 8, cols), BF)],
         compiler_params=VMEM,
         cost_estimate=taking(4),
     )(xl, k, k, v, v)
+
+
+def arrange_kernel(*refs):
+    *parts, out_ref = refs
+    rows = jnp.concatenate([ref[...].astype(F32) for ref in parts], axis=0)
+    n, cols = rows.shape
+    rows = rows.reshape(n // 16, 2, 8, cols)
+    for i in range(2):
+        out_ref[i] = rows[:, i].reshape(n // 2, cols).astype(BF)
+
+
+def arranged(*parts):
+    n, cols = sum(a.shape[0] for a in parts), parts[0].shape[1]
+    width = 256
+    return pl.pallas_call(
+        arrange_kernel,
+        grid=(cols // width,),
+        in_specs=[pl.BlockSpec((a.shape[0], width), lambda c: (0, c)) for a in parts],
+        out_specs=pl.BlockSpec((2, n // 2, width), lambda c: (0, 0, c)),
+        out_shape=jax.ShapeDtypeStruct((2, n // 2, cols), BF),
+        compiler_params=VMEM,
+        cost_estimate=taking(2),
+    )(*parts)
 
 
 def pool_kernel(xl, k_ref, v_ref, got_ref, up_ref, down_ref, mid_ref, far_ref, scratch):
@@ -121,6 +145,32 @@
     )(xl, k, v, got)
 
 
+def forward_kernel(below_ref, above_ref, up_ref, down_ref, near_ref, scratch):
+    below, above = below_ref[0], above_ref[0]
+    below_near = halved(below[0:128].astype(F32), scratch)
+    above_near = halved(above[0:128].astype(F32), scratch)
+    near_ref[0, 0:64] = below_near
+    near_ref[0, 64:128] = above_near
+    up_ref[0, 0:32] = below[256:288]
+    up_ref[0, 32:128] = halved(jnp.concatenate([below[128:256], below_near], axis=0).astype(F32), scratch)
+    down_ref[0, 0:96] = halved(jnp.concatenate([above_near, above[128:256]], axis=0).astype(F32), scratch)
+    down_ref[0, 96:128] = above[256:288]
+
+
+def forwarded(below, above):
+    _, rows, cols = below.shape
+    width = 512
+    return pl.pallas_call(
+        forward_kernel,
+        grid=(2, cols // width),
+        in_specs=[pl.BlockSpec((1, rows, width), lambda i, c: (i, 0, c))] * 2,
+        out_specs=[pl.BlockSpec((1, 128, width), lambda i, c: (i, 0, c))] * 3,
+        out_shape=[jax.ShapeDtypeStruct((2, 128, cols), BF)] * 3,
+        scratch_shapes=[pltpu.VMEM((width // D, 192, D), F32)],
+        compiler_params=VMEM, cost_estimate=taking(4),
+    )(below, above)
+
+
 def flags(blocks, first, unit, ref):
     ny, nz = lax.axis_size("y"), lax.axis_size("z")
     at = 4 * (lax.axis_index("y") * nz + lax.axis_index("z"))
@@ -159,72 +209,61 @@
 
 
 def near_kernel(
-    xl, q_own, q_got, k_own, v_own, kv_got, mid, far, below1, above1,
-    below_own, below_got, above_own, above_got, edge_own, edge_got,
-    out, stat, kf, vf, km, vm, kr, vr, kfar, vfar, scratch,
+    xl, q_own, q_got, k_own, v_own, kv_got, mid, below1, above1, near, coarse0, coarse1, coarse2, coarse3,
+    out, stat, kf, vf, km, vm, kc, vc, mask,
 ):
     low = xl[0] == 0
+    coarse_n = mask.shape[1]
 
     @pl.when(pl.program_id(0) == 0)
     def _():
         flags(6, -1, 128, vf)
         flags(10, -3, 64, vm)
-        flags(22, -9, 32, vr)
+        vc[:, D : 2 * D] = jnp.ones((coarse_n, D), BF)
+        y, z = lax.axis_index("y"), lax.axis_index("z")
+        ny, nz = lax.axis_size("y"), lax.axis_size("z")
+        at = lax.broadcasted_iota(jnp.int32, (16, coarse_n), 1)
+        turn = at // (8 * nz)
+        other_y = (y + jnp.where(turn == 0, 0, jnp.where(turn == 1, ny - 1, jnp.where(turn == 2, 1, 2)))) % ny
+        other_z = (z + (at // 8) % nz + nz - LOWEST) % nz
+        block = (other_y * nz + other_z) * 4 + (at % 8) // 2
+        for b in range(4):
+            gap = jnp.abs(block - (4 * (y * nz + z) + b))
+            mask[b * 16 : (b + 1) * 16, :] = jnp.where(gap > FAR_REACH, 1.0, 0.0).astype(BF)
 
     has, has_up = present()
-    for i, (own_ref, fine_w, mid_w, far_w) in enumerate(((k_own, kf, km, kr), (v_own, vf, vm, vr))):
+    for i, (own_ref, fine_w, mid_w) in enumerate(((k_own, kf, km), (v_own, vf, vm))):
         is_key = i == 0
-
-        def spare(rows):
-            return rows if is_key else None
-
         own, got = own_ref[...], kv_got[i]
         first, second = jnp.where(low, own, got), jnp.where(low, got, own)
         fine_w[128:384, 0:D] = first
         fine_w[384:640, 0:D] = second
-        put(fine_w, 0, below1[i, 0:128], has[1], spare(first[0:128]))
-        put(fine_w, 640, above1[i, 0:128], has_up[1], spare(second[128:256]))
+        put(fine_w, 0, below1[i, 0:128], has[1], first[0:128] if is_key else None)
+        put(fine_w, 640, above1[i, 0:128], has_up[1], second[128:256] if is_key else None)
         mid_w[192:448, 0:D] = mid[i]
-        m0, m3 = spare(mid[i, 0:64]), spare(mid[i, 192:256])
-        mid_below = halved(below1[i, 0:128].astype(F32), scratch)
-        mid_above = halved(above1[i, 0:128].astype(F32), scratch)
+        m0 = mid[i, 0:64] if is_key else None
+        m3 = mid[i, 192:256] if is_key else None
         put(mid_w, 0, below1[i, 128:192], has[1], m0)
         put(mid_w, 64, below1[i, 192:256], has[1], m0)
-        put(mid_w, 128, mid_below, has[1], m0)
-        put(mid_w, 448, mid_above, has_up[1], m3)
+        put(mid_w, 128, near[i, 0:64], has[1], m0)
+        put(mid_w, 448, near[i, 64:128], has_up[1], m3)
         put(mid_w, 512, above1[i, 128:192], has_up[1], m3)
         put(mid_w, 576, above1[i, 192:256], has_up[1], m3)
-        far_w[288:416, 0:D] = far[i]
-        f0, f3 = far[i, 0:32], far[i, 96:128]
-        f0_2, f3_2 = spare(jnp.concatenate([f0] * 2, axis=0)), spare(jnp.concatenate([f3] * 2, axis=0))
-        f0_3, f3_3 = spare(jnp.concatenate([f0] * 3, axis=0)), spare(jnp.concatenate([f3] * 3, axis=0))
-        put(far_w, 0, jnp.where(low, edge_got[i], edge_own[i]), has[3], spare(f0))
-        put(far_w, 32, jnp.where(low, below_own[i], below_got[i]), has[2], f0_2)
-        put(far_w, 96, jnp.where(low, below_got[i], below_own[i]), has[2], f0_2)
-        put(far_w, 160, below1[i, 256:288], has[1], spare(f0))
-        rows = jnp.concatenate([below1[i, 128:256], mid_below], axis=0)
-        put(far_w, 192, halved(rows.astype(F32), scratch), has[1], f0_3)
-        rows = jnp.concatenate([mid_above, above1[i, 128:256]], axis=0)
-        put(far_w, 416, halved(rows.astype(F32), scratch), has_up[1], f3_3)
-        put(far_w, 512, above1[i, 256:288], has_up[1], spare(f3))
-        put(far_w, 544, jnp.where(low, above_own[i], above_got[i]), has_up[2], f3_2)
-        put(far_w, 608, jnp.where(low, above_got[i], above_own[i]), has_up[2], f3_2)
-        put(far_w, 672, jnp.where(low, edge_own[i], edge_got[i]), has_up[3], spare(f3))
+    step = coarse_n // 4
+    for t, part in enumerate((coarse0, coarse1, coarse2, coarse3)):
+        kc[t * step : (t + 1) * step] = part[0]
+        vc[t * step : (t + 1) * step, 0:D] = part[1]
     qo, qg = q_own[...], q_got[...]
     queries = (jnp.where(low, qo, qg), jnp.where(low, qg, qo))
     left = lax.broadcasted_iota(jnp.int32, (BLOCK, D), 1) < D // 2
     for b in range(4):
         q = queries[b // 2][(b % 2) * 128 : (b % 2 + 1) * 128]
-        kfar[0:192] = kr[b * 32 : b * 32 + 192]
-        kfar[192:384] = kr[(b + 13) * 32 : (b + 13) * 32 + 192]
-        vfar[0:192] = vr[b * 32 : b * 32 + 192]
-        vfar[192:384] = vr[(b + 13) * 32 : (b + 13) * 32 + 192]
         lo, up = b * 64, (b + 5) * 64
         parts = [
             (scores(q, kf[b * 128 : b * 128 + 384]), vf[b * 128 : b * 128 + 384], 0.0, None),
             (scores(q, km[lo : lo + 128]), vm[lo : lo + 128], 1.0, None),
             (scores(q, km[up : up + 128]), vm[up : up + 128], 1.0, None),
-            (scores(q, kfar[...]), vfar[...], 2.0, None),
+            (scores(q, kc[...]), vc[...], 6.0, mask[b * 16 : b * 16 + 1, :]),
         ]
         top = top_of(parts)
         total = weighted(parts, top)
@@ -232,31 +271,40 @@
         stat[b * 128 : (b + 1) * 128] = jnp.where(left, top, total[:, D : 2 * D])
 
 
-def far_kernel(xl, q_own, q_got, coarse, near_out, near_stat, own_out, send_out, kc, vc, mask):
+def far_kernel(
+    xl, q_own, q_got, far, up, down, below2, above2, edge_own, edge_got, near_out, near_stat,
+    own_out, send_out, kr, vr, kfar, vfar,
+):
     low = xl[0] == 0
-    y = lax.axis_index("y")
-    ny, nz = lax.axis_size("y"), lax.axis_size("z")
-    coarse_n = coarse.shape[0] * coarse.shape[2]
 
     @pl.when(pl.program_id(0) == 0)
     def _():
-        vc[:, D : 2 * D] = jnp.ones((coarse_n, D), BF)
-        at = lax.broadcasted_iota(jnp.int32, (16, coarse_n), 1)
-        turn = (at // 8) % ny
-        other = (y + jnp.where(turn == 0, 0, jnp.where(turn == 1, ny - 1, jnp.where(turn == 2, 1, 2)))) % ny
-        block = (other * nz + at // (8 * ny)) * 4 + (at % 8) // 2
-        for b in range(4):
-            gap = jnp.abs(block - (4 * (y * nz + lax.axis_index("z")) + b))
-            mask[b * 16 : (b + 1) * 16, :] = jnp.where(gap > FAR_REACH, 1.0, 0.0).astype(BF)
-
-    kc[...] = coarse[:, 0].reshape(coarse_n, D)
-    vc[:, 0:D] = coarse[:, 1].reshape(coarse_n, D)
+        flags(22, -9, 32, vr)
+
+    has, has_up = present()
+    for i, far_w in enumerate((kr, vr)):
+        is_key = i == 0
+        far_w[288:416, 0:D] = far[i]
+        f0 = far[i, 0:32] if is_key else None
+        f3 = far[i, 96:128] if is_key else None
+        f0_4 = jnp.concatenate([f0] * 4, axis=0) if is_key else None
+        f3_4 = jnp.concatenate([f3] * 4, axis=0) if is_key else None
+        put(far_w, 0, jnp.where(low, edge_got[i], edge_own[i]), has[3], f0)
+        put(far_w, 32, below2[i], has[2], f0_4)
+        put(far_w, 160, up[i], has[1], f0_4)
+        put(far_w, 416, down[i], has_up[1], f3_4)
+        put(far_w, 544, above2[i], has_up[2], f3_4)
+        put(far_w, 672, jnp.where(low, edge_own[i], edge_got[i]), has_up[3], f3)
     qo, qg = q_own[...], q_got[...]
     queries = (jnp.where(low, qo, qg), jnp.where(low, qg, qo))
     results = []
     for b in range(4):
         q = queries[b // 2][(b % 2) * 128 : (b % 2 + 1) * 128]
-        parts = [(scores(q, kc[...]), vc[...], 6.0, mask[b * 16 : b * 16 + 1, :])]
+        kfar[b, 0:192] = kr[b * 32 : b * 32 + 192]
+        kfar[b, 192:384] = kr[(b + 13) * 32 : (b + 13) * 32 + 192]
+        vfar[b, 0:192] = vr[b * 32 : b * 32 + 192]
+        vfar[b, 192:384] = vr[(b + 13) * 32 : (b + 13) * 32 + 192]
+        parts = [(scores(q, kfar[b]), vfar[b], 2.0, None)]
         here = slice(b * 128, (b + 1) * 128)
         near_top, near_sum = near_stat[here, 0:1], near_stat[here, D - 1 : D]
         top = jnp.maximum(top_of(parts), near_top)
@@ -298,27 +346,26 @@
 def attend_near(xl, q, q_got, k, v, arrays):
     rows, cols = q.shape[0], q.shape[1] // 2
     outs = [jax.ShapeDtypeStruct((2 * rows, cols), F32)] * 2
+    coarse_n = 4 * arrays[-1].shape[1]
     scratch = [
         pltpu.VMEM((768, D), BF), pltpu.VMEM((768, 2 * D), BF),
         pltpu.VMEM((640, D), BF), pltpu.VMEM((640, 2 * D), BF),
-        pltpu.VMEM((704, D), BF), pltpu.VMEM((704, 2 * D), BF),
-        pltpu.VMEM((384, D), BF), pltpu.VMEM((384, 2 * D), BF),
-        pltpu.VMEM((1, 192, D), F32),
-    ]
-    return attend_call(
-        near_kernel, xl, (q, k, v), (q_got, *arrays), outs, [by_head(a) for a in outs], scratch, 15
-    )
-
-
-def attend_far(xl, q, q_got, arrays):
-    rows, cols = q.shape[0], q.shape[1] // 2
-    outs = [jax.ShapeDtypeStruct((rows, 2 * cols), BF), jax.ShapeDtypeStruct((rows, cols), BF)]
-    coarse_n = arrays[0].shape[0] * arrays[0].shape[2]
-    scratch = [
         pltpu.VMEM((coarse_n, D), BF), pltpu.VMEM((coarse_n, 2 * D), BF),
         pltpu.VMEM((64, coarse_n), BF),
     ]
     return attend_call(
+        near_kernel, xl, (q, k, v), (q_got, *arrays), outs, [by_head(a) for a in outs], scratch, 16
+    )
+
+
+def attend_far(xl, q, q_got, arrays):
+    rows, cols = q.shape[0], q.shape[1] // 2
+    outs = [jax.ShapeDtypeStruct((rows, 2 * cols), BF), jax.ShapeDtypeStruct((rows, cols), BF)]
+    scratch = [
+        pltpu.VMEM((704, D), BF), pltpu.VMEM((704, 2 * D), BF),
+        pltpu.VMEM((4, 384, D), BF), pltpu.VMEM((4, 384, 2 * D), BF),
+    ]
+    return attend_call(
         far_kernel, xl, (q,), (q_got, *arrays), outs,
         [pl.BlockSpec((rows, D), column(D)), by_head(outs[1])], scratch, 9,
     )
@@ -334,9 +381,10 @@
     return lax.ppermute(a, YZ, [(i, i + step) for i in range(n) if 0 <= i + step < n])
 
 
-def outward(a):
+def outward(a, step):
     n = lax.axis_size(YZ)
-    route = [(2 * i, 2 * i - 2) for i in range(1, n)] + [(2 * i + 1, 2 * i + 3) for i in range(n - 1)]
+    route = [(2 * i, 2 * (i - step)) for i in range(step, n)]
+    route += [(2 * i + 1, 2 * (i + step) + 1) for i in range(n - step)]
     return lax.ppermute(a, SEQ, route)
 
 
@@ -356,32 +404,32 @@
         (jnp.stack([theirs(key_rows), theirs(value_rows)]), key_rows, value_rows)
     )
     kv_got = swapped(kv_send)
-    unit, fours = native_rows(at, keys, values)
-    turned = (moved(unit, "y", 1), moved(unit, "y", -1), moved(unit, "y", 2))
-    below2, above2 = shifted(fours, 2), shifted(fours, -2)
-    units = jnp.concatenate([unit, *turned], axis=0)
-    units_got = swapped(units)
-    kept = units.reshape(4, 2, 8, half)[:, :, 0:4]
-    came = units_got.reshape(4, 2, 8, half)[:, :, 4:8]
-    units = jnp.concatenate([jnp.where(low, kept, came), jnp.where(low, came, kept)], axis=2)
-    units = jnp.moveaxis(units, 1, 0).reshape(2, 32, half)
-    units, _, _, _ = lax.optimization_barrier((units, kv_got, below2, above2))
-    coarse = lax.all_gather(units, "z")
-    edge = outward(jnp.where(low, above2[:, :, 0:32], below2[:, :, 32:64]))
-    sent = (theirs(queries), below2[1], above2[1], edge[1])
+    unit, outer = native_rows(at, keys, values)
+    unit_got = swapped(unit)
+    kept = unit.reshape(2, 8, half)[:, 0:4]
+    came = unit_got.reshape(2, 8, half)[:, 4:8]
+    unit = jnp.concatenate([jnp.where(low, kept, came), jnp.where(low, came, kept)], axis=1).reshape(16, half)
+    units = jnp.concatenate([moved(unit, "z", 1), unit, moved(unit, "z", -1)], axis=0)
+    units = jnp.concatenate([moved(units, "z", 3), units, moved(units, "z", -3)], axis=0)
+    lower, upper = units[16:64], units[80:144]
+    lower, upper, _, outer = lax.optimization_barrier((lower, upper, kv_got, outer))
+    units = arranged(moved(lower, "z", 4), units, moved(upper, "z", -4))
     up1, down1, mid, far = pooled(at, key_rows, value_rows, kv_got)
-    message = jnp.concatenate([a.reshape(-1, half) for a in sent], axis=0)
-    message, up1, down1 = lax.optimization_barrier((message, up1, down1))
+    up1, down1, units = lax.optimization_barrier((up1, down1, units))
+    below1, above1 = shifted(up1, 1), shifted(down1, -1)
+    coarse = (units, moved(units, "y", 1), moved(units, "y", -1), moved(units, "y", 2))
+    edge = outward(outer, 3)
+    message = jnp.concatenate([theirs(queries), edge[1].reshape(-1, half)], axis=0)
     got = swapped(message)
-    q_got, below_got, above_got, edge_got = (
-        got[i:j].reshape(a.shape) for a, i, j in zip(sent, (0, 256, 384, 512), (256, 384, 512, 576))
-    )
-    below1, above1 = shifted(up1, 1), shifted(down1, -1)
+    q_got, edge_got = got[0 : queries.shape[0]], got[queries.shape[0] :].reshape(edge[1].shape)
+    up, down, near = forwarded(below1, above1)
+    below2, above2 = shifted(up, 1), shifted(down, -1)
     near_out, near_stat = attend_near(
-        at, queries, q_got, key_rows, value_rows,
-        (kv_got, mid, far, below1, above1, below2[0], below_got, above2[0], above_got, edge[0], edge_got),
-    )
-    out, send_out = attend_far(at, queries, q_got, (coarse, near_out, near_stat))
+        at, queries, q_got, key_rows, value_rows, (kv_got, mid, below1, above1, near, *coarse)
+    )
+    out, send_out = attend_far(
+        at, queries, q_got, (far, up, down, below2, above2, edge[0], edge_got, near_out, near_stat)
+    )
     return lax.dynamic_update_slice_in_dim(out, swapped(send_out), (1 - xl) * half, 1)
 
 

time: 174 us -> 183 us (1.052)
  starting transfers between devices: 47.9 us -> 82.3 us
  waiting for transfers between devices: 65.9 us -> 47.4 us
  between operations: 13.6 us -> 0.39 us
  Pallas kernels: 35.8 us -> 41.9 us
    ppermute x7 -> x13, starting transfers between devices: 21.3 us -> 58.7 us  [moved(): return lax.ppermute(a, axis, [(i, (i + step) % n) for i in range(n)])]
    ppermute x4, waiting for transfers between devices: 23.7 us -> 11 us  [shifted(): lax.ppermute(a, YZ, [(i, i + step) for i in range(n) if 0 <= i + step < n])]
    pallas_call x0 -> x2, Pallas kernels: none -> 7.19 us  [the longest x1 4.05 us: forwarded(): pl.pallas_call(forward_kernel, grid=(2, cols // width), in_specs=[pl.Bloc...]
    ppermute x4, starting transfers between devices: 21.1 us -> 16 us  [shifted(): lax.ppermute(a, YZ, [(i, i + step) for i in range(n) if 0 <= i + step < n])]
    ppermute x1, waiting for transfers between devices: 4.13 us -> 0.01 us  [outward(): return lax.ppermute(a, SEQ, route)]
    unnamed x11 -> x28, local copies, waits for them, and re-layouts: 1.92 us -> 4.12 us
    ppermute x1, starting transfers between devices: 5.55 us -> 7.54 us  [outward(): return lax.ppermute(a, SEQ, route)]
    ppermute x7 -> x13, waiting for transfers between devices: 38 us -> 36.4 us  [moved(): return lax.ppermute(a, axis, [(i, (i + step) % n) for i in range(n)])]
  transfers between devices with their start and end apart: 13 -> 18, of which waited for: 8 -> 8; matrix products, arithmetic and copies ran while one was open for 4% -> 2% of each run, Pallas kernels for 14% -> 15%
where the time goes in v3:
time: 183 us; the launch traced here: 181 us
  starting transfers between devices  82.3 us (45%)
  waiting for transfers between devices  47.4 us (26%)
  Pallas kernels  41.9 us (23%)
  local copies, waits for them, and re-layouts  8.49 us (5%)
    ppermute x13, starting transfers between devices, moved(): return lax.ppermute(a, axis, [(i, (i + step) % n) for i in range(n)])  58.7 us
    ppermute x13, waiting for transfers between devices, moved(): return lax.ppermute(a, axis, [(i, (i + step) % n) for i in range(n)])  36.4 us
    pallas_call x2, Pallas kernels, attend_call(): pl.pallas_call(kernel, grid_spec=pltpu.PrefetchScalarGridSpec(num_scalar_...  26.9 us
    ppermute x4, starting transfers between devices, shifted(): lax.ppermute(a, YZ, [(i, i + step) for i in range(n) if 0 <= i + step < n])  16 us
    ppermute x4, waiting for transfers between devices, shifted(): lax.ppermute(a, YZ, [(i, i + step) for i in range(n) if 0 <= i + step < n])  11 us
    ppermute x1, starting transfers between devices, outward(): return lax.ppermute(a, SEQ, route)  7.54 us
    pallas_call x1, Pallas kernels, pooled(): pl.pallas_call(pool_kernel, grid_spec=pltpu.PrefetchScalarGridSpec(num_sc...  4.82 us
    unnamed x28, local copies, waits for them, and re-layouts  4.12 us
  transfers between devices with their start and end apart: 18, of which 8 were waited for; matrix products, arithmetic and copies ran while one was open for 2% of the time, Pallas kernels for 15%

profile of v3, /device:TPU:24, one launch (start us, length us, event | category | flops | bytes accessed | tf_op | source)
XLA Modules:
  0.0 181.5 jit_solution(11485533185492478692)
XLA Ops:
  0.0 1.3 dynamic-slice_bitcast_fusion
  1.4 2.9 %shard_map.37 = (bf16[16,1024]{1,0:T(8,128)(2,1)}, bf16[2,2,32,1024]{3,2,1,0:T(8,128)(2,1)}) custom-call(s32[1]{0:T(128)} %bitcast.xl, bf16[256,2048]{1,0:T(8,128)(2,1)} %k_own.2, bf16[256,2048]{1,0:T(8,128)(2,1)} %k_own.2, bf16[256,2048]{1,0:T(8,128)(2,1)} %v_own.2, bf16[256,2048]{1,0:T(8,128)(2,1)} %v_own.2), custom_call_target="tpu_custom_call" | custom-call | bytes 14400000 | tf_op jit(solution)/shard_map/pallas_call | solution.py:64
  4.3 3.4 %collective-permute-start = (bf16[16,1024]{1,0:T(8,128)(2,1)}, bf16[16,1024]{1,0:T(8,128)(2,1)S(1)}, u32[]{:S(2)}, u32[]{:S(2)}) collective-permute-start(bf16[16,1024]{1,0:T(8,128)(2,1)} %get-tuple-element.29), channel_id=1, source_target_pairs={{0,4},{4,0},{1,5},{5,1},{2,6},{6,2},{3,7},{7,3},{8,12},{12,8},{9,1... | collective-permute-start | bytes 98312 | tf_op jit(solution)/shard_map/ppermute | solution.py:376
  7.7 2.4 %collective-permute-start.5 = (bf16[2,256,1024]{2,1,0:T(8,128)(2,1)S(1)}, bf16[2,256,1024]{2,1,0:T(8,128)(2,1)S(1)}, u32[]{:S(2)}, u32[]{:S(2)}) collective-permute-start(bf16[2,256,1024]{2,1,0:T(8,128)(2,1)S(1)} %pad_maximum_fusion), channel_id=1, source_target_pairs={{0,4},{4,0},{1,5},{5,1},{2,6},{6,2},{3,7},{7,3},{8,12},{12,8},{9,1... | collective-permute-start | bytes 3145736 | tf_op jit(solution)/shard_map/ppermute | solution.py:376
  11.1 11.4 %collective-permute-start.2 = (bf16[16,1024]{1,0:T(8,128)(2,1)S(1)}, bf16[16,1024]{1,0:T(8,128)(2,1)S(1)}, u32[]{:S(2)}, u32[]{:S(2)}) collective-permute-start(bf16[16,1024]{1,0:T(8,128)(2,1)S(1)} %maximum_bitcast_fusion), channel_id=1, source_target_pairs={{0,120},{8,0},{16,8},{24,16},{32,24},{40,32},{48,40},{56,48},{64,5... | collective-permute-start | bytes 98312 | tf_op jit(solution)/shard_map/ppermute | solution.py:376
  22.5 1.9 %collective-permute-start.1 = (bf16[16,1024]{1,0:T(8,128)(2,1)S(1)}, bf16[16,1024]{1,0:T(8,128)(2,1)S(1)}, u32[]{:S(2)}, u32[]{:S(2)}) collective-permute-start(bf16[16,1024]{1,0:T(8,128)(2,1)S(1)} %maximum_bitcast_fusion), channel_id=1, source_target_pairs={{0,8},{8,16},{16,24},{24,32},{32,40},{40,48},{48,56},{56,64},{64,7... | collective-permute-start | bytes 98312 | tf_op jit(solution)/shard_map/ppermute | solution.py:376
  24.5 5.1 %collective-permute-done.1 = bf16[16,1024]{1,0:T(8,128)(2,1)S(1)} collective-permute-done((bf16[16,1024]{1,0:T(8,128)(2,1)S(1)}, bf16[16,1024]{1,0:T(8,128)(2,1)S(1)}, u32[]{:S(2)}, u32[]{:S(2)}) %collective-permute-start.1) | collective-permute-done | bytes 32800 | tf_op jit(solution)/shard_map/ppermute | solution.py:376
  29.6 1.9 %collective-permute-start.3 = (bf16[48,1024]{1,0:T(8,128)(2,1)S(1)}, bf16[48,1024]{1,0:T(8,128)(2,1)S(1)}, u32[]{:S(2)}, u32[]{:S(2)}) collective-permute-start(bf16[48,1024]{1,0:T(8,128)(2,1)S(1)} %pad_maximum_fusion.4), channel_id=1, source_target_pairs={{0,24},{8,32},{16,40},{24,48},{32,56},{40,64},{48,72},{56,80},{64,... | collective-permute-start | bytes 294920 | tf_op jit(solution)/shard_map/ppermute | solution.py:376
  31.5 6.9 %collective-permute-start.4 = (bf16[48,1024]{1,0:T(8,128)(2,1)S(1)}, bf16[48,1024]{1,0:T(8,128)(2,1)S(1)}, u32[]{:S(2)}, u32[]{:S(2)}) collective-permute-start(bf16[48,1024]{1,0:T(8,128)(2,1)S(1)} %pad_maximum_fusion.4), channel_id=1, source_target_pairs={{0,104},{8,112},{16,120},{24,0},{32,8},{40,16},{48,24},{56,32},{64... | collective-permute-start | bytes 294920 | tf_op jit(solution)/shard_map/ppermute | solution.py:376
  38.4 1.8 %collective-permute-done.3 = bf16[48,1024]{1,0:T(8,128)(2,1)S(1)} collective-permute-done((bf16[48,1024]{1,0:T(8,128)(2,1)S(1)}, bf16[48,1024]{1,0:T(8,128)(2,1)S(1)}, u32[]{:S(2)}, u32[]{:S(2)}) %collective-permute-start.3) | collective-permute-done | bytes 98336 | tf_op jit(solution)/shard_map/ppermute | solution.py:376
  41.4 6.0 %collective-permute-start.9 = (bf16[64,1024]{1,0:T(8,128)(2,1)S(1)}, bf16[64,1024]{1,0:T(8,128)(2,1)S(1)}, u32[]{:S(2)}, u32[]{:S(2)}) collective-permute-start(bf16[64,1024]{1,0:T(8,128)(2,1)S(1)} %pad_maximum_fusion.2), channel_id=1, source_target_pairs={{0,96},{8,104},{16,112},{24,120},{32,0},{40,8},{48,16},{56,24},{64... | collective-permute-start | bytes 393224 | tf_op jit(solution)/shard_map/ppermute | solution.py:376
  47.4 3.8 %collective-permute-start.8 = (bf16[48,1024]{1,0:T(8,128)(2,1)S(1)}, bf16[48,1024]{1,0:T(8,128)(2,1)S(1)}, u32[]{:S(2)}, u32[]{:S(2)}) collective-permute-start(bf16[48,1024]{1,0:T(8,128)(2,1)S(1)} %get-tuple-element.36), channel_id=1, source_target_pairs={{0,32},{8,40},{16,48},{24,56},{32,64},{40,72},{48,80},{56,88},{64,... | collective-permute-start | bytes 294920 | tf_op jit(solution)/shard_map/ppermute | solution.py:376
  51.2 7.5 %collective-permute-start.6 = (bf16[2,2,32,1024]{3,2,1,0:T(8,128)(2,1)}, bf16[2,2,32,1024]{3,2,1,0:T(8,128)(2,1)S(1)}, u32[]{:S(2)}, u32[]{:S(2)}) collective-permute-start(bf16[2,2,32,1024]{3,2,1,0:T(8,128)(2,1)} %get-tuple-element.32), channel_id=1, source_target_pairs={{24,0},{32,8},{40,16},{48,24},{56,32},{64,40},{72,48},{80,56},{88,... | collective-permute-start | bytes 786440 | tf_op jit(solution)/shard_map/ppermute | solution.py:388
  58.8 4.8 %shard_map.38 = (bf16[2,288,1024]{2,1,0:T(8,128)(2,1)}, bf16[2,288,1024]{2,1,0:T(8,128)(2,1)}, bf16[2,256,1024]{2,1,0:T(8,128)(2,1)}, bf16[2,128,1024]{2,1,0:T(8,128)(2,1)}) custom-call(s32[1]{0:T(128)} %bitcast.xl, bf16[256,2048]{1,0:T(8,128)(2,1)} %k_own.2, bf16[256,2048]{1,0:T(8,128)(2,1)} %v_own.2, bf16[2,256,1024]{2,1,0:T(8,128)(2,1)} %copy-done.3), custom_call_target="tpu_custom_call" | custom-call | bytes 18000000 | tf_op jit(solution)/shard_map/pallas_call | solution.py:134
  64.9 3.1 %shard_map.39.coarse0 = bf16[2,128,1024]{2,1,0:T(8,128)(2,1)} custom-call(bf16[48,1024]{1,0:T(8,128)(2,1)} %copy-done.12, bf16[144,1024]{1,0:T(8,128)(2,1)} %copy-done.7, bf16[64,1024]{1,0:T(8,128)(2,1)} %copy-done.11), custom_call_target="tpu_custom_call" | custom-call | bytes 7200000 | tf_op jit(solution)/shard_map/pallas_call | solution.py:94
  68.0 2.0 %collective-permute-start.10 = (bf16[2,288,1024]{2,1,0:T(8,128)(2,1)}, bf16[2,288,1024]{2,1,0:T(8,128)(2,1)S(1)}, u32[]{:S(2)}, u32[]{:S(2)}) collective-permute-start(bf16[2,288,1024]{2,1,0:T(8,128)(2,1)} %get-tuple-element.38), channel_id=1, source_target_pairs={{0,8},{8,16},{16,24},{24,32},{32,40},{40,48},{48,56},{56,64},{64,7... | collective-permute-start | bytes 3538952 | tf_op jit(solution)/shard_map/ppermute | solution.py:381
  70.1 6.0 %collective-permute-start.11 = (bf16[2,288,1024]{2,1,0:T(8,128)(2,1)}, bf16[2,288,1024]{2,1,0:T(8,128)(2,1)S(1)}, u32[]{:S(2)}, u32[]{:S(2)}) collective-permute-start(bf16[2,288,1024]{2,1,0:T(8,128)(2,1)} %get-tuple-element.39), channel_id=1, source_target_pairs={{8,0},{16,8},{24,16},{32,24},{40,32},{48,40},{56,48},{64,56},{72,6... | collective-permute-start | bytes 3538952 | tf_op jit(solution)/shard_map/ppermute | solution.py:381
  76.9 5.7 %collective-permute-start.7 = (bf16[320,1024]{1,0:T(8,128)(2,1)S(1)}, bf16[320,1024]{1,0:T(8,128)(2,1)S(1)}, u32[]{:S(2)}, u32[]{:S(2)}) collective-permute-start(bf16[320,1024]{1,0:T(8,128)(2,1)S(1)} %pad_maximum_fusion.1), channel_id=1, source_target_pairs={{0,4},{4,0},{1,5},{5,1},{2,6},{6,2},{3,7},{7,3},{8,12},{12,8},{9,1... | collective-permute-start | bytes 1966088 | tf_op jit(solution)/shard_map/ppermute | solution.py:376
  82.6 2.8 %collective-permute-start.16 = (bf16[2,128,1024]{2,1,0:T(8,128)(2,1)S(1)}, bf16[2,128,1024]{2,1,0:T(8,128)(2,1)S(1)}, u32[]{:S(2)}, u32[]{:S(2)}) collective-permute-start(bf16[2,128,1024]{2,1,0:T(8,128)(2,1)S(1)} %copy-done.4), channel_id=1, source_target_pairs={{0,256},{128,384},{256,0},{384,128},{1,257},{129,385},{257,1},{385... | collective-permute-start | bytes 1572872 | tf_op jit(solution)/shard_map/ppermute | solution.py:376
  85.4 1.9 %collective-permute-start.15 = (bf16[2,128,1024]{2,1,0:T(8,128)(2,1)S(1)}, bf16[2,128,1024]{2,1,0:T(8,128)(2,1)S(1)}, u32[]{:S(2)}, u32[]{:S(2)}) collective-permute-start(bf16[2,128,1024]{2,1,0:T(8,128)(2,1)S(1)} %copy-done.4), channel_id=1, source_target_pairs={{0,384},{128,0},{256,128},{384,256},{1,385},{129,1},{257,129},{385... | collective-permute-start | bytes 1572872 | tf_op jit(solution)/shard_map/ppermute | solution.py:376
  87.3 9.9 %collective-permute-done.10.below_ref.below1 = bf16[2,288,1024]{2,1,0:T(8,128)(2,1)S(1)} collective-permute-done((bf16[2,288,1024]{2,1,0:T(8,128)(2,1)}, bf16[2,288,1024]{2,1,0:T(8,128)(2,1)S(1)}, u32[]{:S(2)}, u32[]{:S(2)}) %collective-permute-start.10) | collective-permute-done | bytes 1179680 | tf_op jit(solution)/shard_map/ppermute | solution.py:381
  97.2 1.9 %collective-permute-start.14 = (bf16[2,128,1024]{2,1,0:T(8,128)(2,1)S(1)}, bf16[2,128,1024]{2,1,0:T(8,128)(2,1)S(1)}, u32[]{:S(2)}, u32[]{:S(2)}) collective-permute-start(bf16[2,128,1024]{2,1,0:T(8,128)(2,1)S(1)} %copy-done.4), channel_id=1, source_target_pairs={{0,128},{128,256},{256,384},{384,0},{1,129},{129,257},{257,385},{3... | collective-permute-start | bytes 1572872 | tf_op jit(solution)/shard_map/ppermute | solution.py:376
  99.2 1.1 collective-permute-done.11.above_ref.above1
  100.3 1.0 copy-done.2
  101.3 4.0 %shard_map.40 = (bf16[2,128,1024]{2,1,0:T(8,128)(2,1)}, bf16[2,128,1024]{2,1,0:T(8,128)(2,1)}, bf16[2,128,1024]{2,1,0:T(8,128)(2,1)}) custom-call(bf16[2,288,1024]{2,1,0:T(8,128)(2,1)} %copy-done.1, bf16[2,288,1024]{2,1,0:T(8,128)(2,1)} %copy-done.2), custom_call_target="tpu_custom_call" | custom-call | bytes 14400000 | tf_op jit(solution)/shard_map/pallas_call | solution.py:163
  105.4 1.9 %collective-permute-start.12 = (bf16[2,128,1024]{2,1,0:T(8,128)(2,1)}, bf16[2,128,1024]{2,1,0:T(8,128)(2,1)S(1)}, u32[]{:S(2)}, u32[]{:S(2)}) collective-permute-start(bf16[2,128,1024]{2,1,0:T(8,128)(2,1)} %get-tuple-element.40.up), channel_id=1, source_target_pairs={{0,8},{8,16},{16,24},{24,32},{32,40},{40,48},{48,56},{56,64},{64,7... | collective-permute-start | bytes 1572872 | tf_op jit(solution)/shard_map/ppermute | solution.py:381
  107.3 6.0 %collective-permute-start.13 = (bf16[2,128,1024]{2,1,0:T(8,128)(2,1)}, bf16[2,128,1024]{2,1,0:T(8,128)(2,1)S(1)}, u32[]{:S(2)}, u32[]{:S(2)}) collective-permute-start(bf16[2,128,1024]{2,1,0:T(8,128)(2,1)} %get-tuple-element.41.down), channel_id=1, source_target_pairs={{8,0},{16,8},{24,16},{32,24},{40,32},{48,40},{56,48},{64,56},{72,6... | collective-permute-start | bytes 1572872 | tf_op jit(solution)/shard_map/ppermute | solution.py:381
  114.9 16.0 %collective-permute-done.14.coarse1 = bf16[2,128,1024]{2,1,0:T(8,128)(2,1)S(1)} collective-permute-done((bf16[2,128,1024]{2,1,0:T(8,128)(2,1)S(1)}, bf16[2,128,1024]{2,1,0:T(8,128)(2,1)S(1)}, u32[]{:S(2)}, u32[]{:S(2)}) %collective-permute-start.14) | collective-permute-done | bytes 524320 | tf_op jit(solution)/shard_map/ppermute | solution.py:376
  131.7 15.5 %shard_map.41 = (f32[512,1024]{1,0:T(8,128)}, f32[512,1024]{1,0:T(8,128)}) custom-call(s32[1]{0:T(128)} %bitcast.xl, bf16[256,2048]{1,0:T(8,128)(2,1)} %q_own.3, bf16[256,1024]{1,0:T(8,128)(2,1)} %slice.34.q_got, bf16[256,2048]{1,0:T(8,128)(2,1)} %k_own.2, bf16[256,2048]{1,0:T(8,128)(2,1)} %v_own.2, bf16[2,256,1024]{2,1,0:T(8,128)(2,1)} %copy-done.3, ...), custom_call_target="tpu_custom_call" | custom-call | bytes 57600000 | tf_op jit(solution)/shard_map/pallas_call | solution.py:331
  148.2 11.5 %shard_map.42 = (bf16[256,2048]{1,0:T(8,128)(2,1)}, bf16[256,1024]{1,0:T(8,128)(2,1)}) custom-call(s32[1]{0:T(128)} %bitcast.xl, bf16[256,2048]{1,0:T(8,128)(2,1)} %q_own.3, bf16[256,1024]{1,0:T(8,128)(2,1)} %slice.34.q_got, bf16[2,128,1024]{2,1,0:T(8,128)(2,1)} %get-tuple-element.33.far, bf16[2,128,1024]{2,1,0:T(8,128)(2,1)} %get-tuple-element.40.up, ...), custom_call_target="tpu_custom_call" | custom-call | bytes 32400000 | tf_op jit(solution)/shard_map/pallas_call | solution.py:331
  159.7 8.7 %collective-permute-start.17 = (bf16[256,1024]{1,0:T(8,128)(2,1)}, bf16[256,1024]{1,0:T(8,128)(2,1)S(1)}, u32[]{:S(2)}, u32[]{:S(2)}) collective-permute-start(bf16[256,1024]{1,0:T(8,128)(2,1)} %get-tuple-element.48), channel_id=1, source_target_pairs={{0,4},{4,0},{1,5},{5,1},{2,6},{6,2},{3,7},{7,3},{8,12},{12,8},{9,1... | collective-permute-start | bytes 1572872 | tf_op jit(solution)/shard_map/ppermute | solution.py:376
  168.3 12.3 %collective-permute-done.17 = bf16[256,1024]{1,0:T(8,128)(2,1)S(1)} collective-permute-done((bf16[256,1024]{1,0:T(8,128)(2,1)}, bf16[256,1024]{1,0:T(8,128)(2,1)S(1)}, u32[]{:S(2)}, u32[]{:S(2)}) %collective-permute-start.17) | collective-permute-done | bytes 524320 | tf_op jit(solution)/shard_map/ppermute | solution.py:376
  (53 shorter events, 8.4 us)
Async XLA Ops:
  4.3 6.0 %collective-permute-start = (bf16[16,1024]{1,0:T(8,128)(2,1)}, bf16[16,1024]{1,0:T(8,128)(2,1)S(1)}, u32[]{:S(2)}, u32[]{:S(2)}) collective-permute-start(bf16[16,1024]{1,0:T(8,128)(2,1)} %get-tuple-element.29), channel_id=1, source_target_pairs={{0,4},{4,0},{1,5},{5,1},{2,6},{6,2},{3,7},{7,3},{8,12},{12,8},{9,1... | collective-permute-start | bytes 98312 | tf_op jit(solution)/shard_map/ppermute | solution.py:376
  7.7 33.7 %collective-permute-start.5 = (bf16[2,256,1024]{2,1,0:T(8,128)(2,1)S(1)}, bf16[2,256,1024]{2,1,0:T(8,128)(2,1)S(1)}, u32[]{:S(2)}, u32[]{:S(2)}) collective-permute-start(bf16[2,256,1024]{2,1,0:T(8,128)(2,1)S(1)} %pad_maximum_fusion), channel_id=1, source_target_pairs={{0,4},{4,0},{1,5},{5,1},{2,6},{6,2},{3,7},{7,3},{8,12},{12,8},{9,1... | collective-permute-start | bytes 3145736 | tf_op jit(solution)/shard_map/ppermute | solution.py:376
  11.1 13.3 %collective-permute-start.2 = (bf16[16,1024]{1,0:T(8,128)(2,1)S(1)}, bf16[16,1024]{1,0:T(8,128)(2,1)S(1)}, u32[]{:S(2)}, u32[]{:S(2)}) collective-permute-start(bf16[16,1024]{1,0:T(8,128)(2,1)S(1)} %maximum_bitcast_fusion), channel_id=1, source_target_pairs={{0,120},{8,0},{16,8},{24,16},{32,24},{40,32},{48,40},{56,48},{64,5... | collective-permute-start | bytes 98312 | tf_op jit(solution)/shard_map/ppermute | solution.py:376
  22.5 7.0 %collective-permute-start.1 = (bf16[16,1024]{1,0:T(8,128)(2,1)S(1)}, bf16[16,1024]{1,0:T(8,128)(2,1)S(1)}, u32[]{:S(2)}, u32[]{:S(2)}) collective-permute-start(bf16[16,1024]{1,0:T(8,128)(2,1)S(1)} %maximum_bitcast_fusion), channel_id=1, source_target_pairs={{0,8},{8,16},{16,24},{24,32},{32,40},{40,48},{48,56},{56,64},{64,7... | collective-permute-start | bytes 98312 | tf_op jit(solution)/shard_map/ppermute | solution.py:376
  29.6 10.7 %collective-permute-start.3 = (bf16[48,1024]{1,0:T(8,128)(2,1)S(1)}, bf16[48,1024]{1,0:T(8,128)(2,1)S(1)}, u32[]{:S(2)}, u32[]{:S(2)}) collective-permute-start(bf16[48,1024]{1,0:T(8,128)(2,1)S(1)} %pad_maximum_fusion.4), channel_id=1, source_target_pairs={{0,24},{8,32},{16,40},{24,48},{32,56},{40,64},{48,72},{56,80},{64,... | collective-permute-start | bytes 294920 | tf_op jit(solution)/shard_map/ppermute | solution.py:376
  31.5 9.9 %collective-permute-start.4 = (bf16[48,1024]{1,0:T(8,128)(2,1)S(1)}, bf16[48,1024]{1,0:T(8,128)(2,1)S(1)}, u32[]{:S(2)}, u32[]{:S(2)}) collective-permute-start(bf16[48,1024]{1,0:T(8,128)(2,1)S(1)} %pad_maximum_fusion.4), channel_id=1, source_target_pairs={{0,104},{8,112},{16,120},{24,0},{32,8},{40,16},{48,24},{56,32},{64... | collective-permute-start | bytes 294920 | tf_op jit(solution)/shard_map/ppermute | solution.py:376
  41.4 17.4 %copy-start.3 = (bf16[2,256,1024]{2,1,0:T(8,128)(2,1)}, bf16[2,256,1024]{2,1,0:T(8,128)(2,1)S(1)}, u32[]{:S(2)}) copy-start(bf16[2,256,1024]{2,1,0:T(8,128)(2,1)S(1)} %collective-permute-done.5.got_ref.kv_got) | copy-start | bytes 3145732
  41.4 22.2 %collective-permute-start.9 = (bf16[64,1024]{1,0:T(8,128)(2,1)S(1)}, bf16[64,1024]{1,0:T(8,128)(2,1)S(1)}, u32[]{:S(2)}, u32[]{:S(2)}) collective-permute-start(bf16[64,1024]{1,0:T(8,128)(2,1)S(1)} %pad_maximum_fusion.2), channel_id=1, source_target_pairs={{0,96},{8,104},{16,112},{24,120},{32,0},{40,8},{48,16},{56,24},{64... | collective-permute-start | bytes 393224 | tf_op jit(solution)/shard_map/ppermute | solution.py:376
  47.4 16.2 %collective-permute-start.8 = (bf16[48,1024]{1,0:T(8,128)(2,1)S(1)}, bf16[48,1024]{1,0:T(8,128)(2,1)S(1)}, u32[]{:S(2)}, u32[]{:S(2)}) collective-permute-start(bf16[48,1024]{1,0:T(8,128)(2,1)S(1)} %get-tuple-element.36), channel_id=1, source_target_pairs={{0,32},{8,40},{16,48},{24,56},{32,64},{40,72},{48,80},{56,88},{64,... | collective-permute-start | bytes 294920 | tf_op jit(solution)/shard_map/ppermute | solution.py:376
  51.2 25.0 %collective-permute-start.6 = (bf16[2,2,32,1024]{3,2,1,0:T(8,128)(2,1)}, bf16[2,2,32,1024]{3,2,1,0:T(8,128)(2,1)S(1)}, u32[]{:S(2)}, u32[]{:S(2)}) collective-permute-start(bf16[2,2,32,1024]{3,2,1,0:T(8,128)(2,1)} %get-tuple-element.32), channel_id=1, source_target_pairs={{24,0},{32,8},{40,16},{48,24},{56,32},{64,40},{72,48},{80,56},{88,... | collective-permute-start | bytes 786440 | tf_op jit(solution)/shard_map/ppermute | solution.py:388
  58.7 4.8 %copy-start.7 = (bf16[144,1024]{1,0:T(8,128)(2,1)}, bf16[144,1024]{1,0:T(8,128)(2,1)S(1)}, u32[]{:S(2)}) copy-start(bf16[144,1024]{1,0:T(8,128)(2,1)S(1)} %constant_dynamic-update-slice_fusion.refs_1_) | copy-start | bytes 884740
  63.6 12.5 %copy-start = (bf16[256,2048]{1,0:T(8,128)(2,1)S(1)}, bf16[256,2048]{1,0:T(8,128)(2,1)}, u32[]{:S(2)}) copy-start(bf16[256,2048]{1,0:T(8,128)(2,1)} %q_own.3) | copy-start | bytes 3145732
  63.6 0.6 copy-start.12
  64.2 0.6 copy-start.11
  68.0 14.5 %copy-start.4 = (bf16[2,128,1024]{2,1,0:T(8,128)(2,1)S(1)}, bf16[2,128,1024]{2,1,0:T(8,128)(2,1)}, u32[]{:S(2)}) copy-start(bf16[2,128,1024]{2,1,0:T(8,128)(2,1)} %shard_map.39.coarse0) | copy-start | bytes 1572868
  68.0 29.2 %collective-permute-start.10 = (bf16[2,288,1024]{2,1,0:T(8,128)(2,1)}, bf16[2,288,1024]{2,1,0:T(8,128)(2,1)S(1)}, u32[]{:S(2)}, u32[]{:S(2)}) collective-permute-start(bf16[2,288,1024]{2,1,0:T(8,128)(2,1)} %get-tuple-element.38), channel_id=1, source_target_pairs={{0,8},{8,16},{16,24},{24,32},{32,40},{40,48},{48,56},{56,64},{64,7... | collective-permute-start | bytes 3538952 | tf_op jit(solution)/shard_map/ppermute | solution.py:381
  70.1 30.2 %collective-permute-start.11 = (bf16[2,288,1024]{2,1,0:T(8,128)(2,1)}, bf16[2,288,1024]{2,1,0:T(8,128)(2,1)S(1)}, u32[]{:S(2)}, u32[]{:S(2)}) collective-permute-start(bf16[2,288,1024]{2,1,0:T(8,128)(2,1)} %get-tuple-element.39), channel_id=1, source_target_pairs={{8,0},{16,8},{24,16},{32,24},{40,32},{48,40},{56,48},{64,56},{72,6... | collective-permute-start | bytes 3538952 | tf_op jit(solution)/shard_map/ppermute | solution.py:381
  76.9 30.4 %collective-permute-start.7 = (bf16[320,1024]{1,0:T(8,128)(2,1)S(1)}, bf16[320,1024]{1,0:T(8,128)(2,1)S(1)}, u32[]{:S(2)}, u32[]{:S(2)}) collective-permute-start(bf16[320,1024]{1,0:T(8,128)(2,1)S(1)} %pad_maximum_fusion.1), channel_id=1, source_target_pairs={{0,4},{4,0},{1,5},{5,1},{2,6},{6,2},{3,7},{7,3},{8,12},{12,8},{9,1... | collective-permute-start | bytes 1966088 | tf_op jit(solution)/shard_map/ppermute | solution.py:376
  82.6 32.4 %collective-permute-start.16 = (bf16[2,128,1024]{2,1,0:T(8,128)(2,1)S(1)}, bf16[2,128,1024]{2,1,0:T(8,128)(2,1)S(1)}, u32[]{:S(2)}, u32[]{:S(2)}) collective-permute-start(bf16[2,128,1024]{2,1,0:T(8,128)(2,1)S(1)} %copy-done.4), channel_id=1, source_target_pairs={{0,256},{128,384},{256,0},{384,128},{1,257},{129,385},{257,1},{385... | collective-permute-start | bytes 1572872 | tf_op jit(solution)/shard_map/ppermute | solution.py:376
  85.4 29.5 %collective-permute-start.15 = (bf16[2,128,1024]{2,1,0:T(8,128)(2,1)S(1)}, bf16[2,128,1024]{2,1,0:T(8,128)(2,1)S(1)}, u32[]{:S(2)}, u32[]{:S(2)}) collective-permute-start(bf16[2,128,1024]{2,1,0:T(8,128)(2,1)S(1)} %copy-done.4), channel_id=1, source_target_pairs={{0,384},{128,0},{256,128},{384,256},{1,385},{129,1},{257,129},{385... | collective-permute-start | bytes 1572872 | tf_op jit(solution)/shard_map/ppermute | solution.py:376
  97.2 3.1 %copy-start.1 = (bf16[2,288,1024]{2,1,0:T(8,128)(2,1)}, bf16[2,288,1024]{2,1,0:T(8,128)(2,1)S(1)}, u32[]{:S(2)}) copy-start(bf16[2,288,1024]{2,1,0:T(8,128)(2,1)S(1)} %collective-permute-done.10.below_ref.below1) | copy-start | bytes 3538948
  97.2 33.7 %collective-permute-start.14 = (bf16[2,128,1024]{2,1,0:T(8,128)(2,1)S(1)}, bf16[2,128,1024]{2,1,0:T(8,128)(2,1)S(1)}, u32[]{:S(2)}, u32[]{:S(2)}) collective-permute-start(bf16[2,128,1024]{2,1,0:T(8,128)(2,1)S(1)} %copy-done.4), channel_id=1, source_target_pairs={{0,128},{128,256},{256,384},{384,0},{1,129},{129,257},{257,385},{3... | collective-permute-start | bytes 1572872 | tf_op jit(solution)/shard_map/ppermute | solution.py:376
  100.3 1.0 copy-start.2
  105.4 41.8 %collective-permute-start.12 = (bf16[2,128,1024]{2,1,0:T(8,128)(2,1)}, bf16[2,128,1024]{2,1,0:T(8,128)(2,1)S(1)}, u32[]{:S(2)}, u32[]{:S(2)}) collective-permute-start(bf16[2,128,1024]{2,1,0:T(8,128)(2,1)} %get-tuple-element.40.up), channel_id=1, source_target_pairs={{0,8},{8,16},{16,24},{24,32},{32,40},{40,48},{48,56},{56,64},{64,7... | collective-permute-start | bytes 1572872 | tf_op jit(solution)/shard_map/ppermute | solution.py:381
  107.3 39.9 %collective-permute-start.13 = (bf16[2,128,1024]{2,1,0:T(8,128)(2,1)}, bf16[2,128,1024]{2,1,0:T(8,128)(2,1)S(1)}, u32[]{:S(2)}, u32[]{:S(2)}) collective-permute-start(bf16[2,128,1024]{2,1,0:T(8,128)(2,1)} %get-tuple-element.41.down), channel_id=1, source_target_pairs={{8,0},{16,8},{24,16},{32,24},{40,32},{48,40},{56,48},{64,56},{72,6... | collective-permute-start | bytes 1572872 | tf_op jit(solution)/shard_map/ppermute | solution.py:381
  114.9 16.0 %copy-start.8 = (bf16[2,128,1024]{2,1,0:T(8,128)(2,1)}, bf16[2,128,1024]{2,1,0:T(8,128)(2,1)S(1)}, u32[]{:S(2)}) copy-start(bf16[2,128,1024]{2,1,0:T(8,128)(2,1)S(1)} %collective-permute-done.16.coarse3) | copy-start | bytes 1572868
  114.9 16.0 %copy-start.9 = (bf16[2,128,1024]{2,1,0:T(8,128)(2,1)}, bf16[2,128,1024]{2,1,0:T(8,128)(2,1)S(1)}, u32[]{:S(2)}) copy-start(bf16[2,128,1024]{2,1,0:T(8,128)(2,1)S(1)} %collective-permute-done.15.coarse2) | copy-start | bytes 1572868
  130.9 0.8 copy-start.10
  147.2 0.8 copy-start.5
  147.2 1.0 copy-start.6
  159.7 21.0 %collective-permute-start.17 = (bf16[256,1024]{1,0:T(8,128)(2,1)}, bf16[256,1024]{1,0:T(8,128)(2,1)S(1)}, u32[]{:S(2)}, u32[]{:S(2)}) collective-permute-start(bf16[256,1024]{1,0:T(8,128)(2,1)} %get-tuple-element.48), channel_id=1, source_target_pairs={{0,4},{4,0},{1,5},{5,1},{2,6},{6,2},{3,7},{7,3},{8,12},{12,8},{9,1... | collective-permute-start | bytes 1572872 | tf_op jit(solution)/shard_map/ppermute | solution.py:376

commit v4 on v3

--- a/solution.py
+++ b/solution.py
@@ -12,7 +12,6 @@
 D = 128
 BLOCK = 128
 FAR_REACH = 9
-LOWEST = 7
 SEQ = ("y", "z", "xl")
 YZ = ("y", "z")
 Z = "z"
@@ -46,60 +45,32 @@
     return index
 
 
-def native_kernel(xl, k_own, k_send, v_own, v_send, unit_ref, far_ref, scratch):
+def coarse_kernel(xl, k_own, k_send, v_own, v_send, unit_ref, scratch):
     pieces = []
-    for i, refs in enumerate(((k_own, k_send), (v_own, v_send))):
-        for j, ref in enumerate(refs):
-            four = halved(halved(ref[...].astype(F32), scratch).astype(F32), scratch)
-            far_ref[j, i] = jnp.where(xl[0] == 0, four[0:32], four[32:64])
-            rows, cols = four.shape
-            pieces.append(jnp.sum(four.astype(F32).reshape(rows // 16, 16, cols), axis=1) * (1.0 / 16))
+    for ref in (k_own, k_send, v_own, v_send):
+        four = halved(halved(ref[...].astype(F32), scratch).astype(F32), scratch)
+        rows, cols = four.shape
+        pieces.append(jnp.sum(four.astype(F32).reshape(rows // 16, 16, cols), axis=1) * (1.0 / 16))
     unit_ref[...] = jnp.concatenate(pieces, axis=0).astype(BF)
 
 
-def native_rows(xl, k, v):
+def coarse_rows(xl, k, v):
     rows, cols = k.shape[0], k.shape[1] // 2
     width = 512
     own, send = (pl.BlockSpec((rows, width), column(width, other)) for other in (False, True))
     return pl.pallas_call(
-        native_kernel,
+        coarse_kernel,
         grid_spec=pltpu.PrefetchScalarGridSpec(
             num_scalar_prefetch=1,
             grid=(cols // width,),
             in_specs=[own, send, own, send],
-            out_specs=[
-                pl.BlockSpec((16, width), lambda c, xl: (0, c)),
-                pl.BlockSpec((2, 2, rows // 8, width), lambda c, xl: (0, 0, 0, c)),
-            ],
+            out_specs=pl.BlockSpec((16, width), lambda c, xl: (0, c)),
             scratch_shapes=[pltpu.VMEM((width // D, rows, D), F32)],
         ),
-        out_shape=[jax.ShapeDtypeStruct((16, cols), BF), jax.ShapeDtypeStruct((2, 2, rows // 8, cols), BF)],
+        out_shape=jax.ShapeDtypeStruct((16, cols), BF),
         compiler_params=VMEM,
-        cost_estimate=taking(4),
+        cost_estimate=taking(3),
     )(xl, k, k, v, v)
-
-
-def arrange_kernel(*refs):
-    *parts, out_ref = refs
-    rows = jnp.concatenate([ref[...].astype(F32) for ref in parts], axis=0)
-    n, cols = rows.shape
-    rows = rows.reshape(n // 16, 2, 8, cols)
-    for i in range(2):
-        out_ref[i] = rows[:, i].reshape(n // 2, cols).astype(BF)
-
-
-def arranged(*parts):
-    n, cols = sum(a.shape[0] for a in parts), parts[0].shape[1]
-    width = 256
-    return pl.pallas_call(
-        arrange_kernel,
-        grid=(cols // width,),
-        in_specs=[pl.BlockSpec((a.shape[0], width), lambda c: (0, c)) for a in parts],
-        out_specs=pl.BlockSpec((2, n // 2, width), lambda c: (0, 0, c)),
-        out_shape=jax.ShapeDtypeStruct((2, n // 2, cols), BF),
-        compiler_params=VMEM,
-        cost_estimate=taking(2),
-    )(*parts)
 
 
 def pool_kernel(xl, k_ref, v_ref, got_ref, up_ref, down_ref, mid_ref, far_ref, scratch):
@@ -225,7 +196,7 @@
         at = lax.broadcasted_iota(jnp.int32, (16, coarse_n), 1)
         turn = at // (8 * nz)
         other_y = (y + jnp.where(turn == 0, 0, jnp.where(turn == 1, ny - 1, jnp.where(turn == 2, 1, 2)))) % ny
-        other_z = (z + (at // 8) % nz + nz - LOWEST) % nz
+        other_z = (at // 8) % nz
         block = (other_y * nz + other_z) * 4 + (at % 8) // 2
         for b in range(4):
             gap = jnp.abs(block - (4 * (y * nz + z) + b))
@@ -272,7 +243,7 @@
 
 
 def far_kernel(
-    xl, q_own, q_got, far, up, down, below2, above2, edge_own, edge_got, near_out, near_stat,
+    xl, q_own, q_got, far, up, down, below2, above2, below3, above3, near_out, near_stat,
     own_out, send_out, kr, vr, kfar, vfar,
 ):
     low = xl[0] == 0
@@ -289,12 +260,12 @@
         f3 = far[i, 96:128] if is_key else None
         f0_4 = jnp.concatenate([f0] * 4, axis=0) if is_key else None
         f3_4 = jnp.concatenate([f3] * 4, axis=0) if is_key else None
-        put(far_w, 0, jnp.where(low, edge_got[i], edge_own[i]), has[3], f0)
+        put(far_w, 0, below3[i], has[3], f0)
         put(far_w, 32, below2[i], has[2], f0_4)
         put(far_w, 160, up[i], has[1], f0_4)
         put(far_w, 416, down[i], has_up[1], f3_4)
         put(far_w, 544, above2[i], has_up[2], f3_4)
-        put(far_w, 672, jnp.where(low, edge_own[i], edge_got[i]), has_up[3], f3)
+        put(far_w, 672, above3[i], has_up[3], f3)
     qo, qg = q_own[...], q_got[...]
     queries = (jnp.where(low, qo, qg), jnp.where(low, qg, qo))
     results = []
@@ -381,13 +352,6 @@
     return lax.ppermute(a, YZ, [(i, i + step) for i in range(n) if 0 <= i + step < n])
 
 
-def outward(a, step):
-    n = lax.axis_size(YZ)
-    route = [(2 * i, 2 * (i - step)) for i in range(step, n)]
-    route += [(2 * i + 1, 2 * (i + step) + 1) for i in range(n - step)]
-    return lax.ppermute(a, SEQ, route)
-
-
 def per_device(queries, key_rows, value_rows):
     xl = lax.axis_index("xl")
     low = xl == 0
@@ -404,31 +368,27 @@
         (jnp.stack([theirs(key_rows), theirs(value_rows)]), key_rows, value_rows)
     )
     kv_got = swapped(kv_send)
-    unit, outer = native_rows(at, keys, values)
+    unit = coarse_rows(at, keys, values)
     unit_got = swapped(unit)
     kept = unit.reshape(2, 8, half)[:, 0:4]
     came = unit_got.reshape(2, 8, half)[:, 4:8]
     unit = jnp.concatenate([jnp.where(low, kept, came), jnp.where(low, came, kept)], axis=1).reshape(16, half)
-    units = jnp.concatenate([moved(unit, "z", 1), unit, moved(unit, "z", -1)], axis=0)
-    units = jnp.concatenate([moved(units, "z", 3), units, moved(units, "z", -3)], axis=0)
-    lower, upper = units[16:64], units[80:144]
-    lower, upper, _, outer = lax.optimization_barrier((lower, upper, kv_got, outer))
-    units = arranged(moved(lower, "z", 4), units, moved(upper, "z", -4))
+    units = lax.all_gather(unit, "z")
+    units = jnp.moveaxis(units.reshape(-1, 2, 8, half), 1, 0).reshape(2, -1, half)
+    q_got = swapped(theirs(queries))
+    kv_got, units, q_got = lax.optimization_barrier((kv_got, units, q_got))
     up1, down1, mid, far = pooled(at, key_rows, value_rows, kv_got)
     up1, down1, units = lax.optimization_barrier((up1, down1, units))
     below1, above1 = shifted(up1, 1), shifted(down1, -1)
     coarse = (units, moved(units, "y", 1), moved(units, "y", -1), moved(units, "y", 2))
-    edge = outward(outer, 3)
-    message = jnp.concatenate([theirs(queries), edge[1].reshape(-1, half)], axis=0)
-    got = swapped(message)
-    q_got, edge_got = got[0 : queries.shape[0]], got[queries.shape[0] :].reshape(edge[1].shape)
+    below3, above3 = shifted(far[:, 96:128], 3), shifted(far[:, 0:32], -3)
     up, down, near = forwarded(below1, above1)
     below2, above2 = shifted(up, 1), shifted(down, -1)
     near_out, near_stat = attend_near(
         at, queries, q_got, key_rows, value_rows, (kv_got, mid, below1, above1, near, *coarse)
     )
     out, send_out = attend_far(
-        at, queries, q_got, (far, up, down, below2, above2, edge[0], edge_got, near_out, near_stat)
+        at, queries, q_got, (far, up, down, below2, above2, below3, above3, near_out, near_stat)
     )
     return lax.dynamic_update_slice_in_dim(out, swapped(send_out), (1 - xl) * half, 1)
 

time: 183 us -> 188 us (1.027)
  the two profiles are of different devices: /device:TPU:24 before, /device:TPU:82 now
where the time goes in v4:
time: 188 us; the launch traced here: 187 us
  starting transfers between devices  67.4 us (36%)
  Pallas kernels  38.6 us (21%)
  waiting for transfers between devices  37.6 us (20%)
  blocking collectives  35.5 us (19%)
  local copies, waits for them, and re-layouts  6.87 us (4%)
    ppermute x6, starting transfers between devices, shifted(): lax.ppermute(a, YZ, [(i, i + step) for i in range(n) if 0 <= i + step < n])  47.6 us
    all_gather x1, blocking collectives, per_device(): units = lax.all_gather(unit, 'z')  35.5 us
    ppermute x7, waiting for transfers between devices, moved(): return lax.ppermute(a, axis, [(i, (i + step) % n) for i in range(n)])  29.3 us
    pallas_call x2, Pallas kernels, attend_call(): pl.pallas_call(kernel, grid_spec=pltpu.PrefetchScalarGridSpec(num_scalar_...  26.9 us
    ppermute x7, starting transfers between devices, moved(): return lax.ppermute(a, axis, [(i, (i + step) % n) for i in range(n)])  19.8 us
    ppermute x6, waiting for transfers between devices, shifted(): lax.ppermute(a, YZ, [(i, i + step) for i in range(n) if 0 <= i + step < n])  8.27 us
    pallas_call x1, Pallas kernels, pooled(): pl.pallas_call(pool_kernel, grid_spec=pltpu.PrefetchScalarGridSpec(num_sc...  4.7 us
    pallas_call x1, Pallas kernels, forwarded(): pl.pallas_call(forward_kernel, grid=(2, cols // width), in_specs=[pl.Bloc...  4.04 us
  transfers between devices with their start and end apart: 13, of which 4 were waited for; matrix products, arithmetic and copies ran while one was open for 1% of the time, Pallas kernels for 12%

profile of v4, /device:TPU:82, one launch (start us, length us, event | category | flops | bytes accessed | tf_op | source)
XLA Modules:
  0.0 187.2 jit_solution(13360786495151521266)
XLA Ops:
  0.0 1.3 dynamic-slice_bitcast_fusion
  1.4 2.4 %collective-permute-start = (bf16[2,256,1024]{2,1,0:T(8,128)(2,1)S(1)}, bf16[2,256,1024]{2,1,0:T(8,128)(2,1)S(1)}, u32[]{:S(2)}, u32[]{:S(2)}) collective-permute-start(bf16[2,256,1024]{2,1,0:T(8,128)(2,1)S(1)} %pad_maximum_fusion), channel_id=1, source_target_pairs={{0,4},{4,0},{1,5},{5,1},{2,6},{6,2},{3,7},{7,3},{8,12},{12,8},{9,1... | collective-permute-start | bytes 3145736 | tf_op jit(solution)/shard_map/ppermute | solution.py:347
  3.8 2.9 %shard_map.37 = bf16[16,1024]{1,0:T(8,128)(2,1)} custom-call(s32[1]{0:T(128)} %bitcast.xl, bf16[256,2048]{1,0:T(8,128)(2,1)} %k_own.2, bf16[256,2048]{1,0:T(8,128)(2,1)} %k_own.2, bf16[256,2048]{1,0:T(8,128)(2,1)} %v_own.2, bf16[256,2048]{1,0:T(8,128)(2,1)} %v_own.2), custom_call_target="tpu_custom_call" | custom-call | bytes 10800000 | tf_op jit(solution)/shard_map/pallas_call | solution.py:61
  6.8 3.4 %collective-permute-start.1 = (bf16[16,1024]{1,0:T(8,128)(2,1)}, bf16[16,1024]{1,0:T(8,128)(2,1)S(1)}, u32[]{:S(2)}, u32[]{:S(2)}) collective-permute-start(bf16[16,1024]{1,0:T(8,128)(2,1)} %shard_map.37), channel_id=1, source_target_pairs={{0,4},{4,0},{1,5},{5,1},{2,6},{6,2},{3,7},{7,3},{8,12},{12,8},{9,1... | collective-permute-start | bytes 98312 | tf_op jit(solution)/shard_map/ppermute | solution.py:347
  10.2 0.8 constant_dynamic-slice_fusion
  11.0 2.4 %collective-permute-start.2 = (bf16[256,1024]{1,0:T(8,128)(2,1)}, bf16[256,1024]{1,0:T(8,128)(2,1)S(1)}, u32[]{:S(2)}, u32[]{:S(2)}) collective-permute-start(bf16[256,1024]{1,0:T(8,128)(2,1)} %constant_dynamic-slice_fusion), channel_id=1, source_target_pairs={{0,4},{4,0},{1,5},{5,1},{2,6},{6,2},{3,7},{7,3},{8,12},{12,8},{9,1... | collective-permute-start | bytes 1572872 | tf_op jit(solution)/shard_map/ppermute | solution.py:347
  13.5 16.6 %collective-permute-done.1 = bf16[16,1024]{1,0:T(8,128)(2,1)S(1)} collective-permute-done((bf16[16,1024]{1,0:T(8,128)(2,1)}, bf16[16,1024]{1,0:T(8,128)(2,1)S(1)}, u32[]{:S(2)}, u32[]{:S(2)}) %collective-permute-start.1) | collective-permute-done | bytes 32800 | tf_op jit(solution)/shard_map/ppermute | solution.py:347
  30.0 0.8 broadcast_select_fusion.1
  30.8 35.5 %all_gather.3 = bf16[16,16,1024]{2,1,0:T(8,128)(2,1)S(1)} all-gather(bf16[1,16,1024]{2,1,0:T(8,128)(2,1)S(1)} %maximum_bitcast_fusion), channel_id=1, replica_groups=mesh['y'=4,'z'=16,'xl'=2,'head'=4] {'z'}, dimensions={0}, use_global_device_ids=true | all-gather | bytes 557056 | tf_op jit(solution)/shard_map/all_gather | solution.py:376
  66.4 1.0 copy-done.3
  67.4 4.7 %shard_map.38 = (bf16[2,288,1024]{2,1,0:T(8,128)(2,1)}, bf16[2,288,1024]{2,1,0:T(8,128)(2,1)}, bf16[2,256,1024]{2,1,0:T(8,128)(2,1)}, bf16[2,128,1024]{2,1,0:T(8,128)(2,1)}) custom-call(s32[1]{0:T(128)} %bitcast.xl, bf16[256,2048]{1,0:T(8,128)(2,1)} %k_own.2, bf16[256,2048]{1,0:T(8,128)(2,1)} %v_own.2, bf16[2,256,1024]{2,1,0:T(8,128)(2,1)} %copy-done.3), custom_call_target="tpu_custom_call" | custom-call | bytes 18000000 | tf_op jit(solution)/shard_map/pallas_call | solution.py:105
  72.1 2.0 %collective-permute-start.3 = (bf16[2,288,1024]{2,1,0:T(8,128)(2,1)}, bf16[2,288,1024]{2,1,0:T(8,128)(2,1)S(1)}, u32[]{:S(2)}, u32[]{:S(2)}) collective-permute-start(bf16[2,288,1024]{2,1,0:T(8,128)(2,1)} %get-tuple-element.34), channel_id=1, source_target_pairs={{0,8},{8,16},{16,24},{24,32},{32,40},{40,48},{48,56},{56,64},{64,7... | collective-permute-start | bytes 3538952 | tf_op jit(solution)/shard_map/ppermute | solution.py:352
  74.2 3.9 %collective-permute-start.4 = (bf16[2,288,1024]{2,1,0:T(8,128)(2,1)}, bf16[2,288,1024]{2,1,0:T(8,128)(2,1)S(1)}, u32[]{:S(2)}, u32[]{:S(2)}) collective-permute-start(bf16[2,288,1024]{2,1,0:T(8,128)(2,1)} %get-tuple-element.35), channel_id=1, source_target_pairs={{8,0},{16,8},{24,16},{32,24},{40,32},{48,40},{56,48},{64,56},{72,6... | collective-permute-start | bytes 3538952 | tf_op jit(solution)/shard_map/ppermute | solution.py:352
  78.1 2.4 %collective-permute-start.10 = (bf16[2,128,1024]{2,1,0:T(8,128)(2,1)S(1)}, bf16[2,128,1024]{2,1,0:T(8,128)(2,1)S(1)}, u32[]{:S(2)}, u32[]{:S(2)}) collective-permute-start(bf16[2,128,1024]{2,1,0:T(8,128)(2,1)S(1)} %copy_bitcast_fusion.coarse0), channel_id=1, source_target_pairs={{0,384},{128,0},{256,128},{384,256},{1,385},{129,1},{257,129},{385... | collective-permute-start | bytes 1572872 | tf_op jit(solution)/shard_map/ppermute | solution.py:347
  80.5 4.8 %collective-permute-start.11 = (bf16[2,128,1024]{2,1,0:T(8,128)(2,1)S(1)}, bf16[2,128,1024]{2,1,0:T(8,128)(2,1)S(1)}, u32[]{:S(2)}, u32[]{:S(2)}) collective-permute-start(bf16[2,128,1024]{2,1,0:T(8,128)(2,1)S(1)} %copy_bitcast_fusion.coarse0), channel_id=1, source_target_pairs={{0,256},{128,384},{256,0},{384,128},{1,257},{129,385},{257,1},{385... | collective-permute-start | bytes 1572872 | tf_op jit(solution)/shard_map/ppermute | solution.py:347
  85.3 1.9 %collective-permute-start.9 = (bf16[2,128,1024]{2,1,0:T(8,128)(2,1)S(1)}, bf16[2,128,1024]{2,1,0:T(8,128)(2,1)S(1)}, u32[]{:S(2)}, u32[]{:S(2)}) collective-permute-start(bf16[2,128,1024]{2,1,0:T(8,128)(2,1)S(1)} %copy_bitcast_fusion.coarse0), channel_id=1, source_target_pairs={{0,128},{128,256},{256,384},{384,0},{1,129},{129,257},{257,385},{3... | collective-permute-start | bytes 1572872 | tf_op jit(solution)/shard_map/ppermute | solution.py:347
  87.2 6.3 %collective-permute-done.3.below_ref.below1 = bf16[2,288,1024]{2,1,0:T(8,128)(2,1)S(1)} collective-permute-done((bf16[2,288,1024]{2,1,0:T(8,128)(2,1)}, bf16[2,288,1024]{2,1,0:T(8,128)(2,1)S(1)}, u32[]{:S(2)}, u32[]{:S(2)}) %collective-permute-start.3) | collective-permute-done | bytes 1179680 | tf_op jit(solution)/shard_map/ppermute | solution.py:352
  93.6 1.9 %collective-permute-done.4.above_ref.above1 = bf16[2,288,1024]{2,1,0:T(8,128)(2,1)S(1)} collective-permute-done((bf16[2,288,1024]{2,1,0:T(8,128)(2,1)}, bf16[2,288,1024]{2,1,0:T(8,128)(2,1)S(1)}, u32[]{:S(2)}, u32[]{:S(2)}) %collective-permute-start.4) | collective-permute-done | bytes 1179680 | tf_op jit(solution)/shard_map/ppermute | solution.py:352
  95.5 1.0 copy-done.2
  96.5 4.0 %shard_map.39 = (bf16[2,128,1024]{2,1,0:T(8,128)(2,1)}, bf16[2,128,1024]{2,1,0:T(8,128)(2,1)}, bf16[2,128,1024]{2,1,0:T(8,128)(2,1)}) custom-call(bf16[2,288,1024]{2,1,0:T(8,128)(2,1)} %copy-done.1, bf16[2,288,1024]{2,1,0:T(8,128)(2,1)} %copy-done.2), custom_call_target="tpu_custom_call" | custom-call | bytes 14400000 | tf_op jit(solution)/shard_map/pallas_call | solution.py:134
  100.6 4.8 %collective-permute-start.5 = (bf16[2,128,1024]{2,1,0:T(8,128)(2,1)}, bf16[2,128,1024]{2,1,0:T(8,128)(2,1)S(1)}, u32[]{:S(2)}, u32[]{:S(2)}) collective-permute-start(bf16[2,128,1024]{2,1,0:T(8,128)(2,1)} %get-tuple-element.36.up), channel_id=1, source_target_pairs={{0,8},{8,16},{16,24},{24,32},{32,40},{40,48},{48,56},{56,64},{64,7... | collective-permute-start | bytes 1572872 | tf_op jit(solution)/shard_map/ppermute | solution.py:352
  105.4 1.9 %collective-permute-start.6 = (bf16[2,128,1024]{2,1,0:T(8,128)(2,1)}, bf16[2,128,1024]{2,1,0:T(8,128)(2,1)S(1)}, u32[]{:S(2)}, u32[]{:S(2)}) collective-permute-start(bf16[2,128,1024]{2,1,0:T(8,128)(2,1)} %get-tuple-element.37.down), channel_id=1, source_target_pairs={{8,0},{16,8},{24,16},{32,24},{40,32},{48,40},{56,48},{64,56},{72,6... | collective-permute-start | bytes 1572872 | tf_op jit(solution)/shard_map/ppermute | solution.py:352
  107.4 4.1 %collective-permute-start.7 = (bf16[2,32,1024]{2,1,0:T(8,128)(2,1)S(1)}, bf16[2,32,1024]{2,1,0:T(8,128)(2,1)S(1)}, u32[]{:S(2)}, u32[]{:S(2)}) collective-permute-start(bf16[2,32,1024]{2,1,0:T(8,128)(2,1)S(1)} %get-tuple-element.46), channel_id=1, source_target_pairs={{0,24},{8,32},{16,40},{24,48},{32,56},{40,64},{48,72},{56,80},{64,... | collective-permute-start | bytes 393224 | tf_op jit(solution)/shard_map/ppermute | solution.py:352
  111.5 30.8 %collective-permute-start.8 = (bf16[2,32,1024]{2,1,0:T(8,128)(2,1)S(1)}, bf16[2,32,1024]{2,1,0:T(8,128)(2,1)S(1)}, u32[]{:S(2)}, u32[]{:S(2)}) collective-permute-start(bf16[2,32,1024]{2,1,0:T(8,128)(2,1)S(1)} %get-tuple-element.45), channel_id=1, source_target_pairs={{24,0},{32,8},{40,16},{48,24},{56,32},{64,40},{72,48},{80,56},{88,... | collective-permute-start | bytes 393224 | tf_op jit(solution)/shard_map/ppermute | solution.py:352
  142.4 0.7 copy-done.11
  143.1 15.5 %shard_map.40 = (f32[512,1024]{1,0:T(8,128)}, f32[512,1024]{1,0:T(8,128)}) custom-call(s32[1]{0:T(128)} %bitcast.xl, bf16[256,2048]{1,0:T(8,128)(2,1)} %q_own.3, bf16[256,1024]{1,0:T(8,128)(2,1)} %copy-done.4, bf16[256,2048]{1,0:T(8,128)(2,1)} %k_own.2, bf16[256,2048]{1,0:T(8,128)(2,1)} %v_own.2, bf16[2,256,1024]{2,1,0:T(8,128)(2,1)} %copy-done.3, ...), custom_call_target="tpu_custom_call" | custom-call | bytes 57600000 | tf_op jit(solution)/shard_map/pallas_call | solution.py:302
  158.6 0.6 copy-done.12
  159.5 0.2 copy-done.8
  159.7 11.5 %shard_map.41 = (bf16[256,2048]{1,0:T(8,128)(2,1)}, bf16[256,1024]{1,0:T(8,128)(2,1)}) custom-call(s32[1]{0:T(128)} %bitcast.xl, bf16[256,2048]{1,0:T(8,128)(2,1)} %q_own.3, bf16[256,1024]{1,0:T(8,128)(2,1)} %copy-done.4, bf16[2,128,1024]{2,1,0:T(8,128)(2,1)} %get-tuple-element.30.far, bf16[2,128,1024]{2,1,0:T(8,128)(2,1)} %get-tuple-element.36.up, ...), custom_call_target="tpu_custom_call" | custom-call | bytes 32400000 | tf_op jit(solution)/shard_map/pallas_call | solution.py:302
  171.2 2.4 %collective-permute-start.12 = (bf16[256,1024]{1,0:T(8,128)(2,1)}, bf16[256,1024]{1,0:T(8,128)(2,1)S(1)}, u32[]{:S(2)}, u32[]{:S(2)}) collective-permute-start(bf16[256,1024]{1,0:T(8,128)(2,1)} %get-tuple-element.44), channel_id=1, source_target_pairs={{0,4},{4,0},{1,5},{5,1},{2,6},{6,2},{3,7},{7,3},{8,12},{12,8},{9,1... | collective-permute-start | bytes 1572872 | tf_op jit(solution)/shard_map/ppermute | solution.py:347
  173.6 12.8 %collective-permute-done.12 = bf16[256,1024]{1,0:T(8,128)(2,1)S(1)} collective-permute-done((bf16[256,1024]{1,0:T(8,128)(2,1)}, bf16[256,1024]{1,0:T(8,128)(2,1)S(1)}, u32[]{:S(2)}, u32[]{:S(2)}) %collective-permute-start.12) | collective-permute-done | bytes 524320 | tf_op jit(solution)/shard_map/ppermute | solution.py:347
  186.4 0.8 constant_dynamic-update-slice_fusion
  (36 shorter events, 0.5 us)
Async XLA Ops:
  1.4 65.0 %collective-permute-start = (bf16[2,256,1024]{2,1,0:T(8,128)(2,1)S(1)}, bf16[2,256,1024]{2,1,0:T(8,128)(2,1)S(1)}, u32[]{:S(2)}, u32[]{:S(2)}) collective-permute-start(bf16[2,256,1024]{2,1,0:T(8,128)(2,1)S(1)} %pad_maximum_fusion), channel_id=1, source_target_pairs={{0,4},{4,0},{1,5},{5,1},{2,6},{6,2},{3,7},{7,3},{8,12},{12,8},{9,1... | collective-permute-start | bytes 3145736 | tf_op jit(solution)/shard_map/ppermute | solution.py:347
  3.8 6.3 %copy-start = (bf16[256,2048]{1,0:T(8,128)(2,1)S(1)}, bf16[256,2048]{1,0:T(8,128)(2,1)}, u32[]{:S(2)}) copy-start(bf16[256,2048]{1,0:T(8,128)(2,1)} %q_own.3) | copy-start | bytes 3145732
  6.8 23.2 %collective-permute-start.1 = (bf16[16,1024]{1,0:T(8,128)(2,1)}, bf16[16,1024]{1,0:T(8,128)(2,1)S(1)}, u32[]{:S(2)}, u32[]{:S(2)}) collective-permute-start(bf16[16,1024]{1,0:T(8,128)(2,1)} %shard_map.37), channel_id=1, source_target_pairs={{0,4},{4,0},{1,5},{5,1},{2,6},{6,2},{3,7},{7,3},{8,12},{12,8},{9,1... | collective-permute-start | bytes 98312 | tf_op jit(solution)/shard_map/ppermute | solution.py:347
  11.0 55.4 %collective-permute-start.2 = (bf16[256,1024]{1,0:T(8,128)(2,1)}, bf16[256,1024]{1,0:T(8,128)(2,1)S(1)}, u32[]{:S(2)}, u32[]{:S(2)}) collective-permute-start(bf16[256,1024]{1,0:T(8,128)(2,1)} %constant_dynamic-slice_fusion), channel_id=1, source_target_pairs={{0,4},{4,0},{1,5},{5,1},{2,6},{6,2},{3,7},{7,3},{8,12},{12,8},{9,1... | collective-permute-start | bytes 1572872 | tf_op jit(solution)/shard_map/ppermute | solution.py:347
  66.4 76.0 %copy-start.5 = (bf16[2,128,1024]{2,1,0:T(8,128)(2,1)}, bf16[2,128,1024]{2,1,0:T(8,128)(2,1)S(1)}, u32[]{:S(2)}) copy-start(bf16[2,128,1024]{2,1,0:T(8,128)(2,1)S(1)} %copy_bitcast_fusion.coarse0) | copy-start | bytes 1572868
  66.4 75.9 %copy-start.4 = (bf16[256,1024]{1,0:T(8,128)(2,1)}, bf16[256,1024]{1,0:T(8,128)(2,1)S(1)}, u32[]{:S(2)}) copy-start(bf16[256,1024]{1,0:T(8,128)(2,1)S(1)} %collective-permute-done.2.q_got) | copy-start | bytes 1572868
  66.4 1.0 copy-start.3
  72.1 35.2 %copy-start.6 = (bf16[2,128,1024]{2,1,0:T(8,128)(2,1)S(1)}, bf16[2,128,1024]{2,1,0:T(8,128)(2,1)}, u32[]{:S(2)}) copy-start(bf16[2,128,1024]{2,1,0:T(8,128)(2,1)} %get-tuple-element.30.far) | copy-start | bytes 1572868
  72.1 21.4 %collective-permute-start.3 = (bf16[2,288,1024]{2,1,0:T(8,128)(2,1)}, bf16[2,288,1024]{2,1,0:T(8,128)(2,1)S(1)}, u32[]{:S(2)}, u32[]{:S(2)}) collective-permute-start(bf16[2,288,1024]{2,1,0:T(8,128)(2,1)} %get-tuple-element.34), channel_id=1, source_target_pairs={{0,8},{8,16},{16,24},{24,32},{32,40},{40,48},{48,56},{56,64},{64,7... | collective-permute-start | bytes 3538952 | tf_op jit(solution)/shard_map/ppermute | solution.py:352
  74.2 21.3 %collective-permute-start.4 = (bf16[2,288,1024]{2,1,0:T(8,128)(2,1)}, bf16[2,288,1024]{2,1,0:T(8,128)(2,1)S(1)}, u32[]{:S(2)}, u32[]{:S(2)}) collective-permute-start(bf16[2,288,1024]{2,1,0:T(8,128)(2,1)} %get-tuple-element.35), channel_id=1, source_target_pairs={{8,0},{16,8},{24,16},{32,24},{40,32},{48,40},{56,48},{64,56},{72,6... | collective-permute-start | bytes 3538952 | tf_op jit(solution)/shard_map/ppermute | solution.py:352
  78.1 29.3 %collective-permute-start.10 = (bf16[2,128,1024]{2,1,0:T(8,128)(2,1)S(1)}, bf16[2,128,1024]{2,1,0:T(8,128)(2,1)S(1)}, u32[]{:S(2)}, u32[]{:S(2)}) collective-permute-start(bf16[2,128,1024]{2,1,0:T(8,128)(2,1)S(1)} %copy_bitcast_fusion.coarse0), channel_id=1, source_target_pairs={{0,384},{128,0},{256,128},{384,256},{1,385},{129,1},{257,129},{385... | collective-permute-start | bytes 1572872 | tf_op jit(solution)/shard_map/ppermute | solution.py:347
  80.5 31.0 %collective-permute-start.11 = (bf16[2,128,1024]{2,1,0:T(8,128)(2,1)S(1)}, bf16[2,128,1024]{2,1,0:T(8,128)(2,1)S(1)}, u32[]{:S(2)}, u32[]{:S(2)}) collective-permute-start(bf16[2,128,1024]{2,1,0:T(8,128)(2,1)S(1)} %copy_bitcast_fusion.coarse0), channel_id=1, source_target_pairs={{0,256},{128,384},{256,0},{384,128},{1,257},{129,385},{257,1},{385... | collective-permute-start | bytes 1572872 | tf_op jit(solution)/shard_map/ppermute | solution.py:347
  85.3 57.0 %collective-permute-start.9 = (bf16[2,128,1024]{2,1,0:T(8,128)(2,1)S(1)}, bf16[2,128,1024]{2,1,0:T(8,128)(2,1)S(1)}, u32[]{:S(2)}, u32[]{:S(2)}) collective-permute-start(bf16[2,128,1024]{2,1,0:T(8,128)(2,1)S(1)} %copy_bitcast_fusion.coarse0), channel_id=1, source_target_pairs={{0,128},{128,256},{256,384},{384,0},{1,129},{129,257},{257,385},{3... | collective-permute-start | bytes 1572872 | tf_op jit(solution)/shard_map/ppermute | solution.py:347
  93.6 1.9 %copy-start.1 = (bf16[2,288,1024]{2,1,0:T(8,128)(2,1)}, bf16[2,288,1024]{2,1,0:T(8,128)(2,1)S(1)}, u32[]{:S(2)}) copy-start(bf16[2,288,1024]{2,1,0:T(8,128)(2,1)S(1)} %collective-permute-done.3.below_ref.below1) | copy-start | bytes 3538948
  95.5 1.0 copy-start.2
  100.6 58.1 %collective-permute-start.5 = (bf16[2,128,1024]{2,1,0:T(8,128)(2,1)}, bf16[2,128,1024]{2,1,0:T(8,128)(2,1)S(1)}, u32[]{:S(2)}, u32[]{:S(2)}) collective-permute-start(bf16[2,128,1024]{2,1,0:T(8,128)(2,1)} %get-tuple-element.36.up), channel_id=1, source_target_pairs={{0,8},{8,16},{16,24},{24,32},{32,40},{40,48},{48,56},{56,64},{64,7... | collective-permute-start | bytes 1572872 | tf_op jit(solution)/shard_map/ppermute | solution.py:352
  105.4 53.2 %collective-permute-start.6 = (bf16[2,128,1024]{2,1,0:T(8,128)(2,1)}, bf16[2,128,1024]{2,1,0:T(8,128)(2,1)S(1)}, u32[]{:S(2)}, u32[]{:S(2)}) collective-permute-start(bf16[2,128,1024]{2,1,0:T(8,128)(2,1)} %get-tuple-element.37.down), channel_id=1, source_target_pairs={{8,0},{16,8},{24,16},{32,24},{40,32},{48,40},{56,48},{64,56},{72,6... | collective-permute-start | bytes 1572872 | tf_op jit(solution)/shard_map/ppermute | solution.py:352
  107.4 35.0 %copy-start.9 = (bf16[2,128,1024]{2,1,0:T(8,128)(2,1)}, bf16[2,128,1024]{2,1,0:T(8,128)(2,1)S(1)}, u32[]{:S(2)}) copy-start(bf16[2,128,1024]{2,1,0:T(8,128)(2,1)S(1)} %collective-permute-done.10.coarse2) | copy-start | bytes 1572868
  107.4 51.2 %collective-permute-start.7 = (bf16[2,32,1024]{2,1,0:T(8,128)(2,1)S(1)}, bf16[2,32,1024]{2,1,0:T(8,128)(2,1)S(1)}, u32[]{:S(2)}, u32[]{:S(2)}) collective-permute-start(bf16[2,32,1024]{2,1,0:T(8,128)(2,1)S(1)} %get-tuple-element.46), channel_id=1, source_target_pairs={{0,24},{8,32},{16,40},{24,48},{32,56},{40,64},{48,72},{56,80},{64,... | collective-permute-start | bytes 393224 | tf_op jit(solution)/shard_map/ppermute | solution.py:352
  111.5 30.8 %copy-start.10 = (bf16[2,128,1024]{2,1,0:T(8,128)(2,1)}, bf16[2,128,1024]{2,1,0:T(8,128)(2,1)S(1)}, u32[]{:S(2)}) copy-start(bf16[2,128,1024]{2,1,0:T(8,128)(2,1)S(1)} %collective-permute-done.11.coarse3) | copy-start | bytes 1572868
  111.5 47.1 %collective-permute-start.8 = (bf16[2,32,1024]{2,1,0:T(8,128)(2,1)S(1)}, bf16[2,32,1024]{2,1,0:T(8,128)(2,1)S(1)}, u32[]{:S(2)}, u32[]{:S(2)}) collective-permute-start(bf16[2,32,1024]{2,1,0:T(8,128)(2,1)S(1)} %get-tuple-element.45), channel_id=1, source_target_pairs={{24,0},{32,8},{40,16},{48,24},{56,32},{64,40},{72,48},{80,56},{88,... | collective-permute-start | bytes 393224 | tf_op jit(solution)/shard_map/ppermute | solution.py:352
  142.3 0.8 copy-start.11
  158.6 0.7 copy-start.12
  158.6 0.7 copy-start.13
  158.6 0.9 copy-start.7
  158.6 1.0 copy-start.8
  171.2 15.2 %collective-permute-start.12 = (bf16[256,1024]{1,0:T(8,128)(2,1)}, bf16[256,1024]{1,0:T(8,128)(2,1)S(1)}, u32[]{:S(2)}, u32[]{:S(2)}) collective-permute-start(bf16[256,1024]{1,0:T(8,128)(2,1)} %get-tuple-element.44), channel_id=1, source_target_pairs={{0,4},{4,0},{1,5},{5,1},{2,6},{6,2},{3,7},{7,3},{8,12},{12,8},{9,1... | collective-permute-start | bytes 1572872 | tf_op jit(solution)/shard_map/ppermute | solution.py:347

commit v5 on v4

--- a/solution.py
+++ b/solution.py
@@ -179,28 +179,13 @@
     )
 
 
-def near_kernel(
-    xl, q_own, q_got, k_own, v_own, kv_got, mid, below1, above1, near, coarse0, coarse1, coarse2, coarse3,
-    out, stat, kf, vf, km, vm, kc, vc, mask,
-):
+def near_kernel(xl, q_own, q_got, k_own, v_own, kv_got, mid, below1, above1, near, out, stat, kf, vf, km, vm):
     low = xl[0] == 0
-    coarse_n = mask.shape[1]
 
     @pl.when(pl.program_id(0) == 0)
     def _():
         flags(6, -1, 128, vf)
         flags(10, -3, 64, vm)
-        vc[:, D : 2 * D] = jnp.ones((coarse_n, D), BF)
-        y, z = lax.axis_index("y"), lax.axis_index("z")
-        ny, nz = lax.axis_size("y"), lax.axis_size("z")
-        at = lax.broadcasted_iota(jnp.int32, (16, coarse_n), 1)
-        turn = at // (8 * nz)
-        other_y = (y + jnp.where(turn == 0, 0, jnp.where(turn == 1, ny - 1, jnp.where(turn == 2, 1, 2)))) % ny
-        other_z = (at // 8) % nz
-        block = (other_y * nz + other_z) * 4 + (at % 8) // 2
-        for b in range(4):
-            gap = jnp.abs(block - (4 * (y * nz + z) + b))
-            mask[b * 16 : (b + 1) * 16, :] = jnp.where(gap > FAR_REACH, 1.0, 0.0).astype(BF)
 
     has, has_up = present()
     for i, (own_ref, fine_w, mid_w) in enumerate(((k_own, kf, km), (v_own, vf, vm))):
@@ -220,10 +205,6 @@
         put(mid_w, 448, near[i, 64:128], has_up[1], m3)
         put(mid_w, 512, above1[i, 128:192], has_up[1], m3)
         put(mid_w, 576, above1[i, 192:256], has_up[1], m3)
-    step = coarse_n // 4
-    for t, part in enumerate((coarse0, coarse1, coarse2, coarse3)):
-        kc[t * step : (t + 1) * step] = part[0]
-        vc[t * step : (t + 1) * step, 0:D] = part[1]
     qo, qg = q_own[...], q_got[...]
     queries = (jnp.where(low, qo, qg), jnp.where(low, qg, qo))
     left = lax.broadcasted_iota(jnp.int32, (BLOCK, D), 1) < D // 2
@@ -234,7 +215,6 @@
             (scores(q, kf[b * 128 : b * 128 + 384]), vf[b * 128 : b * 128 + 384], 0.0, None),
             (scores(q, km[lo : lo + 128]), vm[lo : lo + 128], 1.0, None),
             (scores(q, km[up : up + 128]), vm[up : up + 128], 1.0, None),
-            (scores(q, kc[...]), vc[...], 6.0, mask[b * 16 : b * 16 + 1, :]),
         ]
         top = top_of(parts)
         total = weighted(parts, top)
@@ -243,14 +223,26 @@
 
 
 def far_kernel(
-    xl, q_own, q_got, far, up, down, below2, above2, below3, above3, near_out, near_stat,
-    own_out, send_out, kr, vr, kfar, vfar,
+    xl, q_own, q_got, far, up, down, below2, above2, below3, above3, coarse0, coarse1, near_out, near_stat,
+    own_out, send_out, kr, vr, kc, vc, kfar, vfar, mask,
 ):
     low = xl[0] == 0
+    y = lax.axis_index("y")
+    ny, nz = lax.axis_size("y"), lax.axis_size("z")
+    coarse_n = 2 * coarse0.shape[1]
 
     @pl.when(pl.program_id(0) == 0)
     def _():
         flags(22, -9, 32, vr)
+        vc[:, D : 2 * D] = jnp.ones((coarse_n, D), BF)
+        for b in range(4):
+            at = lax.broadcasted_iota(jnp.int32, (16, coarse_n), 1)
+            turn = at // (8 * nz)
+            other = jnp.where(turn < 2, y, ny - 1 - y)
+            other = jnp.where(turn % 2 == 0, other, other + 1 - 2 * (other % 2))
+            block = (other * nz + (at // 8) % nz) * 4 + (at % 8) // 2
+            gap = jnp.abs(block - (4 * (y * nz + lax.axis_index("z")) + b))
+            mask[b * 16 : (b + 1) * 16, :] = jnp.where(gap > FAR_REACH, 1.0, 0.0).astype(BF)
 
     has, has_up = present()
     for i, far_w in enumerate((kr, vr)):
@@ -266,16 +258,23 @@
         put(far_w, 416, down[i], has_up[1], f3_4)
         put(far_w, 544, above2[i], has_up[2], f3_4)
         put(far_w, 672, above3[i], has_up[3], f3)
+    step = coarse_n // 2
+    for t, part in enumerate((coarse0, coarse1)):
+        kc[t * step : (t + 1) * step] = part[0]
+        vc[t * step : (t + 1) * step, 0:D] = part[1]
     qo, qg = q_own[...], q_got[...]
     queries = (jnp.where(low, qo, qg), jnp.where(low, qg, qo))
     results = []
     for b in range(4):
         q = queries[b // 2][(b % 2) * 128 : (b % 2 + 1) * 128]
-        kfar[b, 0:192] = kr[b * 32 : b * 32 + 192]
-        kfar[b, 192:384] = kr[(b + 13) * 32 : (b + 13) * 32 + 192]
-        vfar[b, 0:192] = vr[b * 32 : b * 32 + 192]
-        vfar[b, 192:384] = vr[(b + 13) * 32 : (b + 13) * 32 + 192]
-        parts = [(scores(q, kfar[b]), vfar[b], 2.0, None)]
+        kfar[0:192] = kr[b * 32 : b * 32 + 192]
+        kfar[192:384] = kr[(b + 13) * 32 : (b + 13) * 32 + 192]
+        vfar[0:192] = vr[b * 32 : b * 32 + 192]
+        vfar[192:384] = vr[(b + 13) * 32 : (b + 13) * 32 + 192]
+        parts = [
+            (scores(q, kfar[...]), vfar[...], 2.0, None),
+            (scores(q, kc[...]), vc[...], 6.0, mask[b * 16 : b * 16 + 1, :]),
+        ]
         here = slice(b * 128, (b + 1) * 128)
         near_top, near_sum = near_stat[here, 0:1], near_stat[here, D - 1 : D]
         top = jnp.maximum(top_of(parts), near_top)
@@ -317,28 +316,28 @@
 def attend_near(xl, q, q_got, k, v, arrays):
     rows, cols = q.shape[0], q.shape[1] // 2
     outs = [jax.ShapeDtypeStruct((2 * rows, cols), F32)] * 2
-    coarse_n = 4 * arrays[-1].shape[1]
     scratch = [
         pltpu.VMEM((768, D), BF), pltpu.VMEM((768, 2 * D), BF),
         pltpu.VMEM((640, D), BF), pltpu.VMEM((640, 2 * D), BF),
+    ]
+    return attend_call(
+        near_kernel, xl, (q, k, v), (q_got, *arrays), outs, [by_head(a) for a in outs], scratch, 12
+    )
+
+
+def attend_far(xl, q, q_got, arrays):
+    rows, cols = q.shape[0], q.shape[1] // 2
+    outs = [jax.ShapeDtypeStruct((rows, 2 * cols), BF), jax.ShapeDtypeStruct((rows, cols), BF)]
+    coarse_n = 2 * arrays[7].shape[1]
+    scratch = [
+        pltpu.VMEM((704, D), BF), pltpu.VMEM((704, 2 * D), BF),
         pltpu.VMEM((coarse_n, D), BF), pltpu.VMEM((coarse_n, 2 * D), BF),
+        pltpu.VMEM((384, D), BF), pltpu.VMEM((384, 2 * D), BF),
         pltpu.VMEM((64, coarse_n), BF),
     ]
     return attend_call(
-        near_kernel, xl, (q, k, v), (q_got, *arrays), outs, [by_head(a) for a in outs], scratch, 16
-    )
-
-
-def attend_far(xl, q, q_got, arrays):
-    rows, cols = q.shape[0], q.shape[1] // 2
-    outs = [jax.ShapeDtypeStruct((rows, 2 * cols), BF), jax.ShapeDtypeStruct((rows, cols), BF)]
-    scratch = [
-        pltpu.VMEM((704, D), BF), pltpu.VMEM((704, 2 * D), BF),
-        pltpu.VMEM((4, 384, D), BF), pltpu.VMEM((4, 384, 2 * D), BF),
-    ]
-    return attend_call(
         far_kernel, xl, (q,), (q_got, *arrays), outs,
-        [pl.BlockSpec((rows, D), column(D)), by_head(outs[1])], scratch, 9,
+        [pl.BlockSpec((rows, D), column(D)), by_head(outs[1])], scratch, 15,
     )
 
 
@@ -364,31 +363,32 @@
     def swapped(a):
         return moved(a, "xl", 1)
 
-    kv_send, keys, values = lax.optimization_barrier(
-        (jnp.stack([theirs(key_rows), theirs(value_rows)]), key_rows, value_rows)
-    )
-    kv_got = swapped(kv_send)
-    unit = coarse_rows(at, keys, values)
+    unit = coarse_rows(at, key_rows, value_rows)
     unit_got = swapped(unit)
+    kv_send = jnp.stack([theirs(key_rows), theirs(value_rows)])
+    kv_send, q_send, unit_got = lax.optimization_barrier((kv_send, theirs(queries), unit_got))
+    kv_got, q_got = swapped(kv_send), swapped(q_send)
     kept = unit.reshape(2, 8, half)[:, 0:4]
     came = unit_got.reshape(2, 8, half)[:, 4:8]
     unit = jnp.concatenate([jnp.where(low, kept, came), jnp.where(low, came, kept)], axis=1).reshape(16, half)
     units = lax.all_gather(unit, "z")
     units = jnp.moveaxis(units.reshape(-1, 2, 8, half), 1, 0).reshape(2, -1, half)
-    q_got = swapped(theirs(queries))
     kv_got, units, q_got = lax.optimization_barrier((kv_got, units, q_got))
     up1, down1, mid, far = pooled(at, key_rows, value_rows, kv_got)
     up1, down1, units = lax.optimization_barrier((up1, down1, units))
     below1, above1 = shifted(up1, 1), shifted(down1, -1)
-    coarse = (units, moved(units, "y", 1), moved(units, "y", -1), moved(units, "y", 2))
+    ny = lax.axis_size("y")
+    coarse0 = jnp.concatenate([units, lax.ppermute(units, "y", [(i, i ^ 1) for i in range(ny)])], axis=1)
+    coarse1 = lax.ppermute(coarse0, "y", [(i, ny - 1 - i) for i in range(ny)])
     below3, above3 = shifted(far[:, 96:128], 3), shifted(far[:, 0:32], -3)
     up, down, near = forwarded(below1, above1)
     below2, above2 = shifted(up, 1), shifted(down, -1)
     near_out, near_stat = attend_near(
-        at, queries, q_got, key_rows, value_rows, (kv_got, mid, below1, above1, near, *coarse)
+        at, queries, q_got, key_rows, value_rows, (kv_got, mid, below1, above1, near)
     )
     out, send_out = attend_far(
-        at, queries, q_got, (far, up, down, below2, above2, below3, above3, near_out, near_stat)
+        at, queries, q_got,
+        (far, up, down, below2, above2, below3, above3, coarse0, coarse1, near_out, near_stat),
     )
     return lax.dynamic_update_slice_in_dim(out, swapped(send_out), (1 - xl) * half, 1)
 

time: 188 us -> 174 us (0.926)
  the two profiles are of different devices: /device:TPU:82 before, /device:TPU:24 now
where the time goes in v5:
time: 174 us; the launch traced here: 172 us
  starting transfers between devices  43.7 us (25%)
  waiting for transfers between devices  42.6 us (24%)
  Pallas kernels  39.2 us (23%)
  blocking collectives  38.5 us (22%)
  local copies, waits for them, and re-layouts  7.52 us (4%)
    all_gather x1, blocking collectives, per_device(): units = lax.all_gather(unit, 'z')  38.5 us
    ppermute x1, waiting for transfers between devices, per_device(): lax.ppermute(units, 'y', [(i, i ^ 1) for i in range(ny)])  29.5 us
    pallas_call x2, Pallas kernels, attend_call(): pl.pallas_call(kernel, grid_spec=pltpu.PrefetchScalarGridSpec(num_scalar_...  27.5 us
    ppermute x6, starting transfers between devices, shifted(): lax.ppermute(a, YZ, [(i, i + step) for i in range(n) if 0 <= i + step < n])  27.3 us
    ppermute x4, waiting for transfers between devices, moved(): return lax.ppermute(a, axis, [(i, (i + step) % n) for i in range(n)])  13 us
    ppermute x4, starting transfers between devices, moved(): return lax.ppermute(a, axis, [(i, (i + step) % n) for i in range(n)])  11.7 us
    unnamed x31, local copies, waits for them, and re-layouts  5.66 us
    pallas_call x1, Pallas kernels, pooled(): pl.pallas_call(pool_kernel, grid_spec=pltpu.PrefetchScalarGridSpec(num_sc...  4.73 us
  transfers between devices with their start and end apart: 12, of which 3 were waited for; matrix products, arithmetic and copies ran while one was open for 1% of the time, Pallas kernels for 10%

profile of v5, /device:TPU:24, one launch (start us, length us, event | category | flops | bytes accessed | tf_op | source)
XLA Modules:
  0.0 172.1 jit_solution(16614672926569976522)
XLA Ops:
  0.0 3.0 %shard_map.37 = bf16[16,1024]{1,0:T(8,128)(2,1)} custom-call(s32[1]{0:T(128)} %bitcast.xl, bf16[256,2048]{1,0:T(8,128)(2,1)} %k_own.3, bf16[256,2048]{1,0:T(8,128)(2,1)} %k_own.3, bf16[256,2048]{1,0:T(8,128)(2,1)} %v_own.3, bf16[256,2048]{1,0:T(8,128)(2,1)} %v_own.3), custom_call_target="tpu_custom_call" | custom-call | bytes 10800000 | tf_op jit(solution)/shard_map/pallas_call | solution.py:61
  3.0 3.4 %collective-permute-start = (bf16[16,1024]{1,0:T(8,128)(2,1)}, bf16[16,1024]{1,0:T(8,128)(2,1)S(1)}, u32[]{:S(2)}, u32[]{:S(2)}) collective-permute-start(bf16[16,1024]{1,0:T(8,128)(2,1)} %shard_map.37), channel_id=1, source_target_pairs={{0,4},{4,0},{1,5},{5,1},{2,6},{6,2},{3,7},{7,3},{8,12},{12,8},{9,1... | collective-permute-start | bytes 98312 | tf_op jit(solution)/shard_map/ppermute | solution.py:346
  6.5 0.1 pad_maximum_fusion
  6.6 1.1 copy-done.2
  7.7 0.8 constant_dynamic-slice_fusion
  8.6 0.4 collective-permute-done
  9.0 3.4 %collective-permute-start.1 = (bf16[2,256,1024]{2,1,0:T(8,128)(2,1)S(1)}, bf16[2,256,1024]{2,1,0:T(8,128)(2,1)S(1)}, u32[]{:S(2)}, u32[]{:S(2)}) collective-permute-start(bf16[2,256,1024]{2,1,0:T(8,128)(2,1)S(1)} %pad_maximum_fusion), channel_id=1, source_target_pairs={{0,4},{4,0},{1,5},{5,1},{2,6},{6,2},{3,7},{7,3},{8,12},{12,8},{9,1... | collective-permute-start | bytes 3145736 | tf_op jit(solution)/shard_map/ppermute | solution.py:346
  12.4 2.4 %collective-permute-start.2 = (bf16[256,1024]{1,0:T(8,128)(2,1)}, bf16[256,1024]{1,0:T(8,128)(2,1)S(1)}, u32[]{:S(2)}, u32[]{:S(2)}) collective-permute-start(bf16[256,1024]{1,0:T(8,128)(2,1)} %constant_dynamic-slice_fusion), channel_id=1, source_target_pairs={{0,4},{4,0},{1,5},{5,1},{2,6},{6,2},{3,7},{7,3},{8,12},{12,8},{9,1... | collective-permute-start | bytes 1572872 | tf_op jit(solution)/shard_map/ppermute | solution.py:346
  14.9 38.5 %all_gather.3 = bf16[16,16,1024]{2,1,0:T(8,128)(2,1)S(1)} all-gather(bf16[1,16,1024]{2,1,0:T(8,128)(2,1)S(1)} %maximum_bitcast_fusion), channel_id=1, replica_groups=mesh['y'=4,'z'=16,'xl'=2,'head'=4] {'z'}, dimensions={0}, use_global_device_ids=true | all-gather | bytes 557056 | tf_op jit(solution)/shard_map/all_gather | solution.py:374
  53.5 1.0 copy-done.5
  54.5 4.7 %shard_map.38 = (bf16[2,288,1024]{2,1,0:T(8,128)(2,1)}, bf16[2,288,1024]{2,1,0:T(8,128)(2,1)}, bf16[2,256,1024]{2,1,0:T(8,128)(2,1)}, bf16[2,128,1024]{2,1,0:T(8,128)(2,1)}) custom-call(s32[1]{0:T(128)} %bitcast.xl, bf16[256,2048]{1,0:T(8,128)(2,1)} %k_own.3, bf16[256,2048]{1,0:T(8,128)(2,1)} %v_own.3, bf16[2,256,1024]{2,1,0:T(8,128)(2,1)} %copy-done.5), custom_call_target="tpu_custom_call" | custom-call | bytes 18000000 | tf_op jit(solution)/shard_map/pallas_call | solution.py:105
  59.2 2.0 %collective-permute-start.3 = (bf16[2,288,1024]{2,1,0:T(8,128)(2,1)}, bf16[2,288,1024]{2,1,0:T(8,128)(2,1)S(1)}, u32[]{:S(2)}, u32[]{:S(2)}) collective-permute-start(bf16[2,288,1024]{2,1,0:T(8,128)(2,1)} %get-tuple-element.34), channel_id=1, source_target_pairs={{0,8},{8,16},{16,24},{24,32},{32,40},{40,48},{48,56},{56,64},{64,7... | collective-permute-start | bytes 3538952 | tf_op jit(solution)/shard_map/ppermute | solution.py:351
  61.3 5.9 %collective-permute-start.4 = (bf16[2,288,1024]{2,1,0:T(8,128)(2,1)}, bf16[2,288,1024]{2,1,0:T(8,128)(2,1)S(1)}, u32[]{:S(2)}, u32[]{:S(2)}) collective-permute-start(bf16[2,288,1024]{2,1,0:T(8,128)(2,1)} %get-tuple-element.35), channel_id=1, source_target_pairs={{8,0},{16,8},{24,16},{32,24},{40,32},{48,40},{56,48},{64,56},{72,6... | collective-permute-start | bytes 3538952 | tf_op jit(solution)/shard_map/ppermute | solution.py:351
  67.2 2.7 %collective-permute-start.9 = (bf16[2,128,1024]{2,1,0:T(8,128)(2,1)S(1)}, bf16[2,128,1024]{2,1,0:T(8,128)(2,1)S(1)}, u32[]{:S(2)}, u32[]{:S(2)}) collective-permute-start(bf16[2,128,1024]{2,1,0:T(8,128)(2,1)S(1)} %copy_bitcast_fusion), channel_id=1, source_target_pairs={{0,128},{128,0},{256,384},{384,256},{1,129},{129,1},{257,385},{385... | collective-permute-start | bytes 1572872 | tf_op jit(solution)/shard_map/ppermute | solution.py:381
  69.9 29.5 %collective-permute-done.9 = bf16[2,128,1024]{2,1,0:T(8,128)(2,1)S(1)} collective-permute-done((bf16[2,128,1024]{2,1,0:T(8,128)(2,1)S(1)}, bf16[2,128,1024]{2,1,0:T(8,128)(2,1)S(1)}, u32[]{:S(2)}, u32[]{:S(2)}) %collective-permute-start.9) | collective-permute-done | bytes 524320 | tf_op jit(solution)/shard_map/ppermute | solution.py:381
  99.5 2.1 %collective-permute-start.10 = (bf16[2,256,1024]{2,1,0:T(8,128)(2,1)S(1)}, bf16[2,256,1024]{2,1,0:T(8,128)(2,1)S(1)}, u32[]{:S(2)}, u32[]{:S(2)}) collective-permute-start(bf16[2,256,1024]{2,1,0:T(8,128)(2,1)S(1)} %constant_dynamic-update-slice_fusion.coarse0), channel_id=1, source_target_pairs={{0,384},{128,256},{256,128},{384,0},{1,385},{129,257},{257,129},{3... | collective-permute-start | bytes 3145736 | tf_op jit(solution)/shard_map/ppermute | solution.py:382
  101.6 1.0 copy-done.3
  102.6 1.0 copy-done.4
  103.6 4.1 %shard_map.39 = (bf16[2,128,1024]{2,1,0:T(8,128)(2,1)}, bf16[2,128,1024]{2,1,0:T(8,128)(2,1)}, bf16[2,128,1024]{2,1,0:T(8,128)(2,1)}) custom-call(bf16[2,288,1024]{2,1,0:T(8,128)(2,1)} %copy-done.3, bf16[2,288,1024]{2,1,0:T(8,128)(2,1)} %copy-done.4), custom_call_target="tpu_custom_call" | custom-call | bytes 14400000 | tf_op jit(solution)/shard_map/pallas_call | solution.py:134
  107.7 1.9 %collective-permute-start.5 = (bf16[2,128,1024]{2,1,0:T(8,128)(2,1)}, bf16[2,128,1024]{2,1,0:T(8,128)(2,1)S(1)}, u32[]{:S(2)}, u32[]{:S(2)}) collective-permute-start(bf16[2,128,1024]{2,1,0:T(8,128)(2,1)} %get-tuple-element.36.up), channel_id=1, source_target_pairs={{0,8},{8,16},{16,24},{24,32},{32,40},{40,48},{48,56},{56,64},{64,7... | collective-permute-start | bytes 1572872 | tf_op jit(solution)/shard_map/ppermute | solution.py:351
  109.6 7.7 %collective-permute-start.6 = (bf16[2,128,1024]{2,1,0:T(8,128)(2,1)}, bf16[2,128,1024]{2,1,0:T(8,128)(2,1)S(1)}, u32[]{:S(2)}, u32[]{:S(2)}) collective-permute-start(bf16[2,128,1024]{2,1,0:T(8,128)(2,1)} %get-tuple-element.37.down), channel_id=1, source_target_pairs={{8,0},{16,8},{24,16},{32,24},{40,32},{48,40},{56,48},{64,56},{72,6... | collective-permute-start | bytes 1572872 | tf_op jit(solution)/shard_map/ppermute | solution.py:351
  117.4 1.9 %collective-permute-start.7 = (bf16[2,32,1024]{2,1,0:T(8,128)(2,1)S(1)}, bf16[2,32,1024]{2,1,0:T(8,128)(2,1)S(1)}, u32[]{:S(2)}, u32[]{:S(2)}) collective-permute-start(bf16[2,32,1024]{2,1,0:T(8,128)(2,1)S(1)} %get-tuple-element.46), channel_id=1, source_target_pairs={{0,24},{8,32},{16,40},{24,48},{32,56},{40,64},{48,72},{56,80},{64,... | collective-permute-start | bytes 393224 | tf_op jit(solution)/shard_map/ppermute | solution.py:351
  119.3 7.8 %collective-permute-start.8 = (bf16[2,32,1024]{2,1,0:T(8,128)(2,1)S(1)}, bf16[2,32,1024]{2,1,0:T(8,128)(2,1)S(1)}, u32[]{:S(2)}, u32[]{:S(2)}) collective-permute-start(bf16[2,32,1024]{2,1,0:T(8,128)(2,1)S(1)} %get-tuple-element.45), channel_id=1, source_target_pairs={{24,0},{32,8},{40,16},{48,24},{56,32},{64,40},{72,48},{80,56},{88,... | collective-permute-start | bytes 393224 | tf_op jit(solution)/shard_map/ppermute | solution.py:351
  127.1 12.4 %shard_map.40 = (f32[512,1024]{1,0:T(8,128)}, f32[512,1024]{1,0:T(8,128)}) custom-call(s32[1]{0:T(128)} %bitcast.xl, bf16[256,2048]{1,0:T(8,128)(2,1)} %q_own.3, bf16[256,1024]{1,0:T(8,128)(2,1)} %copy-done.7, bf16[256,2048]{1,0:T(8,128)(2,1)} %k_own.3, bf16[256,2048]{1,0:T(8,128)(2,1)} %v_own.3, bf16[2,256,1024]{2,1,0:T(8,128)(2,1)} %copy-done.5, ...), custom_call_target="tpu_custom_call" | custom-call | bytes 43200000 | tf_op jit(solution)/shard_map/pallas_call | solution.py:301
  139.6 0.6 copy-done.12
  140.2 0.4 copy-done.9
  140.6 0.3 copy-done.10
  140.9 0.1 copy-done.11
  141.0 15.1 %shard_map.41 = (bf16[256,2048]{1,0:T(8,128)(2,1)}, bf16[256,1024]{1,0:T(8,128)(2,1)}) custom-call(s32[1]{0:T(128)} %bitcast.xl, bf16[256,2048]{1,0:T(8,128)(2,1)} %q_own.3, bf16[256,1024]{1,0:T(8,128)(2,1)} %copy-done.7, bf16[2,128,1024]{2,1,0:T(8,128)(2,1)} %get-tuple-element.30.far, bf16[2,128,1024]{2,1,0:T(8,128)(2,1)} %get-tuple-element.36.up, ...), custom_call_target="tpu_custom_call" | custom-call | bytes 54000000 | tf_op jit(solution)/shard_map/pallas_call | solution.py:301
  156.1 2.5 %collective-permute-start.11 = (bf16[256,1024]{1,0:T(8,128)(2,1)}, bf16[256,1024]{1,0:T(8,128)(2,1)S(1)}, u32[]{:S(2)}, u32[]{:S(2)}) collective-permute-start(bf16[256,1024]{1,0:T(8,128)(2,1)} %get-tuple-element.44), channel_id=1, source_target_pairs={{0,4},{4,0},{1,5},{5,1},{2,6},{6,2},{3,7},{7,3},{8,12},{12,8},{9,1... | collective-permute-start | bytes 1572872 | tf_op jit(solution)/shard_map/ppermute | solution.py:346
  158.6 12.6 %collective-permute-done.11 = bf16[256,1024]{1,0:T(8,128)(2,1)S(1)} collective-permute-done((bf16[256,1024]{1,0:T(8,128)(2,1)}, bf16[256,1024]{1,0:T(8,128)(2,1)S(1)}, u32[]{:S(2)}, u32[]{:S(2)}) %collective-permute-start.11) | collective-permute-done | bytes 524320 | tf_op jit(solution)/shard_map/ppermute | solution.py:346
  171.2 0.8 constant_dynamic-update-slice_fusion.2
  (38 shorter events, 0.4 us)
Async XLA Ops:
  0.0 6.4 %copy-start = (bf16[256,2048]{1,0:T(8,128)(2,1)S(1)}, bf16[256,2048]{1,0:T(8,128)(2,1)}, u32[]{:S(2)}) copy-start(bf16[256,2048]{1,0:T(8,128)(2,1)} %k_own.3) | copy-start | bytes 3145732
  0.0 6.4 %copy-start.1 = (bf16[256,2048]{1,0:T(8,128)(2,1)S(1)}, bf16[256,2048]{1,0:T(8,128)(2,1)}, u32[]{:S(2)}) copy-start(bf16[256,2048]{1,0:T(8,128)(2,1)} %v_own.3) | copy-start | bytes 3145732
  3.0 6.0 %collective-permute-start = (bf16[16,1024]{1,0:T(8,128)(2,1)}, bf16[16,1024]{1,0:T(8,128)(2,1)S(1)}, u32[]{:S(2)}, u32[]{:S(2)}) collective-permute-start(bf16[16,1024]{1,0:T(8,128)(2,1)} %shard_map.37), channel_id=1, source_target_pairs={{0,4},{4,0},{1,5},{5,1},{2,6},{6,2},{3,7},{7,3},{8,12},{12,8},{9,1... | collective-permute-start | bytes 98312 | tf_op jit(solution)/shard_map/ppermute | solution.py:346
  6.5 1.2 copy-start.2
  6.5 8.3 %copy-start.14 = (bf16[16,1024]{1,0:T(8,128)(2,1)S(1)}, bf16[16,1024]{1,0:T(8,128)(2,1)}, u32[]{:S(2)}) copy-start(bf16[16,1024]{1,0:T(8,128)(2,1)} %shard_map.37) | copy-start | bytes 98308
  9.0 44.5 %collective-permute-start.1 = (bf16[2,256,1024]{2,1,0:T(8,128)(2,1)S(1)}, bf16[2,256,1024]{2,1,0:T(8,128)(2,1)S(1)}, u32[]{:S(2)}, u32[]{:S(2)}) collective-permute-start(bf16[2,256,1024]{2,1,0:T(8,128)(2,1)S(1)} %pad_maximum_fusion), channel_id=1, source_target_pairs={{0,4},{4,0},{1,5},{5,1},{2,6},{6,2},{3,7},{7,3},{8,12},{12,8},{9,1... | collective-permute-start | bytes 3145736 | tf_op jit(solution)/shard_map/ppermute | solution.py:346
  12.4 41.1 %collective-permute-start.2 = (bf16[256,1024]{1,0:T(8,128)(2,1)}, bf16[256,1024]{1,0:T(8,128)(2,1)S(1)}, u32[]{:S(2)}, u32[]{:S(2)}) collective-permute-start(bf16[256,1024]{1,0:T(8,128)(2,1)} %constant_dynamic-slice_fusion), channel_id=1, source_target_pairs={{0,4},{4,0},{1,5},{5,1},{2,6},{6,2},{3,7},{7,3},{8,12},{12,8},{9,1... | collective-permute-start | bytes 1572872 | tf_op jit(solution)/shard_map/ppermute | solution.py:346
  53.5 54.2 %copy-start.7 = (bf16[256,1024]{1,0:T(8,128)(2,1)}, bf16[256,1024]{1,0:T(8,128)(2,1)S(1)}, u32[]{:S(2)}) copy-start(bf16[256,1024]{1,0:T(8,128)(2,1)S(1)} %collective-permute-done.2.q_got) | copy-start | bytes 1572868
  53.5 1.0 copy-start.5
  59.2 42.3 %collective-permute-start.3 = (bf16[2,288,1024]{2,1,0:T(8,128)(2,1)}, bf16[2,288,1024]{2,1,0:T(8,128)(2,1)S(1)}, u32[]{:S(2)}, u32[]{:S(2)}) collective-permute-start(bf16[2,288,1024]{2,1,0:T(8,128)(2,1)} %get-tuple-element.34), channel_id=1, source_target_pairs={{0,8},{8,16},{16,24},{24,32},{32,40},{40,48},{48,56},{56,64},{64,7... | collective-permute-start | bytes 3538952 | tf_op jit(solution)/shard_map/ppermute | solution.py:351
  61.3 40.3 %collective-permute-start.4 = (bf16[2,288,1024]{2,1,0:T(8,128)(2,1)}, bf16[2,288,1024]{2,1,0:T(8,128)(2,1)S(1)}, u32[]{:S(2)}, u32[]{:S(2)}) collective-permute-start(bf16[2,288,1024]{2,1,0:T(8,128)(2,1)} %get-tuple-element.35), channel_id=1, source_target_pairs={{8,0},{16,8},{24,16},{32,24},{40,32},{48,40},{56,48},{64,56},{72,6... | collective-permute-start | bytes 3538952 | tf_op jit(solution)/shard_map/ppermute | solution.py:351
  67.2 32.2 %collective-permute-start.9 = (bf16[2,128,1024]{2,1,0:T(8,128)(2,1)S(1)}, bf16[2,128,1024]{2,1,0:T(8,128)(2,1)S(1)}, u32[]{:S(2)}, u32[]{:S(2)}) collective-permute-start(bf16[2,128,1024]{2,1,0:T(8,128)(2,1)S(1)} %copy_bitcast_fusion), channel_id=1, source_target_pairs={{0,128},{128,0},{256,384},{384,256},{1,129},{129,1},{257,385},{385... | collective-permute-start | bytes 1572872 | tf_op jit(solution)/shard_map/ppermute | solution.py:381
  99.5 40.0 %copy-start.6 = (bf16[2,256,1024]{2,1,0:T(8,128)(2,1)}, bf16[2,256,1024]{2,1,0:T(8,128)(2,1)S(1)}, u32[]{:S(2)}) copy-start(bf16[2,256,1024]{2,1,0:T(8,128)(2,1)S(1)} %constant_dynamic-update-slice_fusion.coarse0) | copy-start | bytes 3145732
  99.5 17.9 %copy-start.8 = (bf16[2,128,1024]{2,1,0:T(8,128)(2,1)S(1)}, bf16[2,128,1024]{2,1,0:T(8,128)(2,1)}, u32[]{:S(2)}) copy-start(bf16[2,128,1024]{2,1,0:T(8,128)(2,1)} %get-tuple-element.30.far) | copy-start | bytes 1572868
  99.5 40.1 %collective-permute-start.10 = (bf16[2,256,1024]{2,1,0:T(8,128)(2,1)S(1)}, bf16[2,256,1024]{2,1,0:T(8,128)(2,1)S(1)}, u32[]{:S(2)}, u32[]{:S(2)}) collective-permute-start(bf16[2,256,1024]{2,1,0:T(8,128)(2,1)S(1)} %constant_dynamic-update-slice_fusion.coarse0), channel_id=1, source_target_pairs={{0,384},{128,256},{256,128},{384,0},{1,385},{129,257},{257,129},{3... | collective-permute-start | bytes 3145736 | tf_op jit(solution)/shard_map/ppermute | solution.py:382
  101.6 1.1 copy-start.3
  102.6 1.0 copy-start.4
  107.7 31.9 %collective-permute-start.5 = (bf16[2,128,1024]{2,1,0:T(8,128)(2,1)}, bf16[2,128,1024]{2,1,0:T(8,128)(2,1)S(1)}, u32[]{:S(2)}, u32[]{:S(2)}) collective-permute-start(bf16[2,128,1024]{2,1,0:T(8,128)(2,1)} %get-tuple-element.36.up), channel_id=1, source_target_pairs={{0,8},{8,16},{16,24},{24,32},{32,40},{40,48},{48,56},{56,64},{64,7... | collective-permute-start | bytes 1572872 | tf_op jit(solution)/shard_map/ppermute | solution.py:351
  109.6 30.0 %collective-permute-start.6 = (bf16[2,128,1024]{2,1,0:T(8,128)(2,1)}, bf16[2,128,1024]{2,1,0:T(8,128)(2,1)S(1)}, u32[]{:S(2)}, u32[]{:S(2)}) collective-permute-start(bf16[2,128,1024]{2,1,0:T(8,128)(2,1)} %get-tuple-element.37.down), channel_id=1, source_target_pairs={{8,0},{16,8},{24,16},{32,24},{40,32},{48,40},{56,48},{64,56},{72,6... | collective-permute-start | bytes 1572872 | tf_op jit(solution)/shard_map/ppermute | solution.py:351
  117.4 22.1 %collective-permute-start.7 = (bf16[2,32,1024]{2,1,0:T(8,128)(2,1)S(1)}, bf16[2,32,1024]{2,1,0:T(8,128)(2,1)S(1)}, u32[]{:S(2)}, u32[]{:S(2)}) collective-permute-start(bf16[2,32,1024]{2,1,0:T(8,128)(2,1)S(1)} %get-tuple-element.46), channel_id=1, source_target_pairs={{0,24},{8,32},{16,40},{24,48},{32,56},{40,64},{48,72},{56,80},{64,... | collective-permute-start | bytes 393224 | tf_op jit(solution)/shard_map/ppermute | solution.py:351
  119.3 20.2 %collective-permute-start.8 = (bf16[2,32,1024]{2,1,0:T(8,128)(2,1)S(1)}, bf16[2,32,1024]{2,1,0:T(8,128)(2,1)S(1)}, u32[]{:S(2)}, u32[]{:S(2)}) collective-permute-start(bf16[2,32,1024]{2,1,0:T(8,128)(2,1)S(1)} %get-tuple-element.45), channel_id=1, source_target_pairs={{24,0},{32,8},{40,16},{48,24},{56,32},{64,40},{72,48},{80,56},{88,... | collective-permute-start | bytes 393224 | tf_op jit(solution)/shard_map/ppermute | solution.py:351
  139.5 0.7 copy-start.12
  139.5 0.7 copy-start.13
  139.6 1.1 copy-start.9
  139.6 1.3 copy-start.10
  139.6 1.4 copy-start.11
  156.1 15.1 %collective-permute-start.11 = (bf16[256,1024]{1,0:T(8,128)(2,1)}, bf16[256,1024]{1,0:T(8,128)(2,1)S(1)}, u32[]{:S(2)}, u32[]{:S(2)}) collective-permute-start(bf16[256,1024]{1,0:T(8,128)(2,1)} %get-tuple-element.44), channel_id=1, source_target_pairs={{0,4},{4,0},{1,5},{5,1},{2,6},{6,2},{3,7},{7,3},{8,12},{12,8},{9,1... | collective-permute-start | bytes 1572872 | tf_op jit(solution)/shard_map/ppermute | solution.py:346

commit v6 on v5

--- a/solution.py
+++ b/solution.py
@@ -223,13 +223,13 @@
 
 
 def far_kernel(
-    xl, q_own, q_got, far, up, down, below2, above2, below3, above3, coarse0, coarse1, near_out, near_stat,
+    xl, q_own, q_got, far, up, down, below2, above2, below3, above3, coarse0, coarse1, coarse2, coarse3, near_out, near_stat,
     own_out, send_out, kr, vr, kc, vc, kfar, vfar, mask,
 ):
     low = xl[0] == 0
     y = lax.axis_index("y")
     ny, nz = lax.axis_size("y"), lax.axis_size("z")
-    coarse_n = 2 * coarse0.shape[1]
+    coarse_n = 4 * coarse0.shape[1]
 
     @pl.when(pl.program_id(0) == 0)
     def _():
@@ -238,8 +238,7 @@
         for b in range(4):
             at = lax.broadcasted_iota(jnp.int32, (16, coarse_n), 1)
             turn = at // (8 * nz)
-            other = jnp.where(turn < 2, y, ny - 1 - y)
-            other = jnp.where(turn % 2 == 0, other, other + 1 - 2 * (other % 2))
+            other = (y + jnp.where(lax.axis_index("z") < nz // 2, ny - turn, turn)) % ny
             block = (other * nz + (at // 8) % nz) * 4 + (at % 8) // 2
             gap = jnp.abs(block - (4 * (y * nz + lax.axis_index("z")) + b))
             mask[b * 16 : (b + 1) * 16, :] = jnp.where(gap > FAR_REACH, 1.0, 0.0).astype(BF)
@@ -258,8 +257,8 @@
         put(far_w, 416, down[i], has_up[1], f3_4)
         put(far_w, 544, above2[i], has_up[2], f3_4)
         put(far_w, 672, above3[i], has_up[3], f3)
-    step = coarse_n // 2
-    for t, part in enumerate((coarse0, coarse1)):
+    step = coarse_n // 4
+    for t, part in enumerate((coarse0, coarse1, coarse2, coarse3)):
         kc[t * step : (t + 1) * step] = part[0]
         vc[t * step : (t + 1) * step, 0:D] = part[1]
     qo, qg = q_own[...], q_got[...]
@@ -328,7 +327,7 @@
 def attend_far(xl, q, q_got, arrays):
     rows, cols = q.shape[0], q.shape[1] // 2
     outs = [jax.ShapeDtypeStruct((rows, 2 * cols), BF), jax.ShapeDtypeStruct((rows, cols), BF)]
-    coarse_n = 2 * arrays[7].shape[1]
+    coarse_n = 4 * arrays[7].shape[1]
     scratch = [
         pltpu.VMEM((704, D), BF), pltpu.VMEM((704, 2 * D), BF),
         pltpu.VMEM((coarse_n, D), BF), pltpu.VMEM((coarse_n, 2 * D), BF),
@@ -349,6 +348,16 @@
 def shifted(a, step):
     n = lax.axis_size(YZ)
     return lax.ppermute(a, YZ, [(i, i + step) for i in range(n) if 0 <= i + step < n])
+
+
+def round_y(a):
+    ny, nz = lax.axis_size("y"), lax.axis_size("z")
+    route = []
+    for y in range(ny):
+        for z in range(nz):
+            to = (y + 1 if z < nz // 2 else y + ny - 1) % ny
+            route.append((y * nz + z, to * nz + z))
+    return lax.ppermute(a, YZ, route)
 
 
 def per_device(queries, key_rows, value_rows):
@@ -375,12 +384,12 @@
     units = jnp.moveaxis(units.reshape(-1, 2, 8, half), 1, 0).reshape(2, -1, half)
     kv_got, units, q_got = lax.optimization_barrier((kv_got, units, q_got))
     up1, down1, mid, far = pooled(at, key_rows, value_rows, kv_got)
-    up1, down1, units = lax.optimization_barrier((up1, down1, units))
     below1, above1 = shifted(up1, 1), shifted(down1, -1)
-    ny = lax.axis_size("y")
-    coarse0 = jnp.concatenate([units, lax.ppermute(units, "y", [(i, i ^ 1) for i in range(ny)])], axis=1)
-    coarse1 = lax.ppermute(coarse0, "y", [(i, ny - 1 - i) for i in range(ny)])
+    coarse = [units]
+    for _ in range(lax.axis_size("y") - 1):
+        coarse.append(round_y(coarse[-1]))
     below3, above3 = shifted(far[:, 96:128], 3), shifted(far[:, 0:32], -3)
+    below1, above1, below3, above3 = lax.optimization_barrier((below1, above1, below3, above3))
     up, down, near = forwarded(below1, above1)
     below2, above2 = shifted(up, 1), shifted(down, -1)
     near_out, near_stat = attend_near(
@@ -388,7 +397,7 @@
     )
     out, send_out = attend_far(
         at, queries, q_got,
-        (far, up, down, below2, above2, below3, above3, coarse0, coarse1, near_out, near_stat),
+        (far, up, down, below2, above2, below3, above3, *coarse, near_out, near_stat),
     )
     return lax.dynamic_update_slice_in_dim(out, swapped(send_out), (1 - xl) * half, 1)
 

time: 174 us -> 182 us (1.046)
  waiting for transfers between devices: 42.6 us -> 48.6 us
    ppermute x2 -> x3, waiting for transfers between devices: 29.5 us -> 36.1 us  [round_y(): return lax.ppermute(a, YZ, route)]
    ppermute x2 -> x3, starting transfers between devices: 4.7 us -> 5.74 us  [round_y(): return lax.ppermute(a, YZ, route)]
    unnamed x31 -> x32, local copies, waits for them, and re-layouts: 5.66 us -> 5.43 us
  transfers between devices with their start and end apart: 12 -> 13, of which waited for: 3 -> 4; matrix products, arithmetic and copies ran while one was open for 1% -> 1% of each run, Pallas kernels for 10% -> 9%
where the time goes in v6:
time: 182 us; the launch traced here: 180 us
  waiting for transfers between devices  48.6 us (27%)
  starting transfers between devices  45.2 us (25%)
  Pallas kernels  39.2 us (22%)
  blocking collectives  38.5 us (21%)
  local copies, waits for them, and re-layouts  8.22 us (5%)
    all_gather x1, blocking collectives, per_device(): units = lax.all_gather(unit, 'z')  38.5 us
    ppermute x3, waiting for transfers between devices, round_y(): return lax.ppermute(a, YZ, route)  36.1 us
    ppermute x6, starting transfers between devices, shifted(): lax.ppermute(a, YZ, [(i, i + step) for i in range(n) if 0 <= i + step < n])  27.7 us
    pallas_call x2, Pallas kernels, attend_call(): pl.pallas_call(kernel, grid_spec=pltpu.PrefetchScalarGridSpec(num_scalar_...  27.5 us
    ppermute x4, waiting for transfers between devices, moved(): return lax.ppermute(a, axis, [(i, (i + step) % n) for i in range(n)])  12.5 us
    ppermute x4, starting transfers between devices, moved(): return lax.ppermute(a, axis, [(i, (i + step) % n) for i in range(n)])  11.7 us
    ppermute x3, starting transfers between devices, round_y(): return lax.ppermute(a, YZ, route)  5.74 us
    unnamed x32, local copies, waits for them, and re-layouts  5.43 us
  transfers between devices with their start and end apart: 13, of which 4 were waited for; matrix products, arithmetic and copies ran while one was open for 1% of the time, Pallas kernels for 9%

profile of v6, /device:TPU:24, one launch (start us, length us, event | category | flops | bytes accessed | tf_op | source)
XLA Modules:
  0.0 180.2 jit_solution(5300163868061925187)
XLA Ops:
  0.0 3.0 %shard_map.37 = bf16[16,1024]{1,0:T(8,128)(2,1)} custom-call(s32[1]{0:T(128)} %bitcast.xl, bf16[256,2048]{1,0:T(8,128)(2,1)} %k_own.3, bf16[256,2048]{1,0:T(8,128)(2,1)} %k_own.3, bf16[256,2048]{1,0:T(8,128)(2,1)} %v_own.3, bf16[256,2048]{1,0:T(8,128)(2,1)} %v_own.3), custom_call_target="tpu_custom_call" | custom-call | bytes 10800000 | tf_op jit(solution)/shard_map/pallas_call | solution.py:61
  3.0 3.4 %collective-permute-start = (bf16[16,1024]{1,0:T(8,128)(2,1)}, bf16[16,1024]{1,0:T(8,128)(2,1)S(1)}, u32[]{:S(2)}, u32[]{:S(2)}) collective-permute-start(bf16[16,1024]{1,0:T(8,128)(2,1)} %shard_map.37), channel_id=1, source_target_pairs={{0,4},{4,0},{1,5},{5,1},{2,6},{6,2},{3,7},{7,3},{8,12},{12,8},{9,1... | collective-permute-start | bytes 98312 | tf_op jit(solution)/shard_map/ppermute | solution.py:345
  6.6 1.1 copy-done.2
  7.7 0.8 constant_dynamic-slice_fusion
  8.6 0.4 collective-permute-done
  9.0 3.4 %collective-permute-start.1 = (bf16[2,256,1024]{2,1,0:T(8,128)(2,1)S(1)}, bf16[2,256,1024]{2,1,0:T(8,128)(2,1)S(1)}, u32[]{:S(2)}, u32[]{:S(2)}) collective-permute-start(bf16[2,256,1024]{2,1,0:T(8,128)(2,1)S(1)} %pad_maximum_fusion), channel_id=1, source_target_pairs={{0,4},{4,0},{1,5},{5,1},{2,6},{6,2},{3,7},{7,3},{8,12},{12,8},{9,1... | collective-permute-start | bytes 3145736 | tf_op jit(solution)/shard_map/ppermute | solution.py:345
  12.4 2.4 %collective-permute-start.2 = (bf16[256,1024]{1,0:T(8,128)(2,1)}, bf16[256,1024]{1,0:T(8,128)(2,1)S(1)}, u32[]{:S(2)}, u32[]{:S(2)}) collective-permute-start(bf16[256,1024]{1,0:T(8,128)(2,1)} %constant_dynamic-slice_fusion), channel_id=1, source_target_pairs={{0,4},{4,0},{1,5},{5,1},{2,6},{6,2},{3,7},{7,3},{8,12},{12,8},{9,1... | collective-permute-start | bytes 1572872 | tf_op jit(solution)/shard_map/ppermute | solution.py:345
  14.9 38.5 %all_gather.3 = bf16[16,16,1024]{2,1,0:T(8,128)(2,1)S(1)} all-gather(bf16[1,16,1024]{2,1,0:T(8,128)(2,1)S(1)} %maximum_bitcast_fusion), channel_id=1, replica_groups=mesh['y'=4,'z'=16,'xl'=2,'head'=4] {'z'}, dimensions={0}, use_global_device_ids=true | all-gather | bytes 557056 | tf_op jit(solution)/shard_map/all_gather | solution.py:383
  53.5 1.0 copy-done.5
  54.5 4.7 %shard_map.38 = (bf16[2,288,1024]{2,1,0:T(8,128)(2,1)}, bf16[2,288,1024]{2,1,0:T(8,128)(2,1)}, bf16[2,256,1024]{2,1,0:T(8,128)(2,1)}, bf16[2,128,1024]{2,1,0:T(8,128)(2,1)}) custom-call(s32[1]{0:T(128)} %bitcast.xl, bf16[256,2048]{1,0:T(8,128)(2,1)} %k_own.3, bf16[256,2048]{1,0:T(8,128)(2,1)} %v_own.3, bf16[2,256,1024]{2,1,0:T(8,128)(2,1)} %copy-done.5), custom_call_target="tpu_custom_call" | custom-call | bytes 18000000 | tf_op jit(solution)/shard_map/pallas_call | solution.py:105
  59.2 2.0 %collective-permute-start.3 = (bf16[2,288,1024]{2,1,0:T(8,128)(2,1)}, bf16[2,288,1024]{2,1,0:T(8,128)(2,1)S(1)}, u32[]{:S(2)}, u32[]{:S(2)}) collective-permute-start(bf16[2,288,1024]{2,1,0:T(8,128)(2,1)} %get-tuple-element.32), channel_id=1, source_target_pairs={{0,8},{8,16},{16,24},{24,32},{32,40},{40,48},{48,56},{56,64},{64,7... | collective-permute-start | bytes 3538952 | tf_op jit(solution)/shard_map/ppermute | solution.py:350
  61.2 5.9 %collective-permute-start.4 = (bf16[2,288,1024]{2,1,0:T(8,128)(2,1)}, bf16[2,288,1024]{2,1,0:T(8,128)(2,1)S(1)}, u32[]{:S(2)}, u32[]{:S(2)}) collective-permute-start(bf16[2,288,1024]{2,1,0:T(8,128)(2,1)} %get-tuple-element.33), channel_id=1, source_target_pairs={{8,0},{16,8},{24,16},{32,24},{40,32},{48,40},{56,48},{64,56},{72,6... | collective-permute-start | bytes 3538952 | tf_op jit(solution)/shard_map/ppermute | solution.py:350
  67.1 1.9 %collective-permute-start.9 = (bf16[2,128,1024]{2,1,0:T(8,128)(2,1)S(1)}, bf16[2,128,1024]{2,1,0:T(8,128)(2,1)S(1)}, u32[]{:S(2)}, u32[]{:S(2)}) collective-permute-start(bf16[2,128,1024]{2,1,0:T(8,128)(2,1)S(1)} %copy_bitcast_fusion.coarse0), channel_id=1, source_target_pairs={{0,128},{8,136},{16,144},{24,152},{32,160},{40,168},{48,176},{56,1... | collective-permute-start | bytes 1572872 | tf_op jit(solution)/shard_map/ppermute | solution.py:360
  69.1 30.3 %collective-permute-done.9.coarse1 = bf16[2,128,1024]{2,1,0:T(8,128)(2,1)S(1)} collective-permute-done((bf16[2,128,1024]{2,1,0:T(8,128)(2,1)S(1)}, bf16[2,128,1024]{2,1,0:T(8,128)(2,1)S(1)}, u32[]{:S(2)}, u32[]{:S(2)}) %collective-permute-start.9) | collective-permute-done | bytes 524320 | tf_op jit(solution)/shard_map/ppermute | solution.py:360
  99.3 1.9 %collective-permute-start.10 = (bf16[2,128,1024]{2,1,0:T(8,128)(2,1)S(1)}, bf16[2,128,1024]{2,1,0:T(8,128)(2,1)S(1)}, u32[]{:S(2)}, u32[]{:S(2)}) collective-permute-start(bf16[2,128,1024]{2,1,0:T(8,128)(2,1)S(1)} %collective-permute-done.9.coarse1), channel_id=1, source_target_pairs={{0,128},{8,136},{16,144},{24,152},{32,160},{40,168},{48,176},{56,1... | collective-permute-start | bytes 1572872 | tf_op jit(solution)/shard_map/ppermute | solution.py:360
  101.3 1.0 fusion
  102.3 1.9 %collective-permute-start.5 = (bf16[2,32,1024]{2,1,0:T(8,128)(2,1)S(1)}, bf16[2,32,1024]{2,1,0:T(8,128)(2,1)S(1)}, u32[]{:S(2)}, u32[]{:S(2)}) collective-permute-start(bf16[2,32,1024]{2,1,0:T(8,128)(2,1)S(1)} %get-tuple-element.48), channel_id=1, source_target_pairs={{0,24},{8,32},{16,40},{24,48},{32,56},{40,64},{48,72},{56,80},{64,... | collective-permute-start | bytes 393224 | tf_op jit(solution)/shard_map/ppermute | solution.py:350
  104.2 7.8 %collective-permute-start.6 = (bf16[2,32,1024]{2,1,0:T(8,128)(2,1)S(1)}, bf16[2,32,1024]{2,1,0:T(8,128)(2,1)S(1)}, u32[]{:S(2)}, u32[]{:S(2)}) collective-permute-start(bf16[2,32,1024]{2,1,0:T(8,128)(2,1)S(1)} %get-tuple-element.47), channel_id=1, source_target_pairs={{24,0},{32,8},{40,16},{48,24},{56,32},{64,40},{72,48},{80,56},{88,... | collective-permute-start | bytes 393224 | tf_op jit(solution)/shard_map/ppermute | solution.py:350
  112.0 5.9 %collective-permute-done.10.coarse2 = bf16[2,128,1024]{2,1,0:T(8,128)(2,1)S(1)} collective-permute-done((bf16[2,128,1024]{2,1,0:T(8,128)(2,1)S(1)}, bf16[2,128,1024]{2,1,0:T(8,128)(2,1)S(1)}, u32[]{:S(2)}, u32[]{:S(2)}) %collective-permute-start.10) | collective-permute-done | bytes 524320 | tf_op jit(solution)/shard_map/ppermute | solution.py:360
  117.9 1.9 %collective-permute-start.11 = (bf16[2,128,1024]{2,1,0:T(8,128)(2,1)S(1)}, bf16[2,128,1024]{2,1,0:T(8,128)(2,1)S(1)}, u32[]{:S(2)}, u32[]{:S(2)}) collective-permute-start(bf16[2,128,1024]{2,1,0:T(8,128)(2,1)S(1)} %collective-permute-done.10.coarse2), channel_id=1, source_target_pairs={{0,128},{8,136},{16,144},{24,152},{32,160},{40,168},{48,176},{56,1... | collective-permute-start | bytes 1572872 | tf_op jit(solution)/shard_map/ppermute | solution.py:360
  119.9 1.1 copy-done.3
  121.0 1.0 copy-done.4
  122.0 4.1 %shard_map.39 = (bf16[2,128,1024]{2,1,0:T(8,128)(2,1)}, bf16[2,128,1024]{2,1,0:T(8,128)(2,1)}, bf16[2,128,1024]{2,1,0:T(8,128)(2,1)}) custom-call(bf16[2,288,1024]{2,1,0:T(8,128)(2,1)} %copy-done.3, bf16[2,288,1024]{2,1,0:T(8,128)(2,1)} %copy-done.4), custom_call_target="tpu_custom_call" | custom-call | bytes 14400000 | tf_op jit(solution)/shard_map/pallas_call | solution.py:134
  126.1 1.9 %collective-permute-start.7 = (bf16[2,128,1024]{2,1,0:T(8,128)(2,1)}, bf16[2,128,1024]{2,1,0:T(8,128)(2,1)S(1)}, u32[]{:S(2)}, u32[]{:S(2)}) collective-permute-start(bf16[2,128,1024]{2,1,0:T(8,128)(2,1)} %get-tuple-element.36.up), channel_id=1, source_target_pairs={{0,8},{8,16},{16,24},{24,32},{32,40},{40,48},{48,56},{56,64},{64,7... | collective-permute-start | bytes 1572872 | tf_op jit(solution)/shard_map/ppermute | solution.py:350
  128.0 8.1 %collective-permute-start.8 = (bf16[2,128,1024]{2,1,0:T(8,128)(2,1)}, bf16[2,128,1024]{2,1,0:T(8,128)(2,1)S(1)}, u32[]{:S(2)}, u32[]{:S(2)}) collective-permute-start(bf16[2,128,1024]{2,1,0:T(8,128)(2,1)} %get-tuple-element.37.down), channel_id=1, source_target_pairs={{8,0},{16,8},{24,16},{32,24},{40,32},{48,40},{56,48},{64,56},{72,6... | collective-permute-start | bytes 1572872 | tf_op jit(solution)/shard_map/ppermute | solution.py:350
  136.1 12.4 %shard_map.40 = (f32[512,1024]{1,0:T(8,128)}, f32[512,1024]{1,0:T(8,128)}) custom-call(s32[1]{0:T(128)} %bitcast.xl, bf16[256,2048]{1,0:T(8,128)(2,1)} %q_own.3, bf16[256,1024]{1,0:T(8,128)(2,1)} %copy-done.6, bf16[256,2048]{1,0:T(8,128)(2,1)} %k_own.3, bf16[256,2048]{1,0:T(8,128)(2,1)} %v_own.3, bf16[2,256,1024]{2,1,0:T(8,128)(2,1)} %copy-done.5, ...), custom_call_target="tpu_custom_call" | custom-call | bytes 43200000 | tf_op jit(solution)/shard_map/pallas_call | solution.py:300
  148.6 0.7 copy-done.10
  149.5 0.2 copy-done.12
  149.8 15.1 %shard_map.41 = (bf16[256,2048]{1,0:T(8,128)(2,1)}, bf16[256,1024]{1,0:T(8,128)(2,1)}) custom-call(s32[1]{0:T(128)} %bitcast.xl, bf16[256,2048]{1,0:T(8,128)(2,1)} %q_own.3, bf16[256,1024]{1,0:T(8,128)(2,1)} %copy-done.6, bf16[2,128,1024]{2,1,0:T(8,128)(2,1)} %get-tuple-element.31.far, bf16[2,128,1024]{2,1,0:T(8,128)(2,1)} %get-tuple-element.36.up, ...), custom_call_target="tpu_custom_call" | custom-call | bytes 54000000 | tf_op jit(solution)/shard_map/pallas_call | solution.py:300
  164.9 2.5 %collective-permute-start.12 = (bf16[256,1024]{1,0:T(8,128)(2,1)}, bf16[256,1024]{1,0:T(8,128)(2,1)S(1)}, u32[]{:S(2)}, u32[]{:S(2)}) collective-permute-start(bf16[256,1024]{1,0:T(8,128)(2,1)} %get-tuple-element.46), channel_id=1, source_target_pairs={{0,4},{4,0},{1,5},{5,1},{2,6},{6,2},{3,7},{7,3},{8,12},{12,8},{9,1... | collective-permute-start | bytes 1572872 | tf_op jit(solution)/shard_map/ppermute | solution.py:345
  167.3 12.1 %collective-permute-done.12 = bf16[256,1024]{1,0:T(8,128)(2,1)S(1)} collective-permute-done((bf16[256,1024]{1,0:T(8,128)(2,1)}, bf16[256,1024]{1,0:T(8,128)(2,1)S(1)}, u32[]{:S(2)}, u32[]{:S(2)}) %collective-permute-start.12) | collective-permute-done | bytes 524320 | tf_op jit(solution)/shard_map/ppermute | solution.py:345
  179.4 0.8 constant_dynamic-update-slice_fusion
  (40 shorter events, 0.5 us)
Async XLA Ops:
  0.0 6.4 %copy-start = (bf16[256,2048]{1,0:T(8,128)(2,1)S(1)}, bf16[256,2048]{1,0:T(8,128)(2,1)}, u32[]{:S(2)}) copy-start(bf16[256,2048]{1,0:T(8,128)(2,1)} %k_own.3) | copy-start | bytes 3145732
  0.0 6.4 %copy-start.1 = (bf16[256,2048]{1,0:T(8,128)(2,1)S(1)}, bf16[256,2048]{1,0:T(8,128)(2,1)}, u32[]{:S(2)}) copy-start(bf16[256,2048]{1,0:T(8,128)(2,1)} %v_own.3) | copy-start | bytes 3145732
  3.0 6.0 %collective-permute-start = (bf16[16,1024]{1,0:T(8,128)(2,1)}, bf16[16,1024]{1,0:T(8,128)(2,1)S(1)}, u32[]{:S(2)}, u32[]{:S(2)}) collective-permute-start(bf16[16,1024]{1,0:T(8,128)(2,1)} %shard_map.37), channel_id=1, source_target_pairs={{0,4},{4,0},{1,5},{5,1},{2,6},{6,2},{3,7},{7,3},{8,12},{12,8},{9,1... | collective-permute-start | bytes 98312 | tf_op jit(solution)/shard_map/ppermute | solution.py:345
  6.5 1.2 copy-start.2
  6.5 8.3 %copy-start.15 = (bf16[16,1024]{1,0:T(8,128)(2,1)S(1)}, bf16[16,1024]{1,0:T(8,128)(2,1)}, u32[]{:S(2)}) copy-start(bf16[16,1024]{1,0:T(8,128)(2,1)} %shard_map.37) | copy-start | bytes 98308
  9.0 44.5 %collective-permute-start.1 = (bf16[2,256,1024]{2,1,0:T(8,128)(2,1)S(1)}, bf16[2,256,1024]{2,1,0:T(8,128)(2,1)S(1)}, u32[]{:S(2)}, u32[]{:S(2)}) collective-permute-start(bf16[2,256,1024]{2,1,0:T(8,128)(2,1)S(1)} %pad_maximum_fusion), channel_id=1, source_target_pairs={{0,4},{4,0},{1,5},{5,1},{2,6},{6,2},{3,7},{7,3},{8,12},{12,8},{9,1... | collective-permute-start | bytes 3145736 | tf_op jit(solution)/shard_map/ppermute | solution.py:345
  12.4 41.1 %collective-permute-start.2 = (bf16[256,1024]{1,0:T(8,128)(2,1)}, bf16[256,1024]{1,0:T(8,128)(2,1)S(1)}, u32[]{:S(2)}, u32[]{:S(2)}) collective-permute-start(bf16[256,1024]{1,0:T(8,128)(2,1)} %constant_dynamic-slice_fusion), channel_id=1, source_target_pairs={{0,4},{4,0},{1,5},{5,1},{2,6},{6,2},{3,7},{7,3},{8,12},{12,8},{9,1... | collective-permute-start | bytes 1572872 | tf_op jit(solution)/shard_map/ppermute | solution.py:345
  53.5 95.1 %copy-start.7 = (bf16[2,128,1024]{2,1,0:T(8,128)(2,1)}, bf16[2,128,1024]{2,1,0:T(8,128)(2,1)S(1)}, u32[]{:S(2)}) copy-start(bf16[2,128,1024]{2,1,0:T(8,128)(2,1)S(1)} %copy_bitcast_fusion.coarse0) | copy-start | bytes 1572868
  53.5 82.7 %copy-start.6 = (bf16[256,1024]{1,0:T(8,128)(2,1)}, bf16[256,1024]{1,0:T(8,128)(2,1)S(1)}, u32[]{:S(2)}) copy-start(bf16[256,1024]{1,0:T(8,128)(2,1)S(1)} %collective-permute-done.2.q_got) | copy-start | bytes 1572868
  53.5 1.0 copy-start.5
  59.2 60.7 %collective-permute-start.3 = (bf16[2,288,1024]{2,1,0:T(8,128)(2,1)}, bf16[2,288,1024]{2,1,0:T(8,128)(2,1)S(1)}, u32[]{:S(2)}, u32[]{:S(2)}) collective-permute-start(bf16[2,288,1024]{2,1,0:T(8,128)(2,1)} %get-tuple-element.32), channel_id=1, source_target_pairs={{0,8},{8,16},{16,24},{24,32},{32,40},{40,48},{48,56},{56,64},{64,7... | collective-permute-start | bytes 3538952 | tf_op jit(solution)/shard_map/ppermute | solution.py:350
  61.2 58.7 %collective-permute-start.4 = (bf16[2,288,1024]{2,1,0:T(8,128)(2,1)}, bf16[2,288,1024]{2,1,0:T(8,128)(2,1)S(1)}, u32[]{:S(2)}, u32[]{:S(2)}) collective-permute-start(bf16[2,288,1024]{2,1,0:T(8,128)(2,1)} %get-tuple-element.33), channel_id=1, source_target_pairs={{8,0},{16,8},{24,16},{32,24},{40,32},{48,40},{56,48},{64,56},{72,6... | collective-permute-start | bytes 3538952 | tf_op jit(solution)/shard_map/ppermute | solution.py:350
  67.1 32.2 %collective-permute-start.9 = (bf16[2,128,1024]{2,1,0:T(8,128)(2,1)S(1)}, bf16[2,128,1024]{2,1,0:T(8,128)(2,1)S(1)}, u32[]{:S(2)}, u32[]{:S(2)}) collective-permute-start(bf16[2,128,1024]{2,1,0:T(8,128)(2,1)S(1)} %copy_bitcast_fusion.coarse0), channel_id=1, source_target_pairs={{0,128},{8,136},{16,144},{24,152},{32,160},{40,168},{48,176},{56,1... | collective-permute-start | bytes 1572872 | tf_op jit(solution)/shard_map/ppermute | solution.py:360
  99.3 26.7 %copy-start.8 = (bf16[2,128,1024]{2,1,0:T(8,128)(2,1)}, bf16[2,128,1024]{2,1,0:T(8,128)(2,1)S(1)}, u32[]{:S(2)}) copy-start(bf16[2,128,1024]{2,1,0:T(8,128)(2,1)S(1)} %collective-permute-done.9.coarse1) | copy-start | bytes 1572868
  99.3 18.5 %collective-permute-start.10 = (bf16[2,128,1024]{2,1,0:T(8,128)(2,1)S(1)}, bf16[2,128,1024]{2,1,0:T(8,128)(2,1)S(1)}, u32[]{:S(2)}, u32[]{:S(2)}) collective-permute-start(bf16[2,128,1024]{2,1,0:T(8,128)(2,1)S(1)} %collective-permute-done.9.coarse1), channel_id=1, source_target_pairs={{0,128},{8,136},{16,144},{24,152},{32,160},{40,168},{48,176},{56,1... | collective-permute-start | bytes 1572872 | tf_op jit(solution)/shard_map/ppermute | solution.py:360
  102.3 17.5 %collective-permute-start.5 = (bf16[2,32,1024]{2,1,0:T(8,128)(2,1)S(1)}, bf16[2,32,1024]{2,1,0:T(8,128)(2,1)S(1)}, u32[]{:S(2)}, u32[]{:S(2)}) collective-permute-start(bf16[2,32,1024]{2,1,0:T(8,128)(2,1)S(1)} %get-tuple-element.48), channel_id=1, source_target_pairs={{0,24},{8,32},{16,40},{24,48},{32,56},{40,64},{48,72},{56,80},{64,... | collective-permute-start | bytes 393224 | tf_op jit(solution)/shard_map/ppermute | solution.py:350
  104.2 15.6 %collective-permute-start.6 = (bf16[2,32,1024]{2,1,0:T(8,128)(2,1)S(1)}, bf16[2,32,1024]{2,1,0:T(8,128)(2,1)S(1)}, u32[]{:S(2)}, u32[]{:S(2)}) collective-permute-start(bf16[2,32,1024]{2,1,0:T(8,128)(2,1)S(1)} %get-tuple-element.47), channel_id=1, source_target_pairs={{24,0},{32,8},{40,16},{48,24},{56,32},{64,40},{72,48},{80,56},{88,... | collective-permute-start | bytes 393224 | tf_op jit(solution)/shard_map/ppermute | solution.py:350
  117.9 30.6 %copy-start.9 = (bf16[2,128,1024]{2,1,0:T(8,128)(2,1)}, bf16[2,128,1024]{2,1,0:T(8,128)(2,1)S(1)}, u32[]{:S(2)}) copy-start(bf16[2,128,1024]{2,1,0:T(8,128)(2,1)S(1)} %collective-permute-done.10.coarse2) | copy-start | bytes 1572868
  117.9 30.7 %collective-permute-start.11 = (bf16[2,128,1024]{2,1,0:T(8,128)(2,1)S(1)}, bf16[2,128,1024]{2,1,0:T(8,128)(2,1)S(1)}, u32[]{:S(2)}, u32[]{:S(2)}) collective-permute-start(bf16[2,128,1024]{2,1,0:T(8,128)(2,1)S(1)} %collective-permute-done.10.coarse2), channel_id=1, source_target_pairs={{0,128},{8,136},{16,144},{24,152},{32,160},{40,168},{48,176},{56,1... | collective-permute-start | bytes 1572872 | tf_op jit(solution)/shard_map/ppermute | solution.py:360
  119.8 28.7 %copy-start.13 = (bf16[2,32,1024]{2,1,0:T(8,128)(2,1)}, bf16[2,32,1024]{2,1,0:T(8,128)(2,1)S(1)}, u32[]{:S(2)}) copy-start(bf16[2,32,1024]{2,1,0:T(8,128)(2,1)S(1)} %collective-permute-done.5.below3) | copy-start | bytes 393220
  119.8 28.7 %copy-start.14 = (bf16[2,32,1024]{2,1,0:T(8,128)(2,1)}, bf16[2,32,1024]{2,1,0:T(8,128)(2,1)S(1)}, u32[]{:S(2)}) copy-start(bf16[2,32,1024]{2,1,0:T(8,128)(2,1)S(1)} %collective-permute-done.6.above3) | copy-start | bytes 393220
  119.9 1.1 copy-start.3
  121.0 1.0 copy-start.4
  126.1 22.5 %collective-permute-start.7 = (bf16[2,128,1024]{2,1,0:T(8,128)(2,1)}, bf16[2,128,1024]{2,1,0:T(8,128)(2,1)S(1)}, u32[]{:S(2)}, u32[]{:S(2)}) collective-permute-start(bf16[2,128,1024]{2,1,0:T(8,128)(2,1)} %get-tuple-element.36.up), channel_id=1, source_target_pairs={{0,8},{8,16},{16,24},{24,32},{32,40},{40,48},{48,56},{56,64},{64,7... | collective-permute-start | bytes 1572872 | tf_op jit(solution)/shard_map/ppermute | solution.py:350
  128.0 20.6 %collective-permute-start.8 = (bf16[2,128,1024]{2,1,0:T(8,128)(2,1)}, bf16[2,128,1024]{2,1,0:T(8,128)(2,1)S(1)}, u32[]{:S(2)}, u32[]{:S(2)}) collective-permute-start(bf16[2,128,1024]{2,1,0:T(8,128)(2,1)} %get-tuple-element.37.down), channel_id=1, source_target_pairs={{8,0},{16,8},{24,16},{32,24},{40,32},{48,40},{56,48},{64,56},{72,6... | collective-permute-start | bytes 1572872 | tf_op jit(solution)/shard_map/ppermute | solution.py:350
  148.6 0.8 copy-start.10
  148.6 1.0 copy-start.11
  148.6 1.2 copy-start.12
  164.9 14.6 %collective-permute-start.12 = (bf16[256,1024]{1,0:T(8,128)(2,1)}, bf16[256,1024]{1,0:T(8,128)(2,1)S(1)}, u32[]{:S(2)}, u32[]{:S(2)}) collective-permute-start(bf16[256,1024]{1,0:T(8,128)(2,1)} %get-tuple-element.46), channel_id=1, source_target_pairs={{0,4},{4,0},{1,5},{5,1},{2,6},{6,2},{3,7},{7,3},{8,12},{12,8},{9,1... | collective-permute-start | bytes 1572872 | tf_op jit(solution)/shard_map/ppermute | solution.py:345

commit v7 on v6

--- a/solution.py
+++ b/solution.py
@@ -238,7 +238,7 @@
         for b in range(4):
             at = lax.broadcasted_iota(jnp.int32, (16, coarse_n), 1)
             turn = at // (8 * nz)
-            other = (y + jnp.where(lax.axis_index("z") < nz // 2, ny - turn, turn)) % ny
+            other = (y + jnp.where(lax.axis_index("z") < nz // 2, turn, ny - turn)) % ny
             block = (other * nz + (at // 8) % nz) * 4 + (at % 8) // 2
             gap = jnp.abs(block - (4 * (y * nz + lax.axis_index("z")) + b))
             mask[b * 16 : (b + 1) * 16, :] = jnp.where(gap > FAR_REACH, 1.0, 0.0).astype(BF)
@@ -355,7 +355,7 @@
     route = []
     for y in range(ny):
         for z in range(nz):
-            to = (y + 1 if z < nz // 2 else y + ny - 1) % ny
+            to = (y + ny - 1 if z < nz // 2 else y + 1) % ny
             route.append((y * nz + z, to * nz + z))
     return lax.ppermute(a, YZ, route)
 

time: 182 us -> 156 us (0.86)
  waiting for transfers between devices: 48.6 us -> 24.9 us
    ppermute x3, waiting for transfers between devices: 36.1 us -> 10.6 us  [round_y(): return lax.ppermute(a, YZ, route)]
    ppermute x6, waiting for transfers between devices: 0.02 us -> 3.03 us  [shifted(): lax.ppermute(a, YZ, [(i, i + step) for i in range(n) if 0 <= i + step < n])]
    ppermute x6, starting transfers between devices: 27.7 us -> 25.6 us  [shifted(): lax.ppermute(a, YZ, [(i, i + step) for i in range(n) if 0 <= i + step < n])]
  transfers between devices with their start and end apart: 13 -> 13, of which waited for: 4 -> 4; matrix products, arithmetic and copies ran while one was open for 1% -> 1% of each run, Pallas kernels for 9% -> 11%
where the time goes in v7:
time: 156 us; the launch traced here: 155 us
  starting transfers between devices  44.1 us (28%)
  Pallas kernels  39.2 us (25%)
  blocking collectives  38.5 us (25%)
  waiting for transfers between devices  24.9 us (16%)
  local copies, waits for them, and re-layouts  8.19 us (5%)
    all_gather x1, blocking collectives, per_device(): units = lax.all_gather(unit, 'z')  38.5 us
    pallas_call x2, Pallas kernels, attend_call(): pl.pallas_call(kernel, grid_spec=pltpu.PrefetchScalarGridSpec(num_scalar_...  27.5 us
    ppermute x6, starting transfers between devices, shifted(): lax.ppermute(a, YZ, [(i, i + step) for i in range(n) if 0 <= i + step < n])  25.6 us
    ppermute x4, starting transfers between devices, moved(): return lax.ppermute(a, axis, [(i, (i + step) % n) for i in range(n)])  12 us
    ppermute x4, waiting for transfers between devices, moved(): return lax.ppermute(a, axis, [(i, (i + step) % n) for i in range(n)])  11.3 us
    ppermute x3, waiting for transfers between devices, round_y(): return lax.ppermute(a, YZ, route)  10.6 us
    ppermute x3, starting transfers between devices, round_y(): return lax.ppermute(a, YZ, route)  6.52 us
    unnamed x32, local copies, waits for them, and re-layouts  5.4 us
  transfers between devices with their start and end apart: 13, of which 4 were waited for; matrix products, arithmetic and copies ran while one was open for 1% of the time, Pallas kernels for 11%

profile of v7, /device:TPU:24, one launch (start us, length us, event | category | flops | bytes accessed | tf_op | source)
XLA Modules:
  0.0 155.4 jit_solution(9782175276510308761)
XLA Ops:
  0.0 3.0 %shard_map.37 = bf16[16,1024]{1,0:T(8,128)(2,1)} custom-call(s32[1]{0:T(128)} %bitcast.xl, bf16[256,2048]{1,0:T(8,128)(2,1)} %k_own.3, bf16[256,2048]{1,0:T(8,128)(2,1)} %k_own.3, bf16[256,2048]{1,0:T(8,128)(2,1)} %v_own.3, bf16[256,2048]{1,0:T(8,128)(2,1)} %v_own.3), custom_call_target="tpu_custom_call" | custom-call | bytes 10800000 | tf_op jit(solution)/shard_map/pallas_call | solution.py:61
  3.0 3.4 %collective-permute-start = (bf16[16,1024]{1,0:T(8,128)(2,1)}, bf16[16,1024]{1,0:T(8,128)(2,1)S(1)}, u32[]{:S(2)}, u32[]{:S(2)}) collective-permute-start(bf16[16,1024]{1,0:T(8,128)(2,1)} %shard_map.37), channel_id=1, source_target_pairs={{0,4},{4,0},{1,5},{5,1},{2,6},{6,2},{3,7},{7,3},{8,12},{12,8},{9,1... | collective-permute-start | bytes 98312 | tf_op jit(solution)/shard_map/ppermute | solution.py:345
  6.6 1.1 copy-done.2
  7.7 0.8 constant_dynamic-slice_fusion
  8.6 0.4 collective-permute-done
  9.0 3.4 %collective-permute-start.1 = (bf16[2,256,1024]{2,1,0:T(8,128)(2,1)S(1)}, bf16[2,256,1024]{2,1,0:T(8,128)(2,1)S(1)}, u32[]{:S(2)}, u32[]{:S(2)}) collective-permute-start(bf16[2,256,1024]{2,1,0:T(8,128)(2,1)S(1)} %pad_maximum_fusion), channel_id=1, source_target_pairs={{0,4},{4,0},{1,5},{5,1},{2,6},{6,2},{3,7},{7,3},{8,12},{12,8},{9,1... | collective-permute-start | bytes 3145736 | tf_op jit(solution)/shard_map/ppermute | solution.py:345
  12.4 2.4 %collective-permute-start.2 = (bf16[256,1024]{1,0:T(8,128)(2,1)}, bf16[256,1024]{1,0:T(8,128)(2,1)S(1)}, u32[]{:S(2)}, u32[]{:S(2)}) collective-permute-start(bf16[256,1024]{1,0:T(8,128)(2,1)} %constant_dynamic-slice_fusion), channel_id=1, source_target_pairs={{0,4},{4,0},{1,5},{5,1},{2,6},{6,2},{3,7},{7,3},{8,12},{12,8},{9,1... | collective-permute-start | bytes 1572872 | tf_op jit(solution)/shard_map/ppermute | solution.py:345
  14.9 38.5 %all_gather.3 = bf16[16,16,1024]{2,1,0:T(8,128)(2,1)S(1)} all-gather(bf16[1,16,1024]{2,1,0:T(8,128)(2,1)S(1)} %maximum_bitcast_fusion), channel_id=1, replica_groups=mesh['y'=4,'z'=16,'xl'=2,'head'=4] {'z'}, dimensions={0}, use_global_device_ids=true | all-gather | bytes 557056 | tf_op jit(solution)/shard_map/all_gather | solution.py:383
  53.5 1.0 copy-done.5
  54.5 4.7 %shard_map.38 = (bf16[2,288,1024]{2,1,0:T(8,128)(2,1)}, bf16[2,288,1024]{2,1,0:T(8,128)(2,1)}, bf16[2,256,1024]{2,1,0:T(8,128)(2,1)}, bf16[2,128,1024]{2,1,0:T(8,128)(2,1)}) custom-call(s32[1]{0:T(128)} %bitcast.xl, bf16[256,2048]{1,0:T(8,128)(2,1)} %k_own.3, bf16[256,2048]{1,0:T(8,128)(2,1)} %v_own.3, bf16[2,256,1024]{2,1,0:T(8,128)(2,1)} %copy-done.5), custom_call_target="tpu_custom_call" | custom-call | bytes 18000000 | tf_op jit(solution)/shard_map/pallas_call | solution.py:105
  59.2 2.0 %collective-permute-start.3 = (bf16[2,288,1024]{2,1,0:T(8,128)(2,1)}, bf16[2,288,1024]{2,1,0:T(8,128)(2,1)S(1)}, u32[]{:S(2)}, u32[]{:S(2)}) collective-permute-start(bf16[2,288,1024]{2,1,0:T(8,128)(2,1)} %get-tuple-element.32), channel_id=1, source_target_pairs={{0,8},{8,16},{16,24},{24,32},{32,40},{40,48},{48,56},{56,64},{64,7... | collective-permute-start | bytes 3538952 | tf_op jit(solution)/shard_map/ppermute | solution.py:350
  61.2 5.9 %collective-permute-start.4 = (bf16[2,288,1024]{2,1,0:T(8,128)(2,1)}, bf16[2,288,1024]{2,1,0:T(8,128)(2,1)S(1)}, u32[]{:S(2)}, u32[]{:S(2)}) collective-permute-start(bf16[2,288,1024]{2,1,0:T(8,128)(2,1)} %get-tuple-element.33), channel_id=1, source_target_pairs={{8,0},{16,8},{24,16},{32,24},{40,32},{48,40},{56,48},{64,56},{72,6... | collective-permute-start | bytes 3538952 | tf_op jit(solution)/shard_map/ppermute | solution.py:350
  67.1 2.7 %collective-permute-start.9 = (bf16[2,128,1024]{2,1,0:T(8,128)(2,1)S(1)}, bf16[2,128,1024]{2,1,0:T(8,128)(2,1)S(1)}, u32[]{:S(2)}, u32[]{:S(2)}) collective-permute-start(bf16[2,128,1024]{2,1,0:T(8,128)(2,1)S(1)} %copy_bitcast_fusion.coarse0), channel_id=1, source_target_pairs={{0,384},{8,392},{16,400},{24,408},{32,416},{40,424},{48,432},{56,4... | collective-permute-start | bytes 1572872 | tf_op jit(solution)/shard_map/ppermute | solution.py:360
  69.8 10.6 %collective-permute-done.9.coarse1 = bf16[2,128,1024]{2,1,0:T(8,128)(2,1)S(1)} collective-permute-done((bf16[2,128,1024]{2,1,0:T(8,128)(2,1)S(1)}, bf16[2,128,1024]{2,1,0:T(8,128)(2,1)S(1)}, u32[]{:S(2)}, u32[]{:S(2)}) %collective-permute-start.9) | collective-permute-done | bytes 524320 | tf_op jit(solution)/shard_map/ppermute | solution.py:360
  80.4 1.9 %collective-permute-start.10 = (bf16[2,128,1024]{2,1,0:T(8,128)(2,1)S(1)}, bf16[2,128,1024]{2,1,0:T(8,128)(2,1)S(1)}, u32[]{:S(2)}, u32[]{:S(2)}) collective-permute-start(bf16[2,128,1024]{2,1,0:T(8,128)(2,1)S(1)} %collective-permute-done.9.coarse1), channel_id=1, source_target_pairs={{0,384},{8,392},{16,400},{24,408},{32,416},{40,424},{48,432},{56,4... | collective-permute-start | bytes 1572872 | tf_op jit(solution)/shard_map/ppermute | solution.py:360
  82.3 1.0 fusion
  83.3 1.9 %collective-permute-start.5 = (bf16[2,32,1024]{2,1,0:T(8,128)(2,1)S(1)}, bf16[2,32,1024]{2,1,0:T(8,128)(2,1)S(1)}, u32[]{:S(2)}, u32[]{:S(2)}) collective-permute-start(bf16[2,32,1024]{2,1,0:T(8,128)(2,1)S(1)} %get-tuple-element.48), channel_id=1, source_target_pairs={{0,24},{8,32},{16,40},{24,48},{32,56},{40,64},{48,72},{56,80},{64,... | collective-permute-start | bytes 393224 | tf_op jit(solution)/shard_map/ppermute | solution.py:350
  85.2 7.8 %collective-permute-start.6 = (bf16[2,32,1024]{2,1,0:T(8,128)(2,1)S(1)}, bf16[2,32,1024]{2,1,0:T(8,128)(2,1)S(1)}, u32[]{:S(2)}, u32[]{:S(2)}) collective-permute-start(bf16[2,32,1024]{2,1,0:T(8,128)(2,1)S(1)} %get-tuple-element.47), channel_id=1, source_target_pairs={{24,0},{32,8},{40,16},{48,24},{56,32},{64,40},{72,48},{80,56},{88,... | collective-permute-start | bytes 393224 | tf_op jit(solution)/shard_map/ppermute | solution.py:350
  93.1 2.0 %collective-permute-start.11 = (bf16[2,128,1024]{2,1,0:T(8,128)(2,1)S(1)}, bf16[2,128,1024]{2,1,0:T(8,128)(2,1)S(1)}, u32[]{:S(2)}, u32[]{:S(2)}) collective-permute-start(bf16[2,128,1024]{2,1,0:T(8,128)(2,1)S(1)} %collective-permute-done.10.coarse2), channel_id=1, source_target_pairs={{0,384},{8,392},{16,400},{24,408},{32,416},{40,424},{48,432},{56,4... | collective-permute-start | bytes 1572872 | tf_op jit(solution)/shard_map/ppermute | solution.py:360
  95.0 3.0 %collective-permute-done.5.below3 = bf16[2,32,1024]{2,1,0:T(8,128)(2,1)S(1)} collective-permute-done((bf16[2,32,1024]{2,1,0:T(8,128)(2,1)S(1)}, bf16[2,32,1024]{2,1,0:T(8,128)(2,1)S(1)}, u32[]{:S(2)}, u32[]{:S(2)}) %collective-permute-start.5) | collective-permute-done | bytes 131104 | tf_op jit(solution)/shard_map/ppermute | solution.py:350
  98.1 1.1 copy-done.3
  99.2 1.0 copy-done.4
  100.2 4.1 %shard_map.39 = (bf16[2,128,1024]{2,1,0:T(8,128)(2,1)}, bf16[2,128,1024]{2,1,0:T(8,128)(2,1)}, bf16[2,128,1024]{2,1,0:T(8,128)(2,1)}) custom-call(bf16[2,288,1024]{2,1,0:T(8,128)(2,1)} %copy-done.3, bf16[2,288,1024]{2,1,0:T(8,128)(2,1)} %copy-done.4), custom_call_target="tpu_custom_call" | custom-call | bytes 14400000 | tf_op jit(solution)/shard_map/pallas_call | solution.py:134
  104.3 2.7 %collective-permute-start.7 = (bf16[2,128,1024]{2,1,0:T(8,128)(2,1)}, bf16[2,128,1024]{2,1,0:T(8,128)(2,1)S(1)}, u32[]{:S(2)}, u32[]{:S(2)}) collective-permute-start(bf16[2,128,1024]{2,1,0:T(8,128)(2,1)} %get-tuple-element.36.up), channel_id=1, source_target_pairs={{0,8},{8,16},{16,24},{24,32},{32,40},{40,48},{48,56},{56,64},{64,7... | collective-permute-start | bytes 1572872 | tf_op jit(solution)/shard_map/ppermute | solution.py:350
  106.9 5.3 %collective-permute-start.8 = (bf16[2,128,1024]{2,1,0:T(8,128)(2,1)}, bf16[2,128,1024]{2,1,0:T(8,128)(2,1)S(1)}, u32[]{:S(2)}, u32[]{:S(2)}) collective-permute-start(bf16[2,128,1024]{2,1,0:T(8,128)(2,1)} %get-tuple-element.37.down), channel_id=1, source_target_pairs={{8,0},{16,8},{24,16},{32,24},{40,32},{48,40},{56,48},{64,56},{72,6... | collective-permute-start | bytes 1572872 | tf_op jit(solution)/shard_map/ppermute | solution.py:350
  112.2 12.4 %shard_map.40 = (f32[512,1024]{1,0:T(8,128)}, f32[512,1024]{1,0:T(8,128)}) custom-call(s32[1]{0:T(128)} %bitcast.xl, bf16[256,2048]{1,0:T(8,128)(2,1)} %q_own.3, bf16[256,1024]{1,0:T(8,128)(2,1)} %copy-done.6, bf16[256,2048]{1,0:T(8,128)(2,1)} %k_own.3, bf16[256,2048]{1,0:T(8,128)(2,1)} %v_own.3, bf16[2,256,1024]{2,1,0:T(8,128)(2,1)} %copy-done.5, ...), custom_call_target="tpu_custom_call" | custom-call | bytes 43200000 | tf_op jit(solution)/shard_map/pallas_call | solution.py:300
  124.7 0.7 copy-done.10
  125.6 0.2 copy-done.12
  125.9 15.1 %shard_map.41 = (bf16[256,2048]{1,0:T(8,128)(2,1)}, bf16[256,1024]{1,0:T(8,128)(2,1)}) custom-call(s32[1]{0:T(128)} %bitcast.xl, bf16[256,2048]{1,0:T(8,128)(2,1)} %q_own.3, bf16[256,1024]{1,0:T(8,128)(2,1)} %copy-done.6, bf16[2,128,1024]{2,1,0:T(8,128)(2,1)} %get-tuple-element.31.far, bf16[2,128,1024]{2,1,0:T(8,128)(2,1)} %get-tuple-element.36.up, ...), custom_call_target="tpu_custom_call" | custom-call | bytes 54000000 | tf_op jit(solution)/shard_map/pallas_call | solution.py:300
  141.0 2.8 %collective-permute-start.12 = (bf16[256,1024]{1,0:T(8,128)(2,1)}, bf16[256,1024]{1,0:T(8,128)(2,1)S(1)}, u32[]{:S(2)}, u32[]{:S(2)}) collective-permute-start(bf16[256,1024]{1,0:T(8,128)(2,1)} %get-tuple-element.46), channel_id=1, source_target_pairs={{0,4},{4,0},{1,5},{5,1},{2,6},{6,2},{3,7},{7,3},{8,12},{12,8},{9,1... | collective-permute-start | bytes 1572872 | tf_op jit(solution)/shard_map/ppermute | solution.py:345
  143.7 10.8 %collective-permute-done.12 = bf16[256,1024]{1,0:T(8,128)(2,1)S(1)} collective-permute-done((bf16[256,1024]{1,0:T(8,128)(2,1)}, bf16[256,1024]{1,0:T(8,128)(2,1)S(1)}, u32[]{:S(2)}, u32[]{:S(2)}) %collective-permute-start.12) | collective-permute-done | bytes 524320 | tf_op jit(solution)/shard_map/ppermute | solution.py:345
  154.6 0.8 constant_dynamic-update-slice_fusion
  (40 shorter events, 0.5 us)
Async XLA Ops:
  0.0 6.4 %copy-start = (bf16[256,2048]{1,0:T(8,128)(2,1)S(1)}, bf16[256,2048]{1,0:T(8,128)(2,1)}, u32[]{:S(2)}) copy-start(bf16[256,2048]{1,0:T(8,128)(2,1)} %k_own.3) | copy-start | bytes 3145732
  0.0 6.4 %copy-start.1 = (bf16[256,2048]{1,0:T(8,128)(2,1)S(1)}, bf16[256,2048]{1,0:T(8,128)(2,1)}, u32[]{:S(2)}) copy-start(bf16[256,2048]{1,0:T(8,128)(2,1)} %v_own.3) | copy-start | bytes 3145732
  3.0 6.0 %collective-permute-start = (bf16[16,1024]{1,0:T(8,128)(2,1)}, bf16[16,1024]{1,0:T(8,128)(2,1)S(1)}, u32[]{:S(2)}, u32[]{:S(2)}) collective-permute-start(bf16[16,1024]{1,0:T(8,128)(2,1)} %shard_map.37), channel_id=1, source_target_pairs={{0,4},{4,0},{1,5},{5,1},{2,6},{6,2},{3,7},{7,3},{8,12},{12,8},{9,1... | collective-permute-start | bytes 98312 | tf_op jit(solution)/shard_map/ppermute | solution.py:345
  6.5 1.2 copy-start.2
  6.5 8.3 %copy-start.15 = (bf16[16,1024]{1,0:T(8,128)(2,1)S(1)}, bf16[16,1024]{1,0:T(8,128)(2,1)}, u32[]{:S(2)}) copy-start(bf16[16,1024]{1,0:T(8,128)(2,1)} %shard_map.37) | copy-start | bytes 98308
  9.0 44.5 %collective-permute-start.1 = (bf16[2,256,1024]{2,1,0:T(8,128)(2,1)S(1)}, bf16[2,256,1024]{2,1,0:T(8,128)(2,1)S(1)}, u32[]{:S(2)}, u32[]{:S(2)}) collective-permute-start(bf16[2,256,1024]{2,1,0:T(8,128)(2,1)S(1)} %pad_maximum_fusion), channel_id=1, source_target_pairs={{0,4},{4,0},{1,5},{5,1},{2,6},{6,2},{3,7},{7,3},{8,12},{12,8},{9,1... | collective-permute-start | bytes 3145736 | tf_op jit(solution)/shard_map/ppermute | solution.py:345
  12.4 41.1 %collective-permute-start.2 = (bf16[256,1024]{1,0:T(8,128)(2,1)}, bf16[256,1024]{1,0:T(8,128)(2,1)S(1)}, u32[]{:S(2)}, u32[]{:S(2)}) collective-permute-start(bf16[256,1024]{1,0:T(8,128)(2,1)} %constant_dynamic-slice_fusion), channel_id=1, source_target_pairs={{0,4},{4,0},{1,5},{5,1},{2,6},{6,2},{3,7},{7,3},{8,12},{12,8},{9,1... | collective-permute-start | bytes 1572872 | tf_op jit(solution)/shard_map/ppermute | solution.py:345
  53.5 71.2 %copy-start.7 = (bf16[2,128,1024]{2,1,0:T(8,128)(2,1)}, bf16[2,128,1024]{2,1,0:T(8,128)(2,1)S(1)}, u32[]{:S(2)}) copy-start(bf16[2,128,1024]{2,1,0:T(8,128)(2,1)S(1)} %copy_bitcast_fusion.coarse0) | copy-start | bytes 1572868
  53.5 58.7 %copy-start.6 = (bf16[256,1024]{1,0:T(8,128)(2,1)}, bf16[256,1024]{1,0:T(8,128)(2,1)S(1)}, u32[]{:S(2)}) copy-start(bf16[256,1024]{1,0:T(8,128)(2,1)S(1)} %collective-permute-done.2.q_got) | copy-start | bytes 1572868
  53.5 1.0 copy-start.5
  59.2 38.9 %collective-permute-start.3 = (bf16[2,288,1024]{2,1,0:T(8,128)(2,1)}, bf16[2,288,1024]{2,1,0:T(8,128)(2,1)S(1)}, u32[]{:S(2)}, u32[]{:S(2)}) collective-permute-start(bf16[2,288,1024]{2,1,0:T(8,128)(2,1)} %get-tuple-element.32), channel_id=1, source_target_pairs={{0,8},{8,16},{16,24},{24,32},{32,40},{40,48},{48,56},{56,64},{64,7... | collective-permute-start | bytes 3538952 | tf_op jit(solution)/shard_map/ppermute | solution.py:350
  61.2 36.9 %collective-permute-start.4 = (bf16[2,288,1024]{2,1,0:T(8,128)(2,1)}, bf16[2,288,1024]{2,1,0:T(8,128)(2,1)S(1)}, u32[]{:S(2)}, u32[]{:S(2)}) collective-permute-start(bf16[2,288,1024]{2,1,0:T(8,128)(2,1)} %get-tuple-element.33), channel_id=1, source_target_pairs={{8,0},{16,8},{24,16},{32,24},{40,32},{48,40},{56,48},{64,56},{72,6... | collective-permute-start | bytes 3538952 | tf_op jit(solution)/shard_map/ppermute | solution.py:350
  67.1 13.2 %collective-permute-start.9 = (bf16[2,128,1024]{2,1,0:T(8,128)(2,1)S(1)}, bf16[2,128,1024]{2,1,0:T(8,128)(2,1)S(1)}, u32[]{:S(2)}, u32[]{:S(2)}) collective-permute-start(bf16[2,128,1024]{2,1,0:T(8,128)(2,1)S(1)} %copy_bitcast_fusion.coarse0), channel_id=1, source_target_pairs={{0,384},{8,392},{16,400},{24,408},{32,416},{40,424},{48,432},{56,4... | collective-permute-start | bytes 1572872 | tf_op jit(solution)/shard_map/ppermute | solution.py:360
  80.4 23.9 %copy-start.8 = (bf16[2,128,1024]{2,1,0:T(8,128)(2,1)}, bf16[2,128,1024]{2,1,0:T(8,128)(2,1)S(1)}, u32[]{:S(2)}) copy-start(bf16[2,128,1024]{2,1,0:T(8,128)(2,1)S(1)} %collective-permute-done.9.coarse1) | copy-start | bytes 1572868
  80.4 12.7 %collective-permute-start.10 = (bf16[2,128,1024]{2,1,0:T(8,128)(2,1)S(1)}, bf16[2,128,1024]{2,1,0:T(8,128)(2,1)S(1)}, u32[]{:S(2)}, u32[]{:S(2)}) collective-permute-start(bf16[2,128,1024]{2,1,0:T(8,128)(2,1)S(1)} %collective-permute-done.9.coarse1), channel_id=1, source_target_pairs={{0,384},{8,392},{16,400},{24,408},{32,416},{40,424},{48,432},{56,4... | collective-permute-start | bytes 1572872 | tf_op jit(solution)/shard_map/ppermute | solution.py:360
  83.3 14.8 %collective-permute-start.5 = (bf16[2,32,1024]{2,1,0:T(8,128)(2,1)S(1)}, bf16[2,32,1024]{2,1,0:T(8,128)(2,1)S(1)}, u32[]{:S(2)}, u32[]{:S(2)}) collective-permute-start(bf16[2,32,1024]{2,1,0:T(8,128)(2,1)S(1)} %get-tuple-element.48), channel_id=1, source_target_pairs={{0,24},{8,32},{16,40},{24,48},{32,56},{40,64},{48,72},{56,80},{64,... | collective-permute-start | bytes 393224 | tf_op jit(solution)/shard_map/ppermute | solution.py:350
  85.2 12.8 %collective-permute-start.6 = (bf16[2,32,1024]{2,1,0:T(8,128)(2,1)S(1)}, bf16[2,32,1024]{2,1,0:T(8,128)(2,1)S(1)}, u32[]{:S(2)}, u32[]{:S(2)}) collective-permute-start(bf16[2,32,1024]{2,1,0:T(8,128)(2,1)S(1)} %get-tuple-element.47), channel_id=1, source_target_pairs={{24,0},{32,8},{40,16},{48,24},{56,32},{64,40},{72,48},{80,56},{88,... | collective-permute-start | bytes 393224 | tf_op jit(solution)/shard_map/ppermute | solution.py:350
  93.1 31.6 %copy-start.9 = (bf16[2,128,1024]{2,1,0:T(8,128)(2,1)}, bf16[2,128,1024]{2,1,0:T(8,128)(2,1)S(1)}, u32[]{:S(2)}) copy-start(bf16[2,128,1024]{2,1,0:T(8,128)(2,1)S(1)} %collective-permute-done.10.coarse2) | copy-start | bytes 1572868
  93.1 31.6 %collective-permute-start.11 = (bf16[2,128,1024]{2,1,0:T(8,128)(2,1)S(1)}, bf16[2,128,1024]{2,1,0:T(8,128)(2,1)S(1)}, u32[]{:S(2)}, u32[]{:S(2)}) collective-permute-start(bf16[2,128,1024]{2,1,0:T(8,128)(2,1)S(1)} %collective-permute-done.10.coarse2), channel_id=1, source_target_pairs={{0,384},{8,392},{16,400},{24,408},{32,416},{40,424},{48,432},{56,4... | collective-permute-start | bytes 1572872 | tf_op jit(solution)/shard_map/ppermute | solution.py:360
  98.0 26.6 %copy-start.13 = (bf16[2,32,1024]{2,1,0:T(8,128)(2,1)}, bf16[2,32,1024]{2,1,0:T(8,128)(2,1)S(1)}, u32[]{:S(2)}) copy-start(bf16[2,32,1024]{2,1,0:T(8,128)(2,1)S(1)} %collective-permute-done.5.below3) | copy-start | bytes 393220
  98.1 26.6 %copy-start.14 = (bf16[2,32,1024]{2,1,0:T(8,128)(2,1)}, bf16[2,32,1024]{2,1,0:T(8,128)(2,1)S(1)}, u32[]{:S(2)}) copy-start(bf16[2,32,1024]{2,1,0:T(8,128)(2,1)S(1)} %collective-permute-done.6.above3) | copy-start | bytes 393220
  98.1 1.1 copy-start.3
  99.2 1.0 copy-start.4
  104.3 20.4 %collective-permute-start.7 = (bf16[2,128,1024]{2,1,0:T(8,128)(2,1)}, bf16[2,128,1024]{2,1,0:T(8,128)(2,1)S(1)}, u32[]{:S(2)}, u32[]{:S(2)}) collective-permute-start(bf16[2,128,1024]{2,1,0:T(8,128)(2,1)} %get-tuple-element.36.up), channel_id=1, source_target_pairs={{0,8},{8,16},{16,24},{24,32},{32,40},{40,48},{48,56},{56,64},{64,7... | collective-permute-start | bytes 1572872 | tf_op jit(solution)/shard_map/ppermute | solution.py:350
  106.9 17.7 %collective-permute-start.8 = (bf16[2,128,1024]{2,1,0:T(8,128)(2,1)}, bf16[2,128,1024]{2,1,0:T(8,128)(2,1)S(1)}, u32[]{:S(2)}, u32[]{:S(2)}) collective-permute-start(bf16[2,128,1024]{2,1,0:T(8,128)(2,1)} %get-tuple-element.37.down), channel_id=1, source_target_pairs={{8,0},{16,8},{24,16},{32,24},{40,32},{48,40},{56,48},{64,56},{72,6... | collective-permute-start | bytes 1572872 | tf_op jit(solution)/shard_map/ppermute | solution.py:350
  124.7 0.8 copy-start.10
  124.7 1.0 copy-start.11
  124.7 1.2 copy-start.12
  141.0 13.6 %collective-permute-start.12 = (bf16[256,1024]{1,0:T(8,128)(2,1)}, bf16[256,1024]{1,0:T(8,128)(2,1)S(1)}, u32[]{:S(2)}, u32[]{:S(2)}) collective-permute-start(bf16[256,1024]{1,0:T(8,128)(2,1)} %get-tuple-element.46), channel_id=1, source_target_pairs={{0,4},{4,0},{1,5},{5,1},{2,6},{6,2},{3,7},{7,3},{8,12},{12,8},{9,1... | collective-permute-start | bytes 1572872 | tf_op jit(solution)/shard_map/ppermute | solution.py:345

commit v8 on v7

--- a/solution.py
+++ b/solution.py
@@ -19,6 +19,7 @@
 F32 = jnp.float32
 SCALE = math.log2(math.e) / math.sqrt(D)
 VMEM = pltpu.CompilerParams(vmem_limit_bytes=58 * 2**20)
+LITTLE_VMEM = pltpu.CompilerParams(vmem_limit_bytes=24 * 2**20)
 
 
 def taking(microseconds):
@@ -73,7 +74,7 @@
     )(xl, k, k, v, v)
 
 
-def pool_kernel(xl, k_ref, v_ref, got_ref, up_ref, down_ref, mid_ref, far_ref, scratch):
+def pool_kernel(xl, k_ref, v_ref, got_ref, up_ref, down_ref, mid_ref, far_ref, up3_ref, down3_ref, scratch):
     low = xl[0] == 0
     for i, ref in enumerate((k_ref, v_ref)):
         own, got = ref[...], got_ref[i]
@@ -87,6 +88,8 @@
         mid_ref[i, 128:256] = mid_second
         far_ref[i, 0:64] = far_first
         far_ref[i, 64:128] = far_second
+        up3_ref[i] = far_second[32:64]
+        down3_ref[i] = far_first[0:32]
         up_ref[i, 0:128] = second[128:256]
         up_ref[i, 128:192] = mid_first[64:128]
         up_ref[i, 192:256] = mid_second[0:64]
@@ -100,7 +103,7 @@
 def pooled(xl, k, v, got):
     _, rows, cols = got.shape
     width = 256
-    sizes = (288, 288, 256, 128)
+    sizes = (288, 288, 256, 128, 32, 32)
     own = pl.BlockSpec((rows, width), column(width))
     return pl.pallas_call(
         pool_kernel,
@@ -138,7 +141,7 @@
         out_specs=[pl.BlockSpec((1, 128, width), lambda i, c: (i, 0, c))] * 3,
         out_shape=[jax.ShapeDtypeStruct((2, 128, cols), BF)] * 3,
         scratch_shapes=[pltpu.VMEM((width // D, 192, D), F32)],
-        compiler_params=VMEM, cost_estimate=taking(4),
+        compiler_params=LITTLE_VMEM, cost_estimate=taking(4),
     )(below, above)
 
 
@@ -262,25 +265,29 @@
         kc[t * step : (t + 1) * step] = part[0]
         vc[t * step : (t + 1) * step, 0:D] = part[1]
     qo, qg = q_own[...], q_got[...]
-    queries = (jnp.where(low, qo, qg), jnp.where(low, qg, qo))
-    results = []
+    queries = jnp.concatenate([jnp.where(low, qo, qg), jnp.where(low, qg, qo)], axis=0)
+    coarse_scores = scores(queries, kc[...])
+    uppers, sums, coarse_weights = [], [], []
     for b in range(4):
-        q = queries[b // 2][(b % 2) * 128 : (b % 2 + 1) * 128]
+        here = slice(b * 128, (b + 1) * 128)
         kfar[0:192] = kr[b * 32 : b * 32 + 192]
         kfar[192:384] = kr[(b + 13) * 32 : (b + 13) * 32 + 192]
         vfar[0:192] = vr[b * 32 : b * 32 + 192]
         vfar[192:384] = vr[(b + 13) * 32 : (b + 13) * 32 + 192]
-        parts = [
-            (scores(q, kfar[...]), vfar[...], 2.0, None),
-            (scores(q, kc[...]), vc[...], 6.0, mask[b * 16 : b * 16 + 1, :]),
-        ]
+        fours = (scores(queries[here], kfar[...]), vfar[...], 2.0, None)
+        near_top, near_sum = near_stat[here, 0:1], near_stat[here, D - 1 : D]
+        top = jnp.maximum(top_of([fours, (coarse_scores[here], None, 6.0, None)]), near_top)
+        total = weighted([fours], top)
+        scale = jnp.exp2(near_top - top)
+        uppers.append(total[:, 0:D] + near_out[here] * scale)
+        sums.append(total[:, D : 2 * D] + near_sum * scale)
+        weights = jnp.exp2(coarse_scores[here] * SCALE - (top - 6.0)).astype(BF)
+        coarse_weights.append(weights * mask[b * 16 : b * 16 + 1, :])
+    total = jnp.dot(jnp.concatenate(coarse_weights, axis=0), vc[...], preferred_element_type=F32)
+    results = []
+    for b in range(4):
         here = slice(b * 128, (b + 1) * 128)
-        near_top, near_sum = near_stat[here, 0:1], near_stat[here, D - 1 : D]
-        top = jnp.maximum(top_of(parts), near_top)
-        total = weighted(parts, top)
-        scale = jnp.exp2(near_top - top)
-        upper = total[:, 0:D] + near_out[here] * scale
-        results.append((upper / (total[:, D : 2 * D] + near_sum * scale)).astype(BF))
+        results.append(((uppers[b] + total[here, 0:D]) / (sums[b] + total[here, D : 2 * D])).astype(BF))
     out_first = jnp.concatenate(results[0:2], axis=0)
     out_second = jnp.concatenate(results[2:4], axis=0)
     own_out[...] = jnp.where(low, out_first, out_second)
@@ -383,12 +390,12 @@
     units = lax.all_gather(unit, "z")
     units = jnp.moveaxis(units.reshape(-1, 2, 8, half), 1, 0).reshape(2, -1, half)
     kv_got, units, q_got = lax.optimization_barrier((kv_got, units, q_got))
-    up1, down1, mid, far = pooled(at, key_rows, value_rows, kv_got)
+    up1, down1, mid, far, up3, down3 = pooled(at, key_rows, value_rows, kv_got)
     below1, above1 = shifted(up1, 1), shifted(down1, -1)
     coarse = [units]
     for _ in range(lax.axis_size("y") - 1):
         coarse.append(round_y(coarse[-1]))
-    below3, above3 = shifted(far[:, 96:128], 3), shifted(far[:, 0:32], -3)
+    below3, above3 = shifted(up3, 3), shifted(down3, -3)
     below1, above1, below3, above3 = lax.optimization_barrier((below1, above1, below3, above3))
     up, down, near = forwarded(below1, above1)
     below2, above2 = shifted(up, 1), shifted(down, -1)

time: 156 us -> 150 us (0.962)
  Pallas kernels: 39.2 us -> 36.5 us
  local copies, waits for them, and re-layouts: 8.19 us -> 5.55 us
  waiting for transfers between devices: 24.9 us -> 22.7 us
    pallas_call x1, Pallas kernels: 4.06 us -> 1.01 us  [forwarded(): pl.pallas_call(forward_kernel, grid=(2, cols // width), in_specs=[pl.Bloc...]
    ppermute x4, waiting for transfers between devices: 11.3 us -> 8.83 us  [moved(): return lax.ppermute(a, axis, [(i, (i + step) % n) for i in range(n)])]
    unnamed x32 -> x38, local copies, waits for them, and re-layouts: 5.4 us -> 4.55 us
  transfers between devices with their start and end apart: 13 -> 13, of which waited for: 4 -> 6; matrix products, arithmetic and copies ran while one was open for 1% -> 1% of each run, Pallas kernels for 11% -> 9%
where the time goes in v8:
time: 150 us; the launch traced here: 149 us
  starting transfers between devices  44.6 us (30%)
  blocking collectives  38.4 us (26%)
  Pallas kernels  36.5 us (24%)
  waiting for transfers between devices  22.7 us (15%)
  local copies, waits for them, and re-layouts  5.55 us (4%)
    all_gather x1, blocking collectives, per_device(): units = lax.all_gather(unit, 'z')  38.4 us
    pallas_call x2, Pallas kernels, attend_call(): pl.pallas_call(kernel, grid_spec=pltpu.PrefetchScalarGridSpec(num_scalar_...  27.8 us
    ppermute x6, starting transfers between devices, shifted(): lax.ppermute(a, YZ, [(i, i + step) for i in range(n) if 0 <= i + step < n])  25.6 us
    ppermute x4, starting transfers between devices, moved(): return lax.ppermute(a, axis, [(i, (i + step) % n) for i in range(n)])  12.5 us
    ppermute x3, waiting for transfers between devices, round_y(): return lax.ppermute(a, YZ, route)  10.9 us
    ppermute x4, waiting for transfers between devices, moved(): return lax.ppermute(a, axis, [(i, (i + step) % n) for i in range(n)])  8.83 us
    ppermute x3, starting transfers between devices, round_y(): return lax.ppermute(a, YZ, route)  6.47 us
    pallas_call x1, Pallas kernels, pooled(): pl.pallas_call(pool_kernel, grid_spec=pltpu.PrefetchScalarGridSpec(num_sc...  4.75 us
  transfers between devices with their start and end apart: 13, of which 6 were waited for; matrix products, arithmetic and copies ran while one was open for 1% of the time, Pallas kernels for 9%

profile of v8, /device:TPU:24, one launch (start us, length us, event | category | flops | bytes accessed | tf_op | source)
XLA Modules:
  0.0 149.3 jit_solution(15908221991513668088)
XLA Ops:
  0.0 3.0 %shard_map.37 = bf16[16,1024]{1,0:T(8,128)(2,1)} custom-call(s32[1]{0:T(128)} %bitcast.xl, bf16[256,2048]{1,0:T(8,128)(2,1)} %k_own.3, bf16[256,2048]{1,0:T(8,128)(2,1)} %k_own.3, bf16[256,2048]{1,0:T(8,128)(2,1)} %v_own.3, bf16[256,2048]{1,0:T(8,128)(2,1)} %v_own.3), custom_call_target="tpu_custom_call" | custom-call | bytes 10800000 | tf_op jit(solution)/shard_map/pallas_call | solution.py:62
  3.0 3.4 %collective-permute-start = (bf16[16,1024]{1,0:T(8,128)(2,1)}, bf16[16,1024]{1,0:T(8,128)(2,1)S(1)}, u32[]{:S(2)}, u32[]{:S(2)}) collective-permute-start(bf16[16,1024]{1,0:T(8,128)(2,1)} %shard_map.37), channel_id=1, source_target_pairs={{0,4},{4,0},{1,5},{5,1},{2,6},{6,2},{3,7},{7,3},{8,12},{12,8},{9,1... | collective-permute-start | bytes 98312 | tf_op jit(solution)/shard_map/ppermute | solution.py:352
  6.5 1.1 pad_maximum_fusion
  7.6 0.5 copy-done.7
  8.2 0.8 collective-permute-done
  9.0 3.4 %collective-permute-start.1 = (bf16[2,256,1024]{2,1,0:T(8,128)(2,1)}, bf16[2,256,1024]{2,1,0:T(8,128)(2,1)S(1)}, u32[]{:S(2)}, u32[]{:S(2)}) collective-permute-start(bf16[2,256,1024]{2,1,0:T(8,128)(2,1)} %pad_maximum_fusion), channel_id=1, source_target_pairs={{0,4},{4,0},{1,5},{5,1},{2,6},{6,2},{3,7},{7,3},{8,12},{12,8},{9,1... | collective-permute-start | bytes 3145736 | tf_op jit(solution)/shard_map/ppermute | solution.py:352
  12.4 2.4 %collective-permute-start.2 = (bf16[256,1024]{1,0:T(8,128)(2,1)S(1)}, bf16[256,1024]{1,0:T(8,128)(2,1)S(1)}, u32[]{:S(2)}, u32[]{:S(2)}) collective-permute-start(bf16[256,1024]{1,0:T(8,128)(2,1)S(1)} %constant_dynamic-slice_fusion), channel_id=1, source_target_pairs={{0,4},{4,0},{1,5},{5,1},{2,6},{6,2},{3,7},{7,3},{8,12},{12,8},{9,1... | collective-permute-start | bytes 1572872 | tf_op jit(solution)/shard_map/ppermute | solution.py:352
  14.9 38.4 %all_gather.3 = bf16[16,16,1024]{2,1,0:T(8,128)(2,1)S(1)} all-gather(bf16[1,16,1024]{2,1,0:T(8,128)(2,1)S(1)} %maximum_bitcast_fusion), channel_id=1, replica_groups=mesh['y'=4,'z'=16,'xl'=2,'head'=4] {'z'}, dimensions={0}, use_global_device_ids=true | all-gather | bytes 557056 | tf_op jit(solution)/shard_map/all_gather | solution.py:390
  53.4 1.0 copy-done.8
  54.4 4.8 %shard_map.38 = (bf16[2,288,1024]{2,1,0:T(8,128)(2,1)}, bf16[2,288,1024]{2,1,0:T(8,128)(2,1)}, bf16[2,256,1024]{2,1,0:T(8,128)(2,1)}, bf16[2,128,1024]{2,1,0:T(8...) custom-call(s32[1]{0:T(128)} %bitcast.xl, bf16[256,2048]{1,0:T(8,128)(2,1)} %k_own.3, ...), custom_call_target="tpu_custom_call" | custom-call | bytes 18000000 | tf_op jit(solution)/shard_map/pallas_call | solution.py:108
  59.2 1.9 %collective-permute-start.3 = (bf16[2,288,1024]{2,1,0:T(8,128)(2,1)}, bf16[2,288,1024]{2,1,0:T(8,128)(2,1)S(1)}, u32[]{:S(2)}, u32[]{:S(2)}) collective-permute-start(bf16[2,288,1024]{2,1,0:T(8,128)(2,1)} %get-tuple-element.34), channel_id=1, source_target_pairs={{0,8},{8,16},{16,24},{24,32},{32,40},{40,48},{48,56},{56,64},{64,7... | collective-permute-start | bytes 3538952 | tf_op jit(solution)/shard_map/ppermute | solution.py:357
  61.1 6.0 %collective-permute-start.4 = (bf16[2,288,1024]{2,1,0:T(8,128)(2,1)}, bf16[2,288,1024]{2,1,0:T(8,128)(2,1)S(1)}, u32[]{:S(2)}, u32[]{:S(2)}) collective-permute-start(bf16[2,288,1024]{2,1,0:T(8,128)(2,1)} %get-tuple-element.35), channel_id=1, source_target_pairs={{8,0},{16,8},{24,16},{32,24},{40,32},{48,40},{56,48},{64,56},{72,6... | collective-permute-start | bytes 3538952 | tf_op jit(solution)/shard_map/ppermute | solution.py:357
  67.2 2.7 %collective-permute-start.9 = (bf16[2,128,1024]{2,1,0:T(8,128)(2,1)S(1)}, bf16[2,128,1024]{2,1,0:T(8,128)(2,1)S(1)}, u32[]{:S(2)}, u32[]{:S(2)}) collective-permute-start(bf16[2,128,1024]{2,1,0:T(8,128)(2,1)S(1)} %copy_bitcast_fusion.coarse0), channel_id=1, source_target_pairs={{0,384},{8,392},{16,400},{24,408},{32,416},{40,424},{48,432},{56,4... | collective-permute-start | bytes 1572872 | tf_op jit(solution)/shard_map/ppermute | solution.py:367
  69.8 10.0 %collective-permute-done.9.coarse1 = bf16[2,128,1024]{2,1,0:T(8,128)(2,1)S(1)} collective-permute-done((bf16[2,128,1024]{2,1,0:T(8,128)(2,1)S(1)}, bf16[2,128,1024]{2,1,0:T(8,128)(2,1)S(1)}, u32[]{:S(2)}, u32[]{:S(2)}) %collective-permute-start.9) | collective-permute-done | bytes 524320 | tf_op jit(solution)/shard_map/ppermute | solution.py:367
  79.9 1.9 %collective-permute-start.10 = (bf16[2,128,1024]{2,1,0:T(8,128)(2,1)S(1)}, bf16[2,128,1024]{2,1,0:T(8,128)(2,1)S(1)}, u32[]{:S(2)}, u32[]{:S(2)}) collective-permute-start(bf16[2,128,1024]{2,1,0:T(8,128)(2,1)S(1)} %collective-permute-done.9.coarse1), channel_id=1, source_target_pairs={{0,384},{8,392},{16,400},{24,408},{32,416},{40,424},{48,432},{56,4... | collective-permute-start | bytes 1572872 | tf_op jit(solution)/shard_map/ppermute | solution.py:367
  81.8 1.9 %collective-permute-start.5 = (bf16[2,32,1024]{2,1,0:T(8,128)(2,1)}, bf16[2,32,1024]{2,1,0:T(8,128)(2,1)S(1)}, u32[]{:S(2)}, u32[]{:S(2)}) collective-permute-start(bf16[2,32,1024]{2,1,0:T(8,128)(2,1)} %get-tuple-element.36), channel_id=1, source_target_pairs={{0,24},{8,32},{16,40},{24,48},{32,56},{40,64},{48,72},{56,80},{64,... | collective-permute-start | bytes 393224 | tf_op jit(solution)/shard_map/ppermute | solution.py:357
  83.7 7.8 %collective-permute-start.6 = (bf16[2,32,1024]{2,1,0:T(8,128)(2,1)}, bf16[2,32,1024]{2,1,0:T(8,128)(2,1)S(1)}, u32[]{:S(2)}, u32[]{:S(2)}) collective-permute-start(bf16[2,32,1024]{2,1,0:T(8,128)(2,1)} %get-tuple-element.37), channel_id=1, source_target_pairs={{24,0},{32,8},{40,16},{48,24},{56,32},{64,40},{72,48},{80,56},{88,... | collective-permute-start | bytes 393224 | tf_op jit(solution)/shard_map/ppermute | solution.py:357
  91.5 0.8 collective-permute-done.10.coarse2
  92.4 1.9 %collective-permute-start.11 = (bf16[2,128,1024]{2,1,0:T(8,128)(2,1)S(1)}, bf16[2,128,1024]{2,1,0:T(8,128)(2,1)S(1)}, u32[]{:S(2)}, u32[]{:S(2)}) collective-permute-start(bf16[2,128,1024]{2,1,0:T(8,128)(2,1)S(1)} %collective-permute-done.10.coarse2), channel_id=1, source_target_pairs={{0,384},{8,392},{16,400},{24,408},{32,416},{40,424},{48,432},{56,4... | collective-permute-start | bytes 1572872 | tf_op jit(solution)/shard_map/ppermute | solution.py:367
  94.3 2.6 %collective-permute-done.5.below3 = bf16[2,32,1024]{2,1,0:T(8,128)(2,1)S(1)} collective-permute-done((bf16[2,32,1024]{2,1,0:T(8,128)(2,1)}, bf16[2,32,1024]{2,1,0:T(8,128)(2,1)S(1)}, u32[]{:S(2)}, u32[]{:S(2)}) %collective-permute-start.5) | collective-permute-done | bytes 131104 | tf_op jit(solution)/shard_map/ppermute | solution.py:357
  96.9 0.5 collective-permute-done.6.above3
  97.3 0.6 copy-done.17
  98.0 1.0 shard_map.39
  99.4 0.8 copy-done.2
  100.2 3.3 %collective-permute-start.7 = (bf16[2,128,1024]{2,1,0:T(8,128)(2,1)S(1)}, bf16[2,128,1024]{2,1,0:T(8,128)(2,1)S(1)}, u32[]{:S(2)}, u32[]{:S(2)}) collective-permute-start(bf16[2,128,1024]{2,1,0:T(8,128)(2,1)S(1)} %get-tuple-element.40.up), channel_id=1, source_target_pairs={{0,8},{8,16},{16,24},{24,32},{32,40},{40,48},{48,56},{56,64},{64,7... | collective-permute-start | bytes 1572872 | tf_op jit(solution)/shard_map/ppermute | solution.py:357
  103.5 4.6 %collective-permute-start.8 = (bf16[2,128,1024]{2,1,0:T(8,128)(2,1)S(1)}, bf16[2,128,1024]{2,1,0:T(8,128)(2,1)S(1)}, u32[]{:S(2)}, u32[]{:S(2)}) collective-permute-start(bf16[2,128,1024]{2,1,0:T(8,128)(2,1)S(1)} %get-tuple-element.41.down), channel_id=1, source_target_pairs={{8,0},{16,8},{24,16},{32,24},{40,32},{48,40},{56,48},{64,56},{72,6... | collective-permute-start | bytes 1572872 | tf_op jit(solution)/shard_map/ppermute | solution.py:357
  108.2 12.4 %shard_map.40 = (f32[512,1024]{1,0:T(8,128)}, f32[512,1024]{1,0:T(8,128)}) custom-call(s32[1]{0:T(128)} %bitcast.xl, bf16[256,2048]{1,0:T(8,128)(2,1)} %q_own.3, bf16[256,1024]{1,0:T(8,128)(2,1)} %copy-done.9, bf16[256,2048]{1,0:T(8,128)(2,1)} %k_own.3, bf16[256,2048]{1,0:T(8,128)(2,1)} %v_own.3, bf16[2,256,1024]{2,1,0:T(8,128)(2,1)} %copy-done.8, ...), custom_call_target="tpu_custom_call" | custom-call | bytes 43200000 | tf_op jit(solution)/shard_map/pallas_call | solution.py:307
  120.7 0.7 copy-done.13
  121.8 15.4 %shard_map.41 = (bf16[256,2048]{1,0:T(8,128)(2,1)}, bf16[256,1024]{1,0:T(8,128)(2,1)}) custom-call(s32[1]{0:T(128)} %bitcast.xl, bf16[256,2048]{1,0:T(8,128)(2,1)} %q_own.3, bf16[256,1024]{1,0:T(8,128)(2,1)} %copy-done.9, bf16[2,128,1024]{2,1,0:T(8,128)(2,1)} %get-tuple-element.33.far, bf16[2,128,1024]{2,1,0:T(8,128)(2,1)} %copy-done.3, ...), custom_call_target="tpu_custom_call" | custom-call | bytes 54000000 | tf_op jit(solution)/shard_map/pallas_call | solution.py:307
  137.2 3.3 %collective-permute-start.12 = (bf16[256,1024]{1,0:T(8,128)(2,1)}, bf16[256,1024]{1,0:T(8,128)(2,1)S(1)}, u32[]{:S(2)}, u32[]{:S(2)}) collective-permute-start(bf16[256,1024]{1,0:T(8,128)(2,1)} %get-tuple-element.50), channel_id=1, source_target_pairs={{0,4},{4,0},{1,5},{5,1},{2,6},{6,2},{3,7},{7,3},{8,12},{12,8},{9,1... | collective-permute-start | bytes 1572872 | tf_op jit(solution)/shard_map/ppermute | solution.py:352
  140.5 8.0 %collective-permute-done.12 = bf16[256,1024]{1,0:T(8,128)(2,1)S(1)} collective-permute-done((bf16[256,1024]{1,0:T(8,128)(2,1)}, bf16[256,1024]{1,0:T(8,128)(2,1)S(1)}, u32[]{:S(2)}, u32[]{:S(2)}) %collective-permute-start.12) | collective-permute-done | bytes 524320 | tf_op jit(solution)/shard_map/ppermute | solution.py:352
  148.5 0.8 constant_dynamic-update-slice_fusion
  (45 shorter events, 1.1 us)
Async XLA Ops:
  0.0 6.4 %copy-start.5 = (bf16[256,2048]{1,0:T(8,128)(2,1)S(1)}, bf16[256,2048]{1,0:T(8,128)(2,1)}, u32[]{:S(2)}) copy-start(bf16[256,2048]{1,0:T(8,128)(2,1)} %k_own.3) | copy-start | bytes 3145732
  0.0 6.4 %copy-start.6 = (bf16[256,2048]{1,0:T(8,128)(2,1)S(1)}, bf16[256,2048]{1,0:T(8,128)(2,1)}, u32[]{:S(2)}) copy-start(bf16[256,2048]{1,0:T(8,128)(2,1)} %v_own.3) | copy-start | bytes 3145732
  3.0 6.0 %collective-permute-start = (bf16[16,1024]{1,0:T(8,128)(2,1)}, bf16[16,1024]{1,0:T(8,128)(2,1)S(1)}, u32[]{:S(2)}, u32[]{:S(2)}) collective-permute-start(bf16[16,1024]{1,0:T(8,128)(2,1)} %shard_map.37), channel_id=1, source_target_pairs={{0,4},{4,0},{1,5},{5,1},{2,6},{6,2},{3,7},{7,3},{8,12},{12,8},{9,1... | collective-permute-start | bytes 98312 | tf_op jit(solution)/shard_map/ppermute | solution.py:352
  6.5 1.6 %copy-start.7 = (bf16[256,2048]{1,0:T(8,128)(2,1)S(1)}, bf16[256,2048]{1,0:T(8,128)(2,1)}, u32[]{:S(2)}) copy-start(bf16[256,2048]{1,0:T(8,128)(2,1)} %q_own.3) | copy-start | bytes 3145732
  6.5 8.3 %copy-start.18 = (bf16[16,1024]{1,0:T(8,128)(2,1)S(1)}, bf16[16,1024]{1,0:T(8,128)(2,1)}, u32[]{:S(2)}) copy-start(bf16[16,1024]{1,0:T(8,128)(2,1)} %shard_map.37) | copy-start | bytes 98308
  9.0 44.4 %collective-permute-start.1 = (bf16[2,256,1024]{2,1,0:T(8,128)(2,1)}, bf16[2,256,1024]{2,1,0:T(8,128)(2,1)S(1)}, u32[]{:S(2)}, u32[]{:S(2)}) collective-permute-start(bf16[2,256,1024]{2,1,0:T(8,128)(2,1)} %pad_maximum_fusion), channel_id=1, source_target_pairs={{0,4},{4,0},{1,5},{5,1},{2,6},{6,2},{3,7},{7,3},{8,12},{12,8},{9,1... | collective-permute-start | bytes 3145736 | tf_op jit(solution)/shard_map/ppermute | solution.py:352
  12.4 41.0 %collective-permute-start.2 = (bf16[256,1024]{1,0:T(8,128)(2,1)S(1)}, bf16[256,1024]{1,0:T(8,128)(2,1)S(1)}, u32[]{:S(2)}, u32[]{:S(2)}) collective-permute-start(bf16[256,1024]{1,0:T(8,128)(2,1)S(1)} %constant_dynamic-slice_fusion), channel_id=1, source_target_pairs={{0,4},{4,0},{1,5},{5,1},{2,6},{6,2},{3,7},{7,3},{8,12},{12,8},{9,1... | collective-permute-start | bytes 1572872 | tf_op jit(solution)/shard_map/ppermute | solution.py:352
  53.4 67.2 %copy-start.10 = (bf16[2,128,1024]{2,1,0:T(8,128)(2,1)}, bf16[2,128,1024]{2,1,0:T(8,128)(2,1)S(1)}, u32[]{:S(2)}) copy-start(bf16[2,128,1024]{2,1,0:T(8,128)(2,1)S(1)} %copy_bitcast_fusion.coarse0) | copy-start | bytes 1572868
  53.4 54.7 %copy-start.9 = (bf16[256,1024]{1,0:T(8,128)(2,1)}, bf16[256,1024]{1,0:T(8,128)(2,1)S(1)}, u32[]{:S(2)}) copy-start(bf16[256,1024]{1,0:T(8,128)(2,1)S(1)} %collective-permute-done.2.q_got) | copy-start | bytes 1572868
  53.4 1.0 copy-start.8
  59.2 38.1 %collective-permute-start.3 = (bf16[2,288,1024]{2,1,0:T(8,128)(2,1)}, bf16[2,288,1024]{2,1,0:T(8,128)(2,1)S(1)}, u32[]{:S(2)}, u32[]{:S(2)}) collective-permute-start(bf16[2,288,1024]{2,1,0:T(8,128)(2,1)} %get-tuple-element.34), channel_id=1, source_target_pairs={{0,8},{8,16},{16,24},{24,32},{32,40},{40,48},{48,56},{56,64},{64,7... | collective-permute-start | bytes 3538952 | tf_op jit(solution)/shard_map/ppermute | solution.py:357
  61.1 36.9 %collective-permute-start.4 = (bf16[2,288,1024]{2,1,0:T(8,128)(2,1)}, bf16[2,288,1024]{2,1,0:T(8,128)(2,1)S(1)}, u32[]{:S(2)}, u32[]{:S(2)}) collective-permute-start(bf16[2,288,1024]{2,1,0:T(8,128)(2,1)} %get-tuple-element.35), channel_id=1, source_target_pairs={{8,0},{16,8},{24,16},{32,24},{40,32},{48,40},{56,48},{64,56},{72,6... | collective-permute-start | bytes 3538952 | tf_op jit(solution)/shard_map/ppermute | solution.py:357
  67.2 12.7 %collective-permute-start.9 = (bf16[2,128,1024]{2,1,0:T(8,128)(2,1)S(1)}, bf16[2,128,1024]{2,1,0:T(8,128)(2,1)S(1)}, u32[]{:S(2)}, u32[]{:S(2)}) collective-permute-start(bf16[2,128,1024]{2,1,0:T(8,128)(2,1)S(1)} %copy_bitcast_fusion.coarse0), channel_id=1, source_target_pairs={{0,384},{8,392},{16,400},{24,408},{32,416},{40,424},{48,432},{56,4... | collective-permute-start | bytes 1572872 | tf_op jit(solution)/shard_map/ppermute | solution.py:367
  79.9 40.7 %copy-start.11 = (bf16[2,128,1024]{2,1,0:T(8,128)(2,1)}, bf16[2,128,1024]{2,1,0:T(8,128)(2,1)S(1)}, u32[]{:S(2)}) copy-start(bf16[2,128,1024]{2,1,0:T(8,128)(2,1)S(1)} %collective-permute-done.9.coarse1) | copy-start | bytes 1572868
  79.9 12.5 %collective-permute-start.10 = (bf16[2,128,1024]{2,1,0:T(8,128)(2,1)S(1)}, bf16[2,128,1024]{2,1,0:T(8,128)(2,1)S(1)}, u32[]{:S(2)}, u32[]{:S(2)}) collective-permute-start(bf16[2,128,1024]{2,1,0:T(8,128)(2,1)S(1)} %collective-permute-done.9.coarse1), channel_id=1, source_target_pairs={{0,384},{8,392},{16,400},{24,408},{32,416},{40,424},{48,432},{56,4... | collective-permute-start | bytes 1572872 | tf_op jit(solution)/shard_map/ppermute | solution.py:367
  81.8 15.1 %collective-permute-start.5 = (bf16[2,32,1024]{2,1,0:T(8,128)(2,1)}, bf16[2,32,1024]{2,1,0:T(8,128)(2,1)S(1)}, u32[]{:S(2)}, u32[]{:S(2)}) collective-permute-start(bf16[2,32,1024]{2,1,0:T(8,128)(2,1)} %get-tuple-element.36), channel_id=1, source_target_pairs={{0,24},{8,32},{16,40},{24,48},{32,56},{40,64},{48,72},{56,80},{64,... | collective-permute-start | bytes 393224 | tf_op jit(solution)/shard_map/ppermute | solution.py:357
  83.7 13.6 %collective-permute-start.6 = (bf16[2,32,1024]{2,1,0:T(8,128)(2,1)}, bf16[2,32,1024]{2,1,0:T(8,128)(2,1)S(1)}, u32[]{:S(2)}, u32[]{:S(2)}) collective-permute-start(bf16[2,32,1024]{2,1,0:T(8,128)(2,1)} %get-tuple-element.37), channel_id=1, source_target_pairs={{24,0},{32,8},{40,16},{48,24},{56,32},{64,40},{72,48},{80,56},{88,... | collective-permute-start | bytes 393224 | tf_op jit(solution)/shard_map/ppermute | solution.py:357
  92.4 28.2 %copy-start.12 = (bf16[2,128,1024]{2,1,0:T(8,128)(2,1)}, bf16[2,128,1024]{2,1,0:T(8,128)(2,1)S(1)}, u32[]{:S(2)}) copy-start(bf16[2,128,1024]{2,1,0:T(8,128)(2,1)S(1)} %collective-permute-done.10.coarse2) | copy-start | bytes 1572868
  92.4 28.2 %collective-permute-start.11 = (bf16[2,128,1024]{2,1,0:T(8,128)(2,1)S(1)}, bf16[2,128,1024]{2,1,0:T(8,128)(2,1)S(1)}, u32[]{:S(2)}, u32[]{:S(2)}) collective-permute-start(bf16[2,128,1024]{2,1,0:T(8,128)(2,1)S(1)} %collective-permute-done.10.coarse2), channel_id=1, source_target_pairs={{0,384},{8,392},{16,400},{24,408},{32,416},{40,424},{48,432},{56,4... | collective-permute-start | bytes 1572872 | tf_op jit(solution)/shard_map/ppermute | solution.py:367
  96.9 23.7 %copy-start.16 = (bf16[2,32,1024]{2,1,0:T(8,128)(2,1)}, bf16[2,32,1024]{2,1,0:T(8,128)(2,1)S(1)}, u32[]{:S(2)}) copy-start(bf16[2,32,1024]{2,1,0:T(8,128)(2,1)S(1)} %collective-permute-done.5.below3) | copy-start | bytes 393220
  97.3 0.6 copy-start.17
  98.0 1.1 copy-start
  98.0 1.4 copy-start.1
  99.4 0.8 copy-start.2
  100.2 20.4 %copy-start.3 = (bf16[2,128,1024]{2,1,0:T(8,128)(2,1)}, bf16[2,128,1024]{2,1,0:T(8,128)(2,1)S(1)}, u32[]{:S(2)}) copy-start(bf16[2,128,1024]{2,1,0:T(8,128)(2,1)S(1)} %get-tuple-element.40.up) | copy-start | bytes 1572868
  100.2 20.4 %copy-start.4 = (bf16[2,128,1024]{2,1,0:T(8,128)(2,1)}, bf16[2,128,1024]{2,1,0:T(8,128)(2,1)S(1)}, u32[]{:S(2)}) copy-start(bf16[2,128,1024]{2,1,0:T(8,128)(2,1)S(1)} %get-tuple-element.41.down) | copy-start | bytes 1572868
  100.2 20.4 %collective-permute-start.7 = (bf16[2,128,1024]{2,1,0:T(8,128)(2,1)S(1)}, bf16[2,128,1024]{2,1,0:T(8,128)(2,1)S(1)}, u32[]{:S(2)}, u32[]{:S(2)}) collective-permute-start(bf16[2,128,1024]{2,1,0:T(8,128)(2,1)S(1)} %get-tuple-element.40.up), channel_id=1, source_target_pairs={{0,8},{8,16},{16,24},{24,32},{32,40},{40,48},{48,56},{56,64},{64,7... | collective-permute-start | bytes 1572872 | tf_op jit(solution)/shard_map/ppermute | solution.py:357
  103.5 17.1 %collective-permute-start.8 = (bf16[2,128,1024]{2,1,0:T(8,128)(2,1)S(1)}, bf16[2,128,1024]{2,1,0:T(8,128)(2,1)S(1)}, u32[]{:S(2)}, u32[]{:S(2)}) collective-permute-start(bf16[2,128,1024]{2,1,0:T(8,128)(2,1)S(1)} %get-tuple-element.41.down), channel_id=1, source_target_pairs={{8,0},{16,8},{24,16},{32,24},{40,32},{48,40},{56,48},{64,56},{72,6... | collective-permute-start | bytes 1572872 | tf_op jit(solution)/shard_map/ppermute | solution.py:357
  120.6 0.8 copy-start.13
  120.6 0.9 copy-start.14
  120.7 1.1 copy-start.15
  137.2 11.3 %collective-permute-start.12 = (bf16[256,1024]{1,0:T(8,128)(2,1)}, bf16[256,1024]{1,0:T(8,128)(2,1)S(1)}, u32[]{:S(2)}, u32[]{:S(2)}) collective-permute-start(bf16[256,1024]{1,0:T(8,128)(2,1)} %get-tuple-element.50), channel_id=1, source_target_pairs={{0,4},{4,0},{1,5},{5,1},{2,6},{6,2},{3,7},{7,3},{8,12},{12,8},{9,1... | collective-permute-start | bytes 1572872 | tf_op jit(solution)/shard_map/ppermute | solution.py:352

commit v9 on v8

--- a/solution.py
+++ b/solution.py
@@ -18,8 +18,7 @@
 BF = jnp.bfloat16
 F32 = jnp.float32
 SCALE = math.log2(math.e) / math.sqrt(D)
-VMEM = pltpu.CompilerParams(vmem_limit_bytes=58 * 2**20)
-LITTLE_VMEM = pltpu.CompilerParams(vmem_limit_bytes=24 * 2**20)
+VMEM = pltpu.CompilerParams(vmem_limit_bytes=16 * 2**20)
 
 
 def taking(microseconds):
@@ -141,7 +140,7 @@
         out_specs=[pl.BlockSpec((1, 128, width), lambda i, c: (i, 0, c))] * 3,
         out_shape=[jax.ShapeDtypeStruct((2, 128, cols), BF)] * 3,
         scratch_shapes=[pltpu.VMEM((width // D, 192, D), F32)],
-        compiler_params=LITTLE_VMEM, cost_estimate=taking(4),
+        compiler_params=VMEM, cost_estimate=taking(4),
     )(below, above)
 
 

time: 150 us -> 150 us (level)
  waiting for transfers between devices: 22.7 us -> 26.7 us
  Pallas kernels: 36.5 us -> 34.5 us
    ppermute x4, waiting for transfers between devices: 8.83 us -> 11.2 us  [moved(): return lax.ppermute(a, axis, [(i, (i + step) % n) for i in range(n)])]
    ppermute x3, waiting for transfers between devices: 10.9 us -> 13.1 us  [round_y(): return lax.ppermute(a, YZ, route)]
    pallas_call x1, Pallas kernels: 2.97 us -> 1.23 us  [coarse_rows(): pl.pallas_call(coarse_kernel, grid_spec=pltpu.PrefetchScalarGridSpec(num_...]
    unnamed x38 -> x10, local copies, waits for them, and re-layouts: 4.55 us -> 2.99 us
  transfers between devices with their start and end apart: 13 -> 13, of which waited for: 6 -> 4; matrix products, arithmetic and copies ran while one was open for 1% -> 1% of each run, Pallas kernels for 9% -> 9%
where the time goes in v9:
time: 150 us; the launch traced here: 149 us
  starting transfers between devices  43.3 us (29%)
  blocking collectives  38.6 us (26%)
  Pallas kernels  34.5 us (23%)
  waiting for transfers between devices  26.7 us (18%)
  local copies, waits for them, and re-layouts  4.79 us (3%)
    all_gather x1, blocking collectives, per_device(): units = lax.all_gather(unit, 'z')  38.6 us
    pallas_call x2, Pallas kernels, attend_call(): pl.pallas_call(kernel, grid_spec=pltpu.PrefetchScalarGridSpec(num_scalar_...  28.8 us
    ppermute x6, starting transfers between devices, shifted(): lax.ppermute(a, YZ, [(i, i + step) for i in range(n) if 0 <= i + step < n])  25.7 us
    ppermute x3, waiting for transfers between devices, round_y(): return lax.ppermute(a, YZ, route)  13.1 us
    ppermute x4, waiting for transfers between devices, moved(): return lax.ppermute(a, axis, [(i, (i + step) % n) for i in range(n)])  11.2 us
    ppermute x4, starting transfers between devices, moved(): return lax.ppermute(a, axis, [(i, (i + step) % n) for i in range(n)])  11.1 us
    ppermute x3, starting transfers between devices, round_y(): return lax.ppermute(a, YZ, route)  6.47 us
    pallas_call x1, Pallas kernels, pooled(): pl.pallas_call(pool_kernel, grid_spec=pltpu.PrefetchScalarGridSpec(num_sc...  3.42 us
  transfers between devices with their start and end apart: 13, of which 4 were waited for; matrix products, arithmetic and copies ran while one was open for 1% of the time, Pallas kernels for 9%

profile of v9, /device:TPU:24, one launch (start us, length us, event | category | flops | bytes accessed | tf_op | source)
XLA Modules:
  0.0 149.3 jit_solution(17187267385805137030)
XLA Ops:
  0.0 1.2 copy-done
  1.2 1.2 copy-done.2
  2.5 1.2 shard_map.37
  3.7 3.4 %collective-permute-start = (bf16[16,1024]{1,0:T(8,128)(2,1)S(1)}, bf16[16,1024]{1,0:T(8,128)(2,1)S(1)}, u32[]{:S(2)}, u32[]{:S(2)}) collective-permute-start(bf16[16,1024]{1,0:T(8,128)(2,1)S(1)} %shard_map.37), channel_id=1, source_target_pairs={{0,4},{4,0},{1,5},{5,1},{2,6},{6,2},{3,7},{7,3},{8,12},{12,8},{9,1... | collective-permute-start | bytes 98312 | tf_op jit(solution)/shard_map/ppermute | solution.py:351
  7.1 0.1 dynamic-slice_bitcast_fusion
  7.2 0.0 copy-start.4
  7.2 1.1 pad_maximum_fusion
  8.3 0.5 copy-done.4
  8.8 0.8 constant_dynamic-slice_fusion
  9.7 0.0 collective-permute-done
  9.7 3.2 %collective-permute-start.1 = (bf16[2,256,1024]{2,1,0:T(8,128)(2,1)}, bf16[2,256,1024]{2,1,0:T(8,128)(2,1)}, u32[]{:S(2)}, u32[]{:S(2)}) collective-permute-start(bf16[2,256,1024]{2,1,0:T(8,128)(2,1)} %pad_maximum_fusion), channel_id=1, source_target_pairs={{0,4},{4,0},{1,5},{5,1},{2,6},{6,2},{3,7},{7,3},{8,12},{12,8},{9,1... | collective-permute-start | bytes 3145736 | tf_op jit(solution)/shard_map/ppermute | solution.py:351
  12.9 2.6 %collective-permute-start.2 = (bf16[256,1024]{1,0:T(8,128)(2,1)}, bf16[256,1024]{1,0:T(8,128)(2,1)S(1)}, u32[]{:S(2)}, u32[]{:S(2)}) collective-permute-start(bf16[256,1024]{1,0:T(8,128)(2,1)} %constant_dynamic-slice_fusion), channel_id=1, source_target_pairs={{0,4},{4,0},{1,5},{5,1},{2,6},{6,2},{3,7},{7,3},{8,12},{12,8},{9,1... | collective-permute-start | bytes 1572872 | tf_op jit(solution)/shard_map/ppermute | solution.py:351
  15.6 38.6 %all_gather.3 = bf16[16,16,1024]{2,1,0:T(8,128)(2,1)S(1)} all-gather(bf16[1,16,1024]{2,1,0:T(8,128)(2,1)S(1)} %maximum_bitcast_fusion), channel_id=1, replica_groups=mesh['y'=4,'z'=16,'xl'=2,'head'=4] {'z'}, dimensions={0}, use_global_device_ids=true | all-gather | bytes 557056 | tf_op jit(solution)/shard_map/all_gather | solution.py:389
  54.3 3.4 %shard_map.38 = (bf16[2,288,1024]{2,1,0:T(8,128)(2,1)S(1)}, bf16[2,288,1024]{2,1,0:T(8,128)(2,1)S(1)}, bf16[2,256,1024]{2,1,0:T(8,128)(2,1)S(1)}, bf16[2,128,102...) custom-call(s32[1]{0:T(128)} %bitcast.xl, ...), custom_call_target="tpu_custom_call" | custom-call | bytes 18000000 | tf_op jit(solution)/shard_map/pallas_call | solution.py:107
  57.7 1.9 %collective-permute-start.3 = (bf16[2,288,1024]{2,1,0:T(8,128)(2,1)S(1)}, bf16[2,288,1024]{2,1,0:T(8,128)(2,1)S(1)}, u32[]{:S(2)}, u32[]{:S(2)}) collective-permute-start(bf16[2,288,1024]{2,1,0:T(8,128)(2,1)S(1)} %get-tuple-element.34), channel_id=1, source_target_pairs={{0,8},{8,16},{16,24},{24,32},{32,40},{40,48},{48,56},{56,64},{64,7... | collective-permute-start | bytes 3538952 | tf_op jit(solution)/shard_map/ppermute | solution.py:356
  59.6 6.0 %collective-permute-start.4 = (bf16[2,288,1024]{2,1,0:T(8,128)(2,1)S(1)}, bf16[2,288,1024]{2,1,0:T(8,128)(2,1)S(1)}, u32[]{:S(2)}, u32[]{:S(2)}) collective-permute-start(bf16[2,288,1024]{2,1,0:T(8,128)(2,1)S(1)} %get-tuple-element.35), channel_id=1, source_target_pairs={{8,0},{16,8},{24,16},{32,24},{40,32},{48,40},{56,48},{64,56},{72,6... | collective-permute-start | bytes 3538952 | tf_op jit(solution)/shard_map/ppermute | solution.py:356
  65.7 2.7 %collective-permute-start.9 = (bf16[2,128,1024]{2,1,0:T(8,128)(2,1)S(1)}, bf16[2,128,1024]{2,1,0:T(8,128)(2,1)S(1)}, u32[]{:S(2)}, u32[]{:S(2)}) collective-permute-start(bf16[2,128,1024]{2,1,0:T(8,128)(2,1)S(1)} %copy_bitcast_fusion.coarse0), channel_id=1, source_target_pairs={{0,384},{8,392},{16,400},{24,408},{32,416},{40,424},{48,432},{56,4... | collective-permute-start | bytes 1572872 | tf_op jit(solution)/shard_map/ppermute | solution.py:366
  68.3 11.5 %collective-permute-done.9.coarse1 = bf16[2,128,1024]{2,1,0:T(8,128)(2,1)S(1)} collective-permute-done((bf16[2,128,1024]{2,1,0:T(8,128)(2,1)S(1)}, bf16[2,128,1024]{2,1,0:T(8,128)(2,1)S(1)}, u32[]{:S(2)}, u32[]{:S(2)}) %collective-permute-start.9) | collective-permute-done | bytes 524320 | tf_op jit(solution)/shard_map/ppermute | solution.py:366
  79.9 1.9 %collective-permute-start.10 = (bf16[2,128,1024]{2,1,0:T(8,128)(2,1)S(1)}, bf16[2,128,1024]{2,1,0:T(8,128)(2,1)S(1)}, u32[]{:S(2)}, u32[]{:S(2)}) collective-permute-start(bf16[2,128,1024]{2,1,0:T(8,128)(2,1)S(1)} %collective-permute-done.9.coarse1), channel_id=1, source_target_pairs={{0,384},{8,392},{16,400},{24,408},{32,416},{40,424},{48,432},{56,4... | collective-permute-start | bytes 1572872 | tf_op jit(solution)/shard_map/ppermute | solution.py:366
  81.8 1.9 %collective-permute-start.5 = (bf16[2,32,1024]{2,1,0:T(8,128)(2,1)S(1)}, bf16[2,32,1024]{2,1,0:T(8,128)(2,1)S(1)}, u32[]{:S(2)}, u32[]{:S(2)}) collective-permute-start(bf16[2,32,1024]{2,1,0:T(8,128)(2,1)S(1)} %get-tuple-element.36), channel_id=1, source_target_pairs={{0,24},{8,32},{16,40},{24,48},{32,56},{40,64},{48,72},{56,80},{64,... | collective-permute-start | bytes 393224 | tf_op jit(solution)/shard_map/ppermute | solution.py:356
  83.7 7.8 %collective-permute-start.6 = (bf16[2,32,1024]{2,1,0:T(8,128)(2,1)S(1)}, bf16[2,32,1024]{2,1,0:T(8,128)(2,1)S(1)}, u32[]{:S(2)}, u32[]{:S(2)}) collective-permute-start(bf16[2,32,1024]{2,1,0:T(8,128)(2,1)S(1)} %get-tuple-element.37), channel_id=1, source_target_pairs={{24,0},{32,8},{40,16},{48,24},{56,32},{64,40},{72,48},{80,56},{88,... | collective-permute-start | bytes 393224 | tf_op jit(solution)/shard_map/ppermute | solution.py:356
  91.5 1.6 %collective-permute-done.10.coarse2 = bf16[2,128,1024]{2,1,0:T(8,128)(2,1)S(1)} collective-permute-done((bf16[2,128,1024]{2,1,0:T(8,128)(2,1)S(1)}, bf16[2,128,1024]{2,1,0:T(8,128)(2,1)S(1)}, u32[]{:S(2)}, u32[]{:S(2)}) %collective-permute-start.10) | collective-permute-done | bytes 524320 | tf_op jit(solution)/shard_map/ppermute | solution.py:366
  93.1 1.9 %collective-permute-start.11 = (bf16[2,128,1024]{2,1,0:T(8,128)(2,1)S(1)}, bf16[2,128,1024]{2,1,0:T(8,128)(2,1)S(1)}, u32[]{:S(2)}, u32[]{:S(2)}) collective-permute-start(bf16[2,128,1024]{2,1,0:T(8,128)(2,1)S(1)} %collective-permute-done.10.coarse2), channel_id=1, source_target_pairs={{0,384},{8,392},{16,400},{24,408},{32,416},{40,424},{48,432},{56,4... | collective-permute-start | bytes 1572872 | tf_op jit(solution)/shard_map/ppermute | solution.py:366
  95.0 2.4 %collective-permute-done.5.below3 = bf16[2,32,1024]{2,1,0:T(8,128)(2,1)S(1)} collective-permute-done((bf16[2,32,1024]{2,1,0:T(8,128)(2,1)S(1)}, bf16[2,32,1024]{2,1,0:T(8,128)(2,1)S(1)}, u32[]{:S(2)}, u32[]{:S(2)}) %collective-permute-start.5) | collective-permute-done | bytes 131104 | tf_op jit(solution)/shard_map/ppermute | solution.py:356
  97.4 1.0 shard_map.39
  98.5 2.6 %collective-permute-start.7 = (bf16[2,128,1024]{2,1,0:T(8,128)(2,1)S(1)}, bf16[2,128,1024]{2,1,0:T(8,128)(2,1)S(1)}, u32[]{:S(2)}, u32[]{:S(2)}) collective-permute-start(bf16[2,128,1024]{2,1,0:T(8,128)(2,1)S(1)} %get-tuple-element.40.up), channel_id=1, source_target_pairs={{0,8},{8,16},{16,24},{24,32},{32,40},{40,48},{48,56},{56,64},{64,7... | collective-permute-start | bytes 1572872 | tf_op jit(solution)/shard_map/ppermute | solution.py:356
  101.1 5.4 %collective-permute-start.8 = (bf16[2,128,1024]{2,1,0:T(8,128)(2,1)S(1)}, bf16[2,128,1024]{2,1,0:T(8,128)(2,1)S(1)}, u32[]{:S(2)}, u32[]{:S(2)}) collective-permute-start(bf16[2,128,1024]{2,1,0:T(8,128)(2,1)S(1)} %get-tuple-element.41.down), channel_id=1, source_target_pairs={{8,0},{16,8},{24,16},{32,24},{40,32},{48,40},{56,48},{64,56},{72,6... | collective-permute-start | bytes 1572872 | tf_op jit(solution)/shard_map/ppermute | solution.py:356
  106.5 12.3 %shard_map.40 = (f32[512,1024]{1,0:T(8,128)S(1)}, f32[512,1024]{1,0:T(8,128)S(1)}) custom-call(s32[1]{0:T(128)} %bitcast.xl, bf16[256,2048]{1,0:T(8,128)(2,1)S(1)} %copy-done.4, bf16[256,1024]{1,0:T(8,128)(2,1)S(1)} %collective-permute-done.2.q_got, bf16[256,2048]{1,0:T(8,128)(2,1)S(1)} %copy-done.1, bf16[256,2048]{1,0:T(8,128)(2,1)S(1)} %copy-done.3, ...), custom_call_target="tpu_custom_call" | custom-call | bytes 43200000 | tf_op jit(solution)/shard_map/pallas_call | solution.py:306
  118.8 16.5 %shard_map.41 = (bf16[256,2048]{1,0:T(8,128)(2,1)}, bf16[256,1024]{1,0:T(8,128)(2,1)S(1)}) custom-call(s32[1]{0:T(128)} %bitcast.xl, bf16[256,2048]{1,0:T(8,128)(2,1)S(1)} %copy-done.4, bf16[256,1024]{1,0:T(8,128)(2,1)S(1)} %collective-permute-done.2.q_got, bf16[2,128,1024]{2,1,0:T(8,128)(2,1)S(1)} %get-tuple-element.33.far, ...), custom_call_target="tpu_custom_call" | custom-call | bytes 54000000 | tf_op jit(solution)/shard_map/pallas_call | solution.py:306
  135.3 1.9 %collective-permute-start.12 = (bf16[256,1024]{1,0:T(8,128)(2,1)S(1)}, bf16[256,1024]{1,0:T(8,128)(2,1)S(1)}, u32[]{:S(2)}, u32[]{:S(2)}) collective-permute-start(bf16[256,1024]{1,0:T(8,128)(2,1)S(1)} %get-tuple-element.50), channel_id=1, source_target_pairs={{0,4},{4,0},{1,5},{5,1},{2,6},{6,2},{3,7},{7,3},{8,12},{12,8},{9,1... | collective-permute-start | bytes 1572872 | tf_op jit(solution)/shard_map/ppermute | solution.py:351
  137.2 11.2 %collective-permute-done.12 = bf16[256,1024]{1,0:T(8,128)(2,1)S(1)} collective-permute-done((bf16[256,1024]{1,0:T(8,128)(2,1)S(1)}, bf16[256,1024]{1,0:T(8,128)(2,1)S(1)}, u32[]{:S(2)}, u32[]{:S(2)}) %collective-permute-start.12) | collective-permute-done | bytes 524320 | tf_op jit(solution)/shard_map/ppermute | solution.py:351
  148.4 0.8 constant_dynamic-update-slice_fusion
  (17 shorter events, 0.1 us)
Async XLA Ops:
  0.0 1.2 copy-start
  1.2 1.2 copy-start.2
  2.5 4.7 %copy-start.1 = (bf16[256,2048]{1,0:T(8,128)(2,1)S(1)}, bf16[256,2048]{1,0:T(8,128)(2,1)}, u32[]{:S(2)}) copy-start(bf16[256,2048]{1,0:T(8,128)(2,1)} %k_own.3) | copy-start | bytes 3145732
  2.5 4.7 %copy-start.3 = (bf16[256,2048]{1,0:T(8,128)(2,1)S(1)}, bf16[256,2048]{1,0:T(8,128)(2,1)}, u32[]{:S(2)}) copy-start(bf16[256,2048]{1,0:T(8,128)(2,1)} %v_own.3) | copy-start | bytes 3145732
  3.7 6.0 %collective-permute-start = (bf16[16,1024]{1,0:T(8,128)(2,1)S(1)}, bf16[16,1024]{1,0:T(8,128)(2,1)S(1)}, u32[]{:S(2)}, u32[]{:S(2)}) collective-permute-start(bf16[16,1024]{1,0:T(8,128)(2,1)S(1)} %shard_map.37), channel_id=1, source_target_pairs={{0,4},{4,0},{1,5},{5,1},{2,6},{6,2},{3,7},{7,3},{8,12},{12,8},{9,1... | collective-permute-start | bytes 98312 | tf_op jit(solution)/shard_map/ppermute | solution.py:351
  7.2 1.6 %copy-start.4 = (bf16[256,2048]{1,0:T(8,128)(2,1)S(1)}, bf16[256,2048]{1,0:T(8,128)(2,1)}, u32[]{:S(2)}) copy-start(bf16[256,2048]{1,0:T(8,128)(2,1)} %q_own.3) | copy-start | bytes 3145732
  9.7 44.6 %collective-permute-start.1 = (bf16[2,256,1024]{2,1,0:T(8,128)(2,1)}, bf16[2,256,1024]{2,1,0:T(8,128)(2,1)}, u32[]{:S(2)}, u32[]{:S(2)}) collective-permute-start(bf16[2,256,1024]{2,1,0:T(8,128)(2,1)} %pad_maximum_fusion), channel_id=1, source_target_pairs={{0,4},{4,0},{1,5},{5,1},{2,6},{6,2},{3,7},{7,3},{8,12},{12,8},{9,1... | collective-permute-start | bytes 3145736 | tf_op jit(solution)/shard_map/ppermute | solution.py:351
  12.9 41.3 %collective-permute-start.2 = (bf16[256,1024]{1,0:T(8,128)(2,1)}, bf16[256,1024]{1,0:T(8,128)(2,1)S(1)}, u32[]{:S(2)}, u32[]{:S(2)}) collective-permute-start(bf16[256,1024]{1,0:T(8,128)(2,1)} %constant_dynamic-slice_fusion), channel_id=1, source_target_pairs={{0,4},{4,0},{1,5},{5,1},{2,6},{6,2},{3,7},{7,3},{8,12},{12,8},{9,1... | collective-permute-start | bytes 1572872 | tf_op jit(solution)/shard_map/ppermute | solution.py:351
  57.7 39.7 %collective-permute-start.3 = (bf16[2,288,1024]{2,1,0:T(8,128)(2,1)S(1)}, bf16[2,288,1024]{2,1,0:T(8,128)(2,1)S(1)}, u32[]{:S(2)}, u32[]{:S(2)}) collective-permute-start(bf16[2,288,1024]{2,1,0:T(8,128)(2,1)S(1)} %get-tuple-element.34), channel_id=1, source_target_pairs={{0,8},{8,16},{16,24},{24,32},{32,40},{40,48},{48,56},{56,64},{64,7... | collective-permute-start | bytes 3538952 | tf_op jit(solution)/shard_map/ppermute | solution.py:356
  59.6 37.8 %collective-permute-start.4 = (bf16[2,288,1024]{2,1,0:T(8,128)(2,1)S(1)}, bf16[2,288,1024]{2,1,0:T(8,128)(2,1)S(1)}, u32[]{:S(2)}, u32[]{:S(2)}) collective-permute-start(bf16[2,288,1024]{2,1,0:T(8,128)(2,1)S(1)} %get-tuple-element.35), channel_id=1, source_target_pairs={{8,0},{16,8},{24,16},{32,24},{40,32},{48,40},{56,48},{64,56},{72,6... | collective-permute-start | bytes 3538952 | tf_op jit(solution)/shard_map/ppermute | solution.py:356
  65.7 14.2 %collective-permute-start.9 = (bf16[2,128,1024]{2,1,0:T(8,128)(2,1)S(1)}, bf16[2,128,1024]{2,1,0:T(8,128)(2,1)S(1)}, u32[]{:S(2)}, u32[]{:S(2)}) collective-permute-start(bf16[2,128,1024]{2,1,0:T(8,128)(2,1)S(1)} %copy_bitcast_fusion.coarse0), channel_id=1, source_target_pairs={{0,384},{8,392},{16,400},{24,408},{32,416},{40,424},{48,432},{56,4... | collective-permute-start | bytes 1572872 | tf_op jit(solution)/shard_map/ppermute | solution.py:366
  79.9 13.3 %collective-permute-start.10 = (bf16[2,128,1024]{2,1,0:T(8,128)(2,1)S(1)}, bf16[2,128,1024]{2,1,0:T(8,128)(2,1)S(1)}, u32[]{:S(2)}, u32[]{:S(2)}) collective-permute-start(bf16[2,128,1024]{2,1,0:T(8,128)(2,1)S(1)} %collective-permute-done.9.coarse1), channel_id=1, source_target_pairs={{0,384},{8,392},{16,400},{24,408},{32,416},{40,424},{48,432},{56,4... | collective-permute-start | bytes 1572872 | tf_op jit(solution)/shard_map/ppermute | solution.py:366
  81.8 15.7 %collective-permute-start.5 = (bf16[2,32,1024]{2,1,0:T(8,128)(2,1)S(1)}, bf16[2,32,1024]{2,1,0:T(8,128)(2,1)S(1)}, u32[]{:S(2)}, u32[]{:S(2)}) collective-permute-start(bf16[2,32,1024]{2,1,0:T(8,128)(2,1)S(1)} %get-tuple-element.36), channel_id=1, source_target_pairs={{0,24},{8,32},{16,40},{24,48},{32,56},{40,64},{48,72},{56,80},{64,... | collective-permute-start | bytes 393224 | tf_op jit(solution)/shard_map/ppermute | solution.py:356
  83.7 13.7 %collective-permute-start.6 = (bf16[2,32,1024]{2,1,0:T(8,128)(2,1)S(1)}, bf16[2,32,1024]{2,1,0:T(8,128)(2,1)S(1)}, u32[]{:S(2)}, u32[]{:S(2)}) collective-permute-start(bf16[2,32,1024]{2,1,0:T(8,128)(2,1)S(1)} %get-tuple-element.37), channel_id=1, source_target_pairs={{24,0},{32,8},{40,16},{48,24},{56,32},{64,40},{72,48},{80,56},{88,... | collective-permute-start | bytes 393224 | tf_op jit(solution)/shard_map/ppermute | solution.py:356
  93.1 25.6 %collective-permute-start.11 = (bf16[2,128,1024]{2,1,0:T(8,128)(2,1)S(1)}, bf16[2,128,1024]{2,1,0:T(8,128)(2,1)S(1)}, u32[]{:S(2)}, u32[]{:S(2)}) collective-permute-start(bf16[2,128,1024]{2,1,0:T(8,128)(2,1)S(1)} %collective-permute-done.10.coarse2), channel_id=1, source_target_pairs={{0,384},{8,392},{16,400},{24,408},{32,416},{40,424},{48,432},{56,4... | collective-permute-start | bytes 1572872 | tf_op jit(solution)/shard_map/ppermute | solution.py:366
  98.5 20.3 %collective-permute-start.7 = (bf16[2,128,1024]{2,1,0:T(8,128)(2,1)S(1)}, bf16[2,128,1024]{2,1,0:T(8,128)(2,1)S(1)}, u32[]{:S(2)}, u32[]{:S(2)}) collective-permute-start(bf16[2,128,1024]{2,1,0:T(8,128)(2,1)S(1)} %get-tuple-element.40.up), channel_id=1, source_target_pairs={{0,8},{8,16},{16,24},{24,32},{32,40},{40,48},{48,56},{56,64},{64,7... | collective-permute-start | bytes 1572872 | tf_op jit(solution)/shard_map/ppermute | solution.py:356
  101.1 17.7 %collective-permute-start.8 = (bf16[2,128,1024]{2,1,0:T(8,128)(2,1)S(1)}, bf16[2,128,1024]{2,1,0:T(8,128)(2,1)S(1)}, u32[]{:S(2)}, u32[]{:S(2)}) collective-permute-start(bf16[2,128,1024]{2,1,0:T(8,128)(2,1)S(1)} %get-tuple-element.41.down), channel_id=1, source_target_pairs={{8,0},{16,8},{24,16},{32,24},{40,32},{48,40},{56,48},{64,56},{72,6... | collective-permute-start | bytes 1572872 | tf_op jit(solution)/shard_map/ppermute | solution.py:356
  135.3 13.1 %collective-permute-start.12 = (bf16[256,1024]{1,0:T(8,128)(2,1)S(1)}, bf16[256,1024]{1,0:T(8,128)(2,1)S(1)}, u32[]{:S(2)}, u32[]{:S(2)}) collective-permute-start(bf16[256,1024]{1,0:T(8,128)(2,1)S(1)} %get-tuple-element.50), channel_id=1, source_target_pairs={{0,4},{4,0},{1,5},{5,1},{2,6},{6,2},{3,7},{7,3},{8,12},{12,8},{9,1... | collective-permute-start | bytes 1572872 | tf_op jit(solution)/shard_map/ppermute | solution.py:351

commit v10 on v7

--- a/solution.py
+++ b/solution.py
@@ -18,7 +18,7 @@
 BF = jnp.bfloat16
 F32 = jnp.float32
 SCALE = math.log2(math.e) / math.sqrt(D)
-VMEM = pltpu.CompilerParams(vmem_limit_bytes=58 * 2**20)
+VMEM = pltpu.CompilerParams(vmem_limit_bytes=16 * 2**20)
 
 
 def taking(microseconds):
@@ -73,7 +73,7 @@
     )(xl, k, k, v, v)
 
 
-def pool_kernel(xl, k_ref, v_ref, got_ref, up_ref, down_ref, mid_ref, far_ref, scratch):
+def pool_kernel(xl, k_ref, v_ref, got_ref, up_ref, down_ref, mid_ref, far_ref, up3_ref, down3_ref, scratch):
     low = xl[0] == 0
     for i, ref in enumerate((k_ref, v_ref)):
         own, got = ref[...], got_ref[i]
@@ -87,6 +87,8 @@
         mid_ref[i, 128:256] = mid_second
         far_ref[i, 0:64] = far_first
         far_ref[i, 64:128] = far_second
+        up3_ref[i] = far_second[32:64]
+        down3_ref[i] = far_first[0:32]
         up_ref[i, 0:128] = second[128:256]
         up_ref[i, 128:192] = mid_first[64:128]
         up_ref[i, 192:256] = mid_second[0:64]
@@ -100,7 +102,7 @@
 def pooled(xl, k, v, got):
     _, rows, cols = got.shape
     width = 256
-    sizes = (288, 288, 256, 128)
+    sizes = (288, 288, 256, 128, 32, 32)
     own = pl.BlockSpec((rows, width), column(width))
     return pl.pallas_call(
         pool_kernel,
@@ -383,12 +385,12 @@
     units = lax.all_gather(unit, "z")
     units = jnp.moveaxis(units.reshape(-1, 2, 8, half), 1, 0).reshape(2, -1, half)
     kv_got, units, q_got = lax.optimization_barrier((kv_got, units, q_got))
-    up1, down1, mid, far = pooled(at, key_rows, value_rows, kv_got)
+    up1, down1, mid, far, up3, down3 = pooled(at, key_rows, value_rows, kv_got)
     below1, above1 = shifted(up1, 1), shifted(down1, -1)
     coarse = [units]
     for _ in range(lax.axis_size("y") - 1):
         coarse.append(round_y(coarse[-1]))
-    below3, above3 = shifted(far[:, 96:128], 3), shifted(far[:, 0:32], -3)
+    below3, above3 = shifted(up3, 3), shifted(down3, -3)
     below1, above1, below3, above3 = lax.optimization_barrier((below1, above1, below3, above3))
     up, down, near = forwarded(below1, above1)
     below2, above2 = shifted(up, 1), shifted(down, -1)

time: 156 us -> 150 us (0.962)
  Pallas kernels: 39.2 us -> 34.2 us
  local copies, waits for them, and re-layouts: 8.19 us -> 4.79 us
  waiting for transfers between devices: 24.9 us -> 26.7 us
    pallas_call x1, Pallas kernels: 4.06 us -> 1.03 us  [forwarded(): pl.pallas_call(forward_kernel, grid=(2, cols // width), in_specs=[pl.Bloc...]
    ppermute x3, waiting for transfers between devices: 10.6 us -> 13.1 us  [round_y(): return lax.ppermute(a, YZ, route)]
    unnamed x32 -> x10, local copies, waits for them, and re-layouts: 5.4 us -> 2.99 us
    pallas_call x1, Pallas kernels: 2.98 us -> 1.23 us  [coarse_rows(): pl.pallas_call(coarse_kernel, grid_spec=pltpu.PrefetchScalarGridSpec(num_...]
  transfers between devices with their start and end apart: 13 -> 13, of which waited for: 4 -> 4; matrix products, arithmetic and copies ran while one was open for 1% -> 1% of each run, Pallas kernels for 11% -> 9%
where the time goes in v10:
time: 150 us; the launch traced here: 149 us
  starting transfers between devices  43.3 us (29%)
  blocking collectives  38.6 us (26%)
  Pallas kernels  34.2 us (23%)
  waiting for transfers between devices  26.7 us (18%)
  local copies, waits for them, and re-layouts  4.79 us (3%)
    all_gather x1, blocking collectives, per_device(): units = lax.all_gather(unit, 'z')  38.6 us
    pallas_call x2, Pallas kernels, attend_call(): pl.pallas_call(kernel, grid_spec=pltpu.PrefetchScalarGridSpec(num_scalar_...  28.5 us
    ppermute x6, starting transfers between devices, shifted(): lax.ppermute(a, YZ, [(i, i + step) for i in range(n) if 0 <= i + step < n])  25.7 us
    ppermute x3, waiting for transfers between devices, round_y(): return lax.ppermute(a, YZ, route)  13.1 us
    ppermute x4, waiting for transfers between devices, moved(): return lax.ppermute(a, axis, [(i, (i + step) % n) for i in range(n)])  11.2 us
    ppermute x4, starting transfers between devices, moved(): return lax.ppermute(a, axis, [(i, (i + step) % n) for i in range(n)])  11.1 us
    ppermute x3, starting transfers between devices, round_y(): return lax.ppermute(a, YZ, route)  6.47 us
    pallas_call x1, Pallas kernels, pooled(): pl.pallas_call(pool_kernel, grid_spec=pltpu.PrefetchScalarGridSpec(num_sc...  3.42 us
  transfers between devices with their start and end apart: 13, of which 4 were waited for; matrix products, arithmetic and copies ran while one was open for 1% of the time, Pallas kernels for 9%

profile of v10, /device:TPU:24, one launch (start us, length us, event | category | flops | bytes accessed | tf_op | source)
XLA Modules:
  0.0 148.9 jit_solution(12183788598006044127)
XLA Ops:
  0.0 1.2 copy-done
  1.2 1.2 copy-done.2
  2.5 1.2 shard_map.37
  3.7 3.4 %collective-permute-start = (bf16[16,1024]{1,0:T(8,128)(2,1)S(1)}, bf16[16,1024]{1,0:T(8,128)(2,1)S(1)}, u32[]{:S(2)}, u32[]{:S(2)}) collective-permute-start(bf16[16,1024]{1,0:T(8,128)(2,1)S(1)} %shard_map.37), channel_id=1, source_target_pairs={{0,4},{4,0},{1,5},{5,1},{2,6},{6,2},{3,7},{7,3},{8,12},{12,8},{9,1... | collective-permute-start | bytes 98312 | tf_op jit(solution)/shard_map/ppermute | solution.py:347
  7.1 0.1 dynamic-slice_bitcast_fusion
  7.2 0.0 copy-start.4
  7.2 1.1 pad_maximum_fusion
  8.3 0.5 copy-done.4
  8.8 0.8 constant_dynamic-slice_fusion
  9.7 0.0 collective-permute-done
  9.7 3.2 %collective-permute-start.1 = (bf16[2,256,1024]{2,1,0:T(8,128)(2,1)}, bf16[2,256,1024]{2,1,0:T(8,128)(2,1)}, u32[]{:S(2)}, u32[]{:S(2)}) collective-permute-start(bf16[2,256,1024]{2,1,0:T(8,128)(2,1)} %pad_maximum_fusion), channel_id=1, source_target_pairs={{0,4},{4,0},{1,5},{5,1},{2,6},{6,2},{3,7},{7,3},{8,12},{12,8},{9,1... | collective-permute-start | bytes 3145736 | tf_op jit(solution)/shard_map/ppermute | solution.py:347
  12.9 2.6 %collective-permute-start.2 = (bf16[256,1024]{1,0:T(8,128)(2,1)}, bf16[256,1024]{1,0:T(8,128)(2,1)S(1)}, u32[]{:S(2)}, u32[]{:S(2)}) collective-permute-start(bf16[256,1024]{1,0:T(8,128)(2,1)} %constant_dynamic-slice_fusion), channel_id=1, source_target_pairs={{0,4},{4,0},{1,5},{5,1},{2,6},{6,2},{3,7},{7,3},{8,12},{12,8},{9,1... | collective-permute-start | bytes 1572872 | tf_op jit(solution)/shard_map/ppermute | solution.py:347
  15.6 38.6 %all_gather.3 = bf16[16,16,1024]{2,1,0:T(8,128)(2,1)S(1)} all-gather(bf16[1,16,1024]{2,1,0:T(8,128)(2,1)S(1)} %maximum_bitcast_fusion), channel_id=1, replica_groups=mesh['y'=4,'z'=16,'xl'=2,'head'=4] {'z'}, dimensions={0}, use_global_device_ids=true | all-gather | bytes 557056 | tf_op jit(solution)/shard_map/all_gather | solution.py:385
  54.3 3.4 %shard_map.38 = (bf16[2,288,1024]{2,1,0:T(8,128)(2,1)S(1)}, bf16[2,288,1024]{2,1,0:T(8,128)(2,1)S(1)}, bf16[2,256,1024]{2,1,0:T(8,128)(2,1)S(1)}, bf16[2,128,102...) custom-call(s32[1]{0:T(128)} %bitcast.xl, ...), custom_call_target="tpu_custom_call" | custom-call | bytes 18000000 | tf_op jit(solution)/shard_map/pallas_call | solution.py:107
  57.7 1.9 %collective-permute-start.3 = (bf16[2,288,1024]{2,1,0:T(8,128)(2,1)S(1)}, bf16[2,288,1024]{2,1,0:T(8,128)(2,1)S(1)}, u32[]{:S(2)}, u32[]{:S(2)}) collective-permute-start(bf16[2,288,1024]{2,1,0:T(8,128)(2,1)S(1)} %get-tuple-element.34), channel_id=1, source_target_pairs={{0,8},{8,16},{16,24},{24,32},{32,40},{40,48},{48,56},{56,64},{64,7... | collective-permute-start | bytes 3538952 | tf_op jit(solution)/shard_map/ppermute | solution.py:352
  59.6 6.0 %collective-permute-start.4 = (bf16[2,288,1024]{2,1,0:T(8,128)(2,1)S(1)}, bf16[2,288,1024]{2,1,0:T(8,128)(2,1)S(1)}, u32[]{:S(2)}, u32[]{:S(2)}) collective-permute-start(bf16[2,288,1024]{2,1,0:T(8,128)(2,1)S(1)} %get-tuple-element.35), channel_id=1, source_target_pairs={{8,0},{16,8},{24,16},{32,24},{40,32},{48,40},{56,48},{64,56},{72,6... | collective-permute-start | bytes 3538952 | tf_op jit(solution)/shard_map/ppermute | solution.py:352
  65.7 2.7 %collective-permute-start.9 = (bf16[2,128,1024]{2,1,0:T(8,128)(2,1)S(1)}, bf16[2,128,1024]{2,1,0:T(8,128)(2,1)S(1)}, u32[]{:S(2)}, u32[]{:S(2)}) collective-permute-start(bf16[2,128,1024]{2,1,0:T(8,128)(2,1)S(1)} %copy_bitcast_fusion.coarse0), channel_id=1, source_target_pairs={{0,384},{8,392},{16,400},{24,408},{32,416},{40,424},{48,432},{56,4... | collective-permute-start | bytes 1572872 | tf_op jit(solution)/shard_map/ppermute | solution.py:362
  68.3 11.5 %collective-permute-done.9.coarse1 = bf16[2,128,1024]{2,1,0:T(8,128)(2,1)S(1)} collective-permute-done((bf16[2,128,1024]{2,1,0:T(8,128)(2,1)S(1)}, bf16[2,128,1024]{2,1,0:T(8,128)(2,1)S(1)}, u32[]{:S(2)}, u32[]{:S(2)}) %collective-permute-start.9) | collective-permute-done | bytes 524320 | tf_op jit(solution)/shard_map/ppermute | solution.py:362
  79.9 1.9 %collective-permute-start.10 = (bf16[2,128,1024]{2,1,0:T(8,128)(2,1)S(1)}, bf16[2,128,1024]{2,1,0:T(8,128)(2,1)S(1)}, u32[]{:S(2)}, u32[]{:S(2)}) collective-permute-start(bf16[2,128,1024]{2,1,0:T(8,128)(2,1)S(1)} %collective-permute-done.9.coarse1), channel_id=1, source_target_pairs={{0,384},{8,392},{16,400},{24,408},{32,416},{40,424},{48,432},{56,4... | collective-permute-start | bytes 1572872 | tf_op jit(solution)/shard_map/ppermute | solution.py:362
  81.8 1.9 %collective-permute-start.5 = (bf16[2,32,1024]{2,1,0:T(8,128)(2,1)S(1)}, bf16[2,32,1024]{2,1,0:T(8,128)(2,1)S(1)}, u32[]{:S(2)}, u32[]{:S(2)}) collective-permute-start(bf16[2,32,1024]{2,1,0:T(8,128)(2,1)S(1)} %get-tuple-element.36), channel_id=1, source_target_pairs={{0,24},{8,32},{16,40},{24,48},{32,56},{40,64},{48,72},{56,80},{64,... | collective-permute-start | bytes 393224 | tf_op jit(solution)/shard_map/ppermute | solution.py:352
  83.7 7.8 %collective-permute-start.6 = (bf16[2,32,1024]{2,1,0:T(8,128)(2,1)S(1)}, bf16[2,32,1024]{2,1,0:T(8,128)(2,1)S(1)}, u32[]{:S(2)}, u32[]{:S(2)}) collective-permute-start(bf16[2,32,1024]{2,1,0:T(8,128)(2,1)S(1)} %get-tuple-element.37), channel_id=1, source_target_pairs={{24,0},{32,8},{40,16},{48,24},{56,32},{64,40},{72,48},{80,56},{88,... | collective-permute-start | bytes 393224 | tf_op jit(solution)/shard_map/ppermute | solution.py:352
  91.5 1.6 %collective-permute-done.10.coarse2 = bf16[2,128,1024]{2,1,0:T(8,128)(2,1)S(1)} collective-permute-done((bf16[2,128,1024]{2,1,0:T(8,128)(2,1)S(1)}, bf16[2,128,1024]{2,1,0:T(8,128)(2,1)S(1)}, u32[]{:S(2)}, u32[]{:S(2)}) %collective-permute-start.10) | collective-permute-done | bytes 524320 | tf_op jit(solution)/shard_map/ppermute | solution.py:362
  93.1 1.9 %collective-permute-start.11 = (bf16[2,128,1024]{2,1,0:T(8,128)(2,1)S(1)}, bf16[2,128,1024]{2,1,0:T(8,128)(2,1)S(1)}, u32[]{:S(2)}, u32[]{:S(2)}) collective-permute-start(bf16[2,128,1024]{2,1,0:T(8,128)(2,1)S(1)} %collective-permute-done.10.coarse2), channel_id=1, source_target_pairs={{0,384},{8,392},{16,400},{24,408},{32,416},{40,424},{48,432},{56,4... | collective-permute-start | bytes 1572872 | tf_op jit(solution)/shard_map/ppermute | solution.py:362
  95.0 2.4 %collective-permute-done.5.below3 = bf16[2,32,1024]{2,1,0:T(8,128)(2,1)S(1)} collective-permute-done((bf16[2,32,1024]{2,1,0:T(8,128)(2,1)S(1)}, bf16[2,32,1024]{2,1,0:T(8,128)(2,1)S(1)}, u32[]{:S(2)}, u32[]{:S(2)}) %collective-permute-start.5) | collective-permute-done | bytes 131104 | tf_op jit(solution)/shard_map/ppermute | solution.py:352
  97.4 1.0 shard_map.39
  98.5 2.6 %collective-permute-start.7 = (bf16[2,128,1024]{2,1,0:T(8,128)(2,1)S(1)}, bf16[2,128,1024]{2,1,0:T(8,128)(2,1)S(1)}, u32[]{:S(2)}, u32[]{:S(2)}) collective-permute-start(bf16[2,128,1024]{2,1,0:T(8,128)(2,1)S(1)} %get-tuple-element.40.up), channel_id=1, source_target_pairs={{0,8},{8,16},{16,24},{24,32},{32,40},{40,48},{48,56},{56,64},{64,7... | collective-permute-start | bytes 1572872 | tf_op jit(solution)/shard_map/ppermute | solution.py:352
  101.1 5.4 %collective-permute-start.8 = (bf16[2,128,1024]{2,1,0:T(8,128)(2,1)S(1)}, bf16[2,128,1024]{2,1,0:T(8,128)(2,1)S(1)}, u32[]{:S(2)}, u32[]{:S(2)}) collective-permute-start(bf16[2,128,1024]{2,1,0:T(8,128)(2,1)S(1)} %get-tuple-element.41.down), channel_id=1, source_target_pairs={{8,0},{16,8},{24,16},{32,24},{40,32},{48,40},{56,48},{64,56},{72,6... | collective-permute-start | bytes 1572872 | tf_op jit(solution)/shard_map/ppermute | solution.py:352
  106.5 12.3 %shard_map.40 = (f32[512,1024]{1,0:T(8,128)S(1)}, f32[512,1024]{1,0:T(8,128)S(1)}) custom-call(s32[1]{0:T(128)} %bitcast.xl, bf16[256,2048]{1,0:T(8,128)(2,1)S(1)} %copy-done.4, bf16[256,1024]{1,0:T(8,128)(2,1)S(1)} %collective-permute-done.2.q_got, bf16[256,2048]{1,0:T(8,128)(2,1)S(1)} %copy-done.1, bf16[256,2048]{1,0:T(8,128)(2,1)S(1)} %copy-done.3, ...), custom_call_target="tpu_custom_call" | custom-call | bytes 43200000 | tf_op jit(solution)/shard_map/pallas_call | solution.py:302
  118.8 16.2 %shard_map.41 = (bf16[256,2048]{1,0:T(8,128)(2,1)}, bf16[256,1024]{1,0:T(8,128)(2,1)S(1)}) custom-call(s32[1]{0:T(128)} %bitcast.xl, bf16[256,2048]{1,0:T(8,128)(2,1)S(1)} %copy-done.4, bf16[256,1024]{1,0:T(8,128)(2,1)S(1)} %collective-permute-done.2.q_got, bf16[2,128,1024]{2,1,0:T(8,128)(2,1)S(1)} %get-tuple-element.33.far, ...), custom_call_target="tpu_custom_call" | custom-call | bytes 54000000 | tf_op jit(solution)/shard_map/pallas_call | solution.py:302
  135.0 1.9 %collective-permute-start.12 = (bf16[256,1024]{1,0:T(8,128)(2,1)S(1)}, bf16[256,1024]{1,0:T(8,128)(2,1)S(1)}, u32[]{:S(2)}, u32[]{:S(2)}) collective-permute-start(bf16[256,1024]{1,0:T(8,128)(2,1)S(1)} %get-tuple-element.50), channel_id=1, source_target_pairs={{0,4},{4,0},{1,5},{5,1},{2,6},{6,2},{3,7},{7,3},{8,12},{12,8},{9,1... | collective-permute-start | bytes 1572872 | tf_op jit(solution)/shard_map/ppermute | solution.py:347
  136.9 11.2 %collective-permute-done.12 = bf16[256,1024]{1,0:T(8,128)(2,1)S(1)} collective-permute-done((bf16[256,1024]{1,0:T(8,128)(2,1)S(1)}, bf16[256,1024]{1,0:T(8,128)(2,1)S(1)}, u32[]{:S(2)}, u32[]{:S(2)}) %collective-permute-start.12) | collective-permute-done | bytes 524320 | tf_op jit(solution)/shard_map/ppermute | solution.py:347
  148.1 0.8 constant_dynamic-update-slice_fusion
  (17 shorter events, 0.1 us)
Async XLA Ops:
  0.0 1.2 copy-start
  1.2 1.2 copy-start.2
  2.5 4.7 %copy-start.1 = (bf16[256,2048]{1,0:T(8,128)(2,1)S(1)}, bf16[256,2048]{1,0:T(8,128)(2,1)}, u32[]{:S(2)}) copy-start(bf16[256,2048]{1,0:T(8,128)(2,1)} %k_own.3) | copy-start | bytes 3145732
  2.5 4.7 %copy-start.3 = (bf16[256,2048]{1,0:T(8,128)(2,1)S(1)}, bf16[256,2048]{1,0:T(8,128)(2,1)}, u32[]{:S(2)}) copy-start(bf16[256,2048]{1,0:T(8,128)(2,1)} %v_own.3) | copy-start | bytes 3145732
  3.7 6.0 %collective-permute-start = (bf16[16,1024]{1,0:T(8,128)(2,1)S(1)}, bf16[16,1024]{1,0:T(8,128)(2,1)S(1)}, u32[]{:S(2)}, u32[]{:S(2)}) collective-permute-start(bf16[16,1024]{1,0:T(8,128)(2,1)S(1)} %shard_map.37), channel_id=1, source_target_pairs={{0,4},{4,0},{1,5},{5,1},{2,6},{6,2},{3,7},{7,3},{8,12},{12,8},{9,1... | collective-permute-start | bytes 98312 | tf_op jit(solution)/shard_map/ppermute | solution.py:347
  7.2 1.6 %copy-start.4 = (bf16[256,2048]{1,0:T(8,128)(2,1)S(1)}, bf16[256,2048]{1,0:T(8,128)(2,1)}, u32[]{:S(2)}) copy-start(bf16[256,2048]{1,0:T(8,128)(2,1)} %q_own.3) | copy-start | bytes 3145732
  9.7 44.6 %collective-permute-start.1 = (bf16[2,256,1024]{2,1,0:T(8,128)(2,1)}, bf16[2,256,1024]{2,1,0:T(8,128)(2,1)}, u32[]{:S(2)}, u32[]{:S(2)}) collective-permute-start(bf16[2,256,1024]{2,1,0:T(8,128)(2,1)} %pad_maximum_fusion), channel_id=1, source_target_pairs={{0,4},{4,0},{1,5},{5,1},{2,6},{6,2},{3,7},{7,3},{8,12},{12,8},{9,1... | collective-permute-start | bytes 3145736 | tf_op jit(solution)/shard_map/ppermute | solution.py:347
  12.9 41.3 %collective-permute-start.2 = (bf16[256,1024]{1,0:T(8,128)(2,1)}, bf16[256,1024]{1,0:T(8,128)(2,1)S(1)}, u32[]{:S(2)}, u32[]{:S(2)}) collective-permute-start(bf16[256,1024]{1,0:T(8,128)(2,1)} %constant_dynamic-slice_fusion), channel_id=1, source_target_pairs={{0,4},{4,0},{1,5},{5,1},{2,6},{6,2},{3,7},{7,3},{8,12},{12,8},{9,1... | collective-permute-start | bytes 1572872 | tf_op jit(solution)/shard_map/ppermute | solution.py:347
  57.7 39.7 %collective-permute-start.3 = (bf16[2,288,1024]{2,1,0:T(8,128)(2,1)S(1)}, bf16[2,288,1024]{2,1,0:T(8,128)(2,1)S(1)}, u32[]{:S(2)}, u32[]{:S(2)}) collective-permute-start(bf16[2,288,1024]{2,1,0:T(8,128)(2,1)S(1)} %get-tuple-element.34), channel_id=1, source_target_pairs={{0,8},{8,16},{16,24},{24,32},{32,40},{40,48},{48,56},{56,64},{64,7... | collective-permute-start | bytes 3538952 | tf_op jit(solution)/shard_map/ppermute | solution.py:352
  59.6 37.8 %collective-permute-start.4 = (bf16[2,288,1024]{2,1,0:T(8,128)(2,1)S(1)}, bf16[2,288,1024]{2,1,0:T(8,128)(2,1)S(1)}, u32[]{:S(2)}, u32[]{:S(2)}) collective-permute-start(bf16[2,288,1024]{2,1,0:T(8,128)(2,1)S(1)} %get-tuple-element.35), channel_id=1, source_target_pairs={{8,0},{16,8},{24,16},{32,24},{40,32},{48,40},{56,48},{64,56},{72,6... | collective-permute-start | bytes 3538952 | tf_op jit(solution)/shard_map/ppermute | solution.py:352
  65.7 14.2 %collective-permute-start.9 = (bf16[2,128,1024]{2,1,0:T(8,128)(2,1)S(1)}, bf16[2,128,1024]{2,1,0:T(8,128)(2,1)S(1)}, u32[]{:S(2)}, u32[]{:S(2)}) collective-permute-start(bf16[2,128,1024]{2,1,0:T(8,128)(2,1)S(1)} %copy_bitcast_fusion.coarse0), channel_id=1, source_target_pairs={{0,384},{8,392},{16,400},{24,408},{32,416},{40,424},{48,432},{56,4... | collective-permute-start | bytes 1572872 | tf_op jit(solution)/shard_map/ppermute | solution.py:362
  79.9 13.3 %collective-permute-start.10 = (bf16[2,128,1024]{2,1,0:T(8,128)(2,1)S(1)}, bf16[2,128,1024]{2,1,0:T(8,128)(2,1)S(1)}, u32[]{:S(2)}, u32[]{:S(2)}) collective-permute-start(bf16[2,128,1024]{2,1,0:T(8,128)(2,1)S(1)} %collective-permute-done.9.coarse1), channel_id=1, source_target_pairs={{0,384},{8,392},{16,400},{24,408},{32,416},{40,424},{48,432},{56,4... | collective-permute-start | bytes 1572872 | tf_op jit(solution)/shard_map/ppermute | solution.py:362
  81.8 15.7 %collective-permute-start.5 = (bf16[2,32,1024]{2,1,0:T(8,128)(2,1)S(1)}, bf16[2,32,1024]{2,1,0:T(8,128)(2,1)S(1)}, u32[]{:S(2)}, u32[]{:S(2)}) collective-permute-start(bf16[2,32,1024]{2,1,0:T(8,128)(2,1)S(1)} %get-tuple-element.36), channel_id=1, source_target_pairs={{0,24},{8,32},{16,40},{24,48},{32,56},{40,64},{48,72},{56,80},{64,... | collective-permute-start | bytes 393224 | tf_op jit(solution)/shard_map/ppermute | solution.py:352
  83.7 13.7 %collective-permute-start.6 = (bf16[2,32,1024]{2,1,0:T(8,128)(2,1)S(1)}, bf16[2,32,1024]{2,1,0:T(8,128)(2,1)S(1)}, u32[]{:S(2)}, u32[]{:S(2)}) collective-permute-start(bf16[2,32,1024]{2,1,0:T(8,128)(2,1)S(1)} %get-tuple-element.37), channel_id=1, source_target_pairs={{24,0},{32,8},{40,16},{48,24},{56,32},{64,40},{72,48},{80,56},{88,... | collective-permute-start | bytes 393224 | tf_op jit(solution)/shard_map/ppermute | solution.py:352
  93.1 25.6 %collective-permute-start.11 = (bf16[2,128,1024]{2,1,0:T(8,128)(2,1)S(1)}, bf16[2,128,1024]{2,1,0:T(8,128)(2,1)S(1)}, u32[]{:S(2)}, u32[]{:S(2)}) collective-permute-start(bf16[2,128,1024]{2,1,0:T(8,128)(2,1)S(1)} %collective-permute-done.10.coarse2), channel_id=1, source_target_pairs={{0,384},{8,392},{16,400},{24,408},{32,416},{40,424},{48,432},{56,4... | collective-permute-start | bytes 1572872 | tf_op jit(solution)/shard_map/ppermute | solution.py:362
  98.5 20.3 %collective-permute-start.7 = (bf16[2,128,1024]{2,1,0:T(8,128)(2,1)S(1)}, bf16[2,128,1024]{2,1,0:T(8,128)(2,1)S(1)}, u32[]{:S(2)}, u32[]{:S(2)}) collective-permute-start(bf16[2,128,1024]{2,1,0:T(8,128)(2,1)S(1)} %get-tuple-element.40.up), channel_id=1, source_target_pairs={{0,8},{8,16},{16,24},{24,32},{32,40},{40,48},{48,56},{56,64},{64,7... | collective-permute-start | bytes 1572872 | tf_op jit(solution)/shard_map/ppermute | solution.py:352
  101.1 17.7 %collective-permute-start.8 = (bf16[2,128,1024]{2,1,0:T(8,128)(2,1)S(1)}, bf16[2,128,1024]{2,1,0:T(8,128)(2,1)S(1)}, u32[]{:S(2)}, u32[]{:S(2)}) collective-permute-start(bf16[2,128,1024]{2,1,0:T(8,128)(2,1)S(1)} %get-tuple-element.41.down), channel_id=1, source_target_pairs={{8,0},{16,8},{24,16},{32,24},{40,32},{48,40},{56,48},{64,56},{72,6... | collective-permute-start | bytes 1572872 | tf_op jit(solution)/shard_map/ppermute | solution.py:352
  135.0 13.1 %collective-permute-start.12 = (bf16[256,1024]{1,0:T(8,128)(2,1)S(1)}, bf16[256,1024]{1,0:T(8,128)(2,1)S(1)}, u32[]{:S(2)}, u32[]{:S(2)}) collective-permute-start(bf16[256,1024]{1,0:T(8,128)(2,1)S(1)} %get-tuple-element.50), channel_id=1, source_target_pairs={{0,4},{4,0},{1,5},{5,1},{2,6},{6,2},{3,7},{7,3},{8,12},{12,8},{9,1... | collective-permute-start | bytes 1572872 | tf_op jit(solution)/shard_map/ppermute | solution.py:347
